TPU v7x, 32 devices: a whole 2x2x4 slice. The times are simulated.
32 devices in a mesh: grp: 2 (over y), band: 4 (over z), var: 2 (over x), sub: 2 (over core).
Axes of the slice: x: 2, y: 2, z: 4, core: 2. Of those that a mesh axis runs over, the one named last changes fastest.
Arguments:
- ocean_fields: bfloat16 [576, 4, 48, 128], P(('grp', 'band', 'sub'), None, 'var'), parts along dimension 0, may hold values from -6 to 6
- ocean_dest: int32 [288, 1], P(('band', 'sub')), may hold values from 0 to 3, as said below
- ocean_weights: bfloat16 [4, 2, 4, 14, 128, 128], P('band', 'sub'), may hold values from -0.5 to 0.5
- ocean_tiles: int32 [4, 2, 4, 14], P('band', 'sub'), may hold values from 0 to 15, as said below
- atmos_fields: bfloat16 [576, 4, 48, 128], P(('grp', 'band', 'sub'), None, 'var'), parts along dimension 0, may hold values from -6 to 6
- atmos_dest: int32 [288, 1], P(('band', 'sub')), may hold values from 0 to 3, as said below
- atmos_weights: bfloat16 [4, 2, 4, 14, 128, 128], P('band', 'sub'), may hold values from -0.5 to 0.5
- atmos_tiles: int32 [4, 2, 4, 14], P('band', 'sub'), may hold values from 0 to 15, as said below
- land_fraction: float32 [4, 2, 8, 2, 128], P('band', 'sub'), may hold values from 0 to 1
- embed_weight: bfloat16 [12288, 1024], P(('var', 'sub')), may hold values from -0.0546875 to 0.0546875
- embed_bias: float32 [1024], replicated, may hold values from -4 to 4
- embed_gain: float32 [1024], replicated, may hold values from 0.5 to 1.5
Outputs:
- patch_embed: bfloat16 [2, 8, 4, 8, 1024], P('sub', 'var', None, ('grp', 'band')), parts along dimension 3
There are 2 independent parts, one for each index of `grp`. A program takes and returns all parts, laid end to end along the dimension named above; an argument that names none is the same for every part. Nothing has to cross between parts.
Inputs may be any that keep to these rules, and one draw needn't show every extreme that they name: `ocean_dest`: each device holds at least 4 and at most 14 blocks naming each band; one band is named by exactly 14 blocks on every device. `atmos_dest`: each device holds at least 4 and at most 14 blocks naming each band; one band is named by exactly 14 blocks on every device. `ocean_tiles`: for each band b and half h, the entries [b, h, j, r] with r < 4 name every half-patch. `atmos_tiles`: for each band b and half h, the entries [b, h, j, r] with r < 4 name every half-patch.
All inputs are finite; a program needn't handle non-finite values.
Results may differ from a plain program's by a relative error of at most 0.0045.
Values may be sent and summed in bfloat16 or wider, within the bound.
No kernel may reach another device: no remote copies, remote signals or barrier semaphores. Data moves between devices by JAX's collectives and lax.ppermute only.
A program may use at most 128 MiB of HBM per device.

v0:
```python
import jax
import jax.numpy as jnp
from jax import lax
from jax.sharding import PartitionSpec as P


def slot_blocks(fields, targets, band_count, slot_cap):
    block_count = fields.shape[0]
    serial = jnp.arange(block_count, dtype=jnp.int32)
    dest_band = targets[:, 0]
    earlier = (dest_band[:, None] == dest_band[None, :]) & (serial[None, :] < serial[:, None])
    position = jnp.sum(earlier.astype(jnp.int32), axis=1)
    slot_index = dest_band * slot_cap + position
    placing = (
        slot_index[:, None] == jnp.arange(band_count * slot_cap, dtype=jnp.int32)[None, :]
    ).astype(jnp.bfloat16)
    flattened = fields.reshape(block_count, -1)
    packed = jnp.einsum("gs,gk->sk", placing, flattened, preferred_element_type=jnp.float32).astype(
        jnp.bfloat16
    )
    return packed.reshape((band_count, slot_cap) + fields.shape[1:])


def regrid_owner(received, weights, tile_lookup, patches):
    slot_total = received.shape[0] * received.shape[1]
    steps_time = received.shape[2]
    var_local = received.shape[3]
    block_rows = received.shape[4]
    stacked = received.reshape(slot_total, steps_time * var_local, block_rows)
    block_weights = weights.reshape(slot_total, block_rows, weights.shape[-1])
    products = jnp.einsum(
        "smb,sbh->smh", stacked, block_weights, preferred_element_type=jnp.float32
    )
    tile_ids = tile_lookup.reshape(slot_total)
    placing = (tile_ids[None, :] == jnp.arange(2 * patches, dtype=jnp.int32)[:, None]).astype(
        jnp.float32
    )
    placing = placing.reshape(patches, 2, slot_total)
    gathered = jnp.einsum("pqs,smh->pmqh", placing, products, precision=lax.Precision.HIGHEST)
    return gathered.reshape(patches, steps_time, var_local, 2, gathered.shape[-1])


def embed_patches(row_feats, embed_weight, embed_bias, embed_gain):
    partial_sum = jnp.dot(
        row_feats,
        lax.all_gather(embed_weight, "sub", axis=0, tiled=True),
        preferred_element_type=jnp.float32,
    )
    summed = lax.psum_scatter(partial_sum, "var", scatter_dimension=0, tiled=True)
    shifted = summed + embed_bias
    inverse = lax.rsqrt(jnp.mean(shifted * shifted, axis=-1, keepdims=True) + 1e-05)
    return (shifted * inverse * embed_gain).astype(jnp.bfloat16)


def per_device(
    ocean_fields,
    ocean_dest,
    ocean_weights,
    ocean_tiles,
    atmos_fields,
    atmos_dest,
    atmos_weights,
    atmos_tiles,
    land_fraction,
    embed_weight,
    embed_bias,
    embed_gain,
):
    band_count = lax.axis_size("band")
    var_count = lax.axis_size("var")
    slot_cap = ocean_weights.shape[3]
    patches = land_fraction.shape[2]
    send_ocean = slot_blocks(ocean_fields, ocean_dest, band_count, slot_cap)
    send_atmos = slot_blocks(atmos_fields, atmos_dest, band_count, slot_cap)
    recv_ocean, recv_atmos = (
        lax.all_to_all(send_ocean, "band", split_axis=0, concat_axis=0, tiled=True),
        lax.all_to_all(send_atmos, "band", split_axis=0, concat_axis=0, tiled=True),
    )
    ocean_part = regrid_owner(recv_ocean, ocean_weights, ocean_tiles, patches)
    atmos_part = regrid_owner(recv_atmos, atmos_weights, atmos_tiles, patches)
    land_frac = land_fraction.reshape(patches, 1, 1, 2, land_fraction.shape[-1])
    merged = (land_frac * atmos_part + (1.0 - land_frac) * ocean_part).astype(jnp.bfloat16)
    steps_time = merged.shape[1]
    width = merged.shape[2] * merged.shape[3] * merged.shape[4]
    share = patches // var_count
    regrouped = lax.all_to_all(merged, "band", split_axis=1, concat_axis=1, tiled=True)
    finished = embed_patches(regrouped.reshape(-1, width), embed_weight, embed_bias, embed_gain)
    return finished.reshape(1, share, band_count, steps_time // band_count, finished.shape[-1])


def solution(mesh):
    in_specs = (
        P(("grp", "band", "sub"), None, "var", None),
        P(("band", "sub"), None),
        P("band", "sub", None, None, None, None),
        P("band", "sub", None, None),
        P(("grp", "band", "sub"), None, "var", None),
        P(("band", "sub"), None),
        P("band", "sub", None, None, None, None),
        P("band", "sub", None, None),
        P("band", "sub", None, None, None),
        P(("var", "sub"), None),
        P(),
        P(),
    )
    out_specs = P("sub", "var", None, ("grp", "band"), None)
    return jax.shard_map(
        per_device, mesh=mesh, in_specs=in_specs, out_specs=out_specs, check_vma=False
    )
```

profile of v0, /device:TPU:0, one launch (start us, length us, event | category | flops | bytes accessed | tf_op | source)
XLA Modules:
  0.0 135.7 jit_solution(6290667516423531903)
XLA Ops:
  6.5 0.0 copy-start
  6.5 0.0 all-gather.2.cloned.1.call-start
  6.5 0.7 all-gather.2.cloned.1.call-update
  7.3 0.6 copy-done.2
  7.8 0.1 pad.1
  7.9 0.4 copy.57
  8.3 0.2 copy-done.8
  8.5 0.2 convert_reduce_fusion
  8.7 0.6 fusion.5
  9.3 1.4 %copy.58 = bf16[7,8,96,128]{3,2,1,0:T(8,128)(2,1)} copy(bf16[7,8,96,128]{3,1,2,0:T(8,128)(2,1)S(1)} %fusion.5) | data formatting | bytes 2752512
  10.7 6.3 %all-to-all-start.1 = ((bf16[4,14,4,24,128]{4,3,2,1,0:T(8,128)(2,1)}), bf16[4,14,4,24,128]{4,3,2,1,0:T(8,128)(2,1)S(1)}, u32[]{:S(2)}, u32[]{:S(2)}) async-start(bf16[4,14,4,24,128]{4,3,2,1,0:T(8,128)(2,1)} %bitcast.64), calls=%async_computation.1 | async-start | bytes 2752512 | tf_op jit(solution)/shard_map/all_to_all | solution.py:76
  17.0 1.4 %pad = bf16[40,96,128]{2,1,0:T(8,128)(2,1)S(1)} pad(bf16[36,96,128]{2,1,0:T(8,128)(2,1)} %bitcast.73, bf16[]{:T(256)} %constant.25), padding=0_4x0_0x0_0 | pad | bytes 1867778
  18.5 0.4 copy.55
  18.9 0.0 copy-done.9
  18.9 0.2 convert_reduce_fusion.1
  19.1 0.6 fusion.4
  19.7 1.3 copy.56
  21.1 28.7 %all-to-all-done.1 = bf16[4,14,4,24,128]{4,3,2,1,0:T(8,128)(2,1)S(1)} async-done(((bf16[4,14,4,24,128]{4,3,2,1,0:T(8,128)(2,1)}), bf16[4,14,4,24,128]{4,3,2,1,0:T(8,128)(2,1)S(1)}, u32[]{:S(2)}, u32[]{:S(2)}) %all-to-all-start.1) | async-done | bytes 1376288 | tf_op jit(solution)/shard_map/all_to_all | solution.py:76
  49.8 4.3 %all-to-all-start = ((bf16[4,14,4,24,128]{4,3,2,1,0:T(8,128)(2,1)}), bf16[4,14,4,24,128]{4,3,2,1,0:T(8,128)(2,1)}, u32[]{:S(2)}, u32[]{:S(2)}) async-start(bf16[4,14,4,24,128]{4,3,2,1,0:T(8,128)(2,1)} %bitcast.63), calls=%async_computation | async-start | bytes 2752512 | tf_op jit(solution)/shard_map/all_to_all | solution.py:77
  54.1 0.0 reduce-scatter.2.cloned.1.call-start
  54.2 0.0 copy-done.6
  54.2 0.1 eq.125
  54.3 0.0 copy-done.7
  54.3 0.1 eq.110
  54.3 0.0 copy-done.3
  54.4 0.0 copy-done
  54.4 2.1 %convolution_bitcast_fusion = f32[56,96,128,1]{2,1,0,3:T(8,128)} fusion(bf16[56,96,128]{2,1,0:T(8,128)(2,1)S(1)} %bitcast.62, bf16[56,128,128]{2,1,0:T(8,128)(2,1)S(1)} %bitcast.61), kind=kOutput, calls=%fused_computation.6 | convolution fusion | flops 176160768 | bytes 5963776 | tf_op jit(solution)/shard_map/smb,sbh->smh/dot_general | solution.py:31
  56.5 29.9 %all-to-all-done = bf16[4,14,4,24,128]{4,3,2,1,0:T(8,128)(2,1)} async-done(((bf16[4,14,4,24,128]{4,3,2,1,0:T(8,128)(2,1)}), bf16[4,14,4,24,128]{4,3,2,1,0:T(8,128)(2,1)}, u32[]{:S(2)}, u32[]{:S(2)}) %all-to-all-start) | async-done | bytes 1376288 | tf_op jit(solution)/shard_map/all_to_all | solution.py:77
  86.4 2.7 %convolution_bitcast_fusion.1 = f32[56,96,128,1]{2,1,0,3:T(8,128)S(1)} fusion(bf16[56,96,128]{2,1,0:T(8,128)(2,1)} %bitcast.4, bf16[56,128,128]{2,1,0:T(8,128)(2,1)} %bitcast.71), kind=kOutput, calls=%fused_computation.7 | convolution fusion | flops 176160768 | bytes 5963776 | tf_op jit(solution)/shard_map/smb,sbh->smh/dot_general | solution.py:31
  89.1 0.1 copy-done.1
  89.2 2.6 %fusion = f32[96,128,8,2]{1,2,3,0:T(8,128)S(1)} fusion(f32[56,96,128,1]{2,1,0,3:T(8,128)S(1)} %copy-done.1, s32[56]{0:T(128)S(1)} %eq.125, s32[8,2]{0,1:T(2,128)S(1)} %multiply_add_fusion), kind=kOutput, calls=%fused_computation.2 | convolution fusion | flops 132121472 | bytes 3539232 | tf_op jit(solution)/shard_map/pqs,smh->pmqh/dot_general | solution.py:39
  91.7 2.6 %fusion.2 = f32[96,128,8,2]{1,2,3,0:T(8,128)S(1)} fusion(f32[56,96,128,1]{2,1,0,3:T(8,128)S(1)} %convolution_bitcast_fusion.1, s32[8,2]{0,1:T(2,128)S(1)} %multiply_add_fusion, s32[56]{0:T(128)S(1)} %eq.110), kind=kOutput, calls=%fused_computation.4 | convolution fusion | flops 132121472 | bytes 3539232 | tf_op jit(solution)/shard_map/pqs,smh->pmqh/dot_general | solution.py:39
  94.3 0.5 fusion.7
  94.8 0.3 copy.42
  95.1 13.6 %all_to_all.15 = bf16[8,4,24,2,128]{4,3,2,0,1:T(2,128)(2,1)S(1)} all-to-all(bf16[8,4,24,2,128]{4,3,2,0,1:T(2,128)(2,1)S(1)} %copy.42), channel_id=1, replica_groups=mesh['grp'=2,'band'=4,'var'=2,'sub'=2] {'band'}, dimensions={1} | all-to-all | bytes 786432 | tf_op jit(solution)/shard_map/all_to_all | solution.py:86
  108.7 0.3 copy.43
  108.9 0.3 reshape.95
  109.2 0.0 copy-start.4
  109.3 0.0 copy-start.5
  109.3 0.0 all-gather.2.cloned.1.call-done
  109.3 7.5 %fusion.22 = f32[32,1024]{1,0:T(8,128)} fusion(bf16[32,6144]{1,0:T(8,128)(2,1)S(1)} %reshape.95, bf16[6144,1024]{1,0:T(8,128)(2,1)} %all-gather.2.cloned.1.call-done), kind=kOutput, calls=%fused_computation.40 | convolution fusion | flops 402653184 | bytes 13107200 | tf_op jit(solution)/shard_map/dot_general | solution.py:44
  116.8 0.0 reduce-scatter.2.cloned.1.call-update
  116.8 9.5 %reduce-scatter.2.cloned.1.call-done = f32[16,1024]{1,0:T(8,128)} async-done(((f32[32,1024]{1,0:T(8,128)}), f32[16,1024]{1,0:T(8,128)}) %reduce-scatter.2.cloned.1.call-update) | async-done | bytes 65552 | tf_op jit(solution)/shard_map/reduce_scatter | solution.py:49
  126.3 0.0 copy-done.4
  126.3 1.0 multiply_reduce_fusion
  127.3 0.0 copy-done.5
  127.3 0.9 multiply_convert_fusion
  128.2 0.6 reshape.96
  (12 shorter events, 0.0 us)
Async XLA Ops:
  6.5 47.8 %copy-start = (bf16[1,1,4,14,128,128]{5,4,3,2,1,0:T(8,128)(2,1)S(1)}, bf16[1,1,4,14,128,128]{5,4,3,2,1,0:T(8,128)(2,1)}, u32[]{:S(2)}) copy-start(bf16[1,1,4,14,128,128]{5,4,3,2,1,0:T(8,128)(2,1)} %param.14) | copy-start | bytes 5505028
  6.5 1.3 copy-start.2
  6.5 102.7 %all-gather.2.cloned.1.call-start = ((), (), s32[]{:S(2)}) async-start(), calls=%async_computation.4 | async-start | bytes 18874368 | tf_op jit(solution)/shard_map/all_gather | solution.py:46
  7.8 0.7 copy-start.8
  10.7 39.1 %all-to-all-start.1 = ((bf16[4,14,4,24,128]{4,3,2,1,0:T(8,128)(2,1)}), bf16[4,14,4,24,128]{4,3,2,1,0:T(8,128)(2,1)S(1)}, u32[]{:S(2)}, u32[]{:S(2)}) async-start(bf16[4,14,4,24,128]{4,3,2,1,0:T(8,128)(2,1)} %bitcast.64), calls=%async_computation.1 | async-start | bytes 2752512 | tf_op jit(solution)/shard_map/all_to_all | solution.py:76
  17.0 1.8 %copy-start.9 = (s32[36,1]{0,1:T(1,128)S(1)}, s32[36,1]{0,1:T(1,128)}, u32[]{:S(2)}) copy-start(s32[36,1]{0,1:T(1,128)} %param.17) | copy-start | bytes 436
  21.1 33.1 %copy-start.6 = (s32[1,1,4,14]{3,2,1,0:T(4,128)S(1)}, s32[1,1,4,14]{3,2,1,0:T(4,128)}, u32[]{:S(2)}) copy-start(s32[1,1,4,14]{3,2,1,0:T(4,128)} %param.15) | copy-start | bytes 676
  21.1 33.2 %copy-start.7 = (s32[1,1,4,14]{3,2,1,0:T(4,128)S(1)}, s32[1,1,4,14]{3,2,1,0:T(4,128)}, u32[]{:S(2)}) copy-start(s32[1,1,4,14]{3,2,1,0:T(4,128)} %param.19) | copy-start | bytes 676
  21.1 33.3 %copy-start.3 = (f32[1,1,8,2,128]{4,3,2,1,0:T(2,128)S(1)}, f32[1,1,8,2,128]{4,3,2,1,0:T(2,128)}, u32[]{:S(2)}) copy-start(f32[1,1,8,2,128]{4,3,2,1,0:T(2,128)} %param.20) | copy-start | bytes 24580
  49.8 36.6 %all-to-all-start = ((bf16[4,14,4,24,128]{4,3,2,1,0:T(8,128)(2,1)}), bf16[4,14,4,24,128]{4,3,2,1,0:T(8,128)(2,1)}, u32[]{:S(2)}, u32[]{:S(2)}) async-start(bf16[4,14,4,24,128]{4,3,2,1,0:T(8,128)(2,1)} %bitcast.63), calls=%async_computation | async-start | bytes 2752512 | tf_op jit(solution)/shard_map/all_to_all | solution.py:77
  54.1 72.2 %reduce-scatter.2.cloned.1.call-start = ((), (), s32[]{:S(2)}) async-start(), calls=%async_computation.5 | async-start | bytes 196608 | tf_op jit(solution)/shard_map/reduce_scatter | solution.py:49
  86.4 2.7 %copy-start.1 = (f32[56,96,128,1]{2,1,0,3:T(8,128)S(1)}, f32[56,96,128,1]{2,1,0,3:T(8,128)}, u32[]{:S(2)}) copy-start(f32[56,96,128,1]{2,1,0,3:T(8,128)} %convolution_bitcast_fusion) | copy-start | bytes 8257540
  109.2 17.1 %copy-start.4 = (f32[1024]{0:T(1024)S(1)}, f32[1024]{0:T(1024)}, u32[]{:S(2)}) copy-start(f32[1024]{0:T(1024)} %param.22) | copy-start | bytes 12292
  109.3 18.0 %copy-start.5 = (f32[1024]{0:T(1024)S(1)}, f32[1024]{0:T(1024)}, u32[]{:S(2)}) copy-start(f32[1024]{0:T(1024)} %param.23) | copy-start | bytes 12292
Sparse Core Ops, SparseCore 0:
  8.9 27.5 all-gather.1
  116.9 9.3 reduce-scatter.1
where the time goes:
time: 136 us
  waiting for transfers between devices  68.9 us (51%)
  matrix products  18.7 us (14%)
  blocking collectives  13.6 us (10%)
  between operations  13.6 us (10%)
  starting transfers between devices  10.7 us (8%)
  local copies, waits for them, and re-layouts  7.55 us (6%)
  other arithmetic  2.75 us (2%)
    all_to_all x1, waiting for transfers between devices, per_device(): lax.all_to_all(send_atmos, 'band', split_axis=0, concat_axis=0, tiled=True)  29.9 us
    all_to_all x1, waiting for transfers between devices, per_device(): lax.all_to_all(send_ocean, 'band', split_axis=0, concat_axis=0, tiled=True)  28.7 us
    all_to_all x1, blocking collectives, per_device(): lax.all_to_all(merged, 'band', split_axis=1, concat_axis=1, tiled=True)  13.6 us
    reduce_scatter x1, waiting for transfers between devices, embed_patches(): lax.psum_scatter(partial_sum, 'var', scatter_dimension=0, tiled=True)  9.51 us
    dot_general x1, matrix products, embed_patches(): jnp.dot(row_feats, lax.all_gather(embed_weight, 'sub', axis=0, tiled=True...  7.49 us
    all_to_all x1, starting transfers between devices, per_device(): lax.all_to_all(send_ocean, 'band', split_axis=0, concat_axis=0, tiled=True)  6.32 us
    unnamed x26, local copies, waits for them, and re-layouts  5.89 us
    dot_general x2, matrix products, regrid_owner(): jnp.einsum('pqs,smh->pmqh', placing, products, precision=lax.Precision.HI...  5.12 us
  transfers between devices with their start and end apart: 4, of which 3 were waited for; matrix products, arithmetic and copies ran while one was open for 13% of the time, Pallas kernels for 0%

commit v1 on v0

v1 whole, which is shorter than its diff:
```python
import functools

import jax
import jax.numpy as jnp
from jax import lax
from jax.experimental import pallas as pl
from jax.experimental.pallas import tpu as pltpu
from jax.sharding import PartitionSpec as P

REPL = ("grp", "var")


def slot_tables(dest, band_count, cap):
    count = dest.shape[0]
    serial = jnp.arange(count, dtype=jnp.int32)
    band_of = dest[:, 0]
    earlier = (band_of[:, None] == band_of[None, :]) & (serial[None, :] < serial[:, None])
    position = jnp.sum(earlier.astype(jnp.int32), axis=1)
    slot = band_of * cap + position
    hit = slot[None, :] == jnp.arange(band_count * cap, dtype=jnp.int32)[:, None]
    block = jnp.sum(jnp.where(hit, serial[None, :], 0), axis=1)
    used = jnp.any(hit, axis=1)
    return block.reshape(band_count, cap), used.reshape(band_count, cap)


def regrid_kernel(part_slots, table, where, *refs):
    part_count = len(part_slots)
    fields, land = refs[0], refs[1]
    parts = refs[2 : 2 + part_count]
    out, acc = refs[-2], refs[-1]
    acc[...] = jnp.zeros_like(acc)
    slots = table.shape[2]
    band = where[0]
    for at, (part, size) in enumerate(zip(parts, part_slots)):
        first = where[1 + at]

        def product(s, part=part, first=first):
            block = table[0, band, first + s]
            scale = table[2, band, first + s]
            w = part[0, s] if len(part.shape) == 4 else part[s]
            dense = jnp.dot(fields[block], w, preferred_element_type=jnp.float32)
            return dense * land[band, pl.ds(scale, 1), :]

        for s in range(size):
            tile = table[1, band, first + s]
            acc[tile] += product(s)
    out[0] = acc[...].astype(out.dtype)


def regrid(table, where, fields, land, parts, part_slots, own, previous, band_count, tiles):
    rows, cells = fields.shape[1], parts[0].shape[-1]
    whole = lambda a: pl.BlockSpec(a.shape, lambda i, t, w, n=a.ndim: (0,) * n)
    part_specs = []
    for part in parts:
        if own:
            part_specs.append(pl.BlockSpec((1,) + part.shape[1:], lambda i, t, w: (w[0], 0, 0, 0)))
        else:
            part_specs.append(whole(part))
    in_specs = [whole(fields), whole(land)] + part_specs
    operands = [fields, land] + list(parts)
    aliases = {}
    if previous is not None:
        aliases = {2 + len(operands): 0}
        in_specs.append(pl.BlockSpec(memory_space=pl.ANY))
        operands.append(previous)
    total = sum(part_slots)
    return pl.pallas_call(
        functools.partial(regrid_kernel, tuple(part_slots)),
        out_shape=jax.ShapeDtypeStruct((band_count, tiles, rows, cells), jnp.bfloat16),
        grid_spec=pltpu.PrefetchScalarGridSpec(
            num_scalar_prefetch=2,
            grid=(1,),
            in_specs=in_specs,
            out_specs=pl.BlockSpec((1, tiles, rows, cells), lambda i, t, w: (w[0], 0, 0, 0)),
            scratch_shapes=[pltpu.VMEM((tiles, rows, cells), jnp.float32)],
        ),
        input_output_aliases=aliases,
        cost_estimate=pl.CostEstimate(
            flops=2 * total * rows * cells * cells, bytes_accessed=6 << 20, transcendentals=0
        ),
        compiler_params=pltpu.CompilerParams(vmem_limit_bytes=24 << 20),
    )(table, where, *operands)


def other(x, axis):
    return lax.ppermute(x, axis, [(0, 1), (1, 0)])


def per_device(
    ocean_fields,
    ocean_dest,
    ocean_weights,
    ocean_tiles,
    atmos_fields,
    atmos_dest,
    atmos_weights,
    atmos_tiles,
    land_fraction,
    embed_weight,
    embed_bias,
    embed_gain,
):
    nb = lax.axis_size("band")
    nv = lax.axis_size("var")
    ng = lax.axis_size("grp")
    rep = nv * ng
    cap = ocean_weights.shape[3]
    cells = ocean_weights.shape[-1]
    block_count, steps, local_vars, _ = ocean_fields.shape
    patches = land_fraction.shape[2]
    tiles = 2 * patches
    slots = 2 * cap
    me = lax.axis_index("band")
    x, y = lax.axis_index("var"), lax.axis_index("grp")
    quarter = y * nv + x

    embed_other = other(embed_weight, "sub")

    ocean_w = ocean_weights.reshape(nb, cap, cells, cells)
    atmos_w = atmos_weights.reshape(nb, cap, cells, cells)
    both = jnp.concatenate([ocean_w, atmos_w], axis=1).reshape(nb, slots * cells, cells)
    share_rows = slots * cells // rep

    tile_ids = jnp.concatenate([ocean_tiles.reshape(nb, cap), atmos_tiles.reshape(nb, cap)], axis=1)
    flat = tile_ids.reshape(-1).astype(jnp.float32)
    tile_rows = -(-flat.shape[0] // cells)
    flat = jnp.pad(flat, (0, tile_rows * cells - flat.shape[0])).reshape(tile_rows, cells)
    meta = lax.all_gather(
        jnp.concatenate([land_fraction.reshape(tiles, cells), flat], axis=0), "band", axis=0
    )
    land_all = meta[:, :tiles]
    land_all = jnp.concatenate(
        [1.0 - land_all, land_all, jnp.zeros((nb, 8, cells), jnp.float32)], axis=1
    )
    tile_all = meta[:, tiles:].reshape(nb, -1)[:, : nb * slots].reshape(nb, nb, slots)
    tile_all = lax.dynamic_index_in_dim(tile_all, me, 1, keepdims=False).astype(jnp.int32)
    ocean_block, ocean_used = slot_tables(ocean_dest, nb, cap)
    atmos_block, atmos_used = slot_tables(atmos_dest, nb, cap)
    block_all = jnp.concatenate([ocean_block, atmos_block + block_count], axis=1)
    used_all = jnp.concatenate([ocean_used, atmos_used], axis=1)
    grid_row = jnp.where(jnp.arange(slots) < cap, 0, tiles)[None, :]
    scale_all = jnp.where(used_all, tile_all + grid_row, 2 * tiles)
    table = jnp.stack([block_all, tile_all, scale_all]).astype(jnp.int32)
    fields = jnp.concatenate([ocean_fields, atmos_fields], axis=0).reshape(
        2 * block_count, steps * local_vars, cells
    )

    call = functools.partial(regrid, band_count=nb, tiles=tiles)
    own_where = jnp.stack([me, jnp.int32(0), jnp.int32(cap)]).astype(jnp.int32)
    partial_rows = call(
        table, own_where, fields, land_all, [ocean_w, atmos_w], [cap, cap], True, None
    )
    order = [1, nb - 1] + list(range(2, nb - 1))
    for shift in order[: nb - 1]:
        target = (me + shift) % nb
        piece = lax.dynamic_slice(
            both, (target, quarter * share_rows, 0), (1, share_rows, cells)
        )[0]
        piece = lax.ppermute(piece, "band", [(b, (b + shift) % nb) for b in range(nb)])
        band = (me - shift) % nb
        if nv == 2 and ng == 2 and slots % rep == 0:
            each = slots // rep
            head = (each + 1) // 2
            piece = piece.reshape(each, cells, cells)
            by_x = other(piece, "var")
            by_y = other(piece, "grp")
            on_y = other(by_x[:head], "grp")
            on_x = other(by_y[head:], "var")
            qx = y * nv + (1 - x)
            qy = (1 - y) * nv + x
            qd = (1 - y) * nv + (1 - x)
            parts = [piece, by_x, by_y, on_y, on_x]
            sizes = [each, each, each, head, each - head]
            firsts = [quarter * each, qx * each, qy * each, qd * each, qd * each + head]
        else:
            parts = [
                lax.all_gather(piece, REPL, axis=0, tiled=True).reshape(slots, cells, cells)
            ]
            sizes, firsts = [slots], [jnp.int32(0)]
        where = jnp.stack([band] + firsts).astype(jnp.int32)
        partial_rows = call(
            table, where, fields, land_all, parts, sizes, False, partial_rows
        )

    share, local_steps = patches // nv, steps // nb
    rows = partial_rows.reshape(nb, nv, share, 2, nb, local_steps, local_vars, cells)
    rows = rows.transpose(4, 1, 2, 0, 5, 6, 3, 7)
    rows = rows.reshape(-1, 2, local_vars // 2 * 2 * cells)
    sub = lax.axis_index("sub")
    mine = lax.dynamic_index_in_dim(rows, sub, 1, keepdims=False)
    theirs = lax.dynamic_index_in_dim(rows, 1 - sub, 1, keepdims=False)
    summed = jnp.dot(mine, embed_weight, preferred_element_type=jnp.float32)
    summed = summed + jnp.dot(theirs, embed_other, preferred_element_type=jnp.float32)
    width = summed.shape[-1]
    sent = summed.astype(jnp.bfloat16).reshape(nb * nv, -1, width)
    got = lax.all_to_all(sent, ("band", "var"), split_axis=0, concat_axis=0, tiled=True)
    shifted = jnp.sum(got.astype(jnp.float32), axis=0) + embed_bias
    inverse = lax.rsqrt(jnp.mean(shifted * shifted, axis=-1, keepdims=True) + 1e-05)
    finished = (shifted * inverse * embed_gain).astype(jnp.bfloat16)
    return finished.reshape(1, share, nb, local_steps, width)


def solution(mesh):
    in_specs = (
        P(("grp", "band", "sub"), None, "var", None),
        P(("band", "sub"), None),
        P("band", "sub", None, None, None, None),
        P("band", "sub", None, None),
        P(("grp", "band", "sub"), None, "var", None),
        P(("band", "sub"), None),
        P("band", "sub", None, None, None, None),
        P("band", "sub", None, None),
        P("band", "sub", None, None, None),
        P(("var", "sub"), None),
        P(),
        P(),
    )
    out_specs = P("sub", "var", None, ("grp", "band"), None)
    return jax.shard_map(
        per_device, mesh=mesh, in_specs=in_specs, out_specs=out_specs, check_vma=False
    )
```

time: 136 us -> 93.9 us (0.69)
  waiting for transfers between devices: 68.9 us -> 3.78 us
  blocking collectives: 13.6 us -> 37.2 us
  between operations: 13.6 us -> 0.28 us
  matrix products: 18.7 us -> 7.75 us
  starting transfers between devices: 10.7 us -> 20.8 us
  Pallas kernels: 0 us -> 6.27 us
  local copies, waits for them, and re-layouts: 7.55 us -> 11.4 us
  other arithmetic: 2.75 us -> 6.04 us
    all_to_all x2 -> x0, waiting for transfers between devices: 58.6 us -> none  [the longest x1 29.9 us: per_device(): lax.all_to_all(send_atmos, 'band', split_axis=0, concat_axis=0, tiled=True)]
    all_gather x0 -> x1, blocking collectives: none -> 24.8 us  [per_device(): lax.all_gather(jnp.concatenate([land_fraction.reshape(tiles, cells), flat...]
    ppermute x0 -> x16, starting transfers between devices: none -> 20.8 us  [the longest x13 15.2 us: other(): return lax.ppermute(x, axis, [(0, 1), (1, 0)])]
    dot_general x7 -> x2, matrix products: 18.7 us -> 7.75 us  [the longest x1 3.89 us: per_device(): jnp.dot(theirs, embed_other, preferred_element_type=jnp.float32)]
    all_to_all x2 -> x0, starting transfers between devices: 10.6 us -> none  [the longest x1 6.32 us: per_device(): lax.all_to_all(send_ocean, 'band', split_axis=0, concat_axis=0, tiled=True)]
    reduce_scatter x1 -> x0, waiting for transfers between devices: 9.51 us -> none  [embed_patches(): lax.psum_scatter(partial_sum, 'var', scatter_dimension=0, tiled=True)]
    pallas_call x0 -> x4, Pallas kernels: none -> 6.27 us  [regrid(): pl.pallas_call(functools.partial(regrid_kernel, tuple(part_slots)), out_s...]
    concatenate x0 -> x3, other arithmetic: none -> 4.09 us  [the longest x1 2.42 us: per_device(): jnp.concatenate([ocean_w, atmos_w], axis=1)]
  transfers between devices with their start and end apart: 4 -> 16, of which waited for: 3 -> 3; matrix products, arithmetic and copies ran while one was open for 13% -> 19% of each run, Pallas kernels for 0% -> 7%
where the time goes in v1:
time: 93.9 us; the launch traced here: 93.6 us
  blocking collectives  37.2 us (40%)
  starting transfers between devices  20.8 us (22%)
  local copies, waits for them, and re-layouts  11.4 us (12%)
  matrix products  7.75 us (8%)
  Pallas kernels  6.27 us (7%)
  other arithmetic  6.04 us (6%)
  waiting for transfers between devices  3.78 us (4%)
    all_gather x1, blocking collectives, per_device(): lax.all_gather(jnp.concatenate([land_fraction.reshape(tiles, cells), flat...  24.8 us
    ppermute x13, starting transfers between devices, other(): return lax.ppermute(x, axis, [(0, 1), (1, 0)])  15.2 us
    all_to_all x1, blocking collectives, per_device(): lax.all_to_all(sent, ('band', 'var'), split_axis=0, concat_axis=0, tiled=...  12.4 us
    pallas_call x4, Pallas kernels, regrid(): pl.pallas_call(functools.partial(regrid_kernel, tuple(part_slots)), out_s...  6.27 us
    ppermute x3, starting transfers between devices, per_device(): lax.ppermute(piece, 'band', [(b, (b + shift) % nb) for b in range(nb)])  5.67 us
    dot_general x1, matrix products, per_device(): jnp.dot(theirs, embed_other, preferred_element_type=jnp.float32)  3.89 us
    dot_general x1, matrix products, per_device(): summed = jnp.dot(mine, embed_weight, preferred_element_type=jnp.float32)  3.86 us
    ppermute x13, waiting for transfers between devices, other(): return lax.ppermute(x, axis, [(0, 1), (1, 0)])  3.77 us
  transfers between devices with their start and end apart: 16, of which 3 were waited for; matrix products, arithmetic and copies ran while one was open for 19% of the time, Pallas kernels for 7%

profile of v1, /device:TPU:0, one launch (start us, length us, event | category | flops | bytes accessed | tf_op | source)
XLA Modules:
  0.0 93.6 jit_solution(13845135306961308896)
XLA Ops:
  0.0 0.5 collective-permute-start.15
  0.5 2.4 %pad_maximum_fusion = bf16[4,28,128,128]{3,2,1,0:T(8,128)(2,1)S(1)} fusion(bf16[4,14,128,128]{3,2,1,0:T(8,128)(2,1)} %bitcast.62, bf16[4,14,128,128]{3,2,1,0:T(8,128)(2,1)} %bitcast.64), kind=kLoop, calls=%fused_computation | loop fusion | flops 1835008 | bytes 7340032 | tf_op jit(solution)/shard_map/concatenate | solution.py:121
  3.0 2.6 %collective-permute-start.10 = (bf16[896,128]{1,0:T(8,128)(2,1)S(1)}, bf16[896,128]{1,0:T(8,128)(2,1)S(1)}, u32[]{:S(2)}, u32[]{:S(2)}) collective-permute-start(bf16[896,128]{1,0:T(8,128)(2,1)S(1)} %get-tuple-element.5), channel_id=1, source_target_pairs={{0,4},{4,8},{8,12},{12,0},{1,5},{5,9},{9,13},{13,1},{2,6},{6,10},{... | collective-permute-start | bytes 688136 | tf_op jit(solution)/shard_map/ppermute | solution.py:159
  5.6 2.1 %collective-permute-start.5 = (bf16[896,128]{1,0:T(8,128)(2,1)S(1)}, bf16[896,128]{1,0:T(8,128)(2,1)}, u32[]{:S(2)}, u32[]{:S(2)}) collective-permute-start(bf16[896,128]{1,0:T(8,128)(2,1)S(1)} %get-tuple-element.6), channel_id=1, source_target_pairs={{0,12},{4,0},{8,4},{12,8},{1,13},{5,1},{9,5},{13,9},{2,14},{6,2},{... | collective-permute-start | bytes 688136 | tf_op jit(solution)/shard_map/ppermute | solution.py:159
  7.7 0.9 %collective-permute-start = (bf16[896,128]{1,0:T(8,128)(2,1)S(1)}, bf16[896,128]{1,0:T(8,128)(2,1)S(1)}, u32[]{:S(2)}, u32[]{:S(2)}) collective-permute-start(bf16[896,128]{1,0:T(8,128)(2,1)S(1)} %get-tuple-element.7), channel_id=1, source_target_pairs={{0,8},{4,12},{8,0},{12,4},{1,9},{5,13},{9,1},{13,5},{2,10},{6,14},... | collective-permute-start | bytes 688136 | tf_op jit(solution)/shard_map/ppermute | solution.py:159
  8.6 0.2 convert_reduce_fusion.1
  8.8 0.1 fusion.6
  8.9 0.1 concatenate.36
  9.0 0.2 convert_reduce_fusion.2
  9.2 0.1 fusion.7
  9.3 0.1 concatenate.35
  9.5 0.1 convert_element_type.50
  9.6 24.8 %all-gather.1 = f32[4,17,128]{2,1,0:T(8,128)S(1)} all-gather(f32[1,17,128]{2,1,0:T(8,128)S(1)} %maximum_bitcast_fusion), channel_id=2, replica_groups=mesh['grp'=2,'band'=4,'var'=2,'sub'=2] {'band'}, dimensions={0}, use_global_device_ids=true | all-gather | bytes 43520 | tf_op jit(solution)/shard_map/all_gather | solution.py:128
  34.8 0.1 select_reduce_fusion
  34.9 1.6 %collective-permute-start.12 = (bf16[7,128,128]{2,1,0:T(8,128)(2,1)S(1)}, bf16[7,128,128]{2,1,0:T(8,128)(2,1)S(1)}, u32[]{:S(2)}, u32[]{:S(2)}) collective-permute-start(bf16[7,128,128]{2,1,0:T(8,128)(2,1)S(1)} %bitcast.69), channel_id=1, source_target_pairs={{0,16},{16,0},{1,17},{17,1},{2,18},{18,2},{3,19},{19,3},{4,20},{20... | collective-permute-start | bytes 688136 | tf_op jit(solution)/shard_map/ppermute | solution.py:86
  36.5 1.5 %collective-permute-start.11 = (bf16[7,128,128]{2,1,0:T(8,128)(2,1)S(1)}, bf16[7,128,128]{2,1,0:T(8,128)(2,1)S(1)}, u32[]{:S(2)}, u32[]{:S(2)}) collective-permute-start(bf16[7,128,128]{2,1,0:T(8,128)(2,1)S(1)} %bitcast.70), channel_id=1, source_target_pairs={{0,2},{2,0},{1,3},{3,1},{4,6},{6,4},{5,7},{7,5},{8,10},{10,8},{9,1... | collective-permute-start | bytes 688136 | tf_op jit(solution)/shard_map/ppermute | solution.py:86
  37.9 0.5 collective-permute-start.7
  38.5 0.5 collective-permute-start.6
  39.0 1.6 %pad_maximum_fusion.1 = bf16[72,4,24,128]{3,2,1,0:T(8,128)(2,1)S(1)} fusion(bf16[36,4,24,128]{3,2,1,0:T(8,128)(2,1)} %param.16, bf16[36,4,24,128]{3,2,1,0:T(8,128)(2,1)} %param.12), kind=kLoop, calls=%fused_computation.1 | loop fusion | flops 884736 | bytes 3538944 | tf_op jit(solution)/shard_map/concatenate | solution.py:144
  40.6 2.8 %collective-permute-done.12.refs_4_ = bf16[7,128,128]{2,1,0:T(8,128)(2,1)S(1)} collective-permute-done((bf16[7,128,128]{2,1,0:T(8,128)(2,1)S(1)}, bf16[7,128,128]{2,1,0:T(8,128)(2,1)S(1)}, u32[]{:S(2)}, u32[]{:S(2)}) %collective-permute-start.12) | collective-permute-done | bytes 229408 | tf_op jit(solution)/shard_map/ppermute | solution.py:86
  43.4 1.6 %collective-permute-start.2 = (bf16[7,128,128]{2,1,0:T(8,128)(2,1)S(1)}, bf16[7,128,128]{2,1,0:T(8,128)(2,1)S(1)}, u32[]{:S(2)}, u32[]{:S(2)}) collective-permute-start(bf16[7,128,128]{2,1,0:T(8,128)(2,1)S(1)} %bitcast.66), channel_id=1, source_target_pairs={{0,16},{16,0},{1,17},{17,1},{2,18},{18,2},{3,19},{19,3},{4,20},{20... | collective-permute-start | bytes 688136 | tf_op jit(solution)/shard_map/ppermute | solution.py:86
  45.0 1.5 %collective-permute-start.1 = (bf16[7,128,128]{2,1,0:T(8,128)(2,1)S(1)}, bf16[7,128,128]{2,1,0:T(8,128)(2,1)S(1)}, u32[]{:S(2)}, u32[]{:S(2)}) collective-permute-start(bf16[7,128,128]{2,1,0:T(8,128)(2,1)S(1)} %bitcast.67), channel_id=1, source_target_pairs={{0,2},{2,0},{1,3},{3,1},{4,6},{6,4},{5,7},{7,5},{8,10},{10,8},{9,1... | collective-permute-start | bytes 688136 | tf_op jit(solution)/shard_map/ppermute | solution.py:86
  46.5 0.1 select_reduce_fusion.1
  46.7 0.7 slice.42
  47.4 0.9 collective-permute-done.7.refs_4_
  48.3 1.6 %collective-permute-start.13 = (bf16[4,128,128]{2,1,0:T(8,128)(2,1)}, bf16[4,128,128]{2,1,0:T(8,128)(2,1)}, u32[]{:S(2)}, u32[]{:S(2)}) collective-permute-start(bf16[4,128,128]{2,1,0:T(8,128)(2,1)} %slice.42), channel_id=1, source_target_pairs={{0,16},{16,0},{1,17},{17,1},{2,18},{18,2},{3,19},{19,3},{4,20},{20... | collective-permute-start | bytes 393224 | tf_op jit(solution)/shard_map/ppermute | solution.py:86
  50.0 0.6 slice.43
  50.6 1.5 %collective-permute-start.14 = (bf16[3,128,128]{2,1,0:T(8,128)(2,1)}, bf16[3,128,128]{2,1,0:T(8,128)(2,1)}, u32[]{:S(2)}, u32[]{:S(2)}) collective-permute-start(bf16[3,128,128]{2,1,0:T(8,128)(2,1)} %slice.43), channel_id=1, source_target_pairs={{0,2},{2,0},{1,3},{3,1},{4,6},{6,4},{5,7},{7,5},{8,10},{10,8},{9,1... | collective-permute-start | bytes 294920 | tf_op jit(solution)/shard_map/ppermute | solution.py:86
  52.1 0.7 slice.40
  52.8 0.1 collective-permute-done.2.refs_4_
  52.9 1.5 %collective-permute-start.8 = (bf16[4,128,128]{2,1,0:T(8,128)(2,1)}, bf16[4,128,128]{2,1,0:T(8,128)(2,1)}, u32[]{:S(2)}, u32[]{:S(2)}) collective-permute-start(bf16[4,128,128]{2,1,0:T(8,128)(2,1)} %slice.40), channel_id=1, source_target_pairs={{0,16},{16,0},{1,17},{17,1},{2,18},{18,2},{3,19},{19,3},{4,20},{20... | collective-permute-start | bytes 393224 | tf_op jit(solution)/shard_map/ppermute | solution.py:86
  54.7 1.8 %collective-permute-start.9 = (bf16[3,128,128]{2,1,0:T(8,128)(2,1)S(1)}, bf16[3,128,128]{2,1,0:T(8,128)(2,1)S(1)}, u32[]{:S(2)}, u32[]{:S(2)}) collective-permute-start(bf16[3,128,128]{2,1,0:T(8,128)(2,1)S(1)} %slice.41), channel_id=1, source_target_pairs={{0,2},{2,0},{1,3},{3,1},{4,6},{6,4},{5,7},{7,5},{8,10},{10,8},{9,1... | collective-permute-start | bytes 294920 | tf_op jit(solution)/shard_map/ppermute | solution.py:86
  56.5 0.5 collective-permute-start.4
  57.1 0.5 collective-permute-start.3
  57.6 1.5 %copy-done = bf16[1,1,4,14,128,128]{5,4,3,2,1,0:T(8,128)(2,1)S(1)} copy-done((bf16[1,1,4,14,128,128]{5,4,3,2,1,0:T(8,128)(2,1)S(1)}, bf16[1,1,4,14,128,128]{5,4,3,2,1,0:T(8,128)(2,1)}, u32[]{:S(2)}) %copy-start) | copy-done | bytes 1835032
  59.1 1.5 %copy-done.1 = bf16[1,1,4,14,128,128]{5,4,3,2,1,0:T(8,128)(2,1)S(1)} copy-done((bf16[1,1,4,14,128,128]{5,4,3,2,1,0:T(8,128)(2,1)S(1)}, bf16[1,1,4,14,128,128]{5,4,3,2,1,0:T(8,128)(2,1)}, u32[]{:S(2)}) %copy-start.1) | copy-done | bytes 1835032
  60.6 1.1 %shard_map.118.refs_7_ = bf16[4,16,96,128]{3,2,1,0:T(8,128)(2,1)S(1)} custom-call(s32[3,4,28]{2,1,0:T(4,128)S(1)} %pad_add_fusion.table, s32[3]{0:T(128)S(1)} %pad_add_fusion.1.where, bf16[72,96,128]{2,1,0:T(8,128)(2,1)S(1)} %bitcast.57, f32[4,40,128]{2,1,0:T(8,128)S(1)} %maximum_maximum_fusion.refs_1_, bf16[4,14,128,128]{3,2,1,0:T(8,128)(2,1)S(1)} %bitcast.65, ...), custom_call_target="tpu_custom_call" | custom-call | flops 88080384 | bytes 6291456 | tf_op jit(solution)/shard_map/pallas_call | solution.py:67
  61.7 2.0 %shard_map.119.refs_7_ = bf16[4,16,96,128]{3,2,1,0:T(8,128)(2,1)S(1)} custom-call(s32[3,4,28]{2,1,0:T(4,128)S(1)} %pad_add_fusion.table, s32[6]{0:T(128)S(1)} %stack.69.where, bf16[72,96,128]{2,1,0:T(8,128)(2,1)S(1)} %bitcast.58, f32[4,40,128]{2,1,0:T(8,128)S(1)} %maximum_maximum_fusion.refs_1_, ...), custom_call_target="tpu_custom_call", output_to_operand_aliasing={{}: (9, {})} | custom-call | flops 88080384 | bytes 6291456 | tf_op jit(solution)/shard_map/pallas_call | solution.py:67
  63.8 2.1 %shard_map.120.refs_7_ = bf16[4,16,96,128]{3,2,1,0:T(8,128)(2,1)S(1)} custom-call(s32[3,4,28]{2,1,0:T(4,128)S(1)} %pad_add_fusion.table, s32[6]{0:T(128)S(1)} %stack.67.where, bf16[72,96,128]{2,1,0:T(8,128)(2,1)S(1)} %bitcast.59, f32[4,40,128]{2,1,0:T(8,128)S(1)} %maximum_maximum_fusion.refs_1_, ...), custom_call_target="tpu_custom_call", output_to_operand_aliasing={{}: (9, {})} | custom-call | flops 88080384 | bytes 6291456 | tf_op jit(solution)/shard_map/pallas_call | solution.py:67
  65.9 1.1 %shard_map.121 = bf16[4,16,96,128]{3,2,1,0:T(8,128)(2,1)S(1)} custom-call(s32[3,4,28]{2,1,0:T(4,128)S(1)} %pad_add_fusion.table, s32[6]{0:T(128)S(1)} %stack.65.where, bf16[72,96,128]{2,1,0:T(8,128)(2,1)S(1)} %bitcast.60, f32[4,40,128]{2,1,0:T(8,128)S(1)} %maximum_maximum_fusion.refs_1_, ...), custom_call_target="tpu_custom_call", output_to_operand_aliasing={{}: (9, {})} | custom-call | flops 88080384 | bytes 6291456 | tf_op jit(solution)/shard_map/pallas_call | solution.py:67
  67.0 1.7 %copy.35 = bf16[4,2,4,2,4,1,24,128]{7,3,6,0,2,1,4,5:T(2,128)(2,1)S(1)} copy(bf16[4,2,4,2,4,1,24,128]{7,6,4,3,2,1,0,5:T(8,128)(2,1)S(1)} %bitcast.61) | data formatting | bytes 3145728 | tf_op jit(solution)/shard_map/reshape | solution.py:186
  68.7 0.4 reshape.219
  69.1 3.2 %constant_dynamic-slice_fusion = (bf16[128,1,3072]{2,1,0:T(2,128)(2,1)S(1)}, bf16[128,1,3072]{2,1,0:T(2,128)(2,1)S(1)}) fusion(bf16[128,2,3072]{2,1,0:T(2,128)(2,1)S(1)} %reshape.219, s32[]{:T(128)S(6)} %select_n.94, s32[]{:T(128)S(6)} %select_n.93), kind=kLoop, calls=%fused_computation.36 | loop fusion | bytes 3145736 | tf_op jit(solution)/shard_map/jit(dynamic_index_in_dim)/dynamic_slice | solution.py:191
  72.4 3.9 %fusion.3 = f32[128,1024]{1,0:T(8,128)S(1)} fusion(bf16[3072,1024]{1,0:T(8,128)(2,1)} %param.21, bf16[128,1,3072]{2,1,0:T(2,128)(2,1)S(1)} %get-tuple-element.9), kind=kOutput, calls=%fused_computation.7 | convolution fusion | flops 805306368 | bytes 7602176 | tf_op jit(solution)/shard_map/dot_general | solution.py:192
  76.3 3.9 %fusion = bf16[128,1024]{1,0:T(8,128)(2,1)S(1)} fusion(f32[128,1024]{1,0:T(8,128)S(1)} %fusion.3, bf16[3072,1024]{1,0:T(8,128)(2,1)} %collective-permute-done.15, bf16[128,1,3072]{2,1,0:T(2,128)(2,1)S(1)} %get-tuple-element.8), kind=kOutput, calls=%fused_computation.4 | convolution fusion | flops 805568512 | bytes 7864320 | tf_op jit(solution)/shard_map/dot_general | solution.py:193
  80.2 12.4 %all_to_all.5 = bf16[8,16,1024]{2,1,0:T(8,128)(2,1)S(1)} all-to-all(bf16[8,16,1024]{2,1,0:T(8,128)(2,1)S(1)} %bitcast.74), channel_id=1, replica_groups=mesh['grp'=2,'band'=4,'var'=2,'sub'=2] {'band','var'}, dimensions={0} | all-to-all | bytes 524288 | tf_op jit(solution)/shard_map/all_to_all | solution.py:196
  92.7 0.1 multiply_reduce_fusion
  92.9 0.7 multiply_convert_fusion
  (65 shorter events, 1.3 us)
Async XLA Ops:
  0.0 76.3 %collective-permute-start.15 = (bf16[3072,1024]{1,0:T(8,128)(2,1)}, bf16[3072,1024]{1,0:T(8,128)(2,1)}, u32[]{:S(2)}, u32[]{:S(2)}) collective-permute-start(bf16[3072,1024]{1,0:T(8,128)(2,1)} %param.21), channel_id=1, source_target_pairs={{0,1},{1,0},{2,3},{3,2},{4,5},{5,4},{6,7},{7,6},{8,9},{9,8},{10,11... | collective-permute-start | bytes 18874376 | tf_op jit(solution)/shard_map/ppermute | solution.py:86
  0.5 8.2 %copy-start.9 = (s32[36,1]{0,1:T(1,128)S(1)}, s32[36,1]{0,1:T(1,128)}, u32[]{:S(2)}) copy-start(s32[36,1]{0,1:T(1,128)} %param.17) | copy-start | bytes 436
  0.5 8.6 %copy-start.10 = (s32[36,1]{0,1:T(1,128)S(1)}, s32[36,1]{0,1:T(1,128)}, u32[]{:S(2)}) copy-start(s32[36,1]{0,1:T(1,128)} %param.13) | copy-start | bytes 436
  0.5 8.9 %copy-start.7 = (s32[1,1,4,14]{3,2,1,0:T(4,128)S(1)}, s32[1,1,4,14]{3,2,1,0:T(4,128)}, u32[]{:S(2)}) copy-start(s32[1,1,4,14]{3,2,1,0:T(4,128)} %param.19) | copy-start | bytes 676
  0.5 8.9 %copy-start.8 = (s32[1,1,4,14]{3,2,1,0:T(4,128)S(1)}, s32[1,1,4,14]{3,2,1,0:T(4,128)}, u32[]{:S(2)}) copy-start(s32[1,1,4,14]{3,2,1,0:T(4,128)} %param.15) | copy-start | bytes 676
  0.5 9.1 %copy-start.5 = (f32[1,1,8,2,128]{4,3,2,1,0:T(2,128)S(1)}, f32[1,1,8,2,128]{4,3,2,1,0:T(2,128)}, u32[]{:S(2)}) copy-start(f32[1,1,8,2,128]{4,3,2,1,0:T(2,128)} %param.20) | copy-start | bytes 24580
  3.0 31.9 %collective-permute-start.10 = (bf16[896,128]{1,0:T(8,128)(2,1)S(1)}, bf16[896,128]{1,0:T(8,128)(2,1)S(1)}, u32[]{:S(2)}, u32[]{:S(2)}) collective-permute-start(bf16[896,128]{1,0:T(8,128)(2,1)S(1)} %get-tuple-element.5), channel_id=1, source_target_pairs={{0,4},{4,8},{8,12},{12,0},{1,5},{5,9},{9,13},{13,1},{2,6},{6,10},{... | collective-permute-start | bytes 688136 | tf_op jit(solution)/shard_map/ppermute | solution.py:159
  5.6 32.4 %collective-permute-start.5 = (bf16[896,128]{1,0:T(8,128)(2,1)S(1)}, bf16[896,128]{1,0:T(8,128)(2,1)}, u32[]{:S(2)}, u32[]{:S(2)}) collective-permute-start(bf16[896,128]{1,0:T(8,128)(2,1)S(1)} %get-tuple-element.6), channel_id=1, source_target_pairs={{0,12},{4,0},{8,4},{12,8},{1,13},{5,1},{9,5},{13,9},{2,14},{6,2},{... | collective-permute-start | bytes 688136 | tf_op jit(solution)/shard_map/ppermute | solution.py:159
  7.7 30.8 %collective-permute-start = (bf16[896,128]{1,0:T(8,128)(2,1)S(1)}, bf16[896,128]{1,0:T(8,128)(2,1)S(1)}, u32[]{:S(2)}, u32[]{:S(2)}) collective-permute-start(bf16[896,128]{1,0:T(8,128)(2,1)S(1)} %get-tuple-element.7), channel_id=1, source_target_pairs={{0,8},{4,12},{8,0},{12,4},{1,9},{5,13},{9,1},{13,5},{2,10},{6,14},... | collective-permute-start | bytes 688136 | tf_op jit(solution)/shard_map/ppermute | solution.py:159
  34.9 5.7 %copy-start.2 = (bf16[896,128]{1,0:T(8,128)(2,1)}, bf16[896,128]{1,0:T(8,128)(2,1)S(1)}, u32[]{:S(2)}) copy-start(bf16[896,128]{1,0:T(8,128)(2,1)S(1)} %collective-permute-done.10) | copy-start | bytes 688132
  34.9 8.5 %collective-permute-start.12 = (bf16[7,128,128]{2,1,0:T(8,128)(2,1)S(1)}, bf16[7,128,128]{2,1,0:T(8,128)(2,1)S(1)}, u32[]{:S(2)}, u32[]{:S(2)}) collective-permute-start(bf16[7,128,128]{2,1,0:T(8,128)(2,1)S(1)} %bitcast.69), channel_id=1, source_target_pairs={{0,16},{16,0},{1,17},{17,1},{2,18},{18,2},{3,19},{19,3},{4,20},{20... | collective-permute-start | bytes 688136 | tf_op jit(solution)/shard_map/ppermute | solution.py:86
  36.5 8.5 %collective-permute-start.11 = (bf16[7,128,128]{2,1,0:T(8,128)(2,1)S(1)}, bf16[7,128,128]{2,1,0:T(8,128)(2,1)S(1)}, u32[]{:S(2)}, u32[]{:S(2)}) collective-permute-start(bf16[7,128,128]{2,1,0:T(8,128)(2,1)S(1)} %bitcast.70), channel_id=1, source_target_pairs={{0,2},{2,0},{1,3},{3,1},{4,6},{6,4},{5,7},{7,5},{8,10},{10,8},{9,1... | collective-permute-start | bytes 688136 | tf_op jit(solution)/shard_map/ppermute | solution.py:86
  37.9 10.3 %collective-permute-start.7 = (bf16[7,128,128]{2,1,0:T(8,128)(2,1)}, bf16[7,128,128]{2,1,0:T(8,128)(2,1)S(1)}, u32[]{:S(2)}, u32[]{:S(2)}) collective-permute-start(bf16[7,128,128]{2,1,0:T(8,128)(2,1)} %bitcast.24.refs_2_), channel_id=1, source_target_pairs={{0,16},{16,0},{1,17},{17,1},{2,18},{18,2},{3,19},{19,3},{4,20},{20... | collective-permute-start | bytes 688136 | tf_op jit(solution)/shard_map/ppermute | solution.py:86
  38.5 12.2 %collective-permute-start.6 = (bf16[7,128,128]{2,1,0:T(8,128)(2,1)}, bf16[7,128,128]{2,1,0:T(8,128)(2,1)S(1)}, u32[]{:S(2)}, u32[]{:S(2)}) collective-permute-start(bf16[7,128,128]{2,1,0:T(8,128)(2,1)} %bitcast.24.refs_2_), channel_id=1, source_target_pairs={{0,2},{2,0},{1,3},{3,1},{4,6},{6,4},{5,7},{7,5},{8,10},{10,8},{9,1... | collective-permute-start | bytes 688136 | tf_op jit(solution)/shard_map/ppermute | solution.py:86
  43.4 9.6 %collective-permute-start.2 = (bf16[7,128,128]{2,1,0:T(8,128)(2,1)S(1)}, bf16[7,128,128]{2,1,0:T(8,128)(2,1)S(1)}, u32[]{:S(2)}, u32[]{:S(2)}) collective-permute-start(bf16[7,128,128]{2,1,0:T(8,128)(2,1)S(1)} %bitcast.66), channel_id=1, source_target_pairs={{0,16},{16,0},{1,17},{17,1},{2,18},{18,2},{3,19},{19,3},{4,20},{20... | collective-permute-start | bytes 688136 | tf_op jit(solution)/shard_map/ppermute | solution.py:86
  45.0 9.7 %collective-permute-start.1 = (bf16[7,128,128]{2,1,0:T(8,128)(2,1)S(1)}, bf16[7,128,128]{2,1,0:T(8,128)(2,1)S(1)}, u32[]{:S(2)}, u32[]{:S(2)}) collective-permute-start(bf16[7,128,128]{2,1,0:T(8,128)(2,1)S(1)} %bitcast.67), channel_id=1, source_target_pairs={{0,2},{2,0},{1,3},{3,1},{4,6},{6,4},{5,7},{7,5},{8,10},{10,8},{9,1... | collective-permute-start | bytes 688136 | tf_op jit(solution)/shard_map/ppermute | solution.py:86
  48.3 8.8 %collective-permute-start.13 = (bf16[4,128,128]{2,1,0:T(8,128)(2,1)}, bf16[4,128,128]{2,1,0:T(8,128)(2,1)}, u32[]{:S(2)}, u32[]{:S(2)}) collective-permute-start(bf16[4,128,128]{2,1,0:T(8,128)(2,1)} %slice.42), channel_id=1, source_target_pairs={{0,16},{16,0},{1,17},{17,1},{2,18},{18,2},{3,19},{19,3},{4,20},{20... | collective-permute-start | bytes 393224 | tf_op jit(solution)/shard_map/ppermute | solution.py:86
  50.6 5.9 %collective-permute-start.14 = (bf16[3,128,128]{2,1,0:T(8,128)(2,1)}, bf16[3,128,128]{2,1,0:T(8,128)(2,1)}, u32[]{:S(2)}, u32[]{:S(2)}) collective-permute-start(bf16[3,128,128]{2,1,0:T(8,128)(2,1)} %slice.43), channel_id=1, source_target_pairs={{0,2},{2,0},{1,3},{3,1},{4,6},{6,4},{5,7},{7,5},{8,10},{10,8},{9,1... | collective-permute-start | bytes 294920 | tf_op jit(solution)/shard_map/ppermute | solution.py:86
  52.9 10.9 %collective-permute-start.8 = (bf16[4,128,128]{2,1,0:T(8,128)(2,1)}, bf16[4,128,128]{2,1,0:T(8,128)(2,1)}, u32[]{:S(2)}, u32[]{:S(2)}) collective-permute-start(bf16[4,128,128]{2,1,0:T(8,128)(2,1)} %slice.40), channel_id=1, source_target_pairs={{0,16},{16,0},{1,17},{17,1},{2,18},{18,2},{3,19},{19,3},{4,20},{20... | collective-permute-start | bytes 393224 | tf_op jit(solution)/shard_map/ppermute | solution.py:86
  54.7 9.1 %collective-permute-start.9 = (bf16[3,128,128]{2,1,0:T(8,128)(2,1)S(1)}, bf16[3,128,128]{2,1,0:T(8,128)(2,1)S(1)}, u32[]{:S(2)}, u32[]{:S(2)}) collective-permute-start(bf16[3,128,128]{2,1,0:T(8,128)(2,1)S(1)} %slice.41), channel_id=1, source_target_pairs={{0,2},{2,0},{1,3},{3,1},{4,6},{6,4},{5,7},{7,5},{8,10},{10,8},{9,1... | collective-permute-start | bytes 294920 | tf_op jit(solution)/shard_map/ppermute | solution.py:86
  56.5 9.4 %collective-permute-start.4 = (bf16[3,128,128]{2,1,0:T(8,128)(2,1)S(1)}, bf16[3,128,128]{2,1,0:T(8,128)(2,1)S(1)}, u32[]{:S(2)}, u32[]{:S(2)}) collective-permute-start(bf16[3,128,128]{2,1,0:T(8,128)(2,1)S(1)} %slice.39), channel_id=1, source_target_pairs={{0,2},{2,0},{1,3},{3,1},{4,6},{6,4},{5,7},{7,5},{8,10},{10,8},{9,1... | collective-permute-start | bytes 294920 | tf_op jit(solution)/shard_map/ppermute | solution.py:86
  57.1 8.8 %collective-permute-start.3 = (bf16[4,128,128]{2,1,0:T(8,128)(2,1)S(1)}, bf16[4,128,128]{2,1,0:T(8,128)(2,1)S(1)}, u32[]{:S(2)}, u32[]{:S(2)}) collective-permute-start(bf16[4,128,128]{2,1,0:T(8,128)(2,1)S(1)} %slice.38), channel_id=1, source_target_pairs={{0,16},{16,0},{1,17},{17,1},{2,18},{18,2},{3,19},{19,3},{4,20},{20... | collective-permute-start | bytes 393224 | tf_op jit(solution)/shard_map/ppermute | solution.py:86
  57.6 1.5 %copy-start = (bf16[1,1,4,14,128,128]{5,4,3,2,1,0:T(8,128)(2,1)S(1)}, bf16[1,1,4,14,128,128]{5,4,3,2,1,0:T(8,128)(2,1)}, u32[]{:S(2)}) copy-start(bf16[1,1,4,14,128,128]{5,4,3,2,1,0:T(8,128)(2,1)} %param.18) | copy-start | bytes 5505028
  59.1 1.5 %copy-start.1 = (bf16[1,1,4,14,128,128]{5,4,3,2,1,0:T(8,128)(2,1)S(1)}, bf16[1,1,4,14,128,128]{5,4,3,2,1,0:T(8,128)(2,1)}, u32[]{:S(2)}) copy-start(bf16[1,1,4,14,128,128]{5,4,3,2,1,0:T(8,128)(2,1)} %param.14) | copy-start | bytes 5505028
  60.6 1.1 %copy-start.3 = (bf16[896,128]{1,0:T(8,128)(2,1)S(1)}, bf16[896,128]{1,0:T(8,128)(2,1)}, u32[]{:S(2)}) copy-start(bf16[896,128]{1,0:T(8,128)(2,1)} %copy-done.2) | copy-start | bytes 688132
  76.3 16.4 %copy-start.4 = (f32[1024]{0:T(1024)S(1)}, f32[1024]{0:T(1024)}, u32[]{:S(2)}) copy-start(f32[1024]{0:T(1024)} %param.22) | copy-start | bytes 12292
  76.3 16.6 %copy-start.6 = (f32[1024]{0:T(1024)S(1)}, f32[1024]{0:T(1024)}, u32[]{:S(2)}) copy-start(f32[1024]{0:T(1024)} %param.23) | copy-start | bytes 12292

commit v2 on v1

v2 whole, which is shorter than its diff:
```python
import functools

import jax
import jax.numpy as jnp
from jax import lax
from jax.experimental import pallas as pl
from jax.experimental.pallas import tpu as pltpu
from jax.sharding import PartitionSpec as P

REPL = ("grp", "var")
META = 48


def slot_tables(dest, band_count, cap):
    count = dest.shape[0]
    serial = jnp.arange(count, dtype=jnp.int32)
    band_of = dest[:, 0]
    earlier = (band_of[:, None] == band_of[None, :]) & (serial[None, :] < serial[:, None])
    position = jnp.sum(earlier.astype(jnp.int32), axis=1)
    slot = band_of * cap + position
    hit = slot[None, :] == jnp.arange(band_count * cap, dtype=jnp.int32)[:, None]
    block = jnp.sum(jnp.where(hit, serial[None, :], 0), axis=1)
    used = jnp.any(hit, axis=1)
    return block.reshape(band_count, cap), used.reshape(band_count, cap)


def regrid_kernel(own, per_part, table, where, fields, *refs):
    out, scale = refs[-2], refs[-1]
    cells = fields.shape[-1]
    halves, _, half_tiles = out.shape[:3]
    tiles = halves * half_tiles
    if own:
        ocean, atmos, land_ref = refs[:3]
        land = land_ref[...]
        part = lambda at, s: (ocean, atmos)[at][0, s]
        part_count = 2
    else:
        parts = refs[0]
        first = per_part * cells
        part = lambda at, s: parts[at, pl.ds(s * cells, cells), :]
        part_count = parts.shape[0]
        if len(refs) > 1 and refs[1].shape == (META, cells):
            meta, first = refs[1], 0
            rows = meta[pl.ds(0, 2 * tiles), :].astype(jnp.float32)
        else:
            rows = parts[0, pl.ds(first, 2 * tiles), :].astype(jnp.float32)
        land = rows[:tiles] + rows[tiles:]
    scale[pl.ds(0, tiles), :] = 1.0 - land
    scale[pl.ds(tiles, tiles), :] = land
    scale[pl.ds(2 * tiles, 8), :] = jnp.zeros((8, cells), jnp.float32)
    out[...] = jnp.zeros_like(out)
    for at in range(part_count):
        for s in range(per_part):
            slot = at * per_part + s
            tile = table[1, slot]
            dense = jnp.dot(fields[table[0, slot]], part(at, s), preferred_element_type=jnp.float32)
            out[tile // half_tiles, 0, tile % half_tiles] += (
                dense * scale[pl.ds(table[2, slot], 1), :]
            )


def regrid(table, where, fields, operands, own, per_part, previous, shape):
    rows, cells = fields.shape[1:]
    whole = lambda a: pl.BlockSpec(a.shape, lambda i, t, w, n=a.ndim: (0,) * n)
    in_specs = [whole(fields)]
    for a in operands:
        if own and a.ndim == 4:
            in_specs.append(pl.BlockSpec((1,) + a.shape[1:], lambda i, t, w: (w[0], 0, 0, 0)))
        else:
            in_specs.append(whole(a))
    operands = [fields] + list(operands)
    aliases = {}
    if previous is not None:
        aliases = {2 + len(operands): 0}
        in_specs.append(pl.BlockSpec(memory_space=pl.ANY))
        operands.append(previous)
    halves, bands, half_tiles = shape
    total = table.shape[1]
    return pl.pallas_call(
        functools.partial(regrid_kernel, own, per_part),
        out_shape=jax.ShapeDtypeStruct(shape + (rows, cells), jnp.float32),
        grid_spec=pltpu.PrefetchScalarGridSpec(
            num_scalar_prefetch=2,
            grid=(1,),
            in_specs=in_specs,
            out_specs=pl.BlockSpec(
                (halves, 1, half_tiles, rows, cells), lambda i, t, w: (0, w[0], 0, 0, 0)
            ),
            scratch_shapes=[pltpu.VMEM((2 * halves * half_tiles + 8, cells), jnp.float32)],
        ),
        input_output_aliases=aliases,
        cost_estimate=pl.CostEstimate(
            flops=2 * total * rows * cells * cells, bytes_accessed=6 << 20, transcendentals=0
        ),
        compiler_params=pltpu.CompilerParams(vmem_limit_bytes=24 << 20),
    )(table, where, *operands)


def embed_kernel(steps, sub, partial, mine, theirs, out, total, left, right):
    at = pl.program_id(0)
    cells = partial.shape[1]
    step_rows = mine.shape[0]
    step_vars = step_rows // (2 * cells)
    half_vars = step_vars * pl.num_programs(0)
    stride = 2 * steps * 2 * half_vars
    block = out.shape[0] * out.shape[1] // steps
    for x_ref, half in ((left, sub[0]), (right, 1 - sub[0])):
        for v in range(step_vars):
            for q in range(2):
                for t in range(steps):
                    start = q * steps * 2 * half_vars + t * 2 * half_vars
                    start = start + half * half_vars + at * step_vars + v
                    x_ref[pl.ds(t * block, block), pl.ds((v * 2 + q) * cells, cells)] = partial[
                        pl.ds(start, block, stride), :
                    ].astype(x_ref.dtype)

    @pl.when(at == 0)
    def _():
        total[...] = jnp.zeros_like(total)

    total[...] += jnp.dot(left[...], mine[...], preferred_element_type=jnp.float32) + jnp.dot(
        right[...], theirs[...], preferred_element_type=jnp.float32
    )

    @pl.when(at == pl.num_programs(0) - 1)
    def _():
        out[...] = total[...].reshape(out.shape).astype(out.dtype)


def embed(partial, sub, mine, theirs, steps, local_vars, chunks):
    cells, width = partial.shape[-1], mine.shape[-1]
    half_vars = local_vars // 2
    step_vars = 2 if half_vars % 2 == 0 else 1
    grid = half_vars // step_vars
    step_rows = step_vars * 2 * cells
    flat = partial.reshape(-1, cells)
    rows = flat.shape[0] // (2 * local_vars)
    weight_spec = pl.BlockSpec((step_rows, width), lambda i, s: (i, 0))
    return pl.pallas_call(
        functools.partial(embed_kernel, steps),
        out_shape=jax.ShapeDtypeStruct((chunks, rows // chunks, width), jnp.bfloat16),
        grid_spec=pltpu.PrefetchScalarGridSpec(
            num_scalar_prefetch=1,
            grid=(grid,),
            in_specs=[
                pl.BlockSpec(flat.shape, lambda i, s: (0, 0)),
                weight_spec,
                weight_spec,
            ],
            out_specs=pl.BlockSpec((chunks, rows // chunks, width), lambda i, s: (0, 0, 0)),
            scratch_shapes=[
                pltpu.VMEM((rows, width), jnp.float32),
                pltpu.VMEM((rows, step_rows), jnp.bfloat16),
                pltpu.VMEM((rows, step_rows), jnp.bfloat16),
            ],
        ),
        cost_estimate=pl.CostEstimate(
            flops=4 * rows * mine.shape[0] * width,
            bytes_accessed=4 * mine.shape[0] * width,
            transcendentals=0,
        ),
        compiler_params=pltpu.CompilerParams(
            vmem_limit_bytes=56 << 20 if rows > 1024 else 24 << 20
        ),
    )(sub, flat, mine, theirs)


def per_device(
    ocean_fields,
    ocean_dest,
    ocean_weights,
    ocean_tiles,
    atmos_fields,
    atmos_dest,
    atmos_weights,
    atmos_tiles,
    land_fraction,
    embed_weight,
    embed_bias,
    embed_gain,
):
    nb = lax.axis_size("band")
    nv = lax.axis_size("var")
    ng = lax.axis_size("grp")
    rep = nv * ng
    cap = ocean_weights.shape[3]
    cells = ocean_weights.shape[-1]
    block_count, steps, local_vars, _ = ocean_fields.shape
    patches = land_fraction.shape[2]
    tiles = 2 * patches
    slots = 2 * cap
    share = patches // nv
    me = lax.axis_index("band")
    x, y = lax.axis_index("var"), lax.axis_index("grp")
    quarter = y * nv + x

    embed_other = lax.ppermute(embed_weight, "sub", [(0, 1), (1, 0)])

    ocean_w = ocean_weights.reshape(nb, cap, cells, cells)
    atmos_w = atmos_weights.reshape(nb, cap, cells, cells)
    aligned = ng == 2 and cap % nv == 0
    share_rows = slots * cells // rep
    if not aligned:
        both = jnp.concatenate([ocean_w, atmos_w], axis=1).reshape(nb, slots * cells, cells)

    def share_of(target):
        if aligned:
            each = cap // nv
            start, size = (target, x * each, 0, 0), (1, each, cells, cells)
            piece = jnp.where(
                y == 0,
                lax.dynamic_slice(ocean_w, start, size),
                lax.dynamic_slice(atmos_w, start, size),
            )
            return piece.reshape(share_rows, cells)
        return lax.dynamic_slice(
            both, (target, quarter * share_rows, 0), (1, share_rows, cells)
        )[0]

    land = land_fraction.reshape(tiles, cells)
    high = lax.reduce_precision(land, 8, 7)
    low = (land - high).astype(jnp.bfloat16)
    tile_ids = jnp.concatenate([ocean_tiles.reshape(nb, cap), atmos_tiles.reshape(nb, cap)], axis=1)
    tile_rows = jnp.pad(tile_ids.astype(jnp.bfloat16), ((0, 0), (0, cells - slots)))

    def meta_of(target):
        row = lax.dynamic_slice(tile_rows, (target, 0), (1, cells))
        return jnp.concatenate(
            [high.astype(jnp.bfloat16), low, jnp.broadcast_to(row, (META - 2 * tiles, cells))]
        )

    ocean_block, ocean_used = slot_tables(ocean_dest, nb, cap)
    atmos_block, atmos_used = slot_tables(atmos_dest, nb, cap)
    block_all = jnp.concatenate([ocean_block, atmos_block + block_count], axis=1)
    used_all = jnp.concatenate([ocean_used, atmos_used], axis=1)
    grid_row = jnp.where(jnp.arange(slots) < cap, 0, tiles)
    fields = jnp.concatenate([ocean_fields, atmos_fields], axis=0).reshape(
        2 * block_count, steps * local_vars, cells
    )

    def table_of(band, tile):
        block = lax.dynamic_index_in_dim(block_all, band, 0, keepdims=False)
        used = lax.dynamic_index_in_dim(used_all, band, 0, keepdims=False)
        scale = jnp.where(used, tile + grid_row, 2 * tiles)
        return jnp.stack([block, tile, scale]).astype(jnp.int32)

    shape = (nv, nb, share * 2)
    own_tile = lax.dynamic_index_in_dim(tile_ids, me, 0, keepdims=False)
    partial = regrid(
        table_of(me, own_tile), me[None], fields, [ocean_w, atmos_w, land], True, cap, None, shape
    )
    order = ([1, nb - 1] + list(range(2, nb - 1)))[: nb - 1]
    gathered, arrived = [], None
    for shift in order:
        target = (me + shift) % nb
        piece = jnp.concatenate([share_of(target), meta_of(target)], axis=0)
        if arrived is not None:
            piece, arrived = lax.optimization_barrier((piece, arrived))
            gathered.append(lax.all_gather(arrived, REPL, axis=0))
        arrived = lax.ppermute(piece, "band", [(b, (b + shift) % nb) for b in range(nb)])
    gathered.append(lax.all_gather(arrived, REPL, axis=0))
    for shift, parts in zip(order, gathered):
        band = (me - shift) % nb
        tile = parts[0, share_rows + 2 * tiles, :slots].astype(jnp.int32)
        table = table_of(band, tile)
        if aligned:
            operands, per_part = [parts], slots // rep
        else:
            operands = [parts[:, :share_rows].reshape(1, slots * cells, cells), parts[0, share_rows:]]
            per_part = slots
        partial = regrid(table, band[None], fields, operands, False, per_part, partial, shape)

    sub = lax.axis_index("sub")
    sent = embed(partial, sub[None], embed_weight, embed_other, steps, local_vars, nb * nv)
    got = lax.all_to_all(sent, ("band", "var"), split_axis=0, concat_axis=0, tiled=True)
    shifted = jnp.sum(got.astype(jnp.float32), axis=0) + embed_bias
    inverse = lax.rsqrt(jnp.mean(shifted * shifted, axis=-1, keepdims=True) + 1e-05)
    finished = (shifted * inverse * embed_gain).astype(jnp.bfloat16)
    width = finished.shape[-1]
    finished = finished.reshape(nb, share, steps // nb, width).transpose(1, 0, 2, 3)
    return finished[None]


def solution(mesh):
    in_specs = (
        P(("grp", "band", "sub"), None, "var", None),
        P(("band", "sub"), None),
        P("band", "sub", None, None, None, None),
        P("band", "sub", None, None),
        P(("grp", "band", "sub"), None, "var", None),
        P(("band", "sub"), None),
        P("band", "sub", None, None, None, None),
        P("band", "sub", None, None),
        P("band", "sub", None, None, None),
        P(("var", "sub"), None),
        P(),
        P(),
    )
    out_specs = P("sub", "var", None, ("grp", "band"), None)
    return jax.shard_map(
        per_device, mesh=mesh, in_specs=in_specs, out_specs=out_specs, check_vma=False
    )
```

time: 93.9 us -> 83.4 us (0.89)
  starting transfers between devices: 20.8 us -> 4.89 us
  blocking collectives: 37.2 us -> 50.1 us
  local copies, waits for them, and re-layouts: 11.4 us -> 2.13 us
  matrix products: 7.75 us -> 0 us
  Pallas kernels: 6.27 us -> 11.1 us
  waiting for transfers between devices: 3.78 us -> 7.93 us
    ppermute x13 -> x1, starting transfers between devices: 15.2 us -> 0.45 us  [per_device(): embed_other = lax.ppermute(embed_weight, 'sub', [(0, 1), (1, 0)])]
    all_gather x1 -> x3, blocking collectives: 24.8 us -> 36.9 us  [per_device(): gathered.append(lax.all_gather(arrived, REPL, axis=0))]
    ppermute x3, waiting for transfers between devices: 0.01 us -> 7.93 us  [per_device(): lax.ppermute(piece, 'band', [(b, (b + shift) % nb) for b in range(nb)])]
    dot_general x2 -> x0, matrix products: 7.75 us -> none  [the longest x1 3.89 us: per_device(): jnp.dot(theirs, embed_other, preferred_element_type=jnp.float32)]
    pallas_call x4 -> x5, Pallas kernels: 6.27 us -> 11.1 us  [the longest x1 7.02 us: embed(): pl.pallas_call(functools.partial(embed_kernel, steps), out_shape=jax.Shap...]
    ppermute x13 -> x1, waiting for transfers between devices: 3.77 us -> 0.01 us  [per_device(): embed_other = lax.ppermute(embed_weight, 'sub', [(0, 1), (1, 0)])]
    dynamic_slice x2 -> x1, local copies, waits for them, and re-layouts: 3.25 us -> 0.01 us  [table_of(): block = lax.dynamic_index_in_dim(block_all, band, 0, keepdims=False)]
    concatenate x2, other arithmetic: 2.5 us -> 0.13 us  [the longest x1 0.08 us: per_device(): used_all = jnp.concatenate([ocean_used, atmos_used], axis=1)]
  transfers between devices with their start and end apart: 16 -> 4, of which waited for: 3 -> 1; matrix products, arithmetic and copies ran while one was open for 19% -> 8% of each run, Pallas kernels for 7% -> 5%
where the time goes in v2:
time: 83.4 us; the launch traced here: 82.9 us
  blocking collectives  50.1 us (60%)
  Pallas kernels  11.1 us (13%)
  waiting for transfers between devices  7.93 us (10%)
  other arithmetic  6.54 us (8%)
  starting transfers between devices  4.89 us (6%)
  local copies, waits for them, and re-layouts  2.13 us (3%)
    all_gather x3, blocking collectives, per_device(): gathered.append(lax.all_gather(arrived, REPL, axis=0))  36.9 us
    all_to_all x1, blocking collectives, per_device(): lax.all_to_all(sent, ('band', 'var'), split_axis=0, concat_axis=0, tiled=...  13.1 us
    ppermute x3, waiting for transfers between devices, per_device(): lax.ppermute(piece, 'band', [(b, (b + shift) % nb) for b in range(nb)])  7.93 us
    pallas_call x1, Pallas kernels, embed(): pl.pallas_call(functools.partial(embed_kernel, steps), out_shape=jax.Shap...  7.02 us
    ppermute x3, starting transfers between devices, per_device(): lax.ppermute(piece, 'band', [(b, (b + shift) % nb) for b in range(nb)])  4.44 us
    pallas_call x4, Pallas kernels, regrid(): pl.pallas_call(functools.partial(regrid_kernel, own, per_part), out_shape...  4.11 us
    reduce_sum x2, other arithmetic, slot_tables(): position = jnp.sum(earlier.astype(jnp.int32), axis=1)  1.82 us
  transfers between devices with their start and end apart: 4, of which 1 were waited for; matrix products, arithmetic and copies ran while one was open for 8% of the time, Pallas kernels for 5%

profile of v2, /device:TPU:0, one launch (start us, length us, event | category | flops | bytes accessed | tf_op | source)
XLA Modules:
  0.0 82.9 jit_solution(3376445335935086955)
XLA Ops:
  0.0 0.5 collective-permute-start.3
  0.5 0.9 %convert_reduce_fusion.1 = s32[36]{0:T(128)S(1)} fusion(s32[36]{0:T(128)} %bitcast.78), kind=kLoop, calls=%fused_computation.20 | loop fusion | flops 6444 | bytes 288 | tf_op jit(solution)/shard_map/reduce_sum | solution.py:19
  1.4 0.7 multiply_add_fusion
  2.0 0.1 select_reduce_fusion
  2.1 0.1 add.164
  2.2 0.9 %convert_reduce_fusion.2 = s32[36]{0:T(128)S(1)} fusion(s32[36]{0:T(128)} %bitcast.79), kind=kLoop, calls=%fused_computation.24 | loop fusion | flops 6444 | bytes 288 | tf_op jit(solution)/shard_map/reduce_sum | solution.py:19
  3.1 0.7 multiply_add_fusion.1
  3.8 0.1 select_reduce_fusion.1
  3.9 0.1 reshape.210
  4.0 0.8 fusion.19
  4.8 0.0 copy-start.3
  4.8 0.0 copy-start.4
  4.8 1.6 %dynamic-slice_select_fusion = (bf16[1,1,1,7,128,128]{5,4,3,2,1,0:T(8,128)(2,1)S(1)}, bf16[1,1,1,7,128,128]{5,4,3,2,1,0:T(8,128)(2,1)S(1)}, bf16[1,1,1,7,128,128]{5,4,3,2,1,0:T(8,128)(2,1)S(1)}) fusion(bf16[1,1,4,14,128,128]{5,4,3,2,1,0:T(8,128)(2,1)} %param.18, s32[]{:T(128)S(6)} %select_n.171, s32[]{:T(128)S(6)} %select_n.163, ...), kind=kLoop, calls=%fused_computation.11 | loop fusion | flops 344064 | bytes 2064401 | tf_op jit(solution)/shard_map/jit(_where)/select_n | solution.py:210
  6.4 0.0 copy-done.2
  6.5 0.1 fusion.2
  6.5 2.6 %collective-permute-start = (bf16[944,128]{1,0:T(8,128)(2,1)S(1)}, bf16[944,128]{1,0:T(8,128)(2,1)S(1)}, u32[]{:S(2)}, u32[]{:S(2)}) collective-permute-start(bf16[944,128]{1,0:T(8,128)(2,1)S(1)} %get-tuple-element.20), channel_id=1, source_target_pairs={{0,4},{4,8},{8,12},{12,0},{1,5},{5,9},{9,13},{13,1},{2,6},{6,10},{... | collective-permute-start | bytes 725000 | tf_op jit(solution)/shard_map/ppermute | solution.py:260
  9.2 0.1 fusion.5
  9.2 0.1 reshape.214
  9.3 0.1 fusion.4
  9.4 0.1 reshape.215
  9.5 0.1 pad_add_fusion.6
  9.6 0.0 copy-done.3
  9.6 0.2 pad_maximum_fusion
  9.8 0.0 copy-start
  9.8 7.9 %collective-permute-done = bf16[944,128]{1,0:T(8,128)(2,1)S(1)} collective-permute-done((bf16[944,128]{1,0:T(8,128)(2,1)S(1)}, bf16[944,128]{1,0:T(8,128)(2,1)S(1)}, u32[]{:S(2)}, u32[]{:S(2)}) %collective-permute-start) | collective-permute-done | bytes 241696 | tf_op jit(solution)/shard_map/ppermute | solution.py:260
  17.7 1.7 %collective-permute-start.1 = (bf16[944,128]{1,0:T(8,128)(2,1)S(1)}, bf16[944,128]{1,0:T(8,128)(2,1)S(1)}, u32[]{:S(2)}, u32[]{:S(2)}) collective-permute-start(bf16[944,128]{1,0:T(8,128)(2,1)S(1)} %get-tuple-element.9), channel_id=1, source_target_pairs={{0,12},{4,0},{8,4},{12,8},{1,13},{5,1},{9,5},{13,9},{2,14},{6,2},{... | collective-permute-start | bytes 725000 | tf_op jit(solution)/shard_map/ppermute | solution.py:260
  19.5 12.4 %all-gather.2 = bf16[3776,128]{1,0:T(8,128)(2,1)S(1)} all-gather(bf16[944,128]{1,0:T(8,128)(2,1)S(1)} %collective-permute-done), channel_id=4, replica_groups=mesh['grp'=2,'band'=4,'var'=2,'sub'=2] {'grp','var'}, dimensions={0}, use_global_device_ids=true | all-gather | bytes 1208320 | tf_op jit(solution)/shard_map/all_gather | solution.py:259
  31.9 0.0 collective-permute-done.1
  31.9 0.1 collective-permute-start.2
  32.0 13.1 %all-gather.1 = bf16[3776,128]{1,0:T(8,128)(2,1)S(1)} all-gather(bf16[944,128]{1,0:T(8,128)(2,1)S(1)} %collective-permute-done.1), channel_id=3, replica_groups=mesh['grp'=2,'band'=4,'var'=2,'sub'=2] {'grp','var'}, dimensions={0}, use_global_device_ids=true | all-gather | bytes 1208320 | tf_op jit(solution)/shard_map/all_gather | solution.py:259
  45.1 0.0 collective-permute-done.2
  45.1 11.4 %all-gather = bf16[3776,128]{1,0:T(8,128)(2,1)S(1)} all-gather(bf16[944,128]{1,0:T(8,128)(2,1)S(1)} %collective-permute-done.2), channel_id=2, replica_groups=mesh['grp'=2,'band'=4,'var'=2,'sub'=2] {'grp','var'}, dimensions={0}, use_global_device_ids=true | all-gather | bytes 1208320 | tf_op jit(solution)/shard_map/all_gather | solution.py:261
  56.5 0.0 copy-done.1
  56.6 1.0 %shard_map.118.refs_1_ = f32[2,4,8,96,128]{4,3,2,1,0:T(8,128)S(1)} custom-call(s32[3,28]{1,0:T(4,128)S(1)} %pad_add_fusion.5.table, s32[1]{0:T(128)} %bitcast.25.where, bf16[72,96,128]{2,1,0:T(8,128)(2,1)S(1)} %bitcast.54, bf16[4,14,128,128]{3,2,1,0:T(8,128)(2,1)S(1)} %bitcast.70, bf16[4,14,128,128]{3,2,1,0:T(8,128)(2,1)S(1)} %bitcast.69, f32[16,128]{1,0:T(8,128)S(1)} %bitcast.72), custom_call_target="tpu_custom_call" | custom-call | flops 88080384 | bytes 6291456 | tf_op jit(solution)/shard_map/pallas_call | solution.py:79
  57.6 1.0 %shard_map.119.refs_1_ = f32[2,4,8,96,128]{4,3,2,1,0:T(8,128)S(1)} custom-call(s32[3,28]{1,0:T(4,128)S(1)} %pad_add_fusion.4.table, s32[1]{0:T(128)} %bitcast.24.where, bf16[72,96,128]{2,1,0:T(8,128)(2,1)S(1)} %bitcast.55, bf16[4,944,128]{2,1,0:T(8,128)(2,1)S(1)} %bitcast.65, ...), custom_call_target="tpu_custom_call", output_to_operand_aliasing={{}: (4, {})} | custom-call | flops 88080384 | bytes 6291456 | tf_op jit(solution)/shard_map/pallas_call | solution.py:79
  58.7 0.0 slice-start
  58.7 1.0 %shard_map.120.refs_1_ = f32[2,4,8,96,128]{4,3,2,1,0:T(8,128)S(1)} custom-call(s32[3,28]{1,0:T(4,128)S(1)} %pad_add_fusion.3.table, s32[1]{0:T(128)} %bitcast.20.where, bf16[72,96,128]{2,1,0:T(8,128)(2,1)S(1)} %bitcast.56, bf16[4,944,128]{2,1,0:T(8,128)(2,1)S(1)} %bitcast.68, ...), custom_call_target="tpu_custom_call", output_to_operand_aliasing={{}: (4, {})} | custom-call | flops 88080384 | bytes 6291456 | tf_op jit(solution)/shard_map/pallas_call | solution.py:79
  59.7 0.0 slice-start.1
  59.7 1.0 %shard_map.121 = f32[2,4,8,96,128]{4,3,2,1,0:T(8,128)S(1)} custom-call(s32[3,28]{1,0:T(4,128)S(1)} %pad_add_fusion.2.table, s32[1]{0:T(128)} %bitcast.15.where, bf16[72,96,128]{2,1,0:T(8,128)(2,1)S(1)} %bitcast.57, bf16[4,944,128]{2,1,0:T(8,128)(2,1)S(1)} %bitcast.62, f32[2,4,8,96,128]{4,3,2,1,0:T(8,128)S(1)} %shard_map.120.refs_1_), custom_call_target="tpu_custom_call", output_to_operand_aliasing={{}: (4, {})} | custom-call | flops 88080384 | bytes 6291456 | tf_op jit(solution)/shard_map/pallas_call | solution.py:79
  60.8 0.0 collective-permute-done.3.theirs
  60.8 0.1 slice-done
  60.8 0.9 %slice-done.1 = s8[2097152]{0:T(1024)(128)(4,1)S(1)} async-done(((s8[6291456]{0:T(1024)(128)(4,1)}), s8[2097152]{0:T(1024)(128)(4,1)S(1)}, s32[]{:S(2)}) %slice-start.1) | async-done | bytes 2097176
  61.8 7.0 %shard_map.122 = bf16[8,16,1024]{2,1,0:T(8,128)(2,1)S(1)} custom-call(s32[1]{0:T(128)} %bitcast.sub, f32[6144,128]{1,0:T(8,128)S(1)} %bitcast.53, bf16[3072,1024]{1,0:T(8,128)(2,1)S(1)} %bitcast.59, bf16[3072,1024]{1,0:T(8,128)(2,1)} %collective-permute-done.3.theirs), custom_call_target="tpu_custom_call" | custom-call | flops 1610612736 | bytes 12582912 | tf_op jit(solution)/shard_map/pallas_call | solution.py:139
  68.8 13.1 %all_to_all.5 = bf16[8,16,1024]{2,1,0:T(8,128)(2,1)S(1)} all-to-all(bf16[8,16,1024]{2,1,0:T(8,128)(2,1)S(1)} %shard_map.122), channel_id=1, replica_groups=mesh['grp'=2,'band'=4,'var'=2,'sub'=2] {'band','var'}, dimensions={0} | all-to-all | bytes 524288 | tf_op jit(solution)/shard_map/all_to_all | solution.py:275
  82.0 0.1 multiply_reduce_fusion
  82.1 0.1 rsqrt.12
  82.2 0.1 fusion.3
  82.3 0.6 copy.18
  (27 shorter events, 0.2 us)
Async XLA Ops:
  0.0 6.4 %copy-start.2 = (f32[1,1,8,2,128]{4,3,2,1,0:T(2,128)S(1)}, f32[1,1,8,2,128]{4,3,2,1,0:T(2,128)}, u32[]{:S(2)}) copy-start(f32[1,1,8,2,128]{4,3,2,1,0:T(2,128)} %param.20) | copy-start | bytes 24580
  0.0 60.8 %collective-permute-start.3 = (bf16[3072,1024]{1,0:T(8,128)(2,1)}, bf16[3072,1024]{1,0:T(8,128)(2,1)}, u32[]{:S(2)}, u32[]{:S(2)}) collective-permute-start(bf16[3072,1024]{1,0:T(8,128)(2,1)} %mine.1), channel_id=1, source_target_pairs={{0,1},{1,0},{2,3},{3,2},{4,5},{5,4},{6,7},{7,6},{8,9},{9,8},{10,11... | collective-permute-start | bytes 18874376 | tf_op jit(solution)/shard_map/ppermute | solution.py:197
  4.8 4.8 %copy-start.3 = (bf16[36,4,24,128]{3,2,1,0:T(8,128)(2,1)S(1)}, bf16[36,4,24,128]{3,2,1,0:T(8,128)(2,1)}, u32[]{:S(2)}) copy-start(bf16[36,4,24,128]{3,2,1,0:T(8,128)(2,1)} %param.16) | copy-start | bytes 2654212
  4.8 4.8 %copy-start.4 = (bf16[36,4,24,128]{3,2,1,0:T(8,128)(2,1)S(1)}, bf16[36,4,24,128]{3,2,1,0:T(8,128)(2,1)}, u32[]{:S(2)}) copy-start(bf16[36,4,24,128]{3,2,1,0:T(8,128)(2,1)} %param.12) | copy-start | bytes 2654212
  6.5 11.2 %collective-permute-start = (bf16[944,128]{1,0:T(8,128)(2,1)S(1)}, bf16[944,128]{1,0:T(8,128)(2,1)S(1)}, u32[]{:S(2)}, u32[]{:S(2)}) collective-permute-start(bf16[944,128]{1,0:T(8,128)(2,1)S(1)} %get-tuple-element.20), channel_id=1, source_target_pairs={{0,4},{4,8},{8,12},{12,0},{1,5},{5,9},{9,13},{13,1},{2,6},{6,10},{... | collective-permute-start | bytes 725000 | tf_op jit(solution)/shard_map/ppermute | solution.py:260
  9.6 46.9 %copy-start.1 = (bf16[1,1,4,14,128,128]{5,4,3,2,1,0:T(8,128)(2,1)S(1)}, bf16[1,1,4,14,128,128]{5,4,3,2,1,0:T(8,128)(2,1)}, u32[]{:S(2)}) copy-start(bf16[1,1,4,14,128,128]{5,4,3,2,1,0:T(8,128)(2,1)} %param.14) | copy-start | bytes 5505028
  9.8 46.8 %copy-start = (bf16[1,1,4,14,128,128]{5,4,3,2,1,0:T(8,128)(2,1)S(1)}, bf16[1,1,4,14,128,128]{5,4,3,2,1,0:T(8,128)(2,1)}, u32[]{:S(2)}) copy-start(bf16[1,1,4,14,128,128]{5,4,3,2,1,0:T(8,128)(2,1)} %param.18) | copy-start | bytes 5505028
  17.7 14.2 %collective-permute-start.1 = (bf16[944,128]{1,0:T(8,128)(2,1)S(1)}, bf16[944,128]{1,0:T(8,128)(2,1)S(1)}, u32[]{:S(2)}, u32[]{:S(2)}) collective-permute-start(bf16[944,128]{1,0:T(8,128)(2,1)S(1)} %get-tuple-element.9), channel_id=1, source_target_pairs={{0,12},{4,0},{8,4},{12,8},{1,13},{5,1},{9,5},{13,9},{2,14},{6,2},{... | collective-permute-start | bytes 725000 | tf_op jit(solution)/shard_map/ppermute | solution.py:260
  31.9 13.2 %collective-permute-start.2 = (bf16[944,128]{1,0:T(8,128)(2,1)S(1)}, bf16[944,128]{1,0:T(8,128)(2,1)S(1)}, u32[]{:S(2)}, u32[]{:S(2)}) collective-permute-start(bf16[944,128]{1,0:T(8,128)(2,1)S(1)} %get-tuple-element.10), channel_id=1, source_target_pairs={{0,8},{4,12},{8,0},{12,4},{1,9},{5,13},{9,1},{13,5},{2,10},{6,14},... | collective-permute-start | bytes 725000 | tf_op jit(solution)/shard_map/ppermute | solution.py:260
  58.7 2.2 %slice-start = ((s8[6291456]{0:T(1024)(128)(4,1)}), s8[4194304]{0:T(1024)(128)(4,1)S(1)}, s32[]{:S(2)}) async-start(s8[6291456]{0:T(1024)(128)(4,1)} %bitcast.58), calls=%async_computation.1 | async-start | bytes 8388608
  59.7 2.0 %slice-start.1 = ((s8[6291456]{0:T(1024)(128)(4,1)}), s8[2097152]{0:T(1024)(128)(4,1)S(1)}, s32[]{:S(2)}) async-start(s8[6291456]{0:T(1024)(128)(4,1)} %bitcast.58), calls=%async_computation.2 | async-start | bytes 4194304
  61.8 20.2 %copy-start.5 = (f32[1024]{0:T(1024)S(1)}, f32[1024]{0:T(1024)}, u32[]{:S(2)}) copy-start(f32[1024]{0:T(1024)} %param.22) | copy-start | bytes 12292
  61.8 20.5 %copy-start.6 = (f32[1024]{0:T(1024)S(1)}, f32[1024]{0:T(1024)}, u32[]{:S(2)}) copy-start(f32[1024]{0:T(1024)} %param.23) | copy-start | bytes 12292

commit v3 on v1

v3 whole, which is shorter than its diff:
```python
import functools

import jax
import jax.numpy as jnp
from jax import lax
from jax.experimental import pallas as pl
from jax.experimental.pallas import tpu as pltpu
from jax.sharding import PartitionSpec as P

REPL = ("grp", "var")


def slot_tables(dest, band_count, cap):
    count = dest.shape[0]
    serial = jnp.arange(count, dtype=jnp.int32)
    band_of = dest[:, 0]
    earlier = (band_of[:, None] == band_of[None, :]) & (serial[None, :] < serial[:, None])
    position = jnp.sum(earlier.astype(jnp.int32), axis=1)
    slot = band_of * cap + position
    hit = slot[None, :] == jnp.arange(band_count * cap, dtype=jnp.int32)[:, None]
    block = jnp.sum(jnp.where(hit, serial[None, :], 0), axis=1)
    used = jnp.any(hit, axis=1)
    return block.reshape(band_count, cap), used.reshape(band_count, cap)


def pack_kernel(shifts, head, each, ocean, atmos, ocean_tiles, atmos_tiles, land, *refs):
    outs, sem = refs[:-1], refs[-1]
    me, bands = lax.axis_index("band"), ocean.shape[0]
    x, y = lax.axis_index("var"), lax.axis_index("grp")
    cells = land.shape[-1]
    tiles = land.shape[0]

    def copies(weights):
        found = []
        for at, shift in enumerate(shifts):
            target = lax.rem(me + shift, bands)
            for half, (first, size) in enumerate(((0, head), (head, each - head))):
                start = pl.multiple_of((x * each + first) * cells, cells)
                found.append(
                    pltpu.make_async_copy(
                        weights.at[target, pl.ds(start, size * cells), :],
                        outs[2 * at + half].at[pl.ds(0, size * cells), :],
                        sem.at[2 * at + half],
                    )
                )
        return found

    @pl.when(y == 0)
    def _():
        for copy in copies(ocean):
            copy.start()

    @pl.when(y == 1)
    def _():
        for copy in copies(atmos):
            copy.start()

    fraction = land[...]
    high = fraction.astype(jnp.bfloat16)
    low = (fraction - high.astype(jnp.float32)).astype(jnp.bfloat16)
    cap = ocean_tiles.shape[-1]
    for at, shift in enumerate(shifts):
        target = lax.rem(me + shift, bands)
        out, base = outs[2 * at], head * cells
        out[pl.ds(base, tiles), :] = high
        out[pl.ds(base + tiles, tiles), :] = low
        out[pl.ds(base + 2 * tiles, 32), :] = jnp.zeros((32, cells), jnp.bfloat16)
        for grid, ids in enumerate((ocean_tiles, atmos_tiles)):
            row = ids[pl.ds(target, 1), :].astype(jnp.float32)
            out[pl.ds(base + 2 * tiles + 16 * grid, 16), pl.ds(0, cap)] = jnp.broadcast_to(
                row, (16, cap)
            ).astype(jnp.bfloat16)
    for copy in copies(ocean):
        copy.wait()


def pack(shifts, head, each, ocean, atmos, ocean_tiles, atmos_tiles, land):
    cells = land.shape[-1]
    meta = 2 * land.shape[0] + 32
    any_spec = pl.BlockSpec(memory_space=pltpu.HBM)
    vmem = pl.BlockSpec(memory_space=pltpu.VMEM)
    sizes = [head * cells + meta, (each - head) * cells] * len(shifts)
    return pl.pallas_call(
        functools.partial(pack_kernel, shifts, head, each),
        out_shape=[jax.ShapeDtypeStruct((n, cells), jnp.bfloat16) for n in sizes],
        in_specs=[any_spec, any_spec, vmem, vmem, vmem],
        out_specs=[vmem] * len(sizes),
        scratch_shapes=[pltpu.SemaphoreType.DMA((len(sizes),))],
        cost_estimate=pl.CostEstimate(flops=0, bytes_accessed=2 << 20, transcendentals=0),
        compiler_params=pltpu.CompilerParams(vmem_limit_bytes=16 << 20),
    )(ocean, atmos, ocean_tiles, atmos_tiles, land)


def regrid_kernel(own, steps, meta_at, part_slots, table, where, fields, *refs):
    out, acc, scale = refs[-3:]
    parts, rest = refs[: len(part_slots)], refs[len(part_slots) :]
    rows, cells = fields.shape[1:]
    tiles = acc.shape[0] // rows
    if own:
        land = rest[0][...]
    else:
        meta, first = (parts[0], meta_at) if meta_at else (rest[0], 0)
        high = meta[pl.ds(first, tiles), :].astype(jnp.float32)
        land = high + meta[pl.ds(first + tiles, tiles), :].astype(jnp.float32)
    scale[pl.ds(0, tiles), :] = 1.0 - land
    scale[pl.ds(tiles, tiles), :] = land
    scale[pl.ds(2 * tiles, 8), :] = jnp.zeros((8, cells), jnp.float32)
    acc[...] = jnp.zeros_like(acc)
    for at, (part, size) in enumerate(zip(parts, part_slots)):
        first = where[1 + at]
        for s in range(size):
            slot = first + s
            weight = part[0, s] if own else part[pl.ds(s * cells, cells), :]
            dense = jnp.dot(
                fields[table[0, slot]], weight, preferred_element_type=jnp.float32
            )
            span = pl.ds(pl.multiple_of(table[1, slot] * rows, rows), rows)
            acc[span, :] += dense * scale[pl.ds(table[2, slot], 1), :]
    local_vars = rows // steps
    half_vars = local_vars // 2
    for v in range(local_vars):
        for q in range(2):
            column = (v % half_vars * 2 + q) * cells
            pieces = [
                acc[pl.ds(q * rows + t * local_vars + v, tiles // 2, 2 * rows), :]
                for t in range(steps)
            ]
            out[0, v // half_vars, :, pl.ds(column, cells)] = jnp.concatenate(
                pieces, axis=0
            ).astype(out.dtype)


def regrid(table, where, fields, parts, part_slots, rest, own, meta_at, previous, bands, steps, tiles):
    rows, cells = fields.shape[1:]
    whole = lambda a: pl.BlockSpec(a.shape, lambda i, t, w, n=a.ndim: (0,) * n)
    in_specs = [whole(fields)]
    for part in parts:
        if own:
            in_specs.append(pl.BlockSpec((1,) + part.shape[1:], lambda i, t, w: (w[0], 0, 0, 0)))
        else:
            in_specs.append(whole(part))
    in_specs += [whole(a) for a in rest]
    operands = [fields] + list(parts) + list(rest)
    aliases = {}
    if previous is not None:
        aliases = {2 + len(operands): 0}
        in_specs.append(pl.BlockSpec(memory_space=pl.ANY))
        operands.append(previous)
    row_count, width = steps * tiles // 2, rows // steps // 2 * 2 * cells
    return pl.pallas_call(
        functools.partial(regrid_kernel, own, steps, meta_at, tuple(part_slots)),
        out_shape=jax.ShapeDtypeStruct((bands, 2, row_count, width), jnp.bfloat16),
        grid_spec=pltpu.PrefetchScalarGridSpec(
            num_scalar_prefetch=2,
            grid=(1,),
            in_specs=in_specs,
            out_specs=pl.BlockSpec((1, 2, row_count, width), lambda i, t, w: (w[0], 0, 0, 0)),
            scratch_shapes=[
                pltpu.VMEM((tiles * rows, cells), jnp.float32),
                pltpu.VMEM((2 * tiles + 8, cells), jnp.float32),
            ],
        ),
        input_output_aliases=aliases,
        cost_estimate=pl.CostEstimate(
            flops=2 * sum(part_slots) * rows * cells * cells,
            bytes_accessed=4 << 20,
            transcendentals=0,
        ),
        compiler_params=pltpu.CompilerParams(vmem_limit_bytes=20 << 20),
    )(table, where, *operands)


def embed_kernel(steps, halves, rows_x, mine, theirs, out, total):
    at = pl.program_id(0)
    sub = lax.axis_index("sub")
    bands, _, row_count, width = rows_x.shape

    @pl.when(at == 0)
    def _():
        total[...] = jnp.zeros_like(total)

    left = rows_x[:, sub].reshape(bands * row_count, width)
    right = rows_x[:, 1 - sub].reshape(bands * row_count, width)
    total[...] += jnp.dot(left, mine[...], preferred_element_type=jnp.float32) + jnp.dot(
        right, theirs[...], preferred_element_type=jnp.float32
    )

    @pl.when(at == pl.num_programs(0) - 1)
    def _():
        if out.ndim == 2:
            out[...] = total[...].astype(out.dtype)
        else:
            share = row_count // (steps * halves)
            for chunk in range(steps * halves):
                pieces = [
                    total[pl.ds(b * row_count + chunk * share, share), :] for b in range(bands)
                ]
                out[chunk] = jnp.concatenate(pieces, axis=0).astype(out.dtype)


def embed(rows_x, mine, theirs, steps, halves):
    bands, _, row_count, half_width = rows_x.shape
    width = mine.shape[-1]
    grid = 6 if half_width % (6 * 256) == 0 else 3
    step_rows = half_width // grid
    rows = bands * row_count
    share = row_count // (steps * halves)
    if share % 4 == 0:
        shape = (steps * halves, bands * share, width)
    else:
        shape = (rows, width)
    weight_spec = pl.BlockSpec((step_rows, width), lambda i: (i, 0))
    out = pl.pallas_call(
        functools.partial(embed_kernel, steps, halves),
        out_shape=jax.ShapeDtypeStruct(shape, jnp.bfloat16),
        grid=(grid,),
        in_specs=[
            pl.BlockSpec((bands, 2, row_count, step_rows), lambda i: (0, 0, 0, i)),
            weight_spec,
            weight_spec,
        ],
        out_specs=pl.BlockSpec(shape, lambda i: (0,) * len(shape)),
        scratch_shapes=[pltpu.VMEM((rows, width), jnp.float32)],
        cost_estimate=pl.CostEstimate(
            flops=4 * rows * mine.shape[0] * width,
            bytes_accessed=4 * mine.shape[0] * width,
            transcendentals=0,
        ),
        compiler_params=pltpu.CompilerParams(
            vmem_limit_bytes=(48 if rows > 1024 else 16) << 20
        ),
    )(rows_x, mine, theirs)
    if share % 4:
        out = out.reshape(bands, steps * halves, share, width).transpose(1, 0, 2, 3)
        out = out.reshape(steps * halves, bands * share, width)
    return out


def swap(x, axis):
    return lax.ppermute(x, axis, [(0, 1), (1, 0)])


def per_device(
    ocean_fields,
    ocean_dest,
    ocean_weights,
    ocean_tiles,
    atmos_fields,
    atmos_dest,
    atmos_weights,
    atmos_tiles,
    land_fraction,
    embed_weight,
    embed_bias,
    embed_gain,
):
    nb = lax.axis_size("band")
    nv = lax.axis_size("var")
    ng = lax.axis_size("grp")
    rep = nv * ng
    cap = ocean_weights.shape[3]
    cells = ocean_weights.shape[-1]
    block_count, steps, local_vars, _ = ocean_fields.shape
    patches = land_fraction.shape[2]
    tiles = 2 * patches
    slots = 2 * cap
    share = patches // nv
    me = lax.axis_index("band")
    x, y = lax.axis_index("var"), lax.axis_index("grp")
    quarter = y * nv + x

    embed_other = swap(embed_weight, "sub")

    ocean_w = ocean_weights.reshape(nb, cap, cells, cells)
    atmos_w = atmos_weights.reshape(nb, cap, cells, cells)
    ocean_ids, atmos_ids = ocean_tiles.reshape(nb, cap), atmos_tiles.reshape(nb, cap)
    land = land_fraction.reshape(tiles, cells)
    order = ([1, nb - 1] + list(range(2, nb - 1)))[: nb - 1]
    paired = ng == 2 and nv == 2 and cap % 2 == 0
    each = cap // 2
    head = (each + 1) // 2
    if paired:
        flat = (nb, cap * cells, cells)
        pieces = pack(
            order, head, each, ocean_w.reshape(flat), atmos_w.reshape(flat), ocean_ids, atmos_ids, land
        )

    def slots_of(ocean_dest, atmos_dest):
        ocean_block, ocean_used = slot_tables(ocean_dest, nb, cap)
        atmos_block, atmos_used = slot_tables(atmos_dest, nb, cap)
        return (
            jnp.concatenate([ocean_block, atmos_block + block_count], axis=1),
            jnp.concatenate([ocean_used, atmos_used], axis=1),
        )

    block_all, used_all = slots_of(ocean_dest, atmos_dest)
    grid_row = jnp.where(jnp.arange(slots) < cap, 0, tiles)
    fields = jnp.concatenate([ocean_fields, atmos_fields], axis=0).reshape(
        2 * block_count, steps * local_vars, cells
    )

    def table_of(band, tile):
        block = lax.dynamic_index_in_dim(block_all, band, 0, keepdims=False)
        used = lax.dynamic_index_in_dim(used_all, band, 0, keepdims=False)
        scale = jnp.where(used, tile + grid_row, 2 * tiles)
        return jnp.stack([block, tile, scale]).astype(jnp.int32)

    tile_ids = jnp.concatenate([ocean_ids, atmos_ids], axis=1)
    own_tile = lax.dynamic_index_in_dim(tile_ids, me, 0, keepdims=False)
    where = jnp.stack([me, jnp.int32(0), jnp.int32(cap)])
    call = functools.partial(regrid, bands=nb, steps=steps, tiles=tiles)
    rows_x = call(
        table_of(me, own_tile), where, fields, [ocean_w, atmos_w], [cap, cap], [land], True, 0, None
    )

    if paired:
        sent = []
        for at, piece in enumerate(pieces):
            shift = order[at // 2]
            if at >= 2:
                piece, sent[at - 2] = lax.optimization_barrier((piece, sent[at - 2]))
            sent.append(lax.ppermute(piece, "band", [(b, (b + shift) % nb) for b in range(nb)]))
        for at, shift in enumerate(order):
            parts, sizes, firsts = [], [], []
            for half, (first, size) in enumerate(((0, head), (head, each - head))):
                piece = sent[2 * at + half]
                axes = ("var", "grp") if (half + at) % 2 == 0 else ("grp", "var")
                one, two = swap(piece, axes[0]), swap(piece, axes[1])
                both = swap(one, axes[1])
                by_x, by_y = (one, two) if axes[0] == "var" else (two, one)
                parts += [piece, by_x, by_y, both]
                sizes += [size] * 4
                firsts += [
                    (qy * 2 + qx) * each + first
                    for qx, qy in ((x, y), (1 - x, y), (x, 1 - y), (1 - x, 1 - y))
                ]
            band = (me - shift) % nb
            tail = parts[0][head * cells + 2 * tiles :]
            tile = jnp.concatenate([tail[0, :cap], tail[16, :cap]]).astype(jnp.int32)
            where = jnp.stack([band] + firsts).astype(jnp.int32)
            rows_x = call(
                table_of(band, tile), where, fields, parts, sizes, [], False, head * cells, rows_x
            )
    else:
        both = jnp.concatenate([ocean_w, atmos_w], axis=1).reshape(nb, slots * cells, cells)
        share_rows = slots * cells // rep
        high = lax.reduce_precision(land, 8, 7)
        low = (land - high).astype(jnp.bfloat16)
        tile_rows = jnp.pad(tile_ids.astype(jnp.bfloat16), ((0, 0), (0, cells - slots)))
        for shift in order:
            target, band = (me + shift) % nb, (me - shift) % nb
            piece = lax.dynamic_slice(
                both, (target, quarter * share_rows, 0), (1, share_rows, cells)
            )[0]
            row = lax.dynamic_slice(tile_rows, (target, 0), (1, cells))
            row = jnp.broadcast_to(row, (16, cells))
            piece = jnp.concatenate([piece, high.astype(jnp.bfloat16), low, row], axis=0)
            piece = lax.ppermute(piece, "band", [(b, (b + shift) % nb) for b in range(nb)])
            parts = lax.all_gather(piece, REPL, axis=0)
            meta = parts[0, share_rows:]
            tile = meta[2 * tiles, :slots].astype(jnp.int32)
            parts = parts[:, :share_rows].reshape(slots * cells, cells)
            where = jnp.stack([band, jnp.int32(0)]).astype(jnp.int32)
            rows_x = call(
                table_of(band, tile), where, fields, [parts], [slots], [meta], False, 0, rows_x
            )

    sent = embed(rows_x, embed_weight, embed_other, steps, nv)
    got = lax.all_to_all(sent, ("band", "var"), split_axis=0, concat_axis=0, tiled=True)
    shifted = jnp.sum(got.astype(jnp.float32), axis=0) + embed_bias
    inverse = lax.rsqrt(jnp.mean(shifted * shifted, axis=-1, keepdims=True) + 1e-05)
    finished = (shifted * inverse * embed_gain).astype(jnp.bfloat16)
    width = finished.shape[-1]
    finished = finished.reshape(nb, share, steps // nb, width).transpose(1, 0, 2, 3)
    return finished[None]


def solution(mesh):
    in_specs = (
        P(("grp", "band", "sub"), None, "var", None),
        P(("band", "sub"), None),
        P("band", "sub", None, None, None, None),
        P("band", "sub", None, None),
        P(("grp", "band", "sub"), None, "var", None),
        P(("band", "sub"), None),
        P("band", "sub", None, None, None, None),
        P("band", "sub", None, None),
        P("band", "sub", None, None, None),
        P(("var", "sub"), None),
        P(),
        P(),
    )
    out_specs = P("sub", "var", None, ("grp", "band"), None)
    return jax.shard_map(
        per_device, mesh=mesh, in_specs=in_specs, out_specs=out_specs, check_vma=False
    )
```

time: 93.9 us -> 90 us (0.958)
  blocking collectives: 37.2 us -> 14.4 us
  waiting for transfers between devices: 3.78 us -> 23.5 us
  matrix products: 7.75 us -> 0 us
  Pallas kernels: 6.27 us -> 12.7 us
  starting transfers between devices: 20.8 us -> 26.1 us
  other arithmetic: 6.04 us -> 3.02 us
  local copies, waits for them, and re-layouts: 11.4 us -> 9.46 us
    all_gather x1 -> x0, blocking collectives: 24.8 us -> none  [per_device(): lax.all_gather(jnp.concatenate([land_fraction.reshape(tiles, cells), flat...]
    ppermute x3 -> x6, waiting for transfers between devices: 0.01 us -> 10.8 us  [per_device(): lax.ppermute(piece, 'band', [(b, (b + shift) % nb) for b in range(nb)])]
    ppermute x13 -> x19, waiting for transfers between devices: 3.77 us -> 12.7 us  [swap(): return lax.ppermute(x, axis, [(0, 1), (1, 0)])]
    dot_general x2 -> x0, matrix products: 7.75 us -> none  [the longest x1 3.89 us: per_device(): jnp.dot(theirs, embed_other, preferred_element_type=jnp.float32)]
    pallas_call x4 -> x6, Pallas kernels: 6.27 us -> 12.7 us  [the longest x1 5.9 us: embed(): pl.pallas_call(functools.partial(embed_kernel, steps, halves), out_shape=...]
    unnamed x22 -> x32, local copies, waits for them, and re-layouts: 3.04 us -> 8.1 us
    dynamic_slice x2 -> x1, local copies, waits for them, and re-layouts: 3.25 us -> 0.01 us  [table_of(): block = lax.dynamic_index_in_dim(block_all, band, 0, keepdims=False)]
    ppermute x13 -> x19, starting transfers between devices: 15.2 us -> 17.9 us  [swap(): return lax.ppermute(x, axis, [(0, 1), (1, 0)])]
  transfers between devices with their start and end apart: 16 -> 25, of which waited for: 3 -> 11; matrix products, arithmetic and copies ran while one was open for 19% -> 4% of each run, Pallas kernels for 7% -> 8%
where the time goes in v3:
time: 90 us; the launch traced here: 89.5 us
  starting transfers between devices  26.1 us (29%)
  waiting for transfers between devices  23.5 us (26%)
  blocking collectives  14.4 us (16%)
  Pallas kernels  12.7 us (14%)
  local copies, waits for them, and re-layouts  9.46 us (11%)
  other arithmetic  3.02 us (3%)
    ppermute x19, starting transfers between devices, swap(): return lax.ppermute(x, axis, [(0, 1), (1, 0)])  17.9 us
    all_to_all x1, blocking collectives, per_device(): lax.all_to_all(sent, ('band', 'var'), split_axis=0, concat_axis=0, tiled=...  14.4 us
    ppermute x19, waiting for transfers between devices, swap(): return lax.ppermute(x, axis, [(0, 1), (1, 0)])  12.7 us
    ppermute x6, waiting for transfers between devices, per_device(): lax.ppermute(piece, 'band', [(b, (b + shift) % nb) for b in range(nb)])  10.8 us
    ppermute x6, starting transfers between devices, per_device(): lax.ppermute(piece, 'band', [(b, (b + shift) % nb) for b in range(nb)])  8.22 us
    unnamed x32, local copies, waits for them, and re-layouts  8.1 us
    pallas_call x1, Pallas kernels, embed(): pl.pallas_call(functools.partial(embed_kernel, steps, halves), out_shape=...  5.9 us
    pallas_call x4, Pallas kernels, regrid(): pl.pallas_call(functools.partial(regrid_kernel, own, steps, meta_at, tupl...  5.79 us
  transfers between devices with their start and end apart: 25, of which 11 were waited for; matrix products, arithmetic and copies ran while one was open for 4% of the time, Pallas kernels for 8%

profile of v3, /device:TPU:0, one launch (start us, length us, event | category | flops | bytes accessed | tf_op | source)
XLA Modules:
  0.0 89.5 jit_solution(1797626744720266098)
XLA Ops:
  0.0 0.5 collective-permute-start.24
  0.5 1.5 %copy-done = bf16[1,1,4,14,128,128]{5,4,3,2,1,0:T(8,128)(2,1)S(1)} copy-done((bf16[1,1,4,14,128,128]{5,4,3,2,1,0:T(8,128)(2,1)S(1)}, bf16[1,1,4,14,128,128]{5,4,3,2,1,0:T(8,128)(2,1)}, u32[]{:S(2)}) %copy-start) | copy-done | bytes 1835032
  2.0 1.5 %copy-done.2 = bf16[1,1,4,14,128,128]{5,4,3,2,1,0:T(8,128)(2,1)S(1)} copy-done((bf16[1,1,4,14,128,128]{5,4,3,2,1,0:T(8,128)(2,1)S(1)}, bf16[1,1,4,14,128,128]{5,4,3,2,1,0:T(8,128)(2,1)}, u32[]{:S(2)}) %copy-start.2) | copy-done | bytes 1835032
  3.5 0.7 copy-done.4
  4.2 0.7 copy-done.6
  4.8 0.7 copy-done.8
  5.5 1.0 %shard_map.118 = (bf16[576,128]{1,0:T(8,128)(2,1)S(1)}, bf16[384,128]{1,0:T(8,128)(2,1)S(1)}, bf16[576,128]{1,0:T(8,128)(2,1)S(1)}, bf16[384,128]{1,0:T(8,128)(2...) custom-call(bf16[4,1792,128]{2,1,0:T(8,128)(2,1)S(1)} %bitcast.32, ...), custom_call_target="tpu_custom_call" | custom-call | bytes 2097152 | tf_op jit(solution)/shard_map/pallas_call | solution.py:83
  6.5 2.6 %collective-permute-start.6 = (bf16[384,128]{1,0:T(8,128)(2,1)S(1)}, bf16[384,128]{1,0:T(8,128)(2,1)S(1)}, u32[]{:S(2)}, u32[]{:S(2)}) collective-permute-start(bf16[384,128]{1,0:T(8,128)(2,1)S(1)} %get-tuple-element.26), channel_id=1, source_target_pairs={{0,4},{4,8},{8,12},{12,0},{1,5},{5,9},{9,13},{13,1},{2,6},{6,10},{... | collective-permute-start | bytes 294920 | tf_op jit(solution)/shard_map/ppermute | solution.py:322
  9.2 1.6 %collective-permute-start = (bf16[576,128]{1,0:T(8,128)(2,1)S(1)}, bf16[576,128]{1,0:T(8,128)(2,1)S(1)}, u32[]{:S(2)}, u32[]{:S(2)}) collective-permute-start(bf16[576,128]{1,0:T(8,128)(2,1)S(1)} %get-tuple-element.21), channel_id=1, source_target_pairs={{0,4},{4,8},{8,12},{12,0},{1,5},{5,9},{9,13},{13,1},{2,6},{6,10},{... | collective-permute-start | bytes 442376 | tf_op jit(solution)/shard_map/ppermute | solution.py:322
  12.0 1.6 %pad_maximum_fusion = bf16[72,4,24,128]{3,2,1,0:T(8,128)(2,1)S(1)} fusion(bf16[36,4,24,128]{3,2,1,0:T(8,128)(2,1)} %param.16, bf16[36,4,24,128]{3,2,1,0:T(8,128)(2,1)} %param.12), kind=kLoop, calls=%fused_computation | loop fusion | flops 884736 | bytes 3538944 | tf_op jit(solution)/shard_map/concatenate | solution.py:298
  14.1 0.8 collective-permute-done.6.refs_4_
  14.8 1.6 %collective-permute-start.22 = (bf16[384,128]{1,0:T(8,128)(2,1)S(1)}, bf16[384,128]{1,0:T(8,128)(2,1)S(1)}, u32[]{:S(2)}, u32[]{:S(2)}) collective-permute-start(bf16[384,128]{1,0:T(8,128)(2,1)S(1)} %collective-permute-done.6.refs_4_), channel_id=1, source_target_pairs={{0,16},{16,0},{1,17},{17,1},{2,18},{18,2},{3,19},{19,3},{4,20},{20... | collective-permute-start | bytes 294920 | tf_op jit(solution)/shard_map/ppermute | solution.py:240
  16.5 1.5 %collective-permute-start.21 = (bf16[384,128]{1,0:T(8,128)(2,1)S(1)}, bf16[384,128]{1,0:T(8,128)(2,1)S(1)}, u32[]{:S(2)}, u32[]{:S(2)}) collective-permute-start(bf16[384,128]{1,0:T(8,128)(2,1)S(1)} %collective-permute-done.6.refs_4_), channel_id=1, source_target_pairs={{0,2},{2,0},{1,3},{3,1},{4,6},{6,4},{5,7},{7,5},{8,10},{10,8},{9,1... | collective-permute-start | bytes 294920 | tf_op jit(solution)/shard_map/ppermute | solution.py:240
  18.0 1.8 %collective-permute-start.7 = (bf16[384,128]{1,0:T(8,128)(2,1)S(1)}, bf16[384,128]{1,0:T(8,128)(2,1)S(1)}, u32[]{:S(2)}, u32[]{:S(2)}) collective-permute-start(bf16[384,128]{1,0:T(8,128)(2,1)S(1)} %get-tuple-element.27), channel_id=1, source_target_pairs={{0,12},{4,0},{8,4},{12,8},{1,13},{5,1},{9,5},{13,9},{2,14},{6,2},{... | collective-permute-start | bytes 294920 | tf_op jit(solution)/shard_map/ppermute | solution.py:322
  20.2 3.3 %collective-permute-done.7.refs_4_ = bf16[384,128]{1,0:T(8,128)(2,1)S(1)} collective-permute-done((bf16[384,128]{1,0:T(8,128)(2,1)S(1)}, bf16[384,128]{1,0:T(8,128)(2,1)S(1)}, u32[]{:S(2)}, u32[]{:S(2)}) %collective-permute-start.7) | collective-permute-done | bytes 98336 | tf_op jit(solution)/shard_map/ppermute | solution.py:322
  23.6 0.8 collective-permute-start.8
  24.4 1.4 %collective-permute-done.1.refs_0_ = bf16[576,128]{1,0:T(8,128)(2,1)S(1)} collective-permute-done((bf16[576,128]{1,0:T(8,128)(2,1)S(1)}, bf16[576,128]{1,0:T(8,128)(2,1)S(1)}, u32[]{:S(2)}, u32[]{:S(2)}) %collective-permute-start.1) | collective-permute-done | bytes 147488 | tf_op jit(solution)/shard_map/ppermute | solution.py:322
  25.8 0.8 collective-permute-start.16
  26.6 0.9 %collective-permute-start.2 = (bf16[576,128]{1,0:T(8,128)(2,1)S(1)}, bf16[576,128]{1,0:T(8,128)(2,1)S(1)}, u32[]{:S(2)}, u32[]{:S(2)}) collective-permute-start(bf16[576,128]{1,0:T(8,128)(2,1)S(1)} %get-tuple-element.23), channel_id=1, source_target_pairs={{0,8},{4,12},{8,0},{12,4},{1,9},{5,13},{9,1},{13,5},{2,10},{6,14},... | collective-permute-start | bytes 442376 | tf_op jit(solution)/shard_map/ppermute | solution.py:322
  27.5 1.5 %collective-permute-start.19 = (bf16[576,128]{1,0:T(8,128)(2,1)S(1)}, bf16[576,128]{1,0:T(8,128)(2,1)S(1)}, u32[]{:S(2)}, u32[]{:S(2)}) collective-permute-start(bf16[576,128]{1,0:T(8,128)(2,1)S(1)} %collective-permute-done.refs_0_), channel_id=1, source_target_pairs={{0,16},{16,0},{1,17},{17,1},{2,18},{18,2},{3,19},{19,3},{4,20},{20... | collective-permute-start | bytes 442376 | tf_op jit(solution)/shard_map/ppermute | solution.py:240
  29.0 5.3 %collective-permute-done.8.refs_4_ = bf16[384,128]{1,0:T(8,128)(2,1)S(1)} collective-permute-done((bf16[384,128]{1,0:T(8,128)(2,1)S(1)}, bf16[384,128]{1,0:T(8,128)(2,1)S(1)}, u32[]{:S(2)}, u32[]{:S(2)}) %collective-permute-start.8) | collective-permute-done | bytes 98336 | tf_op jit(solution)/shard_map/ppermute | solution.py:322
  34.4 2.0 %collective-permute-start.15 = (bf16[384,128]{1,0:T(8,128)(2,1)S(1)}, bf16[384,128]{1,0:T(8,128)(2,1)S(1)}, u32[]{:S(2)}, u32[]{:S(2)}) collective-permute-start(bf16[384,128]{1,0:T(8,128)(2,1)S(1)} %collective-permute-done.7.refs_4_), channel_id=1, source_target_pairs={{0,2},{2,0},{1,3},{3,1},{4,6},{6,4},{5,7},{7,5},{8,10},{10,8},{9,1... | collective-permute-start | bytes 294920 | tf_op jit(solution)/shard_map/ppermute | solution.py:240
  36.4 0.6 collective-permute-start.23
  37.0 4.6 %collective-permute-done.15.refs_5_ = bf16[384,128]{1,0:T(8,128)(2,1)S(1)} collective-permute-done((bf16[384,128]{1,0:T(8,128)(2,1)S(1)}, bf16[384,128]{1,0:T(8,128)(2,1)S(1)}, u32[]{:S(2)}, u32[]{:S(2)}) %collective-permute-start.15) | collective-permute-done | bytes 98336 | tf_op jit(solution)/shard_map/ppermute | solution.py:240
  41.5 1.0 %collective-permute-done.23.refs_7_ = bf16[384,128]{1,0:T(8,128)(2,1)S(1)} collective-permute-done((bf16[384,128]{1,0:T(8,128)(2,1)S(1)}, bf16[384,128]{1,0:T(8,128)(2,1)S(1)}, u32[]{:S(2)}, u32[]{:S(2)}) %collective-permute-start.23) | collective-permute-done | bytes 98336 | tf_op jit(solution)/shard_map/ppermute | solution.py:240
  42.6 1.0 %collective-permute-start.10 = (bf16[384,128]{1,0:T(8,128)(2,1)S(1)}, bf16[384,128]{1,0:T(8,128)(2,1)S(1)}, u32[]{:S(2)}, u32[]{:S(2)}) collective-permute-start(bf16[384,128]{1,0:T(8,128)(2,1)S(1)} %collective-permute-done.8.refs_4_), channel_id=1, source_target_pairs={{0,16},{16,0},{1,17},{17,1},{2,18},{18,2},{3,19},{19,3},{4,20},{20... | collective-permute-start | bytes 294920 | tf_op jit(solution)/shard_map/ppermute | solution.py:240
  43.7 1.1 %collective-permute-start.17 = (bf16[384,128]{1,0:T(8,128)(2,1)S(1)}, bf16[384,128]{1,0:T(8,128)(2,1)S(1)}, u32[]{:S(2)}, u32[]{:S(2)}) collective-permute-start(bf16[384,128]{1,0:T(8,128)(2,1)S(1)} %collective-permute-done.15.refs_5_), channel_id=1, source_target_pairs={{0,16},{16,0},{1,17},{17,1},{2,18},{18,2},{3,19},{19,3},{4,20},{20... | collective-permute-start | bytes 294920 | tf_op jit(solution)/shard_map/ppermute | solution.py:240
  44.8 1.0 %collective-permute-start.20 = (bf16[576,128]{1,0:T(8,128)(2,1)S(1)}, bf16[576,128]{1,0:T(8,128)(2,1)S(1)}, u32[]{:S(2)}, u32[]{:S(2)}) collective-permute-start(bf16[576,128]{1,0:T(8,128)(2,1)S(1)} %collective-permute-done.18.refs_1_), channel_id=1, source_target_pairs={{0,16},{16,0},{1,17},{17,1},{2,18},{18,2},{3,19},{19,3},{4,20},{20... | collective-permute-start | bytes 442376 | tf_op jit(solution)/shard_map/ppermute | solution.py:240
  45.7 3.2 %collective-permute-done.10.refs_6_ = bf16[384,128]{1,0:T(8,128)(2,1)S(1)} collective-permute-done((bf16[384,128]{1,0:T(8,128)(2,1)S(1)}, bf16[384,128]{1,0:T(8,128)(2,1)S(1)}, u32[]{:S(2)}, u32[]{:S(2)}) %collective-permute-start.10) | collective-permute-done | bytes 98336 | tf_op jit(solution)/shard_map/ppermute | solution.py:240
  48.9 1.3 %collective-permute-start.3 = (bf16[576,128]{1,0:T(8,128)(2,1)S(1)}, bf16[576,128]{1,0:T(8,128)(2,1)S(1)}, u32[]{:S(2)}, u32[]{:S(2)}) collective-permute-start(bf16[576,128]{1,0:T(8,128)(2,1)S(1)} %collective-permute-done.2.refs_0_), channel_id=1, source_target_pairs={{0,2},{2,0},{1,3},{3,1},{4,6},{6,4},{5,7},{7,5},{8,10},{10,8},{9,1... | collective-permute-start | bytes 442376 | tf_op jit(solution)/shard_map/ppermute | solution.py:240
  50.3 1.0 %collective-permute-start.12 = (bf16[576,128]{1,0:T(8,128)(2,1)S(1)}, bf16[576,128]{1,0:T(8,128)(2,1)S(1)}, u32[]{:S(2)}, u32[]{:S(2)}) collective-permute-start(bf16[576,128]{1,0:T(8,128)(2,1)S(1)} %collective-permute-done.1.refs_0_), channel_id=1, source_target_pairs={{0,2},{2,0},{1,3},{3,1},{4,6},{6,4},{5,7},{7,5},{8,10},{10,8},{9,1... | collective-permute-start | bytes 442376 | tf_op jit(solution)/shard_map/ppermute | solution.py:240
  51.3 1.1 %collective-permute-start.14 = (bf16[576,128]{1,0:T(8,128)(2,1)S(1)}, bf16[576,128]{1,0:T(8,128)(2,1)S(1)}, u32[]{:S(2)}, u32[]{:S(2)}) collective-permute-start(bf16[576,128]{1,0:T(8,128)(2,1)S(1)} %collective-permute-done.13.refs_2_), channel_id=1, source_target_pairs={{0,2},{2,0},{1,3},{3,1},{4,6},{6,4},{5,7},{7,5},{8,10},{10,8},{9,1... | collective-permute-start | bytes 442376 | tf_op jit(solution)/shard_map/ppermute | solution.py:240
  52.4 0.5 collective-permute-done.20.refs_3_
  52.9 1.1 %collective-permute-done.3.refs_1_ = bf16[576,128]{1,0:T(8,128)(2,1)S(1)} collective-permute-done((bf16[576,128]{1,0:T(8,128)(2,1)S(1)}, bf16[576,128]{1,0:T(8,128)(2,1)S(1)}, u32[]{:S(2)}, u32[]{:S(2)}) %collective-permute-start.3) | collective-permute-done | bytes 147488 | tf_op jit(solution)/shard_map/ppermute | solution.py:240
  54.1 0.9 collective-permute-start.5
  55.0 1.5 %copy-done.1 = bf16[1,1,4,14,128,128]{5,4,3,2,1,0:T(8,128)(2,1)S(1)} copy-done((bf16[1,1,4,14,128,128]{5,4,3,2,1,0:T(8,128)(2,1)S(1)}, bf16[1,1,4,14,128,128]{5,4,3,2,1,0:T(8,128)(2,1)}, u32[]{:S(2)}) %copy-start.1) | copy-done | bytes 1835032
  56.5 1.5 %copy-done.3 = bf16[1,1,4,14,128,128]{5,4,3,2,1,0:T(8,128)(2,1)S(1)} copy-done((bf16[1,1,4,14,128,128]{5,4,3,2,1,0:T(8,128)(2,1)S(1)}, bf16[1,1,4,14,128,128]{5,4,3,2,1,0:T(8,128)(2,1)}, u32[]{:S(2)}) %copy-start.3) | copy-done | bytes 1835032
  58.0 1.4 %shard_map.119.refs_8_ = bf16[4,2,32,3072]{3,2,1,0:T(8,128)(2,1)S(1)} custom-call(s32[3,28]{1,0:T(4,128)S(1)} %pad_add_fusion.5.table, s32[3]{0:T(128)S(1)} %pad_add_fusion.7.where, bf16[72,96,128]{2,1,0:T(8,128)(2,1)S(1)} %bitcast.28, bf16[4,14,128,128]{3,2,1,0:T(8,128)(2,1)S(1)} %bitcast.33, bf16[4,14,128,128]{3,2,1,0:T(8,128)(2,1)S(1)} %bitcast.35, ...), custom_call_target="tpu_custom_call" | custom-call | flops 88080384 | bytes 4194304 | tf_op jit(solution)/shard_map/pallas_call | solution.py:150
  59.4 1.5 %shard_map.120.refs_8_ = bf16[4,2,32,3072]{3,2,1,0:T(8,128)(2,1)S(1)} custom-call(s32[3,28]{1,0:T(4,128)S(1)} %pad_add_fusion.3.table, s32[9]{0:T(128)S(1)} %stack.104.where, bf16[72,96,128]{2,1,0:T(8,128)(2,1)S(1)} %bitcast.29, bf16[576,128]{1,0:T(8,128)(2,1)S(1)} %collective-permute-done.refs_0_, ...), custom_call_target="tpu_custom_call", output_to_operand_aliasing={{}: (11, {})} | custom-call | flops 88080384 | bytes 4194304 | tf_op jit(solution)/shard_map/pallas_call | solution.py:150
  60.9 0.6 collective-permute-start.9
  61.4 1.5 %collective-permute-start.11 = (bf16[384,128]{1,0:T(8,128)(2,1)S(1)}, bf16[384,128]{1,0:T(8,128)(2,1)S(1)}, u32[]{:S(2)}, u32[]{:S(2)}) collective-permute-start(bf16[384,128]{1,0:T(8,128)(2,1)S(1)} %collective-permute-done.10.refs_6_), channel_id=1, source_target_pairs={{0,2},{2,0},{1,3},{3,1},{4,6},{6,4},{5,7},{7,5},{8,10},{10,8},{9,1... | collective-permute-start | bytes 294920 | tf_op jit(solution)/shard_map/ppermute | solution.py:240
  63.0 1.5 %shard_map.121.refs_8_ = bf16[4,2,32,3072]{3,2,1,0:T(8,128)(2,1)S(1)} custom-call(s32[3,28]{1,0:T(4,128)S(1)} %pad_add_fusion.2.table, s32[9]{0:T(128)S(1)} %stack.101.where, bf16[72,96,128]{2,1,0:T(8,128)(2,1)S(1)} %bitcast.30, bf16[576,128]{1,0:T(8,128)(2,1)S(1)} %collective-permute-done.1.refs_0_, ...), custom_call_target="tpu_custom_call", output_to_operand_aliasing={{}: (11, {})} | custom-call | flops 88080384 | bytes 4194304 | tf_op jit(solution)/shard_map/pallas_call | solution.py:150
  64.5 1.1 %collective-permute-done.9.refs_5_ = bf16[384,128]{1,0:T(8,128)(2,1)S(1)} collective-permute-done((bf16[384,128]{1,0:T(8,128)(2,1)S(1)}, bf16[384,128]{1,0:T(8,128)(2,1)S(1)}, u32[]{:S(2)}, u32[]{:S(2)}) %collective-permute-start.9) | collective-permute-done | bytes 98336 | tf_op jit(solution)/shard_map/ppermute | solution.py:240
  65.6 1.1 %collective-permute-done.11.refs_7_ = bf16[384,128]{1,0:T(8,128)(2,1)S(1)} collective-permute-done((bf16[384,128]{1,0:T(8,128)(2,1)S(1)}, bf16[384,128]{1,0:T(8,128)(2,1)S(1)}, u32[]{:S(2)}, u32[]{:S(2)}) %collective-permute-start.11) | collective-permute-done | bytes 98336 | tf_op jit(solution)/shard_map/ppermute | solution.py:240
  66.6 1.4 %shard_map.122.rows_x = bf16[4,2,32,3072]{3,2,1,0:T(8,128)(2,1)S(1)} custom-call(s32[3,28]{1,0:T(4,128)S(1)} %pad_add_fusion.1.table, s32[9]{0:T(128)S(1)} %stack.98.where, bf16[72,96,128]{2,1,0:T(8,128)(2,1)S(1)} %bitcast.31, bf16[576,128]{1,0:T(8,128)(2,1)S(1)} %collective-permute-done.2.refs_0_, ...), custom_call_target="tpu_custom_call", output_to_operand_aliasing={{}: (11, {})} | custom-call | flops 88080384 | bytes 4194304 | tf_op jit(solution)/shard_map/pallas_call | solution.py:150
  68.1 5.9 %shard_map.123 = bf16[8,16,1024]{2,1,0:T(8,128)(2,1)S(1)} custom-call(bf16[4,2,32,3072]{3,2,1,0:T(8,128)(2,1)S(1)} %shard_map.122.rows_x, bf16[3072,1024]{1,0:T(8,128)(2,1)S(1)} %bitcast.37, bf16[3072,1024]{1,0:T(8,128)(2,1)} %collective-permute-done.24.theirs), custom_call_target="tpu_custom_call" | custom-call | flops 1610612736 | bytes 12582912 | tf_op jit(solution)/shard_map/pallas_call | solution.py:213
  74.0 14.4 %all_to_all.5 = bf16[8,16,1024]{2,1,0:T(8,128)(2,1)S(1)} all-to-all(bf16[8,16,1024]{2,1,0:T(8,128)(2,1)S(1)} %shard_map.123), channel_id=1, replica_groups=mesh['grp'=2,'band'=4,'var'=2,'sub'=2] {'band','var'}, dimensions={0} | all-to-all | bytes 524288 | tf_op jit(solution)/shard_map/all_to_all | solution.py:369
  88.9 0.6 copy.18
  (79 shorter events, 2.7 us)
Async XLA Ops:
  0.0 68.1 %collective-permute-start.24 = (bf16[3072,1024]{1,0:T(8,128)(2,1)}, bf16[3072,1024]{1,0:T(8,128)(2,1)}, u32[]{:S(2)}, u32[]{:S(2)}) collective-permute-start(bf16[3072,1024]{1,0:T(8,128)(2,1)} %mine.1), channel_id=1, source_target_pairs={{0,1},{1,0},{2,3},{3,2},{4,5},{5,4},{6,7},{7,6},{8,9},{9,8},{10,11... | collective-permute-start | bytes 18874376 | tf_op jit(solution)/shard_map/ppermute | solution.py:240
  0.5 1.5 %copy-start = (bf16[1,1,4,14,128,128]{5,4,3,2,1,0:T(8,128)(2,1)S(1)}, bf16[1,1,4,14,128,128]{5,4,3,2,1,0:T(8,128)(2,1)}, u32[]{:S(2)}) copy-start(bf16[1,1,4,14,128,128]{5,4,3,2,1,0:T(8,128)(2,1)} %param.14) | copy-start | bytes 5505028
  2.0 1.5 %copy-start.2 = (bf16[1,1,4,14,128,128]{5,4,3,2,1,0:T(8,128)(2,1)S(1)}, bf16[1,1,4,14,128,128]{5,4,3,2,1,0:T(8,128)(2,1)}, u32[]{:S(2)}) copy-start(bf16[1,1,4,14,128,128]{5,4,3,2,1,0:T(8,128)(2,1)} %param.18) | copy-start | bytes 5505028
  3.5 0.7 copy-start.4
  4.2 0.7 copy-start.6
  4.8 0.7 copy-start.8
  5.5 5.2 %copy-start.12 = (s32[36,1]{0,1:T(1,128)S(1)}, s32[36,1]{0,1:T(1,128)}, u32[]{:S(2)}) copy-start(s32[36,1]{0,1:T(1,128)} %param.17) | copy-start | bytes 436
  5.5 5.6 %copy-start.13 = (s32[36,1]{0,1:T(1,128)S(1)}, s32[36,1]{0,1:T(1,128)}, u32[]{:S(2)}) copy-start(s32[36,1]{0,1:T(1,128)} %param.13) | copy-start | bytes 436
  5.5 6.3 %copy-start.7 = (s32[1,1,4,14]{3,2,1,0:T(4,128)S(1)}, s32[1,1,4,14]{3,2,1,0:T(4,128)}, u32[]{:S(2)}) copy-start(s32[1,1,4,14]{3,2,1,0:T(4,128)} %param.19) | copy-start | bytes 676
  5.5 6.3 %copy-start.9 = (s32[1,1,4,14]{3,2,1,0:T(4,128)S(1)}, s32[1,1,4,14]{3,2,1,0:T(4,128)}, u32[]{:S(2)}) copy-start(s32[1,1,4,14]{3,2,1,0:T(4,128)} %param.15) | copy-start | bytes 676
  6.5 8.3 %collective-permute-start.6 = (bf16[384,128]{1,0:T(8,128)(2,1)S(1)}, bf16[384,128]{1,0:T(8,128)(2,1)S(1)}, u32[]{:S(2)}, u32[]{:S(2)}) collective-permute-start(bf16[384,128]{1,0:T(8,128)(2,1)S(1)} %get-tuple-element.26), channel_id=1, source_target_pairs={{0,4},{4,8},{8,12},{12,0},{1,5},{5,9},{9,13},{13,1},{2,6},{6,10},{... | collective-permute-start | bytes 294920 | tf_op jit(solution)/shard_map/ppermute | solution.py:322
  9.2 10.6 %collective-permute-start = (bf16[576,128]{1,0:T(8,128)(2,1)S(1)}, bf16[576,128]{1,0:T(8,128)(2,1)S(1)}, u32[]{:S(2)}, u32[]{:S(2)}) collective-permute-start(bf16[576,128]{1,0:T(8,128)(2,1)S(1)} %get-tuple-element.21), channel_id=1, source_target_pairs={{0,4},{4,8},{8,12},{12,0},{1,5},{5,9},{9,13},{13,1},{2,6},{6,10},{... | collective-permute-start | bytes 442376 | tf_op jit(solution)/shard_map/ppermute | solution.py:322
  12.0 42.9 %copy-start.5 = (f32[1,1,8,2,128]{4,3,2,1,0:T(2,128)S(1)}, f32[1,1,8,2,128]{4,3,2,1,0:T(2,128)}, u32[]{:S(2)}) copy-start(f32[1,1,8,2,128]{4,3,2,1,0:T(2,128)} %param.20) | copy-start | bytes 24580
  14.8 11.7 %collective-permute-start.22 = (bf16[384,128]{1,0:T(8,128)(2,1)S(1)}, bf16[384,128]{1,0:T(8,128)(2,1)S(1)}, u32[]{:S(2)}, u32[]{:S(2)}) collective-permute-start(bf16[384,128]{1,0:T(8,128)(2,1)S(1)} %collective-permute-done.6.refs_4_), channel_id=1, source_target_pairs={{0,16},{16,0},{1,17},{17,1},{2,18},{18,2},{3,19},{19,3},{4,20},{20... | collective-permute-start | bytes 294920 | tf_op jit(solution)/shard_map/ppermute | solution.py:240
  16.5 11.0 %collective-permute-start.21 = (bf16[384,128]{1,0:T(8,128)(2,1)S(1)}, bf16[384,128]{1,0:T(8,128)(2,1)S(1)}, u32[]{:S(2)}, u32[]{:S(2)}) collective-permute-start(bf16[384,128]{1,0:T(8,128)(2,1)S(1)} %collective-permute-done.6.refs_4_), channel_id=1, source_target_pairs={{0,2},{2,0},{1,3},{3,1},{4,6},{6,4},{5,7},{7,5},{8,10},{10,8},{9,1... | collective-permute-start | bytes 294920 | tf_op jit(solution)/shard_map/ppermute | solution.py:240
  18.0 5.6 %collective-permute-start.7 = (bf16[384,128]{1,0:T(8,128)(2,1)S(1)}, bf16[384,128]{1,0:T(8,128)(2,1)S(1)}, u32[]{:S(2)}, u32[]{:S(2)}) collective-permute-start(bf16[384,128]{1,0:T(8,128)(2,1)S(1)} %get-tuple-element.27), channel_id=1, source_target_pairs={{0,12},{4,0},{8,4},{12,8},{1,13},{5,1},{9,5},{13,9},{2,14},{6,2},{... | collective-permute-start | bytes 294920 | tf_op jit(solution)/shard_map/ppermute | solution.py:322
  19.8 6.0 %collective-permute-start.1 = (bf16[576,128]{1,0:T(8,128)(2,1)S(1)}, bf16[576,128]{1,0:T(8,128)(2,1)S(1)}, u32[]{:S(2)}, u32[]{:S(2)}) collective-permute-start(bf16[576,128]{1,0:T(8,128)(2,1)S(1)} %get-tuple-element.22), channel_id=1, source_target_pairs={{0,12},{4,0},{8,4},{12,8},{1,13},{5,1},{9,5},{13,9},{2,14},{6,2},{... | collective-permute-start | bytes 442376 | tf_op jit(solution)/shard_map/ppermute | solution.py:322
  23.6 10.8 %collective-permute-start.8 = (bf16[384,128]{1,0:T(8,128)(2,1)S(1)}, bf16[384,128]{1,0:T(8,128)(2,1)S(1)}, u32[]{:S(2)}, u32[]{:S(2)}) collective-permute-start(bf16[384,128]{1,0:T(8,128)(2,1)S(1)} %get-tuple-element.28), channel_id=1, source_target_pairs={{0,8},{4,12},{8,0},{12,4},{1,9},{5,13},{9,1},{13,5},{2,10},{6,14},... | collective-permute-start | bytes 294920 | tf_op jit(solution)/shard_map/ppermute | solution.py:322
  25.8 8.5 %collective-permute-start.16 = (bf16[384,128]{1,0:T(8,128)(2,1)S(1)}, bf16[384,128]{1,0:T(8,128)(2,1)S(1)}, u32[]{:S(2)}, u32[]{:S(2)}) collective-permute-start(bf16[384,128]{1,0:T(8,128)(2,1)S(1)} %collective-permute-done.7.refs_4_), channel_id=1, source_target_pairs={{0,16},{16,0},{1,17},{17,1},{2,18},{18,2},{3,19},{19,3},{4,20},{20... | collective-permute-start | bytes 294920 | tf_op jit(solution)/shard_map/ppermute | solution.py:240
  26.6 9.8 %collective-permute-start.2 = (bf16[576,128]{1,0:T(8,128)(2,1)S(1)}, bf16[576,128]{1,0:T(8,128)(2,1)S(1)}, u32[]{:S(2)}, u32[]{:S(2)}) collective-permute-start(bf16[576,128]{1,0:T(8,128)(2,1)S(1)} %get-tuple-element.23), channel_id=1, source_target_pairs={{0,8},{4,12},{8,0},{12,4},{1,9},{5,13},{9,1},{13,5},{2,10},{6,14},... | collective-permute-start | bytes 442376 | tf_op jit(solution)/shard_map/ppermute | solution.py:322
  27.5 16.1 %collective-permute-start.19 = (bf16[576,128]{1,0:T(8,128)(2,1)S(1)}, bf16[576,128]{1,0:T(8,128)(2,1)S(1)}, u32[]{:S(2)}, u32[]{:S(2)}) collective-permute-start(bf16[576,128]{1,0:T(8,128)(2,1)S(1)} %collective-permute-done.refs_0_), channel_id=1, source_target_pairs={{0,16},{16,0},{1,17},{17,1},{2,18},{18,2},{3,19},{19,3},{4,20},{20... | collective-permute-start | bytes 442376 | tf_op jit(solution)/shard_map/ppermute | solution.py:240
  34.3 10.4 %collective-permute-start.18 = (bf16[576,128]{1,0:T(8,128)(2,1)S(1)}, bf16[576,128]{1,0:T(8,128)(2,1)S(1)}, u32[]{:S(2)}, u32[]{:S(2)}) collective-permute-start(bf16[576,128]{1,0:T(8,128)(2,1)S(1)} %collective-permute-done.refs_0_), channel_id=1, source_target_pairs={{0,2},{2,0},{1,3},{3,1},{4,6},{6,4},{5,7},{7,5},{8,10},{10,8},{9,1... | collective-permute-start | bytes 442376 | tf_op jit(solution)/shard_map/ppermute | solution.py:240
  34.4 7.2 %collective-permute-start.15 = (bf16[384,128]{1,0:T(8,128)(2,1)S(1)}, bf16[384,128]{1,0:T(8,128)(2,1)S(1)}, u32[]{:S(2)}, u32[]{:S(2)}) collective-permute-start(bf16[384,128]{1,0:T(8,128)(2,1)S(1)} %collective-permute-done.7.refs_4_), channel_id=1, source_target_pairs={{0,2},{2,0},{1,3},{3,1},{4,6},{6,4},{5,7},{7,5},{8,10},{10,8},{9,1... | collective-permute-start | bytes 294920 | tf_op jit(solution)/shard_map/ppermute | solution.py:240
  36.4 6.2 %collective-permute-start.23 = (bf16[384,128]{1,0:T(8,128)(2,1)S(1)}, bf16[384,128]{1,0:T(8,128)(2,1)S(1)}, u32[]{:S(2)}, u32[]{:S(2)}) collective-permute-start(bf16[384,128]{1,0:T(8,128)(2,1)S(1)} %collective-permute-done.22.refs_6_), channel_id=1, source_target_pairs={{0,2},{2,0},{1,3},{3,1},{4,6},{6,4},{5,7},{7,5},{8,10},{10,8},{9,1... | collective-permute-start | bytes 294920 | tf_op jit(solution)/shard_map/ppermute | solution.py:240
  41.5 9.7 %collective-permute-start.13 = (bf16[576,128]{1,0:T(8,128)(2,1)S(1)}, bf16[576,128]{1,0:T(8,128)(2,1)S(1)}, u32[]{:S(2)}, u32[]{:S(2)}) collective-permute-start(bf16[576,128]{1,0:T(8,128)(2,1)S(1)} %collective-permute-done.1.refs_0_), channel_id=1, source_target_pairs={{0,16},{16,0},{1,17},{17,1},{2,18},{18,2},{3,19},{19,3},{4,20},{20... | collective-permute-start | bytes 442376 | tf_op jit(solution)/shard_map/ppermute | solution.py:240
  42.6 6.3 %collective-permute-start.10 = (bf16[384,128]{1,0:T(8,128)(2,1)S(1)}, bf16[384,128]{1,0:T(8,128)(2,1)S(1)}, u32[]{:S(2)}, u32[]{:S(2)}) collective-permute-start(bf16[384,128]{1,0:T(8,128)(2,1)S(1)} %collective-permute-done.8.refs_4_), channel_id=1, source_target_pairs={{0,16},{16,0},{1,17},{17,1},{2,18},{18,2},{3,19},{19,3},{4,20},{20... | collective-permute-start | bytes 294920 | tf_op jit(solution)/shard_map/ppermute | solution.py:240
  43.7 6.6 %collective-permute-start.17 = (bf16[384,128]{1,0:T(8,128)(2,1)S(1)}, bf16[384,128]{1,0:T(8,128)(2,1)S(1)}, u32[]{:S(2)}, u32[]{:S(2)}) collective-permute-start(bf16[384,128]{1,0:T(8,128)(2,1)S(1)} %collective-permute-done.15.refs_5_), channel_id=1, source_target_pairs={{0,16},{16,0},{1,17},{17,1},{2,18},{18,2},{3,19},{19,3},{4,20},{20... | collective-permute-start | bytes 294920 | tf_op jit(solution)/shard_map/ppermute | solution.py:240
  44.8 8.2 %collective-permute-start.20 = (bf16[576,128]{1,0:T(8,128)(2,1)S(1)}, bf16[576,128]{1,0:T(8,128)(2,1)S(1)}, u32[]{:S(2)}, u32[]{:S(2)}) collective-permute-start(bf16[576,128]{1,0:T(8,128)(2,1)S(1)} %collective-permute-done.18.refs_1_), channel_id=1, source_target_pairs={{0,16},{16,0},{1,17},{17,1},{2,18},{18,2},{3,19},{19,3},{4,20},{20... | collective-permute-start | bytes 442376 | tf_op jit(solution)/shard_map/ppermute | solution.py:240
  48.9 5.1 %collective-permute-start.3 = (bf16[576,128]{1,0:T(8,128)(2,1)S(1)}, bf16[576,128]{1,0:T(8,128)(2,1)S(1)}, u32[]{:S(2)}, u32[]{:S(2)}) collective-permute-start(bf16[576,128]{1,0:T(8,128)(2,1)S(1)} %collective-permute-done.2.refs_0_), channel_id=1, source_target_pairs={{0,2},{2,0},{1,3},{3,1},{4,6},{6,4},{5,7},{7,5},{8,10},{10,8},{9,1... | collective-permute-start | bytes 442376 | tf_op jit(solution)/shard_map/ppermute | solution.py:240
  50.3 10.6 %collective-permute-start.12 = (bf16[576,128]{1,0:T(8,128)(2,1)S(1)}, bf16[576,128]{1,0:T(8,128)(2,1)S(1)}, u32[]{:S(2)}, u32[]{:S(2)}) collective-permute-start(bf16[576,128]{1,0:T(8,128)(2,1)S(1)} %collective-permute-done.1.refs_0_), channel_id=1, source_target_pairs={{0,2},{2,0},{1,3},{3,1},{4,6},{6,4},{5,7},{7,5},{8,10},{10,8},{9,1... | collective-permute-start | bytes 442376 | tf_op jit(solution)/shard_map/ppermute | solution.py:240
  51.3 10.1 %collective-permute-start.14 = (bf16[576,128]{1,0:T(8,128)(2,1)S(1)}, bf16[576,128]{1,0:T(8,128)(2,1)S(1)}, u32[]{:S(2)}, u32[]{:S(2)}) collective-permute-start(bf16[576,128]{1,0:T(8,128)(2,1)S(1)} %collective-permute-done.13.refs_2_), channel_id=1, source_target_pairs={{0,2},{2,0},{1,3},{3,1},{4,6},{6,4},{5,7},{7,5},{8,10},{10,8},{9,1... | collective-permute-start | bytes 442376 | tf_op jit(solution)/shard_map/ppermute | solution.py:240
  52.9 13.7 %collective-permute-start.4 = (bf16[576,128]{1,0:T(8,128)(2,1)S(1)}, bf16[576,128]{1,0:T(8,128)(2,1)S(1)}, u32[]{:S(2)}, u32[]{:S(2)}) collective-permute-start(bf16[576,128]{1,0:T(8,128)(2,1)S(1)} %collective-permute-done.2.refs_0_), channel_id=1, source_target_pairs={{0,16},{16,0},{1,17},{17,1},{2,18},{18,2},{3,19},{19,3},{4,20},{20... | collective-permute-start | bytes 442376 | tf_op jit(solution)/shard_map/ppermute | solution.py:240
  54.1 12.5 %collective-permute-start.5 = (bf16[576,128]{1,0:T(8,128)(2,1)S(1)}, bf16[576,128]{1,0:T(8,128)(2,1)S(1)}, u32[]{:S(2)}, u32[]{:S(2)}) collective-permute-start(bf16[576,128]{1,0:T(8,128)(2,1)S(1)} %collective-permute-done.3.refs_1_), channel_id=1, source_target_pairs={{0,16},{16,0},{1,17},{17,1},{2,18},{18,2},{3,19},{19,3},{4,20},{20... | collective-permute-start | bytes 442376 | tf_op jit(solution)/shard_map/ppermute | solution.py:240
  55.0 1.5 %copy-start.1 = (bf16[1,1,4,14,128,128]{5,4,3,2,1,0:T(8,128)(2,1)S(1)}, bf16[1,1,4,14,128,128]{5,4,3,2,1,0:T(8,128)(2,1)}, u32[]{:S(2)}) copy-start(bf16[1,1,4,14,128,128]{5,4,3,2,1,0:T(8,128)(2,1)} %param.14) | copy-start | bytes 5505028
  56.5 1.5 %copy-start.3 = (bf16[1,1,4,14,128,128]{5,4,3,2,1,0:T(8,128)(2,1)S(1)}, bf16[1,1,4,14,128,128]{5,4,3,2,1,0:T(8,128)(2,1)}, u32[]{:S(2)}) copy-start(bf16[1,1,4,14,128,128]{5,4,3,2,1,0:T(8,128)(2,1)} %param.18) | copy-start | bytes 5505028
  60.9 4.7 %collective-permute-start.9 = (bf16[384,128]{1,0:T(8,128)(2,1)S(1)}, bf16[384,128]{1,0:T(8,128)(2,1)S(1)}, u32[]{:S(2)}, u32[]{:S(2)}) collective-permute-start(bf16[384,128]{1,0:T(8,128)(2,1)S(1)} %collective-permute-done.8.refs_4_), channel_id=1, source_target_pairs={{0,2},{2,0},{1,3},{3,1},{4,6},{6,4},{5,7},{7,5},{8,10},{10,8},{9,1... | collective-permute-start | bytes 294920 | tf_op jit(solution)/shard_map/ppermute | solution.py:240
  61.4 5.2 %collective-permute-start.11 = (bf16[384,128]{1,0:T(8,128)(2,1)S(1)}, bf16[384,128]{1,0:T(8,128)(2,1)S(1)}, u32[]{:S(2)}, u32[]{:S(2)}) collective-permute-start(bf16[384,128]{1,0:T(8,128)(2,1)S(1)} %collective-permute-done.10.refs_6_), channel_id=1, source_target_pairs={{0,2},{2,0},{1,3},{3,1},{4,6},{6,4},{5,7},{7,5},{8,10},{10,8},{9,1... | collective-permute-start | bytes 294920 | tf_op jit(solution)/shard_map/ppermute | solution.py:240
  63.0 5.1 %slice-start = ((s8[6291456]{0:T(1024)(128)(4,1)}), s8[4194304]{0:T(1024)(128)(4,1)S(1)}, s32[]{:S(2)}) async-start(s8[6291456]{0:T(1024)(128)(4,1)} %bitcast.36), calls=%async_computation.1 | async-start | bytes 8388608
  63.0 5.1 %slice-start.1 = ((s8[6291456]{0:T(1024)(128)(4,1)}), s8[2097152]{0:T(1024)(128)(4,1)S(1)}, s32[]{:S(2)}) async-start(s8[6291456]{0:T(1024)(128)(4,1)} %bitcast.36), calls=%async_computation.2 | async-start | bytes 4194304
  68.1 20.5 %copy-start.10 = (f32[1024]{0:T(1024)S(1)}, f32[1024]{0:T(1024)}, u32[]{:S(2)}) copy-start(f32[1024]{0:T(1024)} %param.22) | copy-start | bytes 12292
  68.1 20.7 %copy-start.11 = (f32[1024]{0:T(1024)S(1)}, f32[1024]{0:T(1024)}, u32[]{:S(2)}) copy-start(f32[1024]{0:T(1024)} %param.23) | copy-start | bytes 12292

commit v4 on v3

v4 whole, which is shorter than its diff:
```python
import functools

import jax
import jax.numpy as jnp
from jax import lax
from jax.experimental import pallas as pl
from jax.experimental.pallas import tpu as pltpu
from jax.sharding import PartitionSpec as P

REPL = ("grp", "var")


def slot_tables(dest, band_count, cap):
    count = dest.shape[0]
    serial = jnp.arange(count, dtype=jnp.int32)
    band_of = dest[:, 0]
    earlier = (band_of[:, None] == band_of[None, :]) & (serial[None, :] < serial[:, None])
    position = jnp.sum(earlier.astype(jnp.int32), axis=1)
    slot = band_of * cap + position
    hit = slot[None, :] == jnp.arange(band_count * cap, dtype=jnp.int32)[:, None]
    block = jnp.sum(jnp.where(hit, serial[None, :], 0), axis=1)
    used = jnp.any(hit, axis=1)
    return block.reshape(band_count, cap), used.reshape(band_count, cap)


def pack_kernel(pieces, ocean, atmos, weights, tiles_of, land, *refs):
    (ocean_w, atmos_w), (ocean_ids, atmos_ids) = weights, tiles_of
    keep, send, own, outs, sem = refs[0], refs[1], refs[2], refs[3:-1], refs[-1]
    me, bands = lax.axis_index("band"), ocean_w.shape[0]
    x, y = lax.axis_index("var"), lax.axis_index("grp")
    cells, tiles = land.shape[-1], land.shape[0]
    cap = ocean_ids.shape[-1]
    each = cap // 2

    def copies(mine, other, weights):
        pairs = []
        for out, (shift, first, size) in zip(outs, pieces):
            start = pl.multiple_of((x * each + first) * cells, cells)
            target = lax.rem(me + shift, bands)
            pairs.append(
                (
                    weights.at[target, pl.ds(start, size * cells), :],
                    out.at[pl.ds(0, size * cells), :],
                )
            )
        pairs += [(other, send), (mine, keep), (weights.at[me], own)]
        return [pltpu.make_async_copy(a, b, sem.at[i]) for i, (a, b) in enumerate(pairs)]

    @pl.when(y == 0)
    def _():
        for copy in copies(ocean, atmos, ocean_w):
            copy.start()

    @pl.when(y == 1)
    def _():
        for copy in copies(atmos, ocean, atmos_w):
            copy.start()

    fraction = land[...]
    high = fraction.astype(jnp.bfloat16)
    low = (fraction - high.astype(jnp.float32)).astype(jnp.bfloat16)
    for out, (shift, first, size) in zip(outs, pieces):
        if first:
            continue
        target, base = lax.rem(me + shift, bands), size * cells
        out[pl.ds(base, tiles), :] = high
        out[pl.ds(base + tiles, tiles), :] = low
        row = jnp.where(y == 0, ocean_ids[pl.ds(target, 1), :], atmos_ids[pl.ds(target, 1), :])
        row = jnp.broadcast_to(row.astype(jnp.float32), (16, cap)).astype(jnp.bfloat16)
        out[pl.ds(base + 2 * tiles, 16), :] = jnp.zeros((16, cells), jnp.bfloat16)
        out[pl.ds(base + 2 * tiles, 16), pl.ds(0, cap)] = row
    for copy in copies(ocean, atmos, ocean_w):
        copy.wait()


def pack(pieces, ocean, atmos, ocean_w, atmos_w, ocean_ids, atmos_ids, land):
    cells, tiles = land.shape[-1], land.shape[0]
    any_spec = pl.BlockSpec(memory_space=pl.ANY)
    vmem = pl.BlockSpec(memory_space=pltpu.VMEM)
    sizes = [size * cells + (0 if first else 2 * tiles + 16) for _, first, size in pieces]
    shapes = [ocean.shape, ocean.shape, ocean_w.shape[1:]] + [(n, cells) for n in sizes]

    def body(o, a, ow, aw, oi, ai, land, *refs):
        pack_kernel(pieces, o, a, (ow, aw), (oi, ai), land, *refs)

    return pl.pallas_call(
        body,
        out_shape=[jax.ShapeDtypeStruct(shape, jnp.bfloat16) for shape in shapes],
        in_specs=[any_spec] * 4 + [vmem] * 3,
        out_specs=[vmem] * len(shapes),
        scratch_shapes=[pltpu.SemaphoreType.DMA((len(shapes),))],
        cost_estimate=pl.CostEstimate(flops=0, bytes_accessed=6 << 20, transcendentals=0),
        compiler_params=pltpu.CompilerParams(vmem_limit_bytes=60 << 20),
    )(ocean, atmos, ocean_w, atmos_w, ocean_ids, atmos_ids, land)


def regrid_kernel(groups, steps, meta_at, part_slots, table, where, *refs):
    out, acc, scale = refs[-3:]
    fields, refs = refs[:groups], refs[groups:]
    parts, rest = refs[: len(part_slots)], refs[len(part_slots) :]
    rows, cells = fields[0].shape[1:]
    tiles = acc.shape[1] // rows
    if meta_at is None:
        land = rest[0][...]
    else:
        meta = rest[0] if meta_at < 0 else parts[0]
        first = max(meta_at, 0)
        high = meta[pl.ds(first, tiles), :].astype(jnp.float32)
        land = high + meta[pl.ds(first + tiles, tiles), :].astype(jnp.float32)
    scale[pl.ds(0, tiles), :] = 1.0 - land
    scale[pl.ds(tiles, tiles), :] = land
    scale[pl.ds(2 * tiles, 8), :] = jnp.zeros((8, cells), jnp.float32)
    acc[...] = jnp.zeros_like(acc)
    for at, (part, size) in enumerate(zip(parts, part_slots)):
        first = where[1 + at]
        for s in range(size):
            slot = first + s
            block = table[0, slot]
            moved = [f[block] for f in fields]
            moved = moved[0] if groups == 1 else jnp.concatenate(moved, axis=0)
            dense = jnp.dot(
                moved, part[pl.ds(s * cells, cells), :], preferred_element_type=jnp.float32
            )
            dense = dense * scale[pl.ds(table[2, slot], 1), :]
            span = pl.ds(pl.multiple_of(table[1, slot] * rows, rows), rows)
            for g in range(groups):
                acc[g, span, :] += dense[g * rows : (g + 1) * rows]
    local_vars = rows // steps
    half_vars = local_vars // 2
    for g in range(groups):
        for v in range(local_vars):
            for q in range(2):
                column = (v % half_vars * 2 + q) * cells
                pieces = [
                    acc[g, pl.ds(q * rows + t * local_vars + v, tiles // 2, 2 * rows), :]
                    for t in range(steps)
                ]
                out[0, g, v // half_vars, :, pl.ds(column, cells)] = jnp.concatenate(
                    pieces, axis=0
                ).astype(out.dtype)


def regrid(table, where, fields, parts, part_slots, rest, meta_at, previous, bands, steps, tiles):
    groups = len(fields)
    rows, cells = fields[0].shape[1:]
    whole = lambda a: pl.BlockSpec(a.shape, lambda i, t, w, n=a.ndim: (0,) * n)
    operands = list(fields) + list(parts) + list(rest)
    in_specs = [whole(a) for a in operands]
    aliases = {}
    if previous is not None:
        aliases = {2 + len(operands): 0}
        in_specs.append(pl.BlockSpec(memory_space=pl.ANY))
        operands.append(previous)
    row_count, width = steps * tiles // 2, rows // steps // 2 * 2 * cells
    block = (groups, 2, row_count, width)
    return pl.pallas_call(
        functools.partial(regrid_kernel, groups, steps, meta_at, tuple(part_slots)),
        out_shape=jax.ShapeDtypeStruct((bands,) + block, jnp.bfloat16),
        grid_spec=pltpu.PrefetchScalarGridSpec(
            num_scalar_prefetch=2,
            grid=(1,),
            in_specs=in_specs,
            out_specs=pl.BlockSpec((1,) + block, lambda i, t, w: (w[0], 0, 0, 0, 0)),
            scratch_shapes=[
                pltpu.VMEM((groups, tiles * rows, cells), jnp.float32),
                pltpu.VMEM((2 * tiles + 8, cells), jnp.float32),
            ],
        ),
        input_output_aliases=aliases,
        cost_estimate=pl.CostEstimate(
            flops=2 * sum(part_slots) * groups * rows * cells * cells,
            bytes_accessed=4 << 20,
            transcendentals=0,
        ),
        compiler_params=pltpu.CompilerParams(vmem_limit_bytes=20 << 20),
    )(table, where, *operands)


def embed_kernel(steps, halves, rows_x, mine, theirs, out, total):
    at = pl.program_id(0)
    sub, mine_group = lax.axis_index("sub"), lax.axis_index("grp")
    bands, groups, _, row_count, width = rows_x.shape
    rows = bands * groups * row_count

    @pl.when(at == 0)
    def _():
        total[...] = jnp.zeros_like(total)

    left = rows_x[:, :, sub].reshape(rows, width)
    right = rows_x[:, :, 1 - sub].reshape(rows, width)
    total[...] += jnp.dot(left, mine[...], preferred_element_type=jnp.float32) + jnp.dot(
        right, theirs[...], preferred_element_type=jnp.float32
    )

    @pl.when(at == pl.num_programs(0) - 1)
    def _():
        if out.ndim == 2:
            out[...] = total[...].astype(out.dtype)
        else:
            count = steps * halves
            share = row_count // count
            for g in range(groups):
                base = (mine_group if g == 0 else 1 - mine_group) * count if groups > 1 else 0
                for chunk in range(count):
                    pieces = [
                        total[pl.ds((b * groups + g) * row_count + chunk * share, share), :]
                        for b in range(bands)
                    ]
                    out[base + chunk] = jnp.concatenate(pieces, axis=0).astype(out.dtype)


def embed(rows_x, mine, theirs, steps, halves):
    bands, groups, _, row_count, half_width = rows_x.shape
    width = mine.shape[-1]
    grid = 6 if half_width % (6 * 256) == 0 else 3
    step_rows = half_width // grid
    rows = bands * groups * row_count
    chunks = groups * steps * halves
    share = row_count // (steps * halves)
    shape = (chunks, bands * share, width) if share % 4 == 0 else (rows, width)
    weight_spec = pl.BlockSpec((step_rows, width), lambda i: (i, 0))
    out = pl.pallas_call(
        functools.partial(embed_kernel, steps, halves),
        out_shape=jax.ShapeDtypeStruct(shape, jnp.bfloat16),
        grid=(grid,),
        in_specs=[
            pl.BlockSpec((bands, groups, 2, row_count, step_rows), lambda i: (0, 0, 0, 0, i)),
            weight_spec,
            weight_spec,
        ],
        out_specs=pl.BlockSpec(shape, lambda i: (0,) * len(shape)),
        scratch_shapes=[pltpu.VMEM((rows, width), jnp.float32)],
        cost_estimate=pl.CostEstimate(
            flops=4 * rows * mine.shape[0] * width,
            bytes_accessed=4 * mine.shape[0] * width,
            transcendentals=0,
        ),
        compiler_params=pltpu.CompilerParams(
            vmem_limit_bytes=(48 if rows > 1024 else 16) << 20
        ),
    )(rows_x, mine, theirs)
    if share % 4:
        out = out.reshape(bands, chunks, share, width).transpose(1, 0, 2, 3)
        out = out.reshape(chunks, bands * share, width)
    return out


def swap(x, axis):
    return lax.ppermute(x, axis, [(0, 1), (1, 0)])


def per_device(
    ocean_fields,
    ocean_dest,
    ocean_weights,
    ocean_tiles,
    atmos_fields,
    atmos_dest,
    atmos_weights,
    atmos_tiles,
    land_fraction,
    embed_weight,
    embed_bias,
    embed_gain,
):
    nb = lax.axis_size("band")
    nv = lax.axis_size("var")
    ng = lax.axis_size("grp")
    rep = nv * ng
    cap = ocean_weights.shape[3]
    cells = ocean_weights.shape[-1]
    block_count, steps, local_vars, _ = ocean_fields.shape
    patches = land_fraction.shape[2]
    tiles = 2 * patches
    slots = 2 * cap
    share = patches // nv
    me = lax.axis_index("band")
    x, y = lax.axis_index("var"), lax.axis_index("grp")
    quarter = y * nv + x

    embed_other = swap(embed_weight, "sub")

    flat = (nb, cap * cells, cells)
    ocean_w, atmos_w = ocean_weights.reshape(flat), atmos_weights.reshape(flat)
    ocean_ids, atmos_ids = ocean_tiles.reshape(nb, cap), atmos_tiles.reshape(nb, cap)
    land = land_fraction.reshape(tiles, cells)
    blocks = (block_count, steps * local_vars, cells)
    ocean_f, atmos_f = ocean_fields.reshape(blocks), atmos_fields.reshape(blocks)
    order = ([1, nb - 1] + list(range(2, nb - 1)))[: nb - 1]
    call = functools.partial(regrid, bands=nb, steps=steps, tiles=tiles)
    along = lambda shift: [(b, (b + shift) % nb) for b in range(nb)]

    if ng == 2 and nv == 2 and cap % 2 == 0:
        each = cap // 2
        head = (each + 1) // 2
        pieces = []
        for shift in order:
            if 2 * shift == nb:
                pieces += [(shift, 0, head), (shift, head, each - head)]
            else:
                pieces.append((shift, 0, each))
        keep, send, own_w, *packed = pack(
            pieces, ocean_f, atmos_f, ocean_w, atmos_w, ocean_ids, atmos_ids, land
        )
        fields = [keep, swap(send, "grp")]
        dest = jnp.where(y == 0, ocean_dest, atmos_dest)
        block_all, used_all = slot_tables(dest, nb, cap)

        def table_of(band, tile):
            block = lax.dynamic_index_in_dim(block_all, band, 0, keepdims=False)
            used = lax.dynamic_index_in_dim(used_all, band, 0, keepdims=False)
            scale = jnp.where(used, tile + y * tiles, 2 * tiles)
            return jnp.stack([block, tile, scale]).astype(jnp.int32)

        sent = []
        for at, (piece, (shift, _, _)) in enumerate(zip(packed, pieces)):
            if at >= 2:
                piece, sent[at - 2] = lax.optimization_barrier((piece, sent[at - 2]))
            sent.append(lax.ppermute(piece, "band", along(shift)))
        crossed = [swap(piece, "var") for piece in sent]

        ids = jnp.where(y == 0, ocean_ids, atmos_ids)
        own_tile = lax.dynamic_index_in_dim(ids, me, 0, keepdims=False)
        where = jnp.stack([me, jnp.int32(0)])
        rows_x = call(table_of(me, own_tile), where, fields, [own_w], [cap], [land], None, None)
        for shift in order:
            band = (me - shift) % nb
            parts, sizes, firsts = [], [], []
            for piece, across, (of, first, size) in zip(sent, crossed, pieces):
                if of == shift:
                    parts += [piece, across]
                    sizes += [size, size]
                    firsts += [x * each + first, (1 - x) * each + first]
            meta_at = sizes[0] * cells
            tile = parts[0][meta_at + 2 * tiles, :cap].astype(jnp.int32)
            where = jnp.stack([band] + firsts).astype(jnp.int32)
            rows_x = call(table_of(band, tile), where, fields, parts, sizes, [], meta_at, rows_x)
        sent = embed(rows_x, embed_weight, embed_other, steps, nv)
        got = lax.all_to_all(sent, ("grp", "band", "var"), split_axis=0, concat_axis=0, tiled=True)
    else:
        both = jnp.concatenate([ocean_w, atmos_w], axis=1)
        fields = [jnp.concatenate([ocean_f, atmos_f], axis=0)]
        ocean_block, ocean_used = slot_tables(ocean_dest, nb, cap)
        atmos_block, atmos_used = slot_tables(atmos_dest, nb, cap)
        block_all = jnp.concatenate([ocean_block, atmos_block + block_count], axis=1)
        used_all = jnp.concatenate([ocean_used, atmos_used], axis=1)
        grid_row = jnp.where(jnp.arange(slots) < cap, 0, tiles)

        def table_of(band, tile):
            block = lax.dynamic_index_in_dim(block_all, band, 0, keepdims=False)
            used = lax.dynamic_index_in_dim(used_all, band, 0, keepdims=False)
            scale = jnp.where(used, tile + grid_row, 2 * tiles)
            return jnp.stack([block, tile, scale]).astype(jnp.int32)

        tile_ids = jnp.concatenate([ocean_ids, atmos_ids], axis=1)
        own_tile = lax.dynamic_index_in_dim(tile_ids, me, 0, keepdims=False)
        own_w = lax.dynamic_index_in_dim(both, me, 0, keepdims=False)
        where = jnp.stack([me, jnp.int32(0)])
        rows_x = call(table_of(me, own_tile), where, fields, [own_w], [slots], [land], None, None)
        share_rows = slots * cells // rep
        high = lax.reduce_precision(land, 8, 7)
        low = (land - high).astype(jnp.bfloat16)
        tile_rows = jnp.pad(tile_ids.astype(jnp.bfloat16), ((0, 0), (0, cells - slots)))
        for shift in order:
            target, band = (me + shift) % nb, (me - shift) % nb
            piece = lax.dynamic_slice(
                both, (target, quarter * share_rows, 0), (1, share_rows, cells)
            )[0]
            row = lax.dynamic_slice(tile_rows, (target, 0), (1, cells))
            row = jnp.broadcast_to(row, (16, cells))
            piece = jnp.concatenate([piece, high.astype(jnp.bfloat16), low, row], axis=0)
            parts = lax.all_gather(lax.ppermute(piece, "band", along(shift)), REPL, axis=0)
            meta = parts[0, share_rows:]
            tile = meta[2 * tiles, :slots].astype(jnp.int32)
            parts = parts[:, :share_rows].reshape(slots * cells, cells)
            where = jnp.stack([band, jnp.int32(0)])
            rows_x = call(
                table_of(band, tile), where, fields, [parts], [slots], [meta], -1, rows_x
            )
        sent = embed(rows_x, embed_weight, embed_other, steps, nv)
        got = lax.all_to_all(sent, ("band", "var"), split_axis=0, concat_axis=0, tiled=True)
    shifted = jnp.sum(got.astype(jnp.float32), axis=0) + embed_bias
    inverse = lax.rsqrt(jnp.mean(shifted * shifted, axis=-1, keepdims=True) + 1e-05)
    finished = (shifted * inverse * embed_gain).astype(jnp.bfloat16)
    width = finished.shape[-1]
    finished = finished.reshape(nb, share, steps // nb, width).transpose(1, 0, 2, 3)
    return finished[None]


def solution(mesh):
    in_specs = (
        P(("grp", "band", "sub"), None, "var", None),
        P(("band", "sub"), None),
        P("band", "sub", None, None, None, None),
        P("band", "sub", None, None),
        P(("grp", "band", "sub"), None, "var", None),
        P(("band", "sub"), None),
        P("band", "sub", None, None, None, None),
        P("band", "sub", None, None),
        P("band", "sub", None, None, None),
        P(("var", "sub"), None),
        P(),
        P(),
    )
    out_specs = P("sub", "var", None, ("grp", "band"), None)
    return jax.shard_map(
        per_device, mesh=mesh, in_specs=in_specs, out_specs=out_specs, check_vma=False
    )
```

time: 90 us -> 71.2 us (0.79)
  waiting for transfers between devices: 23.5 us -> 11.8 us
  Pallas kernels: 12.7 us -> 19 us
  local copies, waits for them, and re-layouts: 9.46 us -> 3.24 us
  starting transfers between devices: 26.1 us -> 20 us
  other arithmetic: 3.02 us -> 0.97 us
  blocking collectives: 14.4 us -> 15.5 us
    ppermute x19 -> x6, waiting for transfers between devices: 12.7 us -> 0.02 us  [swap(): return lax.ppermute(x, axis, [(0, 1), (1, 0)])]
    ppermute x19 -> x6, starting transfers between devices: 17.9 us -> 6.39 us  [swap(): return lax.ppermute(x, axis, [(0, 1), (1, 0)])]
    unnamed x32 -> x24, local copies, waits for them, and re-layouts: 8.1 us -> 2.23 us
    ppermute x6 -> x4, starting transfers between devices: 8.22 us -> 13.6 us  [per_device(): sent.append(lax.ppermute(piece, 'band', along(shift)))]
    pallas_call x5, Pallas kernels: 6.78 us -> 11.9 us  [the longest x4 7.59 us: regrid(): pl.pallas_call(functools.partial(regrid_kernel, groups, steps, meta_at, t...]
    concatenate x4 -> x0, other arithmetic: 1.82 us -> none  [the longest x1 1.59 us: per_device(): jnp.concatenate([ocean_fields, atmos_fields], axis=0)]
    pallas_call x1, Pallas kernels: 5.9 us -> 7.08 us  [embed(): pl.pallas_call(functools.partial(embed_kernel, steps, halves), out_shape=...]
    all_to_all x1, blocking collectives: 14.4 us -> 15.5 us  [per_device(): lax.all_to_all(sent, ('grp', 'band', 'var'), split_axis=0, concat_axis=0,...]
  transfers between devices with their start and end apart: 25 -> 10, of which waited for: 11 -> 3; matrix products, arithmetic and copies ran while one was open for 4% -> 1% of each run, Pallas kernels for 8% -> 17%
where the time goes in v4:
time: 71.2 us; the launch traced here: 70.7 us
  starting transfers between devices  20 us (28%)
  Pallas kernels  19 us (27%)
  blocking collectives  15.5 us (22%)
  waiting for transfers between devices  11.8 us (17%)
  local copies, waits for them, and re-layouts  3.24 us (5%)
  other arithmetic  0.97 us (1%)
    all_to_all x1, blocking collectives, per_device(): lax.all_to_all(sent, ('grp', 'band', 'var'), split_axis=0, concat_axis=0,...  15.5 us
    ppermute x4, starting transfers between devices, per_device(): sent.append(lax.ppermute(piece, 'band', along(shift)))  13.6 us
    ppermute x4, waiting for transfers between devices, per_device(): sent.append(lax.ppermute(piece, 'band', along(shift)))  11.8 us
    pallas_call x4, Pallas kernels, regrid(): pl.pallas_call(functools.partial(regrid_kernel, groups, steps, meta_at, t...  7.59 us
    pallas_call x1, Pallas kernels, embed(): pl.pallas_call(functools.partial(embed_kernel, steps, halves), out_shape=...  7.08 us
    ppermute x6, starting transfers between devices, swap(): return lax.ppermute(x, axis, [(0, 1), (1, 0)])  6.39 us
    pallas_call x1, Pallas kernels, pack(): pl.pallas_call(body, out_shape=[jax.ShapeDtypeStruct(shape, jnp.bfloat16)...  4.3 us
    unnamed x24, local copies, waits for them, and re-layouts  2.23 us
  transfers between devices with their start and end apart: 10, of which 3 were waited for; matrix products, arithmetic and copies ran while one was open for 1% of the time, Pallas kernels for 17%

profile of v4, /device:TPU:0, one launch (start us, length us, event | category | flops | bytes accessed | tf_op | source)
XLA Modules:
  0.0 70.7 jit_solution(3502028986143655688)
XLA Ops:
  0.0 0.5 collective-permute-start.9
  0.5 4.3 %shard_map.118 = (bf16[36,96,128]{2,1,0:T(8,128)(2,1)}, bf16[36,96,128]{2,1,0:T(8,128)(2,1)}, bf16[1792,128]{1,0:T(8,128)(2,1)}, bf16[944,128]{1,0:T(8,128)(2,1)...) custom-call(bf16[36,96,128]{2,1,0:T(8,128)(2,1)} %bitcast.29, ...), custom_call_target="tpu_custom_call" | custom-call | bytes 6291456 | tf_op jit(solution)/shard_map/pallas_call | solution.py:86
  4.9 2.6 %collective-permute-start = (bf16[944,128]{1,0:T(8,128)(2,1)}, bf16[944,128]{1,0:T(8,128)(2,1)S(1)}, u32[]{:S(2)}, u32[]{:S(2)}) collective-permute-start(bf16[944,128]{1,0:T(8,128)(2,1)} %get-tuple-element.17), channel_id=1, source_target_pairs={{0,4},{4,8},{8,12},{12,0},{1,5},{5,9},{9,13},{13,1},{2,6},{6,10},{... | collective-permute-start | bytes 725000 | tf_op jit(solution)/shard_map/ppermute | solution.py:319
  7.5 2.1 %collective-permute-start.4 = (bf16[944,128]{1,0:T(8,128)(2,1)}, bf16[944,128]{1,0:T(8,128)(2,1)S(1)}, u32[]{:S(2)}, u32[]{:S(2)}) collective-permute-start(bf16[944,128]{1,0:T(8,128)(2,1)} %get-tuple-element.22), channel_id=1, source_target_pairs={{0,12},{4,0},{8,4},{12,8},{1,13},{5,1},{9,5},{13,9},{2,14},{6,2},{... | collective-permute-start | bytes 725000 | tf_op jit(solution)/shard_map/ppermute | solution.py:319
  9.6 1.7 %collective-permute-start.2 = (bf16[36,96,128]{2,1,0:T(8,128)(2,1)}, bf16[36,96,128]{2,1,0:T(8,128)(2,1)S(1)}, u32[]{:S(2)}, u32[]{:S(2)}) collective-permute-start(bf16[36,96,128]{2,1,0:T(8,128)(2,1)} %get-tuple-element.20), channel_id=1, source_target_pairs={{0,16},{16,0},{1,17},{17,1},{2,18},{18,2},{3,19},{19,3},{4,20},{20... | collective-permute-start | bytes 2654216 | tf_op jit(solution)/shard_map/ppermute | solution.py:249
  11.3 0.0 copy-done.8
  11.3 0.2 convert_reduce_fusion.1
  11.5 0.1 select_reduce_fusion
  11.6 0.1 reshape.89
  11.6 0.1 add_add_fusion.where
  11.7 0.1 add_add_fusion.1.where
  11.8 0.1 fusion.1
  11.9 0.1 pad_add_fusion.4.where
  12.0 0.1 reshape.97
  12.1 0.1 stack.70.where
  12.2 4.3 %collective-permute-done.refs_2_ = bf16[944,128]{1,0:T(8,128)(2,1)S(1)} collective-permute-done((bf16[944,128]{1,0:T(8,128)(2,1)}, bf16[944,128]{1,0:T(8,128)(2,1)S(1)}, u32[]{:S(2)}, u32[]{:S(2)}) %collective-permute-start) | collective-permute-done | bytes 241696 | tf_op jit(solution)/shard_map/ppermute | solution.py:319
  16.5 7.2 %collective-permute-start.1 = (bf16[560,128]{1,0:T(8,128)(2,1)}, bf16[560,128]{1,0:T(8,128)(2,1)S(1)}, u32[]{:S(2)}, u32[]{:S(2)}) collective-permute-start(bf16[560,128]{1,0:T(8,128)(2,1)} %get-tuple-element.18), channel_id=1, source_target_pairs={{0,8},{4,12},{8,0},{12,4},{1,9},{5,13},{9,1},{13,5},{2,10},{6,14},... | collective-permute-start | bytes 430088 | tf_op jit(solution)/shard_map/ppermute | solution.py:319
  23.7 1.5 %collective-permute-start.8 = (bf16[944,128]{1,0:T(8,128)(2,1)S(1)}, bf16[944,128]{1,0:T(8,128)(2,1)S(1)}, u32[]{:S(2)}, u32[]{:S(2)}) collective-permute-start(bf16[944,128]{1,0:T(8,128)(2,1)S(1)} %collective-permute-done.refs_2_), channel_id=1, source_target_pairs={{0,2},{2,0},{1,3},{3,1},{4,6},{6,4},{5,7},{7,5},{8,10},{10,8},{9,1... | collective-permute-start | bytes 725000 | tf_op jit(solution)/shard_map/ppermute | solution.py:249
  25.2 0.0 collective-permute-done.4.refs_2_
  25.2 0.6 collective-permute-start.7
  25.8 3.5 %collective-permute-done.1.refs_2_ = bf16[560,128]{1,0:T(8,128)(2,1)S(1)} collective-permute-done((bf16[560,128]{1,0:T(8,128)(2,1)}, bf16[560,128]{1,0:T(8,128)(2,1)S(1)}, u32[]{:S(2)}, u32[]{:S(2)}) %collective-permute-start.1) | collective-permute-done | bytes 143392 | tf_op jit(solution)/shard_map/ppermute | solution.py:319
  29.3 1.7 %collective-permute-start.5 = (bf16[384,128]{1,0:T(8,128)(2,1)}, bf16[384,128]{1,0:T(8,128)(2,1)S(1)}, u32[]{:S(2)}, u32[]{:S(2)}) collective-permute-start(bf16[384,128]{1,0:T(8,128)(2,1)} %get-tuple-element.23), channel_id=1, source_target_pairs={{0,8},{4,12},{8,0},{12,4},{1,9},{5,13},{9,1},{13,5},{2,10},{6,14},... | collective-permute-start | bytes 294920 | tf_op jit(solution)/shard_map/ppermute | solution.py:319
  31.1 4.0 %collective-permute-done.5.refs_4_ = bf16[384,128]{1,0:T(8,128)(2,1)S(1)} collective-permute-done((bf16[384,128]{1,0:T(8,128)(2,1)}, bf16[384,128]{1,0:T(8,128)(2,1)S(1)}, u32[]{:S(2)}, u32[]{:S(2)}) %collective-permute-start.5) | collective-permute-done | bytes 98336 | tf_op jit(solution)/shard_map/ppermute | solution.py:319
  35.0 1.5 %collective-permute-start.3 = (bf16[560,128]{1,0:T(8,128)(2,1)S(1)}, bf16[560,128]{1,0:T(8,128)(2,1)S(1)}, u32[]{:S(2)}, u32[]{:S(2)}) collective-permute-start(bf16[560,128]{1,0:T(8,128)(2,1)S(1)} %collective-permute-done.1.refs_2_), channel_id=1, source_target_pairs={{0,2},{2,0},{1,3},{3,1},{4,6},{6,4},{5,7},{7,5},{8,10},{10,8},{9,1... | collective-permute-start | bytes 430088 | tf_op jit(solution)/shard_map/ppermute | solution.py:249
  36.5 0.0 collective-permute-done.2.refs_1_
  36.5 0.6 collective-permute-start.6
  37.2 1.2 %copy-done = bf16[36,96,128]{2,1,0:T(8,128)(2,1)S(1)} copy-done((bf16[36,96,128]{2,1,0:T(8,128)(2,1)S(1)}, bf16[36,96,128]{2,1,0:T(8,128)(2,1)}, u32[]{:S(2)}) %copy-start) | copy-done | bytes 884760
  38.3 1.0 %copy-done.2 = bf16[1792,128]{1,0:T(8,128)(2,1)S(1)} copy-done((bf16[1792,128]{1,0:T(8,128)(2,1)S(1)}, bf16[1792,128]{1,0:T(8,128)(2,1)}, u32[]{:S(2)}) %copy-start.2) | copy-done | bytes 458776
  39.3 1.9 %shard_map.119.refs_4_ = bf16[4,2,2,32,3072]{4,3,2,1,0:T(8,128)(2,1)S(1)} custom-call(s32[3,14]{1,0:T(4,128)S(1)} %pad_add_fusion.3.table, s32[2]{0:T(128)S(1)} %pad_add_fusion.4.where, bf16[36,96,128]{2,1,0:T(8,128)(2,1)S(1)} %copy-done, bf16[36,96,128]{2,1,0:T(8,128)(2,1)S(1)} %collective-permute-done.2.refs_1_, bf16[1792,128]{1,0:T(8,128)(2,1)S(1)} %copy-done.2, ...), custom_call_target="tpu_custom_call" | custom-call | flops 88080384 | bytes 4194304 | tf_op jit(solution)/shard_map/pallas_call | solution.py:156
  41.2 0.0 collective-permute-done.8.refs_3_
  41.3 1.9 %shard_map.120.refs_4_ = bf16[4,2,2,32,3072]{4,3,2,1,0:T(8,128)(2,1)S(1)} custom-call(s32[3,14]{1,0:T(4,128)S(1)} %pad_add_fusion.2.table, s32[3]{0:T(128)S(1)} %add_add_fusion.1.where, bf16[36,96,128]{2,1,0:T(8,128)(2,1)S(1)} %copy-done.1, bf16[36,96,128]{2,1,0:T(8,128)(2,1)S(1)} %collective-permute-done.2.refs_1_, ...), custom_call_target="tpu_custom_call", output_to_operand_aliasing={{}: (6, {})} | custom-call | flops 88080384 | bytes 4194304 | tf_op jit(solution)/shard_map/pallas_call | solution.py:156
  43.2 0.0 collective-permute-done.7.refs_3_
  43.2 0.0 slice-start
  43.2 1.9 %shard_map.121.refs_6_ = bf16[4,2,2,32,3072]{4,3,2,1,0:T(8,128)(2,1)S(1)} custom-call(s32[3,14]{1,0:T(4,128)S(1)} %pad_add_fusion.1.table, s32[3]{0:T(128)S(1)} %add_add_fusion.where, bf16[36,96,128]{2,1,0:T(8,128)(2,1)S(1)} %copy-done.1, bf16[36,96,128]{2,1,0:T(8,128)(2,1)S(1)} %collective-permute-done.2.refs_1_, ...), custom_call_target="tpu_custom_call", output_to_operand_aliasing={{}: (6, {})} | custom-call | flops 88080384 | bytes 4194304 | tf_op jit(solution)/shard_map/pallas_call | solution.py:156
  45.1 0.0 slice-start.1
  45.1 0.0 collective-permute-done.6.refs_5_
  45.1 0.0 collective-permute-done.3.refs_3_
  45.1 1.9 %shard_map.122.rows_x = bf16[4,2,2,32,3072]{4,3,2,1,0:T(8,128)(2,1)S(1)} custom-call(s32[3,14]{1,0:T(4,128)S(1)} %pad_add_fusion.table, s32[5]{0:T(128)S(1)} %stack.70.where, bf16[36,96,128]{2,1,0:T(8,128)(2,1)S(1)} %copy-done.1, bf16[36,96,128]{2,1,0:T(8,128)(2,1)S(1)} %collective-permute-done.2.refs_1_, ...), custom_call_target="tpu_custom_call", output_to_operand_aliasing={{}: (8, {})} | custom-call | flops 88080384 | bytes 4194304 | tf_op jit(solution)/shard_map/pallas_call | solution.py:156
  47.0 0.0 copy-start.4
  47.0 0.0 copy-start.7
  47.1 0.0 collective-permute-done.9.theirs
  47.1 7.1 %shard_map.123 = bf16[16,16,1024]{2,1,0:T(8,128)(2,1)S(1)} custom-call(bf16[4,2,2,32,3072]{4,3,2,1,0:T(8,128)(2,1)S(1)} %shard_map.122.rows_x, bf16[3072,1024]{1,0:T(8,128)(2,1)S(1)} %bitcast.24, bf16[3072,1024]{1,0:T(8,128)(2,1)} %collective-permute-done.9.theirs), custom_call_target="tpu_custom_call" | custom-call | flops 3221225472 | bytes 12582912 | tf_op jit(solution)/shard_map/pallas_call | solution.py:222
  54.2 15.5 %all_to_all.5 = bf16[16,16,1024]{2,1,0:T(8,128)(2,1)S(1)} all-to-all(bf16[16,16,1024]{2,1,0:T(8,128)(2,1)S(1)} %shard_map.123), channel_id=1, replica_groups=mesh['grp'=2,'band'=4,'var'=2,'sub'=2] {'grp','band','var'}, dimensions={0} | all-to-all | bytes 1048576 | tf_op jit(solution)/shard_map/all_to_all | solution.py:339
  69.7 0.1 convert_reduce_fusion
  69.8 0.1 multiply_reduce_fusion
  69.9 0.1 rsqrt.12
  70.0 0.1 fusion
  70.1 0.6 copy.18
  (32 shorter events, 0.2 us)
Async XLA Ops:
  0.0 12.2 %copy-start.6 = (s32[1,1,4,14]{3,2,1,0:T(4,128)S(1)}, s32[1,1,4,14]{3,2,1,0:T(4,128)}, u32[]{:S(2)}) copy-start(s32[1,1,4,14]{3,2,1,0:T(4,128)} %param.15) | copy-start | bytes 676
  0.0 12.2 %copy-start.5 = (s32[1,1,4,14]{3,2,1,0:T(4,128)S(1)}, s32[1,1,4,14]{3,2,1,0:T(4,128)}, u32[]{:S(2)}) copy-start(s32[1,1,4,14]{3,2,1,0:T(4,128)} %param.19) | copy-start | bytes 676
  0.0 37.1 %copy-start.3 = (f32[1,1,8,2,128]{4,3,2,1,0:T(2,128)S(1)}, f32[1,1,8,2,128]{4,3,2,1,0:T(2,128)}, u32[]{:S(2)}) copy-start(f32[1,1,8,2,128]{4,3,2,1,0:T(2,128)} %param.20) | copy-start | bytes 24580
  0.0 11.3 %copy-start.9 = (s32[36,1]{0,1:T(1,128)S(1)}, s32[36,1]{0,1:T(1,128)}, u32[]{:S(2)}) copy-start(s32[36,1]{0,1:T(1,128)} %param.17) | copy-start | bytes 436
  0.0 11.3 %copy-start.8 = (s32[36,1]{0,1:T(1,128)S(1)}, s32[36,1]{0,1:T(1,128)}, u32[]{:S(2)}) copy-start(s32[36,1]{0,1:T(1,128)} %param.13) | copy-start | bytes 436
  0.0 47.0 %collective-permute-start.9 = (bf16[3072,1024]{1,0:T(8,128)(2,1)}, bf16[3072,1024]{1,0:T(8,128)(2,1)}, u32[]{:S(2)}, u32[]{:S(2)}) collective-permute-start(bf16[3072,1024]{1,0:T(8,128)(2,1)} %mine.1), channel_id=1, source_target_pairs={{0,1},{1,0},{2,3},{3,2},{4,5},{5,4},{6,7},{7,6},{8,9},{9,8},{10,11... | collective-permute-start | bytes 18874376 | tf_op jit(solution)/shard_map/ppermute | solution.py:249
  4.9 11.6 %collective-permute-start = (bf16[944,128]{1,0:T(8,128)(2,1)}, bf16[944,128]{1,0:T(8,128)(2,1)S(1)}, u32[]{:S(2)}, u32[]{:S(2)}) collective-permute-start(bf16[944,128]{1,0:T(8,128)(2,1)} %get-tuple-element.17), channel_id=1, source_target_pairs={{0,4},{4,8},{8,12},{12,0},{1,5},{5,9},{9,13},{13,1},{2,6},{6,10},{... | collective-permute-start | bytes 725000 | tf_op jit(solution)/shard_map/ppermute | solution.py:319
  7.5 17.7 %collective-permute-start.4 = (bf16[944,128]{1,0:T(8,128)(2,1)}, bf16[944,128]{1,0:T(8,128)(2,1)S(1)}, u32[]{:S(2)}, u32[]{:S(2)}) collective-permute-start(bf16[944,128]{1,0:T(8,128)(2,1)} %get-tuple-element.22), channel_id=1, source_target_pairs={{0,12},{4,0},{8,4},{12,8},{1,13},{5,1},{9,5},{13,9},{2,14},{6,2},{... | collective-permute-start | bytes 725000 | tf_op jit(solution)/shard_map/ppermute | solution.py:319
  9.6 26.9 %collective-permute-start.2 = (bf16[36,96,128]{2,1,0:T(8,128)(2,1)}, bf16[36,96,128]{2,1,0:T(8,128)(2,1)S(1)}, u32[]{:S(2)}, u32[]{:S(2)}) collective-permute-start(bf16[36,96,128]{2,1,0:T(8,128)(2,1)} %get-tuple-element.20), channel_id=1, source_target_pairs={{0,16},{16,0},{1,17},{17,1},{2,18},{18,2},{3,19},{19,3},{4,20},{20... | collective-permute-start | bytes 2654216 | tf_op jit(solution)/shard_map/ppermute | solution.py:249
  16.5 12.8 %collective-permute-start.1 = (bf16[560,128]{1,0:T(8,128)(2,1)}, bf16[560,128]{1,0:T(8,128)(2,1)S(1)}, u32[]{:S(2)}, u32[]{:S(2)}) collective-permute-start(bf16[560,128]{1,0:T(8,128)(2,1)} %get-tuple-element.18), channel_id=1, source_target_pairs={{0,8},{4,12},{8,0},{12,4},{1,9},{5,13},{9,1},{13,5},{2,10},{6,14},... | collective-permute-start | bytes 430088 | tf_op jit(solution)/shard_map/ppermute | solution.py:319
  23.7 17.5 %collective-permute-start.8 = (bf16[944,128]{1,0:T(8,128)(2,1)S(1)}, bf16[944,128]{1,0:T(8,128)(2,1)S(1)}, u32[]{:S(2)}, u32[]{:S(2)}) collective-permute-start(bf16[944,128]{1,0:T(8,128)(2,1)S(1)} %collective-permute-done.refs_2_), channel_id=1, source_target_pairs={{0,2},{2,0},{1,3},{3,1},{4,6},{6,4},{5,7},{7,5},{8,10},{10,8},{9,1... | collective-permute-start | bytes 725000 | tf_op jit(solution)/shard_map/ppermute | solution.py:249
  25.2 18.0 %collective-permute-start.7 = (bf16[944,128]{1,0:T(8,128)(2,1)S(1)}, bf16[944,128]{1,0:T(8,128)(2,1)S(1)}, u32[]{:S(2)}, u32[]{:S(2)}) collective-permute-start(bf16[944,128]{1,0:T(8,128)(2,1)S(1)} %collective-permute-done.4.refs_2_), channel_id=1, source_target_pairs={{0,2},{2,0},{1,3},{3,1},{4,6},{6,4},{5,7},{7,5},{8,10},{10,8},{9,1... | collective-permute-start | bytes 725000 | tf_op jit(solution)/shard_map/ppermute | solution.py:249
  29.3 5.7 %collective-permute-start.5 = (bf16[384,128]{1,0:T(8,128)(2,1)}, bf16[384,128]{1,0:T(8,128)(2,1)S(1)}, u32[]{:S(2)}, u32[]{:S(2)}) collective-permute-start(bf16[384,128]{1,0:T(8,128)(2,1)} %get-tuple-element.23), channel_id=1, source_target_pairs={{0,8},{4,12},{8,0},{12,4},{1,9},{5,13},{9,1},{13,5},{2,10},{6,14},... | collective-permute-start | bytes 294920 | tf_op jit(solution)/shard_map/ppermute | solution.py:319
  35.0 10.1 %collective-permute-start.3 = (bf16[560,128]{1,0:T(8,128)(2,1)S(1)}, bf16[560,128]{1,0:T(8,128)(2,1)S(1)}, u32[]{:S(2)}, u32[]{:S(2)}) collective-permute-start(bf16[560,128]{1,0:T(8,128)(2,1)S(1)} %collective-permute-done.1.refs_2_), channel_id=1, source_target_pairs={{0,2},{2,0},{1,3},{3,1},{4,6},{6,4},{5,7},{7,5},{8,10},{10,8},{9,1... | collective-permute-start | bytes 430088 | tf_op jit(solution)/shard_map/ppermute | solution.py:249
  36.5 8.6 %collective-permute-start.6 = (bf16[384,128]{1,0:T(8,128)(2,1)S(1)}, bf16[384,128]{1,0:T(8,128)(2,1)S(1)}, u32[]{:S(2)}, u32[]{:S(2)}) collective-permute-start(bf16[384,128]{1,0:T(8,128)(2,1)S(1)} %collective-permute-done.5.refs_4_), channel_id=1, source_target_pairs={{0,2},{2,0},{1,3},{3,1},{4,6},{6,4},{5,7},{7,5},{8,10},{10,8},{9,1... | collective-permute-start | bytes 294920 | tf_op jit(solution)/shard_map/ppermute | solution.py:249
  37.2 1.2 %copy-start = (bf16[36,96,128]{2,1,0:T(8,128)(2,1)S(1)}, bf16[36,96,128]{2,1,0:T(8,128)(2,1)}, u32[]{:S(2)}) copy-start(bf16[36,96,128]{2,1,0:T(8,128)(2,1)} %get-tuple-element.19.refs_0_) | copy-start | bytes 2654212
  38.3 1.0 %copy-start.2 = (bf16[1792,128]{1,0:T(8,128)(2,1)S(1)}, bf16[1792,128]{1,0:T(8,128)(2,1)}, u32[]{:S(2)}) copy-start(bf16[1792,128]{1,0:T(8,128)(2,1)} %get-tuple-element.26.refs_2_) | copy-start | bytes 1376260
  39.3 1.9 %copy-start.1 = (bf16[36,96,128]{2,1,0:T(8,128)(2,1)S(1)}, bf16[36,96,128]{2,1,0:T(8,128)(2,1)}, u32[]{:S(2)}) copy-start(bf16[36,96,128]{2,1,0:T(8,128)(2,1)} %get-tuple-element.19.refs_0_) | copy-start | bytes 2654212
  43.2 3.9 %slice-start = ((s8[6291456]{0:T(1024)(128)(4,1)}), s8[4194304]{0:T(1024)(128)(4,1)S(1)}, s32[]{:S(2)}) async-start(s8[6291456]{0:T(1024)(128)(4,1)} %bitcast.23), calls=%async_computation.1 | async-start | bytes 8388608
  45.1 2.0 %slice-start.1 = ((s8[6291456]{0:T(1024)(128)(4,1)}), s8[2097152]{0:T(1024)(128)(4,1)S(1)}, s32[]{:S(2)}) async-start(s8[6291456]{0:T(1024)(128)(4,1)} %bitcast.23), calls=%async_computation.2 | async-start | bytes 4194304
  47.0 22.8 %copy-start.4 = (f32[1024]{0:T(1024)S(1)}, f32[1024]{0:T(1024)}, u32[]{:S(2)}) copy-start(f32[1024]{0:T(1024)} %param.22) | copy-start | bytes 12292
  47.0 23.0 %copy-start.7 = (f32[1024]{0:T(1024)S(1)}, f32[1024]{0:T(1024)}, u32[]{:S(2)}) copy-start(f32[1024]{0:T(1024)} %param.23) | copy-start | bytes 12292

commit v5 on v4

--- a/solution.py
+++ b/solution.py
@@ -23,53 +23,61 @@
     return block.reshape(band_count, cap), used.reshape(band_count, cap)
 
 
-def pack_kernel(pieces, ocean, atmos, weights, tiles_of, land, *refs):
-    (ocean_w, atmos_w), (ocean_ids, atmos_ids) = weights, tiles_of
-    keep, send, own, outs, sem = refs[0], refs[1], refs[2], refs[3:-1], refs[-1]
+def pack_kernel(pieces, *refs):
+    ocean, atmos, ocean_w, atmos_w, ocean_ids, atmos_ids, land, send = refs[:8]
+    outs, metas, sem = refs[8:-2], refs[-2], refs[-1]
     me, bands = lax.axis_index("band"), ocean_w.shape[0]
     x, y = lax.axis_index("var"), lax.axis_index("grp")
     cells, tiles = land.shape[-1], land.shape[0]
     cap = ocean_ids.shape[-1]
     each = cap // 2
 
-    def copies(mine, other, weights):
-        pairs = []
-        for out, (shift, first, size) in zip(outs, pieces):
+    def copies(weights, fields):
+        found = []
+        for at, (out, (shift, first, size)) in enumerate(zip(outs, pieces)):
             start = pl.multiple_of((x * each + first) * cells, cells)
             target = lax.rem(me + shift, bands)
-            pairs.append(
-                (
+            found.append(
+                pltpu.make_async_copy(
                     weights.at[target, pl.ds(start, size * cells), :],
                     out.at[pl.ds(0, size * cells), :],
+                    sem.at[at],
                 )
             )
-        pairs += [(other, send), (mine, keep), (weights.at[me], own)]
-        return [pltpu.make_async_copy(a, b, sem.at[i]) for i, (a, b) in enumerate(pairs)]
+        return found + [pltpu.make_async_copy(fields, send, sem.at[len(pieces)])]
 
     @pl.when(y == 0)
     def _():
-        for copy in copies(ocean, atmos, ocean_w):
+        for copy in copies(ocean_w, atmos):
             copy.start()
 
     @pl.when(y == 1)
     def _():
-        for copy in copies(atmos, ocean, atmos_w):
+        for copy in copies(atmos_w, ocean):
             copy.start()
 
     fraction = land[...]
     high = fraction.astype(jnp.bfloat16)
     low = (fraction - high.astype(jnp.float32)).astype(jnp.bfloat16)
-    for out, (shift, first, size) in zip(outs, pieces):
+    done = copies(ocean_w, atmos)
+    for at, (out, (shift, first, size)) in enumerate(zip(outs, pieces)):
         if first:
             continue
-        target, base = lax.rem(me + shift, bands), size * cells
-        out[pl.ds(base, tiles), :] = high
-        out[pl.ds(base + tiles, tiles), :] = low
+        target = lax.rem(me + shift, bands)
+        metas[at, pl.ds(0, tiles), :] = high
+        metas[at, pl.ds(tiles, tiles), :] = low
         row = jnp.where(y == 0, ocean_ids[pl.ds(target, 1), :], atmos_ids[pl.ds(target, 1), :])
         row = jnp.broadcast_to(row.astype(jnp.float32), (16, cap)).astype(jnp.bfloat16)
-        out[pl.ds(base + 2 * tiles, 16), :] = jnp.zeros((16, cells), jnp.bfloat16)
-        out[pl.ds(base + 2 * tiles, 16), pl.ds(0, cap)] = row
-    for copy in copies(ocean, atmos, ocean_w):
+        metas[at, pl.ds(2 * tiles, 16), :] = jnp.zeros((16, cells), jnp.bfloat16)
+        metas[at, pl.ds(2 * tiles, 16), pl.ds(0, cap)] = row
+        copy = pltpu.make_async_copy(
+            metas.at[at],
+            out.at[pl.ds(size * cells, metas.shape[1]), :],
+            sem.at[len(pieces) + 1 + at],
+        )
+        copy.start()
+        done.append(copy)
+    for copy in done:
         copy.wait()
 
 
@@ -77,21 +85,58 @@
     cells, tiles = land.shape[-1], land.shape[0]
     any_spec = pl.BlockSpec(memory_space=pl.ANY)
     vmem = pl.BlockSpec(memory_space=pltpu.VMEM)
-    sizes = [size * cells + (0 if first else 2 * tiles + 16) for _, first, size in pieces]
-    shapes = [ocean.shape, ocean.shape, ocean_w.shape[1:]] + [(n, cells) for n in sizes]
-
-    def body(o, a, ow, aw, oi, ai, land, *refs):
-        pack_kernel(pieces, o, a, (ow, aw), (oi, ai), land, *refs)
-
+    meta = 2 * tiles + 16
+    sizes = [size * cells + (0 if first else meta) for _, first, size in pieces]
+    shapes = [ocean.shape] + [(n, cells) for n in sizes]
     return pl.pallas_call(
-        body,
+        functools.partial(pack_kernel, pieces),
         out_shape=[jax.ShapeDtypeStruct(shape, jnp.bfloat16) for shape in shapes],
         in_specs=[any_spec] * 4 + [vmem] * 3,
-        out_specs=[vmem] * len(shapes),
-        scratch_shapes=[pltpu.SemaphoreType.DMA((len(shapes),))],
-        cost_estimate=pl.CostEstimate(flops=0, bytes_accessed=6 << 20, transcendentals=0),
+        out_specs=[any_spec] * len(shapes),
+        scratch_shapes=[
+            pltpu.VMEM((len(pieces), meta, cells), jnp.bfloat16),
+            pltpu.SemaphoreType.DMA((2 * len(pieces) + 1,)),
+        ],
+        cost_estimate=pl.CostEstimate(flops=0, bytes_accessed=4 << 20, transcendentals=0),
         compiler_params=pltpu.CompilerParams(vmem_limit_bytes=60 << 20),
     )(ocean, atmos, ocean_w, atmos_w, ocean_ids, atmos_ids, land)
+
+
+def keep_kernel(ocean, atmos, ocean_w, atmos_w, keep, own, sem):
+    me, y = lax.axis_index("band"), lax.axis_index("grp")
+
+    def copies(fields, weights):
+        return [
+            pltpu.make_async_copy(fields, keep, sem.at[0]),
+            pltpu.make_async_copy(weights.at[me], own, sem.at[1]),
+        ]
+
+    @pl.when(y == 0)
+    def _():
+        for copy in copies(ocean, ocean_w):
+            copy.start()
+
+    @pl.when(y == 1)
+    def _():
+        for copy in copies(atmos, atmos_w):
+            copy.start()
+
+    for copy in copies(ocean, ocean_w):
+        copy.wait()
+
+
+def keep_own(ocean, atmos, ocean_w, atmos_w):
+    any_spec = pl.BlockSpec(memory_space=pl.ANY)
+    shapes = [ocean.shape, ocean_w.shape[1:]]
+    return pl.pallas_call(
+        keep_kernel,
+        out_shape=[jax.ShapeDtypeStruct(shape, jnp.bfloat16) for shape in shapes],
+        in_specs=[any_spec] * 4,
+        out_specs=[any_spec] * 2,
+        scratch_shapes=[pltpu.SemaphoreType.DMA((2,))],
+        cost_estimate=pl.CostEstimate(flops=0, bytes_accessed=3 << 20, transcendentals=0),
+        compiler_params=pltpu.CompilerParams(vmem_limit_bytes=60 << 20),
+    )(ocean, atmos, ocean_w, atmos_w)
 
 
 def regrid_kernel(groups, steps, meta_at, part_slots, table, where, *refs):
@@ -140,7 +185,9 @@
                 ).astype(out.dtype)
 
 
-def regrid(table, where, fields, parts, part_slots, rest, meta_at, previous, bands, steps, tiles):
+def regrid(
+    table, where, fields, parts, part_slots, rest, meta_at, previous, bands, steps, tiles, total, at=0
+):
     groups = len(fields)
     rows, cells = fields[0].shape[1:]
     whole = lambda a: pl.BlockSpec(a.shape, lambda i, t, w, n=a.ndim: (0,) * n)
@@ -152,15 +199,15 @@
         in_specs.append(pl.BlockSpec(memory_space=pl.ANY))
         operands.append(previous)
     row_count, width = steps * tiles // 2, rows // steps // 2 * 2 * cells
-    block = (groups, 2, row_count, width)
+    block = (2, row_count, width)
     return pl.pallas_call(
         functools.partial(regrid_kernel, groups, steps, meta_at, tuple(part_slots)),
-        out_shape=jax.ShapeDtypeStruct((bands,) + block, jnp.bfloat16),
+        out_shape=jax.ShapeDtypeStruct((bands, total) + block, jnp.bfloat16),
         grid_spec=pltpu.PrefetchScalarGridSpec(
             num_scalar_prefetch=2,
             grid=(1,),
             in_specs=in_specs,
-            out_specs=pl.BlockSpec((1,) + block, lambda i, t, w: (w[0], 0, 0, 0, 0)),
+            out_specs=pl.BlockSpec((1, groups) + block, lambda i, t, w: (w[0], at, 0, 0, 0)),
             scratch_shapes=[
                 pltpu.VMEM((groups, tiles * rows, cells), jnp.float32),
                 pltpu.VMEM((2 * tiles + 8, cells), jnp.float32),
@@ -278,8 +325,6 @@
     x, y = lax.axis_index("var"), lax.axis_index("grp")
     quarter = y * nv + x
 
-    embed_other = swap(embed_weight, "sub")
-
     flat = (nb, cap * cells, cells)
     ocean_w, atmos_w = ocean_weights.reshape(flat), atmos_weights.reshape(flat)
     ocean_ids, atmos_ids = ocean_tiles.reshape(nb, cap), atmos_tiles.reshape(nb, cap)
@@ -287,7 +332,7 @@
     blocks = (block_count, steps * local_vars, cells)
     ocean_f, atmos_f = ocean_fields.reshape(blocks), atmos_fields.reshape(blocks)
     order = ([1, nb - 1] + list(range(2, nb - 1)))[: nb - 1]
-    call = functools.partial(regrid, bands=nb, steps=steps, tiles=tiles)
+    call = functools.partial(regrid, bands=nb, steps=steps, tiles=tiles, total=1)
     along = lambda shift: [(b, (b + shift) % nb) for b in range(nb)]
 
     if ng == 2 and nv == 2 and cap % 2 == 0:
@@ -299,10 +344,13 @@
                 pieces += [(shift, 0, head), (shift, head, each - head)]
             else:
                 pieces.append((shift, 0, each))
-        keep, send, own_w, *packed = pack(
+        send, *packed = pack(
             pieces, ocean_f, atmos_f, ocean_w, atmos_w, ocean_ids, atmos_ids, land
         )
-        fields = [keep, swap(send, "grp")]
+        theirs = swap(send, "grp")
+        embed_other, packed[0] = lax.optimization_barrier((embed_weight, packed[0]))
+        embed_other = swap(embed_other, "sub")
+        keep, own_w = keep_own(ocean_f, atmos_f, ocean_w, atmos_w)
         dest = jnp.where(y == 0, ocean_dest, atmos_dest)
         block_all, used_all = slot_tables(dest, nb, cap)
 
@@ -317,13 +365,10 @@
             if at >= 2:
                 piece, sent[at - 2] = lax.optimization_barrier((piece, sent[at - 2]))
             sent.append(lax.ppermute(piece, "band", along(shift)))
-        crossed = [swap(piece, "var") for piece in sent]
 
         ids = jnp.where(y == 0, ocean_ids, atmos_ids)
         own_tile = lax.dynamic_index_in_dim(ids, me, 0, keepdims=False)
-        where = jnp.stack([me, jnp.int32(0)])
-        rows_x = call(table_of(me, own_tile), where, fields, [own_w], [cap], [land], None, None)
-        for shift in order:
+        def call_of(shift):
             band = (me - shift) % nb
             parts, sizes, firsts = [], [], []
             for piece, across, (of, first, size) in zip(sent, crossed, pieces):
@@ -334,10 +379,32 @@
             meta_at = sizes[0] * cells
             tile = parts[0][meta_at + 2 * tiles, :cap].astype(jnp.int32)
             where = jnp.stack([band] + firsts).astype(jnp.int32)
-            rows_x = call(table_of(band, tile), where, fields, parts, sizes, [], meta_at, rows_x)
+            return table_of(band, tile), where, parts, sizes, [], meta_at
+
+        def add(previous, which, fields, at=0):
+            table, where, *rest = which
+            return call(table, where, fields, *rest, previous, total=2, at=at)
+
+        where = jnp.stack([me, jnp.int32(0)])
+        calls = [(table_of(me, own_tile), where, [own_w], [cap], [land], None)]
+        rows_x = add(None, calls[0], [keep])
+        crossed = [swap(piece, "var") for piece in sent[:2]]
+        for at, piece in enumerate(sent[2:]):
+            if at == 1:
+                calls.append(call_of(order[0]))
+                rows_x = add(rows_x, calls[1], [keep])
+            piece, rows_x = lax.optimization_barrier((piece, rows_x))
+            crossed.append(swap(piece, "var"))
+        calls += [call_of(shift) for shift in order[len(calls) - 1 :]]
+        for which in calls[2:-1]:
+            rows_x = add(rows_x, which, [keep])
+        for which in calls[:-1]:
+            rows_x = add(rows_x, which, [theirs], 1)
+        rows_x = add(rows_x, calls[-1], [keep, theirs])
         sent = embed(rows_x, embed_weight, embed_other, steps, nv)
         got = lax.all_to_all(sent, ("grp", "band", "var"), split_axis=0, concat_axis=0, tiled=True)
     else:
+        embed_other = swap(embed_weight, "sub")
         both = jnp.concatenate([ocean_w, atmos_w], axis=1)
         fields = [jnp.concatenate([ocean_f, atmos_f], axis=0)]
         ocean_block, ocean_used = slot_tables(ocean_dest, nb, cap)

time: 71.2 us -> 151 us (2.12)
  Pallas kernels: 19 us -> 108 us
  starting transfers between devices: 20 us -> 12.9 us
  waiting for transfers between devices: 11.8 us -> 6.73 us
  blocking collectives: 15.5 us -> 17.9 us
    pallas_call x1 -> x2, Pallas kernels: 4.3 us -> 91.4 us  [the longest x1 49.6 us: pack(): pl.pallas_call(functools.partial(pack_kernel, pieces), out_shape=[jax.Sha...]
    ppermute x4, starting transfers between devices: 13.6 us -> 5.61 us  [per_device(): sent.append(lax.ppermute(piece, 'band', along(shift)))]
    ppermute x4, waiting for transfers between devices: 11.8 us -> 6.72 us  [per_device(): sent.append(lax.ppermute(piece, 'band', along(shift)))]
    all_to_all x1, blocking collectives: 15.5 us -> 17.9 us  [per_device(): lax.all_to_all(sent, ('grp', 'band', 'var'), split_axis=0, concat_axis=0,...]
    pallas_call x4 -> x7, Pallas kernels: 7.59 us -> 9.73 us  [regrid(): pl.pallas_call(functools.partial(regrid_kernel, groups, steps, meta_at, t...]
  transfers between devices with their start and end apart: 10 -> 10, of which waited for: 3 -> 2; matrix products, arithmetic and copies ran while one was open for 1% -> 1% of each run, Pallas kernels for 17% -> 34%
where the time goes in v5:
time: 151 us; the launch traced here: 150 us
  Pallas kernels  108 us (72%)
  blocking collectives  17.9 us (12%)
  starting transfers between devices  12.9 us (9%)
  waiting for transfers between devices  6.73 us (4%)
  local copies, waits for them, and re-layouts  3.29 us (2%)
    pallas_call x1, Pallas kernels, pack(): pl.pallas_call(functools.partial(pack_kernel, pieces), out_shape=[jax.Sha...  49.6 us
    pallas_call x1, Pallas kernels, keep_own(): pl.pallas_call(keep_kernel, out_shape=[jax.ShapeDtypeStruct(shape, jnp.bf...  41.8 us
    all_to_all x1, blocking collectives, per_device(): lax.all_to_all(sent, ('grp', 'band', 'var'), split_axis=0, concat_axis=0,...  17.9 us
    pallas_call x7, Pallas kernels, regrid(): pl.pallas_call(functools.partial(regrid_kernel, groups, steps, meta_at, t...  9.73 us
    ppermute x6, starting transfers between devices, swap(): return lax.ppermute(x, axis, [(0, 1), (1, 0)])  7.25 us
    pallas_call x1, Pallas kernels, embed(): pl.pallas_call(functools.partial(embed_kernel, steps, halves), out_shape=...  7.07 us
    ppermute x4, waiting for transfers between devices, per_device(): sent.append(lax.ppermute(piece, 'band', along(shift)))  6.72 us
    ppermute x4, starting transfers between devices, per_device(): sent.append(lax.ppermute(piece, 'band', along(shift)))  5.61 us
  transfers between devices with their start and end apart: 10, of which 2 were waited for; matrix products, arithmetic and copies ran while one was open for 1% of the time, Pallas kernels for 34%

profile of v5, /device:TPU:0, one launch (start us, length us, event | category | flops | bytes accessed | tf_op | source)
XLA Modules:
  0.0 150.3 jit_solution(6096545301564397531)
XLA Ops:
  0.0 49.6 %shard_map.118 = (bf16[36,96,128]{2,1,0:T(8,128)(2,1)}, bf16[944,128]{1,0:T(8,128)(2,1)}, bf16[944,128]{1,0:T(8,128)(2,1)}, bf16[560,128]{1,0:T(8,128)(2,1)}, bf16[384,128]{1,0:T(8,128)(2,1)}) custom-call(bf16[36,96,128]{2,1,0:T(8,128)(2,1)} %bitcast.32, bf16[36,96,128]{2,1,0:T(8,128)(2,1)} %bitcast.34, bf16[4,1792,128]{2,1,0:T(8,128)(2,1)} %bitcast.28, ...), custom_call_target="tpu_custom_call" | custom-call | bytes 4194304 | tf_op jit(solution)/shard_map/pallas_call | solution.py:91
  49.6 0.0 copy-start.6
  49.6 0.0 copy-start.7
  49.6 0.0 copy-start.4
  49.7 0.5 collective-permute-start.9
  50.2 2.6 %collective-permute-start = (bf16[944,128]{1,0:T(8,128)(2,1)}, bf16[944,128]{1,0:T(8,128)(2,1)S(1)}, u32[]{:S(2)}, u32[]{:S(2)}) collective-permute-start(bf16[944,128]{1,0:T(8,128)(2,1)} %get-tuple-element.24), channel_id=1, source_target_pairs={{0,4},{4,8},{8,12},{12,0},{1,5},{5,9},{9,13},{13,1},{2,6},{6,10},{... | collective-permute-start | bytes 725000 | tf_op jit(solution)/shard_map/ppermute | solution.py:367
  52.8 2.1 %collective-permute-start.4 = (bf16[944,128]{1,0:T(8,128)(2,1)}, bf16[944,128]{1,0:T(8,128)(2,1)S(1)}, u32[]{:S(2)}, u32[]{:S(2)}) collective-permute-start(bf16[944,128]{1,0:T(8,128)(2,1)} %get-tuple-element.31), channel_id=1, source_target_pairs={{0,12},{4,0},{8,4},{12,8},{1,13},{5,1},{9,5},{13,9},{2,14},{6,2},{... | collective-permute-start | bytes 725000 | tf_op jit(solution)/shard_map/ppermute | solution.py:367
  54.9 1.7 %collective-permute-start.2 = (bf16[36,96,128]{2,1,0:T(8,128)(2,1)}, bf16[36,96,128]{2,1,0:T(8,128)(2,1)S(1)}, u32[]{:S(2)}, u32[]{:S(2)}) collective-permute-start(bf16[36,96,128]{2,1,0:T(8,128)(2,1)} %get-tuple-element.27), channel_id=1, source_target_pairs={{0,16},{16,0},{1,17},{17,1},{2,18},{18,2},{3,19},{19,3},{4,20},{20... | collective-permute-start | bytes 2654216 | tf_op jit(solution)/shard_map/ppermute | solution.py:296
  56.6 0.2 convert_reduce_fusion.1
  56.8 0.1 select_reduce_fusion
  56.9 0.1 reshape.89
  57.0 0.1 add_add_fusion.where
  57.0 0.1 add_add_fusion.1.where
  57.1 0.1 fusion.1
  57.2 0.1 pad_add_fusion.4.where
  57.3 41.8 %shard_map.119 = (bf16[36,96,128]{2,1,0:T(8,128)(2,1)}, bf16[1792,128]{1,0:T(8,128)(2,1)}) custom-call(bf16[36,96,128]{2,1,0:T(8,128)(2,1)} %bitcast.33, bf16[36,96,128]{2,1,0:T(8,128)(2,1)} %bitcast.35, bf16[4,1792,128]{2,1,0:T(8,128)(2,1)} %bitcast.29, bf16[4,1792,128]{2,1,0:T(8,128)(2,1)} %bitcast.31), custom_call_target="tpu_custom_call" | custom-call | bytes 3145728 | tf_op jit(solution)/shard_map/pallas_call | solution.py:131
  99.1 0.1 reshape.97
  99.2 0.1 stack.70.where
  99.3 0.0 collective-permute-done.refs_1_
  99.3 0.9 collective-permute-start.1
  100.2 1.5 collective-permute-start.6
  101.7 0.5 collective-permute-start.8
  102.2 5.6 %collective-permute-done.1.refs_2_ = bf16[560,128]{1,0:T(8,128)(2,1)S(1)} collective-permute-done((bf16[560,128]{1,0:T(8,128)(2,1)S(1)}, bf16[560,128]{1,0:T(8,128)(2,1)S(1)}, u32[]{:S(2)}, u32[]{:S(2)}) %collective-permute-start.1) | collective-permute-done | bytes 143392 | tf_op jit(solution)/shard_map/ppermute | solution.py:367
  107.9 0.0 collective-permute-start.5
  107.9 1.2 copy-done
  109.1 1.0 copy-done.2
  110.1 1.3 shard_map.120.refs_3_
  111.4 1.6 %collective-permute-start.3 = (bf16[560,128]{1,0:T(8,128)(2,1)S(1)}, bf16[560,128]{1,0:T(8,128)(2,1)S(1)}, u32[]{:S(2)}, u32[]{:S(2)}) collective-permute-start(bf16[560,128]{1,0:T(8,128)(2,1)S(1)} %collective-permute-done.1.refs_2_), channel_id=1, source_target_pairs={{0,2},{2,0},{1,3},{3,1},{4,6},{6,4},{5,7},{7,5},{8,10},{10,8},{9,1... | collective-permute-start | bytes 430088 | tf_op jit(solution)/shard_map/ppermute | solution.py:296
  113.0 1.3 shard_map.121.refs_3_
  114.3 1.1 collective-permute-done.5.refs_4_
  115.4 1.5 collective-permute-start.7
  116.9 1.3 shard_map.122.refs_3_
  118.3 1.3 shard_map.123.refs_3_
  119.6 1.3 shard_map.124.refs_3_
  120.9 0.0 slice-start
  120.9 1.3 shard_map.125.refs_6_
  122.2 0.0 slice-start.1
  122.3 1.9 %shard_map.126.rows_x = bf16[4,2,2,32,3072]{4,3,2,1,0:T(8,128)(2,1)S(1)} custom-call(s32[3,14]{1,0:T(4,128)S(1)} %pad_add_fusion.table, s32[5]{0:T(128)S(1)} %stack.70.where, bf16[36,96,128]{2,1,0:T(8,128)(2,1)S(1)} %copy-done.1, bf16[36,96,128]{2,1,0:T(8,128)(2,1)S(1)} %collective-permute-done.2.refs_0_.refs_1_, ...), custom_call_target="tpu_custom_call", output_to_operand_aliasing={{}: (8, {})} | custom-call | flops 88080384 | bytes 4194304 | tf_op jit(solution)/shard_map/pallas_call | solution.py:203
  124.2 0.0 copy-start.5
  124.2 0.0 copy-start.8
  124.2 0.0 slice-done.1
  124.2 7.1 %shard_map.127 = bf16[16,16,1024]{2,1,0:T(8,128)(2,1)S(1)} custom-call(bf16[4,2,2,32,3072]{4,3,2,1,0:T(8,128)(2,1)S(1)} %shard_map.126.rows_x, bf16[3072,1024]{1,0:T(8,128)(2,1)S(1)} %bitcast.24, bf16[3072,1024]{1,0:T(8,128)(2,1)} %collective-permute-done.9.theirs), custom_call_target="tpu_custom_call" | custom-call | flops 3221225472 | bytes 12582912 | tf_op jit(solution)/shard_map/pallas_call | solution.py:269
  131.3 17.9 %all_to_all.5 = bf16[16,16,1024]{2,1,0:T(8,128)(2,1)S(1)} all-to-all(bf16[16,16,1024]{2,1,0:T(8,128)(2,1)S(1)} %shard_map.127), channel_id=1, replica_groups=mesh['grp'=2,'band'=4,'var'=2,'sub'=2] {'grp','band','var'}, dimensions={0} | all-to-all | bytes 1048576 | tf_op jit(solution)/shard_map/all_to_all | solution.py:405
  149.3 0.1 convert_reduce_fusion
  149.4 0.1 multiply_reduce_fusion
  149.5 0.1 rsqrt.12
  149.6 0.1 fusion
  149.7 0.6 copy.21
  (42 shorter events, 0.2 us)
Async XLA Ops:
  0.0 56.6 %copy-start.9 = (s32[36,1]{0,1:T(1,128)S(1)}, s32[36,1]{0,1:T(1,128)}, u32[]{:S(2)}) copy-start(s32[36,1]{0,1:T(1,128)} %param.13) | copy-start | bytes 436
  0.0 56.6 %copy-start.10 = (s32[36,1]{0,1:T(1,128)S(1)}, s32[36,1]{0,1:T(1,128)}, u32[]{:S(2)}) copy-start(s32[36,1]{0,1:T(1,128)} %param.17) | copy-start | bytes 436
  49.6 49.7 %copy-start.6 = (s32[1,1,4,14]{3,2,1,0:T(4,128)S(1)}, s32[1,1,4,14]{3,2,1,0:T(4,128)}, u32[]{:S(2)}) copy-start(s32[1,1,4,14]{3,2,1,0:T(4,128)} %param.15) | copy-start | bytes 676
  49.6 49.7 %copy-start.7 = (s32[1,1,4,14]{3,2,1,0:T(4,128)S(1)}, s32[1,1,4,14]{3,2,1,0:T(4,128)}, u32[]{:S(2)}) copy-start(s32[1,1,4,14]{3,2,1,0:T(4,128)} %param.19) | copy-start | bytes 676
  49.6 49.7 %copy-start.11 = (bf16[560,128]{1,0:T(8,128)(2,1)S(1)}, bf16[560,128]{1,0:T(8,128)(2,1)}, u32[]{:S(2)}) copy-start(bf16[560,128]{1,0:T(8,128)(2,1)} %get-tuple-element.25) | copy-start | bytes 430084
  49.6 58.2 %copy-start.12 = (bf16[384,128]{1,0:T(8,128)(2,1)S(1)}, bf16[384,128]{1,0:T(8,128)(2,1)}, u32[]{:S(2)}) copy-start(bf16[384,128]{1,0:T(8,128)(2,1)} %get-tuple-element.32) | copy-start | bytes 294916
  49.6 58.3 %copy-start.4 = (f32[1,1,8,2,128]{4,3,2,1,0:T(2,128)S(1)}, f32[1,1,8,2,128]{4,3,2,1,0:T(2,128)}, u32[]{:S(2)}) copy-start(f32[1,1,8,2,128]{4,3,2,1,0:T(2,128)} %param.20) | copy-start | bytes 24580
  49.7 74.5 %collective-permute-start.9 = (bf16[3072,1024]{1,0:T(8,128)(2,1)}, bf16[3072,1024]{1,0:T(8,128)(2,1)}, u32[]{:S(2)}, u32[]{:S(2)}) collective-permute-start(bf16[3072,1024]{1,0:T(8,128)(2,1)} %mine.1), channel_id=1, source_target_pairs={{0,1},{1,0},{2,3},{3,2},{4,5},{5,4},{6,7},{7,6},{8,9},{9,8},{10,11... | collective-permute-start | bytes 18874376 | tf_op jit(solution)/shard_map/ppermute | solution.py:296
  50.2 49.1 %collective-permute-start = (bf16[944,128]{1,0:T(8,128)(2,1)}, bf16[944,128]{1,0:T(8,128)(2,1)S(1)}, u32[]{:S(2)}, u32[]{:S(2)}) collective-permute-start(bf16[944,128]{1,0:T(8,128)(2,1)} %get-tuple-element.24), channel_id=1, source_target_pairs={{0,4},{4,8},{8,12},{12,0},{1,5},{5,9},{9,13},{13,1},{2,6},{6,10},{... | collective-permute-start | bytes 725000 | tf_op jit(solution)/shard_map/ppermute | solution.py:367
  52.8 47.4 %collective-permute-start.4 = (bf16[944,128]{1,0:T(8,128)(2,1)}, bf16[944,128]{1,0:T(8,128)(2,1)S(1)}, u32[]{:S(2)}, u32[]{:S(2)}) collective-permute-start(bf16[944,128]{1,0:T(8,128)(2,1)} %get-tuple-element.31), channel_id=1, source_target_pairs={{0,12},{4,0},{8,4},{12,8},{1,13},{5,1},{9,5},{13,9},{2,14},{6,2},{... | collective-permute-start | bytes 725000 | tf_op jit(solution)/shard_map/ppermute | solution.py:367
  54.9 63.3 %collective-permute-start.2 = (bf16[36,96,128]{2,1,0:T(8,128)(2,1)}, bf16[36,96,128]{2,1,0:T(8,128)(2,1)S(1)}, u32[]{:S(2)}, u32[]{:S(2)}) collective-permute-start(bf16[36,96,128]{2,1,0:T(8,128)(2,1)} %get-tuple-element.27), channel_id=1, source_target_pairs={{0,16},{16,0},{1,17},{17,1},{2,18},{18,2},{3,19},{19,3},{4,20},{20... | collective-permute-start | bytes 2654216 | tf_op jit(solution)/shard_map/ppermute | solution.py:296
  99.3 8.5 %collective-permute-start.1 = (bf16[560,128]{1,0:T(8,128)(2,1)S(1)}, bf16[560,128]{1,0:T(8,128)(2,1)S(1)}, u32[]{:S(2)}, u32[]{:S(2)}) collective-permute-start(bf16[560,128]{1,0:T(8,128)(2,1)S(1)} %copy-done.11), channel_id=1, source_target_pairs={{0,8},{4,12},{8,0},{12,4},{1,9},{5,13},{9,1},{13,5},{2,10},{6,14},... | collective-permute-start | bytes 430088 | tf_op jit(solution)/shard_map/ppermute | solution.py:367
  100.2 11.2 %collective-permute-start.6 = (bf16[944,128]{1,0:T(8,128)(2,1)S(1)}, bf16[944,128]{1,0:T(8,128)(2,1)S(1)}, u32[]{:S(2)}, u32[]{:S(2)}) collective-permute-start(bf16[944,128]{1,0:T(8,128)(2,1)S(1)} %collective-permute-done.refs_1_), channel_id=1, source_target_pairs={{0,2},{2,0},{1,3},{3,1},{4,6},{6,4},{5,7},{7,5},{8,10},{10,8},{9,1... | collective-permute-start | bytes 725000 | tf_op jit(solution)/shard_map/ppermute | solution.py:296
  101.7 15.2 %collective-permute-start.8 = (bf16[944,128]{1,0:T(8,128)(2,1)S(1)}, bf16[944,128]{1,0:T(8,128)(2,1)S(1)}, u32[]{:S(2)}, u32[]{:S(2)}) collective-permute-start(bf16[944,128]{1,0:T(8,128)(2,1)S(1)} %collective-permute-done.4.refs_1_), channel_id=1, source_target_pairs={{0,2},{2,0},{1,3},{3,1},{4,6},{6,4},{5,7},{7,5},{8,10},{10,8},{9,1... | collective-permute-start | bytes 725000 | tf_op jit(solution)/shard_map/ppermute | solution.py:296
  107.9 7.6 %collective-permute-start.5 = (bf16[384,128]{1,0:T(8,128)(2,1)S(1)}, bf16[384,128]{1,0:T(8,128)(2,1)S(1)}, u32[]{:S(2)}, u32[]{:S(2)}) collective-permute-start(bf16[384,128]{1,0:T(8,128)(2,1)S(1)} %copy-done.12), channel_id=1, source_target_pairs={{0,8},{4,12},{8,0},{12,4},{1,9},{5,13},{9,1},{13,5},{2,10},{6,14},... | collective-permute-start | bytes 294920 | tf_op jit(solution)/shard_map/ppermute | solution.py:367
  107.9 1.2 copy-start
  109.1 1.0 copy-start.2
  111.4 10.8 %collective-permute-start.3 = (bf16[560,128]{1,0:T(8,128)(2,1)S(1)}, bf16[560,128]{1,0:T(8,128)(2,1)S(1)}, u32[]{:S(2)}, u32[]{:S(2)}) collective-permute-start(bf16[560,128]{1,0:T(8,128)(2,1)S(1)} %collective-permute-done.1.refs_2_), channel_id=1, source_target_pairs={{0,2},{2,0},{1,3},{3,1},{4,6},{6,4},{5,7},{7,5},{8,10},{10,8},{9,1... | collective-permute-start | bytes 430088 | tf_op jit(solution)/shard_map/ppermute | solution.py:296
  115.4 6.8 %collective-permute-start.7 = (bf16[384,128]{1,0:T(8,128)(2,1)S(1)}, bf16[384,128]{1,0:T(8,128)(2,1)S(1)}, u32[]{:S(2)}, u32[]{:S(2)}) collective-permute-start(bf16[384,128]{1,0:T(8,128)(2,1)S(1)} %collective-permute-done.5.refs_4_), channel_id=1, source_target_pairs={{0,2},{2,0},{1,3},{3,1},{4,6},{6,4},{5,7},{7,5},{8,10},{10,8},{9,1... | collective-permute-start | bytes 294920 | tf_op jit(solution)/shard_map/ppermute | solution.py:296
  116.9 1.3 copy-start.3
  120.9 1.4 copy-start.1
  120.9 3.3 %slice-start = ((s8[6291456]{0:T(1024)(128)(4,1)}), s8[4194304]{0:T(1024)(128)(4,1)S(1)}, s32[]{:S(2)}) async-start(s8[6291456]{0:T(1024)(128)(4,1)} %bitcast.23), calls=%async_computation.1 | async-start | bytes 8388608
  122.2 2.0 %slice-start.1 = ((s8[6291456]{0:T(1024)(128)(4,1)}), s8[2097152]{0:T(1024)(128)(4,1)S(1)}, s32[]{:S(2)}) async-start(s8[6291456]{0:T(1024)(128)(4,1)} %bitcast.23), calls=%async_computation.2 | async-start | bytes 4194304
  124.2 25.2 %copy-start.5 = (f32[1024]{0:T(1024)S(1)}, f32[1024]{0:T(1024)}, u32[]{:S(2)}) copy-start(f32[1024]{0:T(1024)} %param.22) | copy-start | bytes 12292
  124.2 25.4 %copy-start.8 = (f32[1024]{0:T(1024)S(1)}, f32[1024]{0:T(1024)}, u32[]{:S(2)}) copy-start(f32[1024]{0:T(1024)} %param.23) | copy-start | bytes 12292

commit v6 on v5

--- a/solution.py
+++ b/solution.py
@@ -24,105 +24,107 @@
 
 
 def pack_kernel(pieces, *refs):
-    ocean, atmos, ocean_w, atmos_w, ocean_ids, atmos_ids, land, send = refs[:8]
-    outs, metas, sem = refs[8:-2], refs[-2], refs[-1]
+    count = len(pieces) + 1
+    ocean, atmos, ocean_w, atmos_w, ocean_ids, atmos_ids, land = refs[:7]
+    outs, stages, sem = refs[7 : 7 + count], refs[7 + count : -1], refs[-1]
     me, bands = lax.axis_index("band"), ocean_w.shape[0]
     x, y = lax.axis_index("var"), lax.axis_index("grp")
     cells, tiles = land.shape[-1], land.shape[0]
     cap = ocean_ids.shape[-1]
     each = cap // 2
 
-    def copies(weights, fields):
+    def loads(weights, fields):
         found = []
-        for at, (out, (shift, first, size)) in enumerate(zip(outs, pieces)):
+        for at, (stage, (shift, first, size)) in enumerate(zip(stages, pieces)):
             start = pl.multiple_of((x * each + first) * cells, cells)
             target = lax.rem(me + shift, bands)
             found.append(
                 pltpu.make_async_copy(
                     weights.at[target, pl.ds(start, size * cells), :],
-                    out.at[pl.ds(0, size * cells), :],
-                    sem.at[at],
+                    stage.at[pl.ds(0, size * cells), :],
+                    sem.at[0, at],
                 )
             )
-        return found + [pltpu.make_async_copy(fields, send, sem.at[len(pieces)])]
+        return found + [pltpu.make_async_copy(fields, stages[-1], sem.at[0, count - 1])]
 
     @pl.when(y == 0)
     def _():
-        for copy in copies(ocean_w, atmos):
+        for copy in loads(ocean_w, atmos):
             copy.start()
 
     @pl.when(y == 1)
     def _():
-        for copy in copies(atmos_w, ocean):
+        for copy in loads(atmos_w, ocean):
             copy.start()
 
     fraction = land[...]
     high = fraction.astype(jnp.bfloat16)
     low = (fraction - high.astype(jnp.float32)).astype(jnp.bfloat16)
-    done = copies(ocean_w, atmos)
-    for at, (out, (shift, first, size)) in enumerate(zip(outs, pieces)):
+    for stage, (shift, first, size) in zip(stages, pieces):
         if first:
             continue
-        target = lax.rem(me + shift, bands)
-        metas[at, pl.ds(0, tiles), :] = high
-        metas[at, pl.ds(tiles, tiles), :] = low
+        target, base = lax.rem(me + shift, bands), size * cells
+        stage[pl.ds(base, tiles), :] = high
+        stage[pl.ds(base + tiles, tiles), :] = low
         row = jnp.where(y == 0, ocean_ids[pl.ds(target, 1), :], atmos_ids[pl.ds(target, 1), :])
         row = jnp.broadcast_to(row.astype(jnp.float32), (16, cap)).astype(jnp.bfloat16)
-        metas[at, pl.ds(2 * tiles, 16), :] = jnp.zeros((16, cells), jnp.bfloat16)
-        metas[at, pl.ds(2 * tiles, 16), pl.ds(0, cap)] = row
-        copy = pltpu.make_async_copy(
-            metas.at[at],
-            out.at[pl.ds(size * cells, metas.shape[1]), :],
-            sem.at[len(pieces) + 1 + at],
-        )
-        copy.start()
-        done.append(copy)
-    for copy in done:
-        copy.wait()
+        stage[pl.ds(base + 2 * tiles, 16), :] = jnp.zeros((16, cells), jnp.bfloat16)
+        stage[pl.ds(base + 2 * tiles, 16), pl.ds(0, cap)] = row
+    stores = []
+    for at, load in enumerate(loads(ocean_w, atmos)):
+        load.wait()
+        stores.append(pltpu.make_async_copy(stages[at], outs[at], sem.at[1, at]))
+        stores[-1].start()
+    for store in stores:
+        store.wait()
 
 
 def pack(pieces, ocean, atmos, ocean_w, atmos_w, ocean_ids, atmos_ids, land):
     cells, tiles = land.shape[-1], land.shape[0]
     any_spec = pl.BlockSpec(memory_space=pl.ANY)
     vmem = pl.BlockSpec(memory_space=pltpu.VMEM)
-    meta = 2 * tiles + 16
-    sizes = [size * cells + (0 if first else meta) for _, first, size in pieces]
-    shapes = [ocean.shape] + [(n, cells) for n in sizes]
+    sizes = [size * cells + (0 if first else 2 * tiles + 16) for _, first, size in pieces]
+    shapes = [(n, cells) for n in sizes] + [ocean.shape]
     return pl.pallas_call(
         functools.partial(pack_kernel, pieces),
         out_shape=[jax.ShapeDtypeStruct(shape, jnp.bfloat16) for shape in shapes],
         in_specs=[any_spec] * 4 + [vmem] * 3,
         out_specs=[any_spec] * len(shapes),
-        scratch_shapes=[
-            pltpu.VMEM((len(pieces), meta, cells), jnp.bfloat16),
-            pltpu.SemaphoreType.DMA((2 * len(pieces) + 1,)),
-        ],
+        scratch_shapes=[pltpu.VMEM(shape, jnp.bfloat16) for shape in shapes]
+        + [pltpu.SemaphoreType.DMA((2, len(shapes)))],
         cost_estimate=pl.CostEstimate(flops=0, bytes_accessed=4 << 20, transcendentals=0),
         compiler_params=pltpu.CompilerParams(vmem_limit_bytes=60 << 20),
     )(ocean, atmos, ocean_w, atmos_w, ocean_ids, atmos_ids, land)
 
 
-def keep_kernel(ocean, atmos, ocean_w, atmos_w, keep, own, sem):
+def keep_kernel(ocean, atmos, ocean_w, atmos_w, keep, own, keep_stage, own_stage, sem):
     me, y = lax.axis_index("band"), lax.axis_index("grp")
 
-    def copies(fields, weights):
+    def loads(fields, weights):
         return [
-            pltpu.make_async_copy(fields, keep, sem.at[0]),
-            pltpu.make_async_copy(weights.at[me], own, sem.at[1]),
+            pltpu.make_async_copy(fields, keep_stage, sem.at[0, 0]),
+            pltpu.make_async_copy(weights.at[me], own_stage, sem.at[0, 1]),
         ]
 
     @pl.when(y == 0)
     def _():
-        for copy in copies(ocean, ocean_w):
+        for copy in loads(ocean, ocean_w):
             copy.start()
 
     @pl.when(y == 1)
     def _():
-        for copy in copies(atmos, atmos_w):
+        for copy in loads(atmos, atmos_w):
             copy.start()
 
-    for copy in copies(ocean, ocean_w):
-        copy.wait()
+    stores = [
+        pltpu.make_async_copy(keep_stage, keep, sem.at[1, 0]),
+        pltpu.make_async_copy(own_stage, own, sem.at[1, 1]),
+    ]
+    for load, store in zip(loads(ocean, ocean_w), stores):
+        load.wait()
+        store.start()
+    for store in stores:
+        store.wait()
 
 
 def keep_own(ocean, atmos, ocean_w, atmos_w):
@@ -133,7 +135,8 @@
         out_shape=[jax.ShapeDtypeStruct(shape, jnp.bfloat16) for shape in shapes],
         in_specs=[any_spec] * 4,
         out_specs=[any_spec] * 2,
-        scratch_shapes=[pltpu.SemaphoreType.DMA((2,))],
+        scratch_shapes=[pltpu.VMEM(shape, jnp.bfloat16) for shape in shapes]
+        + [pltpu.SemaphoreType.DMA((2, 2))],
         cost_estimate=pl.CostEstimate(flops=0, bytes_accessed=3 << 20, transcendentals=0),
         compiler_params=pltpu.CompilerParams(vmem_limit_bytes=60 << 20),
     )(ocean, atmos, ocean_w, atmos_w)
@@ -344,7 +347,7 @@
                 pieces += [(shift, 0, head), (shift, head, each - head)]
             else:
                 pieces.append((shift, 0, each))
-        send, *packed = pack(
+        *packed, send = pack(
             pieces, ocean_f, atmos_f, ocean_w, atmos_w, ocean_ids, atmos_ids, land
         )
         theirs = swap(send, "grp")

time: 151 us -> 68.3 us (0.45)
  Pallas kernels: 108 us -> 22.4 us
  starting transfers between devices: 12.9 us -> 19.4 us
  waiting for transfers between devices: 6.73 us -> 4.87 us
    pallas_call x1, Pallas kernels: 49.6 us -> 3.29 us  [pack(): pl.pallas_call(functools.partial(pack_kernel, pieces), out_shape=[jax.Sha...]
    pallas_call x1, Pallas kernels: 41.8 us -> 2.35 us  [keep_own(): pl.pallas_call(keep_kernel, out_shape=[jax.ShapeDtypeStruct(shape, jnp.bf...]
    ppermute x4, starting transfers between devices: 5.61 us -> 13.1 us  [per_device(): sent.append(lax.ppermute(piece, 'band', along(shift)))]
    ppermute x4, waiting for transfers between devices: 6.72 us -> 4.86 us  [per_device(): sent.append(lax.ppermute(piece, 'band', along(shift)))]
  transfers between devices with their start and end apart: 10 -> 10, of which waited for: 2 -> 2; matrix products, arithmetic and copies ran while one was open for 1% -> 1% of each run, Pallas kernels for 34% -> 18%
where the time goes in v6:
time: 68.3 us; the launch traced here: 67.8 us
  Pallas kernels  22.4 us (33%)
  starting transfers between devices  19.4 us (28%)
  blocking collectives  16.5 us (24%)
  waiting for transfers between devices  4.87 us (7%)
  local copies, waits for them, and re-layouts  3.3 us (5%)
  other arithmetic  0.97 us (1%)
    all_to_all x1, blocking collectives, per_device(): lax.all_to_all(sent, ('grp', 'band', 'var'), split_axis=0, concat_axis=0,...  16.5 us
    ppermute x4, starting transfers between devices, per_device(): sent.append(lax.ppermute(piece, 'band', along(shift)))  13.1 us
    pallas_call x7, Pallas kernels, regrid(): pl.pallas_call(functools.partial(regrid_kernel, groups, steps, meta_at, t...  9.72 us
    pallas_call x1, Pallas kernels, embed(): pl.pallas_call(functools.partial(embed_kernel, steps, halves), out_shape=...  7.07 us
    ppermute x6, starting transfers between devices, swap(): return lax.ppermute(x, axis, [(0, 1), (1, 0)])  6.36 us
    ppermute x4, waiting for transfers between devices, per_device(): sent.append(lax.ppermute(piece, 'band', along(shift)))  4.86 us
    pallas_call x1, Pallas kernels, pack(): pl.pallas_call(functools.partial(pack_kernel, pieces), out_shape=[jax.Sha...  3.29 us
    pallas_call x1, Pallas kernels, keep_own(): pl.pallas_call(keep_kernel, out_shape=[jax.ShapeDtypeStruct(shape, jnp.bf...  2.35 us
  transfers between devices with their start and end apart: 10, of which 2 were waited for; matrix products, arithmetic and copies ran while one was open for 1% of the time, Pallas kernels for 18%

profile of v6, /device:TPU:0, one launch (start us, length us, event | category | flops | bytes accessed | tf_op | source)
XLA Modules:
  0.0 67.8 jit_solution(11087748619310153675)
XLA Ops:
  0.0 3.3 %shard_map.118 = (bf16[944,128]{1,0:T(8,128)(2,1)}, bf16[944,128]{1,0:T(8,128)(2,1)}, bf16[560,128]{1,0:T(8,128)(2,1)}, bf16[384,128]{1,0:T(8,128)(2,1)}, bf16[36,96,128]{2,1,0:T(8,128)(2,1)}) custom-call(bf16[36,96,128]{2,1,0:T(8,128)(2,1)} %bitcast.32, bf16[36,96,128]{2,1,0:T(8,128)(2,1)} %bitcast.34, bf16[4,1792,128]{2,1,0:T(8,128)(2,1)} %bitcast.28, ...), custom_call_target="tpu_custom_call" | custom-call | bytes 4194304 | tf_op jit(solution)/shard_map/pallas_call | solution.py:88
  3.3 0.0 copy-start.6
  3.3 0.0 copy-start.7
  3.3 0.0 copy-start.4
  3.4 0.5 collective-permute-start.9
  3.9 2.6 %collective-permute-start = (bf16[944,128]{1,0:T(8,128)(2,1)}, bf16[944,128]{1,0:T(8,128)(2,1)S(1)}, u32[]{:S(2)}, u32[]{:S(2)}) collective-permute-start(bf16[944,128]{1,0:T(8,128)(2,1)} %get-tuple-element.24), channel_id=1, source_target_pairs={{0,4},{4,8},{8,12},{12,0},{1,5},{5,9},{9,13},{13,1},{2,6},{6,10},{... | collective-permute-start | bytes 725000 | tf_op jit(solution)/shard_map/ppermute | solution.py:370
  6.5 2.1 %collective-permute-start.4 = (bf16[944,128]{1,0:T(8,128)(2,1)}, bf16[944,128]{1,0:T(8,128)(2,1)S(1)}, u32[]{:S(2)}, u32[]{:S(2)}) collective-permute-start(bf16[944,128]{1,0:T(8,128)(2,1)} %get-tuple-element.31), channel_id=1, source_target_pairs={{0,12},{4,0},{8,4},{12,8},{1,13},{5,1},{9,5},{13,9},{2,14},{6,2},{... | collective-permute-start | bytes 725000 | tf_op jit(solution)/shard_map/ppermute | solution.py:370
  8.6 1.7 %collective-permute-start.2 = (bf16[36,96,128]{2,1,0:T(8,128)(2,1)}, bf16[36,96,128]{2,1,0:T(8,128)(2,1)S(1)}, u32[]{:S(2)}, u32[]{:S(2)}) collective-permute-start(bf16[36,96,128]{2,1,0:T(8,128)(2,1)} %get-tuple-element.27), channel_id=1, source_target_pairs={{0,16},{16,0},{1,17},{17,1},{2,18},{18,2},{3,19},{19,3},{4,20},{20... | collective-permute-start | bytes 2654216 | tf_op jit(solution)/shard_map/ppermute | solution.py:299
  10.3 0.2 convert_reduce_fusion.1
  10.5 0.1 select_reduce_fusion
  10.6 0.1 reshape.89
  10.7 0.1 add_add_fusion.where
  10.7 0.1 add_add_fusion.1.where
  10.8 0.1 fusion.1
  10.9 0.1 pad_add_fusion.4.where
  11.0 2.3 %shard_map.119 = (bf16[36,96,128]{2,1,0:T(8,128)(2,1)}, bf16[1792,128]{1,0:T(8,128)(2,1)}) custom-call(bf16[36,96,128]{2,1,0:T(8,128)(2,1)} %bitcast.33, bf16[36,96,128]{2,1,0:T(8,128)(2,1)} %bitcast.35, bf16[4,1792,128]{2,1,0:T(8,128)(2,1)} %bitcast.29, bf16[4,1792,128]{2,1,0:T(8,128)(2,1)} %bitcast.31), custom_call_target="tpu_custom_call" | custom-call | bytes 3145728 | tf_op jit(solution)/shard_map/pallas_call | solution.py:133
  13.4 0.1 reshape.97
  13.4 0.1 stack.70.where
  13.5 2.0 %collective-permute-done.refs_1_ = bf16[944,128]{1,0:T(8,128)(2,1)S(1)} collective-permute-done((bf16[944,128]{1,0:T(8,128)(2,1)}, bf16[944,128]{1,0:T(8,128)(2,1)S(1)}, u32[]{:S(2)}, u32[]{:S(2)}) %collective-permute-start) | collective-permute-done | bytes 241696 | tf_op jit(solution)/shard_map/ppermute | solution.py:370
  15.5 7.2 %collective-permute-start.1 = (bf16[560,128]{1,0:T(8,128)(2,1)S(1)}, bf16[560,128]{1,0:T(8,128)(2,1)S(1)}, u32[]{:S(2)}, u32[]{:S(2)}) collective-permute-start(bf16[560,128]{1,0:T(8,128)(2,1)S(1)} %copy-done.11), channel_id=1, source_target_pairs={{0,8},{4,12},{8,0},{12,4},{1,9},{5,13},{9,1},{13,5},{2,10},{6,14},... | collective-permute-start | bytes 430088 | tf_op jit(solution)/shard_map/ppermute | solution.py:370
  22.7 0.0 collective-permute-done.4.refs_1_
  22.7 1.5 %collective-permute-start.6 = (bf16[944,128]{1,0:T(8,128)(2,1)S(1)}, bf16[944,128]{1,0:T(8,128)(2,1)S(1)}, u32[]{:S(2)}, u32[]{:S(2)}) collective-permute-start(bf16[944,128]{1,0:T(8,128)(2,1)S(1)} %collective-permute-done.refs_1_), channel_id=1, source_target_pairs={{0,2},{2,0},{1,3},{3,1},{4,6},{6,4},{5,7},{7,5},{8,10},{10,8},{9,1... | collective-permute-start | bytes 725000 | tf_op jit(solution)/shard_map/ppermute | solution.py:299
  24.2 0.5 collective-permute-start.8
  24.7 2.9 %collective-permute-done.1.refs_2_ = bf16[560,128]{1,0:T(8,128)(2,1)S(1)} collective-permute-done((bf16[560,128]{1,0:T(8,128)(2,1)S(1)}, bf16[560,128]{1,0:T(8,128)(2,1)S(1)}, u32[]{:S(2)}, u32[]{:S(2)}) %collective-permute-start.1) | collective-permute-done | bytes 143392 | tf_op jit(solution)/shard_map/ppermute | solution.py:370
  27.6 1.2 %collective-permute-start.5 = (bf16[384,128]{1,0:T(8,128)(2,1)S(1)}, bf16[384,128]{1,0:T(8,128)(2,1)S(1)}, u32[]{:S(2)}, u32[]{:S(2)}) collective-permute-start(bf16[384,128]{1,0:T(8,128)(2,1)S(1)} %copy-done.12), channel_id=1, source_target_pairs={{0,8},{4,12},{8,0},{12,4},{1,9},{5,13},{9,1},{13,5},{2,10},{6,14},... | collective-permute-start | bytes 294920 | tf_op jit(solution)/shard_map/ppermute | solution.py:370
  28.9 1.2 %copy-done = bf16[36,96,128]{2,1,0:T(8,128)(2,1)S(1)} copy-done((bf16[36,96,128]{2,1,0:T(8,128)(2,1)S(1)}, bf16[36,96,128]{2,1,0:T(8,128)(2,1)}, u32[]{:S(2)}) %copy-start) | copy-done | bytes 884760
  30.0 1.0 %copy-done.2 = bf16[1792,128]{1,0:T(8,128)(2,1)S(1)} copy-done((bf16[1792,128]{1,0:T(8,128)(2,1)S(1)}, bf16[1792,128]{1,0:T(8,128)(2,1)}, u32[]{:S(2)}) %copy-start.2) | copy-done | bytes 458776
  31.0 1.3 %shard_map.120.refs_3_ = bf16[4,2,2,32,3072]{4,3,2,1,0:T(8,128)(2,1)S(1)} custom-call(s32[3,14]{1,0:T(4,128)S(1)} %pad_add_fusion.1.table, s32[2]{0:T(128)S(1)} %pad_add_fusion.4.where, bf16[36,96,128]{2,1,0:T(8,128)(2,1)S(1)} %copy-done, bf16[1792,128]{1,0:T(8,128)(2,1)S(1)} %copy-done.2, f32[16,128]{1,0:T(8,128)S(1)} %bitcast.26), custom_call_target="tpu_custom_call" | custom-call | flops 44040192 | bytes 4194304 | tf_op jit(solution)/shard_map/pallas_call | solution.py:206
  32.3 1.6 %collective-permute-start.3 = (bf16[560,128]{1,0:T(8,128)(2,1)S(1)}, bf16[560,128]{1,0:T(8,128)(2,1)S(1)}, u32[]{:S(2)}, u32[]{:S(2)}) collective-permute-start(bf16[560,128]{1,0:T(8,128)(2,1)S(1)} %collective-permute-done.1.refs_2_), channel_id=1, source_target_pairs={{0,2},{2,0},{1,3},{3,1},{4,6},{6,4},{5,7},{7,5},{8,10},{10,8},{9,1... | collective-permute-start | bytes 430088 | tf_op jit(solution)/shard_map/ppermute | solution.py:299
  33.9 1.3 %shard_map.121.refs_3_ = bf16[4,2,2,32,3072]{4,3,2,1,0:T(8,128)(2,1)S(1)} custom-call(s32[3,14]{1,0:T(4,128)S(1)} %pad_add_fusion.2.table, s32[3]{0:T(128)S(1)} %add_add_fusion.where, bf16[36,96,128]{2,1,0:T(8,128)(2,1)S(1)} %copy-done, bf16[944,128]{1,0:T(8,128)(2,1)S(1)} %collective-permute-done.refs_1_, ...), custom_call_target="tpu_custom_call", output_to_operand_aliasing={{}: (5, {})} | custom-call | flops 44040192 | bytes 4194304 | tf_op jit(solution)/shard_map/pallas_call | solution.py:206
  35.2 0.6 collective-permute-start.7
  35.9 1.3 %shard_map.122.refs_3_ = bf16[4,2,2,32,3072]{4,3,2,1,0:T(8,128)(2,1)S(1)} custom-call(s32[3,14]{1,0:T(4,128)S(1)} %pad_add_fusion.3.table, s32[3]{0:T(128)S(1)} %add_add_fusion.1.where, bf16[36,96,128]{2,1,0:T(8,128)(2,1)S(1)} %copy-done, bf16[944,128]{1,0:T(8,128)(2,1)S(1)} %collective-permute-done.4.refs_1_, ...), custom_call_target="tpu_custom_call", output_to_operand_aliasing={{}: (5, {})} | custom-call | flops 44040192 | bytes 4194304 | tf_op jit(solution)/shard_map/pallas_call | solution.py:206
  37.2 1.3 %shard_map.123.refs_3_ = bf16[4,2,2,32,3072]{4,3,2,1,0:T(8,128)(2,1)S(1)} custom-call(s32[3,14]{1,0:T(4,128)S(1)} %pad_add_fusion.1.table, s32[2]{0:T(128)S(1)} %pad_add_fusion.4.where, bf16[36,96,128]{2,1,0:T(8,128)(2,1)S(1)} %collective-permute-done.2.refs_0_.refs_1_, bf16[1792,128]{1,0:T(8,128)(2,1)S(1)} %copy-done.3, ...), custom_call_target="tpu_custom_call", output_to_operand_aliasing={{}: (5, {})} | custom-call | flops 44040192 | bytes 4194304 | tf_op jit(solution)/shard_map/pallas_call | solution.py:206
  38.5 1.3 %shard_map.124.refs_3_ = bf16[4,2,2,32,3072]{4,3,2,1,0:T(8,128)(2,1)S(1)} custom-call(s32[3,14]{1,0:T(4,128)S(1)} %pad_add_fusion.2.table, s32[3]{0:T(128)S(1)} %add_add_fusion.where, bf16[36,96,128]{2,1,0:T(8,128)(2,1)S(1)} %collective-permute-done.2.refs_0_.refs_1_, ...), custom_call_target="tpu_custom_call", output_to_operand_aliasing={{}: (5, {})} | custom-call | flops 44040192 | bytes 4194304 | tf_op jit(solution)/shard_map/pallas_call | solution.py:206
  39.8 0.0 slice-start
  39.8 1.3 %shard_map.125.refs_6_ = bf16[4,2,2,32,3072]{4,3,2,1,0:T(8,128)(2,1)S(1)} custom-call(s32[3,14]{1,0:T(4,128)S(1)} %pad_add_fusion.3.table, s32[3]{0:T(128)S(1)} %add_add_fusion.1.where, bf16[36,96,128]{2,1,0:T(8,128)(2,1)S(1)} %collective-permute-done.2.refs_0_.refs_1_, ...), custom_call_target="tpu_custom_call", output_to_operand_aliasing={{}: (5, {})} | custom-call | flops 44040192 | bytes 4194304 | tf_op jit(solution)/shard_map/pallas_call | solution.py:206
  41.1 0.0 slice-start.1
  41.2 1.9 %shard_map.126.rows_x = bf16[4,2,2,32,3072]{4,3,2,1,0:T(8,128)(2,1)S(1)} custom-call(s32[3,14]{1,0:T(4,128)S(1)} %pad_add_fusion.table, s32[5]{0:T(128)S(1)} %stack.70.where, bf16[36,96,128]{2,1,0:T(8,128)(2,1)S(1)} %copy-done.1, bf16[36,96,128]{2,1,0:T(8,128)(2,1)S(1)} %collective-permute-done.2.refs_0_.refs_1_, ...), custom_call_target="tpu_custom_call", output_to_operand_aliasing={{}: (8, {})} | custom-call | flops 88080384 | bytes 4194304 | tf_op jit(solution)/shard_map/pallas_call | solution.py:206
  43.1 0.0 copy-start.5
  43.1 0.0 copy-start.8
  43.1 0.0 slice-done.1
  43.2 7.1 %shard_map.127 = bf16[16,16,1024]{2,1,0:T(8,128)(2,1)S(1)} custom-call(bf16[4,2,2,32,3072]{4,3,2,1,0:T(8,128)(2,1)S(1)} %shard_map.126.rows_x, bf16[3072,1024]{1,0:T(8,128)(2,1)S(1)} %bitcast.24, bf16[3072,1024]{1,0:T(8,128)(2,1)} %collective-permute-done.9.theirs), custom_call_target="tpu_custom_call" | custom-call | flops 3221225472 | bytes 12582912 | tf_op jit(solution)/shard_map/pallas_call | solution.py:272
  50.2 16.5 %all_to_all.5 = bf16[16,16,1024]{2,1,0:T(8,128)(2,1)S(1)} all-to-all(bf16[16,16,1024]{2,1,0:T(8,128)(2,1)S(1)} %shard_map.127), channel_id=1, replica_groups=mesh['grp'=2,'band'=4,'var'=2,'sub'=2] {'grp','band','var'}, dimensions={0} | all-to-all | bytes 1048576 | tf_op jit(solution)/shard_map/all_to_all | solution.py:408
  66.8 0.1 convert_reduce_fusion
  66.9 0.1 multiply_reduce_fusion
  67.0 0.1 rsqrt.12
  67.1 0.1 fusion
  67.2 0.6 copy.21
  (42 shorter events, 0.2 us)
Async XLA Ops:
  0.0 10.3 %copy-start.9 = (s32[36,1]{0,1:T(1,128)S(1)}, s32[36,1]{0,1:T(1,128)}, u32[]{:S(2)}) copy-start(s32[36,1]{0,1:T(1,128)} %param.13) | copy-start | bytes 436
  0.0 10.3 %copy-start.10 = (s32[36,1]{0,1:T(1,128)S(1)}, s32[36,1]{0,1:T(1,128)}, u32[]{:S(2)}) copy-start(s32[36,1]{0,1:T(1,128)} %param.17) | copy-start | bytes 436
  3.3 10.2 %copy-start.6 = (s32[1,1,4,14]{3,2,1,0:T(4,128)S(1)}, s32[1,1,4,14]{3,2,1,0:T(4,128)}, u32[]{:S(2)}) copy-start(s32[1,1,4,14]{3,2,1,0:T(4,128)} %param.15) | copy-start | bytes 676
  3.3 10.2 %copy-start.7 = (s32[1,1,4,14]{3,2,1,0:T(4,128)S(1)}, s32[1,1,4,14]{3,2,1,0:T(4,128)}, u32[]{:S(2)}) copy-start(s32[1,1,4,14]{3,2,1,0:T(4,128)} %param.19) | copy-start | bytes 676
  3.3 12.2 %copy-start.11 = (bf16[560,128]{1,0:T(8,128)(2,1)S(1)}, bf16[560,128]{1,0:T(8,128)(2,1)}, u32[]{:S(2)}) copy-start(bf16[560,128]{1,0:T(8,128)(2,1)} %get-tuple-element.25) | copy-start | bytes 430084
  3.3 24.3 %copy-start.12 = (bf16[384,128]{1,0:T(8,128)(2,1)S(1)}, bf16[384,128]{1,0:T(8,128)(2,1)}, u32[]{:S(2)}) copy-start(bf16[384,128]{1,0:T(8,128)(2,1)} %get-tuple-element.32) | copy-start | bytes 294916
  3.3 25.5 %copy-start.4 = (f32[1,1,8,2,128]{4,3,2,1,0:T(2,128)S(1)}, f32[1,1,8,2,128]{4,3,2,1,0:T(2,128)}, u32[]{:S(2)}) copy-start(f32[1,1,8,2,128]{4,3,2,1,0:T(2,128)} %param.20) | copy-start | bytes 24580
  3.4 39.8 %collective-permute-start.9 = (bf16[3072,1024]{1,0:T(8,128)(2,1)}, bf16[3072,1024]{1,0:T(8,128)(2,1)}, u32[]{:S(2)}, u32[]{:S(2)}) collective-permute-start(bf16[3072,1024]{1,0:T(8,128)(2,1)} %mine.1), channel_id=1, source_target_pairs={{0,1},{1,0},{2,3},{3,2},{4,5},{5,4},{6,7},{7,6},{8,9},{9,8},{10,11... | collective-permute-start | bytes 18874376 | tf_op jit(solution)/shard_map/ppermute | solution.py:299
  3.9 11.6 %collective-permute-start = (bf16[944,128]{1,0:T(8,128)(2,1)}, bf16[944,128]{1,0:T(8,128)(2,1)S(1)}, u32[]{:S(2)}, u32[]{:S(2)}) collective-permute-start(bf16[944,128]{1,0:T(8,128)(2,1)} %get-tuple-element.24), channel_id=1, source_target_pairs={{0,4},{4,8},{8,12},{12,0},{1,5},{5,9},{9,13},{13,1},{2,6},{6,10},{... | collective-permute-start | bytes 725000 | tf_op jit(solution)/shard_map/ppermute | solution.py:370
  6.5 16.2 %collective-permute-start.4 = (bf16[944,128]{1,0:T(8,128)(2,1)}, bf16[944,128]{1,0:T(8,128)(2,1)S(1)}, u32[]{:S(2)}, u32[]{:S(2)}) collective-permute-start(bf16[944,128]{1,0:T(8,128)(2,1)} %get-tuple-element.31), channel_id=1, source_target_pairs={{0,12},{4,0},{8,4},{12,8},{1,13},{5,1},{9,5},{13,9},{2,14},{6,2},{... | collective-permute-start | bytes 725000 | tf_op jit(solution)/shard_map/ppermute | solution.py:370
  8.6 28.6 %collective-permute-start.2 = (bf16[36,96,128]{2,1,0:T(8,128)(2,1)}, bf16[36,96,128]{2,1,0:T(8,128)(2,1)S(1)}, u32[]{:S(2)}, u32[]{:S(2)}) collective-permute-start(bf16[36,96,128]{2,1,0:T(8,128)(2,1)} %get-tuple-element.27), channel_id=1, source_target_pairs={{0,16},{16,0},{1,17},{17,1},{2,18},{18,2},{3,19},{19,3},{4,20},{20... | collective-permute-start | bytes 2654216 | tf_op jit(solution)/shard_map/ppermute | solution.py:299
  15.5 12.1 %collective-permute-start.1 = (bf16[560,128]{1,0:T(8,128)(2,1)S(1)}, bf16[560,128]{1,0:T(8,128)(2,1)S(1)}, u32[]{:S(2)}, u32[]{:S(2)}) collective-permute-start(bf16[560,128]{1,0:T(8,128)(2,1)S(1)} %copy-done.11), channel_id=1, source_target_pairs={{0,8},{4,12},{8,0},{12,4},{1,9},{5,13},{9,1},{13,5},{2,10},{6,14},... | collective-permute-start | bytes 430088 | tf_op jit(solution)/shard_map/ppermute | solution.py:370
  22.7 9.7 %collective-permute-start.6 = (bf16[944,128]{1,0:T(8,128)(2,1)S(1)}, bf16[944,128]{1,0:T(8,128)(2,1)S(1)}, u32[]{:S(2)}, u32[]{:S(2)}) collective-permute-start(bf16[944,128]{1,0:T(8,128)(2,1)S(1)} %collective-permute-done.refs_1_), channel_id=1, source_target_pairs={{0,2},{2,0},{1,3},{3,1},{4,6},{6,4},{5,7},{7,5},{8,10},{10,8},{9,1... | collective-permute-start | bytes 725000 | tf_op jit(solution)/shard_map/ppermute | solution.py:299
  24.2 11.7 %collective-permute-start.8 = (bf16[944,128]{1,0:T(8,128)(2,1)S(1)}, bf16[944,128]{1,0:T(8,128)(2,1)S(1)}, u32[]{:S(2)}, u32[]{:S(2)}) collective-permute-start(bf16[944,128]{1,0:T(8,128)(2,1)S(1)} %collective-permute-done.4.refs_1_), channel_id=1, source_target_pairs={{0,2},{2,0},{1,3},{3,1},{4,6},{6,4},{5,7},{7,5},{8,10},{10,8},{9,1... | collective-permute-start | bytes 725000 | tf_op jit(solution)/shard_map/ppermute | solution.py:299
  27.6 7.6 %collective-permute-start.5 = (bf16[384,128]{1,0:T(8,128)(2,1)S(1)}, bf16[384,128]{1,0:T(8,128)(2,1)S(1)}, u32[]{:S(2)}, u32[]{:S(2)}) collective-permute-start(bf16[384,128]{1,0:T(8,128)(2,1)S(1)} %copy-done.12), channel_id=1, source_target_pairs={{0,8},{4,12},{8,0},{12,4},{1,9},{5,13},{9,1},{13,5},{2,10},{6,14},... | collective-permute-start | bytes 294920 | tf_op jit(solution)/shard_map/ppermute | solution.py:370
  28.8 1.2 %copy-start = (bf16[36,96,128]{2,1,0:T(8,128)(2,1)S(1)}, bf16[36,96,128]{2,1,0:T(8,128)(2,1)}, u32[]{:S(2)}) copy-start(bf16[36,96,128]{2,1,0:T(8,128)(2,1)} %get-tuple-element.26.refs_0_) | copy-start | bytes 2654212
  30.0 1.0 %copy-start.2 = (bf16[1792,128]{1,0:T(8,128)(2,1)S(1)}, bf16[1792,128]{1,0:T(8,128)(2,1)}, u32[]{:S(2)}) copy-start(bf16[1792,128]{1,0:T(8,128)(2,1)} %get-tuple-element.28.refs_1_) | copy-start | bytes 1376260
  32.3 8.8 %collective-permute-start.3 = (bf16[560,128]{1,0:T(8,128)(2,1)S(1)}, bf16[560,128]{1,0:T(8,128)(2,1)S(1)}, u32[]{:S(2)}, u32[]{:S(2)}) collective-permute-start(bf16[560,128]{1,0:T(8,128)(2,1)S(1)} %collective-permute-done.1.refs_2_), channel_id=1, source_target_pairs={{0,2},{2,0},{1,3},{3,1},{4,6},{6,4},{5,7},{7,5},{8,10},{10,8},{9,1... | collective-permute-start | bytes 430088 | tf_op jit(solution)/shard_map/ppermute | solution.py:299
  35.2 5.9 %collective-permute-start.7 = (bf16[384,128]{1,0:T(8,128)(2,1)S(1)}, bf16[384,128]{1,0:T(8,128)(2,1)S(1)}, u32[]{:S(2)}, u32[]{:S(2)}) collective-permute-start(bf16[384,128]{1,0:T(8,128)(2,1)S(1)} %collective-permute-done.5.refs_4_), channel_id=1, source_target_pairs={{0,2},{2,0},{1,3},{3,1},{4,6},{6,4},{5,7},{7,5},{8,10},{10,8},{9,1... | collective-permute-start | bytes 294920 | tf_op jit(solution)/shard_map/ppermute | solution.py:299
  35.8 1.3 %copy-start.3 = (bf16[1792,128]{1,0:T(8,128)(2,1)S(1)}, bf16[1792,128]{1,0:T(8,128)(2,1)}, u32[]{:S(2)}) copy-start(bf16[1792,128]{1,0:T(8,128)(2,1)} %get-tuple-element.28.refs_1_) | copy-start | bytes 1376260
  39.8 1.4 %copy-start.1 = (bf16[36,96,128]{2,1,0:T(8,128)(2,1)S(1)}, bf16[36,96,128]{2,1,0:T(8,128)(2,1)}, u32[]{:S(2)}) copy-start(bf16[36,96,128]{2,1,0:T(8,128)(2,1)} %get-tuple-element.26.refs_0_) | copy-start | bytes 2654212
  39.8 3.3 %slice-start = ((s8[6291456]{0:T(1024)(128)(4,1)}), s8[4194304]{0:T(1024)(128)(4,1)S(1)}, s32[]{:S(2)}) async-start(s8[6291456]{0:T(1024)(128)(4,1)} %bitcast.23), calls=%async_computation.1 | async-start | bytes 8388608
  41.1 2.0 %slice-start.1 = ((s8[6291456]{0:T(1024)(128)(4,1)}), s8[2097152]{0:T(1024)(128)(4,1)S(1)}, s32[]{:S(2)}) async-start(s8[6291456]{0:T(1024)(128)(4,1)} %bitcast.23), calls=%async_computation.2 | async-start | bytes 4194304
  43.1 23.8 %copy-start.5 = (f32[1024]{0:T(1024)S(1)}, f32[1024]{0:T(1024)}, u32[]{:S(2)}) copy-start(f32[1024]{0:T(1024)} %param.22) | copy-start | bytes 12292
  43.1 24.0 %copy-start.8 = (f32[1024]{0:T(1024)S(1)}, f32[1024]{0:T(1024)}, u32[]{:S(2)}) copy-start(f32[1024]{0:T(1024)} %param.23) | copy-start | bytes 12292

commit v7 on v4

v7 whole, which is shorter than its diff:
```python
import functools

import jax
import jax.numpy as jnp
from jax import lax
from jax.experimental import pallas as pl
from jax.experimental.pallas import tpu as pltpu
from jax.sharding import PartitionSpec as P

REPL = ("grp", "var")
PACK_LIMIT = 60 << 20


def slot_tables(dest, band_count, cap):
    count = dest.shape[0]
    serial = jnp.arange(count, dtype=jnp.int32)
    band_of = dest[:, 0]
    earlier = (band_of[:, None] == band_of[None, :]) & (serial[None, :] < serial[:, None])
    position = jnp.sum(earlier.astype(jnp.int32), axis=1)
    slot = band_of * cap + position
    hit = slot[None, :] == jnp.arange(band_count * cap, dtype=jnp.int32)[:, None]
    block = jnp.sum(jnp.where(hit, serial[None, :], 0), axis=1)
    used = jnp.any(hit, axis=1)
    return block.reshape(band_count, cap), used.reshape(band_count, cap)


def pack_kernel(pieces, moved, *refs):
    ocean_w, atmos_w, ocean_ids, atmos_ids, land = refs[:5]
    fields, refs = refs[5 : 5 + 2 * moved], refs[5 + 2 * moved :]
    count = len(pieces) + moved
    stages, sem = refs[:count], refs[-1]
    me, bands = lax.axis_index("band"), ocean_w.shape[0]
    x, y = lax.axis_index("var"), lax.axis_index("grp")
    cells, tiles = land.shape[-1], land.shape[0]
    cap = ocean_ids.shape[-1]

    def loads(weights, other):
        found = []
        for at, (stage, (shift, first, size, split)) in enumerate(zip(stages, pieces)):
            start = first if split is None else x * split + first
            found.append(
                pltpu.make_async_copy(
                    weights.at[
                        lax.rem(me + shift, bands),
                        pl.ds(pl.multiple_of(start * cells, cells), size * cells),
                        :,
                    ],
                    stage.at[pl.ds(0, size * cells), :],
                    sem.at[at],
                )
            )
        if moved:
            found.append(pltpu.make_async_copy(fields[other], stages[-1], sem.at[count - 1]))
        return found

    @pl.when(y == 0)
    def _():
        for copy in loads(ocean_w, 1):
            copy.start()

    @pl.when(y == 1)
    def _():
        for copy in loads(atmos_w, 0):
            copy.start()

    fraction = land[...]
    high = fraction.astype(jnp.bfloat16)
    low = (fraction - high.astype(jnp.float32)).astype(jnp.bfloat16)
    for stage, (shift, first, size, split) in zip(stages, pieces):
        if first:
            continue
        target, base = lax.rem(me + shift, bands), size * cells
        stage[pl.ds(base, tiles), :] = high
        stage[pl.ds(base + tiles, tiles), :] = low
        row = jnp.where(y == 0, ocean_ids[pl.ds(target, 1), :], atmos_ids[pl.ds(target, 1), :])
        row = jnp.broadcast_to(row.astype(jnp.float32), (16, cap)).astype(jnp.bfloat16)
        stage[pl.ds(base + 2 * tiles, 16), :] = jnp.zeros((16, cells), jnp.bfloat16)
        stage[pl.ds(base + 2 * tiles, 16), pl.ds(0, cap)] = row
    for load in loads(ocean_w, 1):
        load.wait()


def pack(pieces, ocean_w, atmos_w, ocean_ids, atmos_ids, land, *fields):
    cells, tiles = land.shape[-1], land.shape[0]
    any_spec = pl.BlockSpec(memory_space=pl.ANY)
    vmem = pl.BlockSpec(memory_space=pltpu.VMEM)
    sizes = [size * cells + (0 if first else 2 * tiles + 16) for _, first, size, _ in pieces]
    shapes = [(n, cells) for n in sizes] + [f.shape for f in fields[:1]]
    return pl.pallas_call(
        functools.partial(pack_kernel, pieces, len(fields) // 2),
        out_shape=[jax.ShapeDtypeStruct(shape, jnp.bfloat16) for shape in shapes],
        in_specs=[any_spec] * 2 + [vmem] * 3 + [any_spec] * len(fields),
        out_specs=[vmem] * len(shapes),
        scratch_shapes=[pltpu.SemaphoreType.DMA((len(shapes),))],
        cost_estimate=pl.CostEstimate(flops=0, bytes_accessed=2 << 20, transcendentals=0),
        compiler_params=pltpu.CompilerParams(vmem_limit_bytes=PACK_LIMIT),
    )(ocean_w, atmos_w, ocean_ids, atmos_ids, land, *fields)


def regrid_kernel(steps, jobs, count, *refs):
    out, acc, scale = refs[-3:]
    local_rows, cells = acc.shape[1] // (scale.shape[0] // 2 - 4), acc.shape[2]
    tiles = acc.shape[1] // local_rows
    local_vars = local_rows // steps
    half_vars = local_vars // 2
    for table, where, meta, meta_at, parts, groups in jobs:
        table, where, meta = refs[table], refs[where], refs[meta]
        if meta.dtype == jnp.float32:
            land = meta[...]
        else:
            high = meta[pl.ds(meta_at, tiles), :].astype(jnp.float32)
            land = high + meta[pl.ds(meta_at + tiles, tiles), :].astype(jnp.float32)
        scale[pl.ds(0, tiles), :] = 1.0 - land
        scale[pl.ds(tiles, tiles), :] = land
        scale[pl.ds(2 * tiles, 8), :] = jnp.zeros((8, cells), jnp.float32)
        acc[pl.ds(0, len(groups))] = jnp.zeros((len(groups),) + acc.shape[1:], jnp.float32)
        for at, (part, size) in enumerate(parts):
            first = where[1 + at]
            for s in range(size):
                slot = first + s
                block = table[0, slot]
                moved = []
                for _, fields in groups:
                    piece = refs[fields[0]][block]
                    if len(fields) > 1:
                        piece = jnp.where(
                            lax.axis_index("grp") == 0, piece, refs[fields[1]][block]
                        )
                    moved.append(piece)
                moved = moved[0] if len(moved) == 1 else jnp.concatenate(moved, axis=0)
                dense = jnp.dot(
                    moved,
                    refs[part][pl.ds(s * cells, cells), :],
                    preferred_element_type=jnp.float32,
                )
                dense = dense * scale[pl.ds(table[2, slot], 1), :]
                span = pl.ds(pl.multiple_of(table[1, slot] * local_rows, local_rows), local_rows)
                for g in range(len(groups)):
                    acc[g, span, :] += dense[g * local_rows : (g + 1) * local_rows]
        for g, (to, _) in enumerate(groups):
            for v in range(local_vars):
                for q in range(2):
                    column = (v % half_vars * 2 + q) * cells
                    rows = [
                        acc[g, pl.ds(q * local_rows + t * local_vars + v, tiles // 2, 2 * local_rows), :]
                        for t in range(steps)
                    ]
                    out[where[0], to, v // half_vars, :, pl.ds(column, cells)] = jnp.concatenate(
                        rows, axis=0
                    ).astype(out.dtype)


def regrid(jobs, previous, bands, groups, steps, tiles, rows, cells):
    operands, specs, places = [], [], {}

    def place(array, space):
        if id(array) not in places:
            places[id(array)] = len(operands)
            operands.append(array)
            specs.append(pl.BlockSpec(memory_space=space))
        return places[id(array)]

    listed, flops, most = [], 0, 1
    for table, where, meta, meta_at, parts, sizes, fields in jobs:
        listed.append(
            (
                place(table, pltpu.SMEM),
                place(where, pltpu.SMEM),
                place(meta, pltpu.VMEM),
                meta_at,
                [(place(part, pltpu.VMEM), size) for part, size in zip(parts, sizes)],
                [(to, [place(f, pltpu.VMEM) for f in pair]) for to, pair in fields],
            )
        )
        flops += 2 * sum(sizes) * len(fields) * rows * cells * cells
        most = max(most, len(fields))
    aliases = {}
    if previous is not None:
        aliases = {len(operands): 0}
        operands.append(previous)
        specs.append(pl.BlockSpec(memory_space=pltpu.VMEM))
    shape = (bands, groups, 2, steps * tiles // 2, rows // steps // 2 * 2 * cells)
    return pl.pallas_call(
        functools.partial(regrid_kernel, steps, listed, len(operands)),
        out_shape=jax.ShapeDtypeStruct(shape, jnp.bfloat16),
        in_specs=specs,
        out_specs=pl.BlockSpec(memory_space=pltpu.VMEM),
        scratch_shapes=[
            pltpu.VMEM((most, tiles * rows, cells), jnp.float32),
            pltpu.VMEM((2 * tiles + 8, cells), jnp.float32),
        ],
        input_output_aliases=aliases,
        cost_estimate=pl.CostEstimate(
            flops=flops, bytes_accessed=len(jobs) * 3 << 20, transcendentals=0
        ),
        compiler_params=pltpu.CompilerParams(vmem_limit_bytes=28 << 20),
    )(*operands)


def embed_kernel(steps, halves, rows_x, mine, theirs, out, total):
    at = pl.program_id(0)
    sub, mine_group = lax.axis_index("sub"), lax.axis_index("grp")
    bands, groups, _, row_count, width = rows_x.shape
    rows = bands * groups * row_count

    @pl.when(at == 0)
    def _():
        total[...] = jnp.zeros_like(total)

    left = rows_x[:, :, sub].reshape(rows, width)
    right = rows_x[:, :, 1 - sub].reshape(rows, width)
    total[...] += jnp.dot(left, mine[...], preferred_element_type=jnp.float32) + jnp.dot(
        right, theirs[...], preferred_element_type=jnp.float32
    )

    @pl.when(at == pl.num_programs(0) - 1)
    def _():
        if out.ndim == 2:
            out[...] = total[...].astype(out.dtype)
        else:
            count = steps * halves
            share = row_count // count
            for g in range(groups):
                base = (mine_group if g == 0 else 1 - mine_group) * count if groups > 1 else 0
                for chunk in range(count):
                    pieces = [
                        total[pl.ds((b * groups + g) * row_count + chunk * share, share), :]
                        for b in range(bands)
                    ]
                    out[base + chunk] = jnp.concatenate(pieces, axis=0).astype(out.dtype)


def embed(rows_x, mine, theirs, steps, halves):
    bands, groups, _, row_count, half_width = rows_x.shape
    width = mine.shape[-1]
    grid = 6 if half_width % (6 * 256) == 0 else 3
    step_rows = half_width // grid
    rows = bands * groups * row_count
    chunks = groups * steps * halves
    share = row_count // (steps * halves)
    shape = (chunks, bands * share, width) if share % 4 == 0 else (rows, width)
    weight_spec = pl.BlockSpec((step_rows, width), lambda i: (i, 0))
    out = pl.pallas_call(
        functools.partial(embed_kernel, steps, halves),
        out_shape=jax.ShapeDtypeStruct(shape, jnp.bfloat16),
        grid=(grid,),
        in_specs=[
            pl.BlockSpec((bands, groups, 2, row_count, step_rows), lambda i: (0, 0, 0, 0, i)),
            weight_spec,
            weight_spec,
        ],
        out_specs=pl.BlockSpec(shape, lambda i: (0,) * len(shape)),
        scratch_shapes=[pltpu.VMEM((rows, width), jnp.float32)],
        cost_estimate=pl.CostEstimate(
            flops=4 * rows * mine.shape[0] * width,
            bytes_accessed=4 * mine.shape[0] * width,
            transcendentals=0,
        ),
        compiler_params=pltpu.CompilerParams(
            vmem_limit_bytes=(48 if rows > 1024 else 16) << 20
        ),
    )(rows_x, mine, theirs)
    if share % 4:
        out = out.reshape(bands, chunks, share, width).transpose(1, 0, 2, 3)
        out = out.reshape(chunks, bands * share, width)
    return out


def swap(x, axis):
    return lax.ppermute(x, axis, [(0, 1), (1, 0)])


def per_device(
    ocean_fields,
    ocean_dest,
    ocean_weights,
    ocean_tiles,
    atmos_fields,
    atmos_dest,
    atmos_weights,
    atmos_tiles,
    land_fraction,
    embed_weight,
    embed_bias,
    embed_gain,
):
    nb = lax.axis_size("band")
    nv = lax.axis_size("var")
    ng = lax.axis_size("grp")
    rep = nv * ng
    cap = ocean_weights.shape[3]
    cells = ocean_weights.shape[-1]
    block_count, steps, local_vars, _ = ocean_fields.shape
    patches = land_fraction.shape[2]
    tiles = 2 * patches
    slots = 2 * cap
    share = patches // nv
    me = lax.axis_index("band")
    x, y = lax.axis_index("var"), lax.axis_index("grp")
    quarter = y * nv + x

    flat = (nb, cap * cells, cells)
    ocean_w, atmos_w = ocean_weights.reshape(flat), atmos_weights.reshape(flat)
    ocean_ids, atmos_ids = ocean_tiles.reshape(nb, cap), atmos_tiles.reshape(nb, cap)
    land = land_fraction.reshape(tiles, cells)
    blocks = (block_count, steps * local_vars, cells)
    ocean_f, atmos_f = ocean_fields.reshape(blocks), atmos_fields.reshape(blocks)
    order = ([1, nb - 1] + list(range(2, nb - 1)))[: nb - 1]
    along = lambda shift: [(b, (b + shift) % nb) for b in range(nb)]
    call = functools.partial(
        regrid, bands=nb, steps=steps, tiles=tiles, rows=steps * local_vars, cells=cells
    )

    if ng == 2 and nv == 2 and cap % 2 == 0:
        each = cap // 2
        pieces = []
        for shift in order:
            pieces.append((shift, 0, each, each))
        *packed, own_w, send = pack(
            pieces + [(0, 0, cap, None)], ocean_w, atmos_w, ocean_ids, atmos_ids, land, ocean_f, atmos_f
        )
        sent = [
            lax.ppermute(piece, "band", along(shift))
            for piece, (shift, _, _, _) in zip(packed, pieces)
        ]
        embed_other, send = lax.optimization_barrier((embed_weight, send))
        embed_other = swap(embed_other, "sub")
        keep, theirs = (ocean_f, atmos_f), (swap(send, "grp"),)
        dest = jnp.where(y == 0, ocean_dest, atmos_dest)
        block_all, used_all = slot_tables(dest, nb, cap)

        def job_of(band, parts, sizes, firsts, fields):
            meta_at = sizes[0] * cells
            tile = parts[0][meta_at + 2 * tiles, :cap].astype(jnp.int32)
            block = lax.dynamic_index_in_dim(block_all, band, 0, keepdims=False)
            used = lax.dynamic_index_in_dim(used_all, band, 0, keepdims=False)
            scale = jnp.where(used, tile + y * tiles, 2 * tiles)
            table = jnp.stack([block, tile, scale]).astype(jnp.int32)
            where = jnp.stack([band] + firsts).astype(jnp.int32)
            return table, where, parts[0], meta_at, parts, sizes, fields

        def with_fields(job, fields):
            return job[:-1] + (fields,)

        def job_at(shift, fields):
            parts, sizes, firsts = [], [], []
            for piece, across, (of, first, size, _) in zip(sent, crossed, pieces):
                if of == shift:
                    parts += [piece, across]
                    sizes += [size, size]
                    firsts += [x * each + first, (1 - x) * each + first]
            return job_of((me - shift) % nb, parts, sizes, firsts, fields)

        ours, others = [(0, keep)], [(1, theirs)]
        own_w, sent[0] = lax.optimization_barrier((own_w, sent[0]))
        jobs = [job_of(me, [own_w], [cap], [jnp.int32(0)], ours)]
        rows_x = call(jobs[:1], None, groups=2)
        crossed = [swap(sent[0], "var")]
        for at in range(1, len(sent)):
            if at > 1:
                jobs.append(job_at(order[at - 2], ours))
                rows_x = call(jobs[-1:], rows_x, groups=2)
            sent[at], rows_x = lax.optimization_barrier((sent[at], rows_x))
            crossed.append(swap(sent[at], "var"))
        done = len(jobs)
        jobs += [job_at(shift, ours) for shift in order[done - 1 :]]
        rows_x = call(
            jobs[done:-1] + [with_fields(job, others) for job in jobs[:-1]], rows_x, groups=2
        )
        rows_x = call([with_fields(jobs[-1], ours + others)], rows_x, groups=2)
        sent = embed(rows_x, embed_weight, embed_other, steps, nv)
        got = lax.all_to_all(sent, ("grp", "band", "var"), split_axis=0, concat_axis=0, tiled=True)
    else:
        embed_other = swap(embed_weight, "sub")
        both = jnp.concatenate([ocean_w, atmos_w], axis=1)
        fields = [(0, (jnp.concatenate([ocean_f, atmos_f], axis=0),))]
        ocean_block, ocean_used = slot_tables(ocean_dest, nb, cap)
        atmos_block, atmos_used = slot_tables(atmos_dest, nb, cap)
        block_all = jnp.concatenate([ocean_block, atmos_block + block_count], axis=1)
        used_all = jnp.concatenate([ocean_used, atmos_used], axis=1)
        grid_row = jnp.where(jnp.arange(slots) < cap, 0, tiles)

        def job_of(band, tile, meta, parts):
            block = lax.dynamic_index_in_dim(block_all, band, 0, keepdims=False)
            used = lax.dynamic_index_in_dim(used_all, band, 0, keepdims=False)
            scale = jnp.where(used, tile + grid_row, 2 * tiles)
            table = jnp.stack([block, tile, scale]).astype(jnp.int32)
            where = jnp.stack([band, jnp.int32(0)])
            return table, where, meta, 0, [parts], [slots], fields

        tile_ids = jnp.concatenate([ocean_ids, atmos_ids], axis=1)
        own_tile = lax.dynamic_index_in_dim(tile_ids, me, 0, keepdims=False)
        own_w = lax.dynamic_index_in_dim(both, me, 0, keepdims=False)
        rows_x = call([job_of(me, own_tile, land, own_w)], None, groups=1)
        share_rows = slots * cells // rep
        high = lax.reduce_precision(land, 8, 7)
        low = (land - high).astype(jnp.bfloat16)
        tile_rows = jnp.pad(tile_ids.astype(jnp.bfloat16), ((0, 0), (0, cells - slots)))
        for shift in order:
            target, band = (me + shift) % nb, (me - shift) % nb
            piece = lax.dynamic_slice(
                both, (target, quarter * share_rows, 0), (1, share_rows, cells)
            )[0]
            row = lax.dynamic_slice(tile_rows, (target, 0), (1, cells))
            row = jnp.broadcast_to(row, (16, cells))
            piece = jnp.concatenate([piece, high.astype(jnp.bfloat16), low, row], axis=0)
            parts = lax.all_gather(lax.ppermute(piece, "band", along(shift)), REPL, axis=0)
            meta = parts[0, share_rows:]
            tile = meta[2 * tiles, :slots].astype(jnp.int32)
            parts = parts[:, :share_rows].reshape(slots * cells, cells)
            rows_x = call([job_of(band, tile, meta, parts)], rows_x, groups=1)
        sent = embed(rows_x, embed_weight, embed_other, steps, nv)
        got = lax.all_to_all(sent, ("band", "var"), split_axis=0, concat_axis=0, tiled=True)
    shifted = jnp.sum(got.astype(jnp.float32), axis=0) + embed_bias
    inverse = lax.rsqrt(jnp.mean(shifted * shifted, axis=-1, keepdims=True) + 1e-05)
    finished = (shifted * inverse * embed_gain).astype(jnp.bfloat16)
    width = finished.shape[-1]
    finished = finished.reshape(nb, share, steps // nb, width).transpose(1, 0, 2, 3)
    return finished[None]


def solution(mesh):
    in_specs = (
        P(("grp", "band", "sub"), None, "var", None),
        P(("band", "sub"), None),
        P("band", "sub", None, None, None, None),
        P("band", "sub", None, None),
        P(("grp", "band", "sub"), None, "var", None),
        P(("band", "sub"), None),
        P("band", "sub", None, None, None, None),
        P("band", "sub", None, None),
        P("band", "sub", None, None, None),
        P(("var", "sub"), None),
        P(),
        P(),
    )
    out_specs = P("sub", "var", None, ("grp", "band"), None)
    return jax.shard_map(
        per_device, mesh=mesh, in_specs=in_specs, out_specs=out_specs, check_vma=False
    )
```

time: 71.2 us -> 79.4 us (1.12)
  blocking collectives: 15.5 us -> 29.7 us
  starting transfers between devices: 20 us -> 14 us
  other arithmetic: 0.97 us -> 2.38 us
  local copies, waits for them, and re-layouts: 3.24 us -> 1.98 us
    all_to_all x1, blocking collectives: 15.5 us -> 29.7 us  [per_device(): lax.all_to_all(sent, ('grp', 'band', 'var'), split_axis=0, concat_axis=0,...]
    ppermute x4 -> x3, starting transfers between devices: 13.6 us -> 7.49 us  [per_device(): lax.ppermute(piece, 'band', along(shift))]
    ppermute x4 -> x3, waiting for transfers between devices: 11.8 us -> 7.31 us  [per_device(): lax.ppermute(piece, 'band', along(shift))]
    ppermute x6 -> x5, waiting for transfers between devices: 0.02 us -> 4.45 us  [swap(): return lax.ppermute(x, axis, [(0, 1), (1, 0)])]
    unnamed x24 -> x20, local copies, waits for them, and re-layouts: 2.23 us -> 1.06 us
    ppermute x6 -> x5, starting transfers between devices: 6.39 us -> 6.52 us  [swap(): return lax.ppermute(x, axis, [(0, 1), (1, 0)])]
  transfers between devices with their start and end apart: 10 -> 8, of which waited for: 3 -> 3; matrix products, arithmetic and copies ran while one was open for 1% -> 3% of each run, Pallas kernels for 17% -> 10%
where the time goes in v7:
time: 79.4 us; the launch traced here: 79.1 us
  blocking collectives  29.7 us (37%)
  Pallas kernels  19 us (24%)
  starting transfers between devices  14 us (18%)
  waiting for transfers between devices  11.8 us (15%)
  other arithmetic  2.38 us (3%)
  local copies, waits for them, and re-layouts  1.98 us (2%)
    all_to_all x1, blocking collectives, per_device(): lax.all_to_all(sent, ('grp', 'band', 'var'), split_axis=0, concat_axis=0,...  29.7 us
    pallas_call x4, Pallas kernels, regrid(): pl.pallas_call(functools.partial(regrid_kernel, steps, listed, len(operan...  7.83 us
    ppermute x3, starting transfers between devices, per_device(): lax.ppermute(piece, 'band', along(shift))  7.49 us
    ppermute x3, waiting for transfers between devices, per_device(): lax.ppermute(piece, 'band', along(shift))  7.31 us
    pallas_call x1, Pallas kernels, embed(): pl.pallas_call(functools.partial(embed_kernel, steps, halves), out_shape=...  7.22 us
    ppermute x5, starting transfers between devices, swap(): return lax.ppermute(x, axis, [(0, 1), (1, 0)])  6.52 us
    ppermute x5, waiting for transfers between devices, swap(): return lax.ppermute(x, axis, [(0, 1), (1, 0)])  4.45 us
    pallas_call x1, Pallas kernels, pack(): pl.pallas_call(functools.partial(pack_kernel, pieces, len(fields) // 2),...  3.91 us
  transfers between devices with their start and end apart: 8, of which 3 were waited for; matrix products, arithmetic and copies ran while one was open for 3% of the time, Pallas kernels for 10%

profile of v7, /device:TPU:0, one launch (start us, length us, event | category | flops | bytes accessed | tf_op | source)
XLA Modules:
  0.0 79.1 jit_solution(12022450341442395723)
XLA Ops:
  0.0 3.9 %shard_map.118 = (bf16[944,128]{1,0:T(8,128)(2,1)}, bf16[944,128]{1,0:T(8,128)(2,1)}, bf16[944,128]{1,0:T(8,128)(2,1)}, bf16[1840,128]{1,0:T(8,128)(2,1)}, bf16[36,96,128]{2,1,0:T(8,128)(2,1)}) custom-call(bf16[4,1792,128]{2,1,0:T(8,128)(2,1)} %bitcast.31, bf16[4,1792,128]{2,1,0:T(8,128)(2,1)} %bitcast.32, s32[4,14]{1,0:T(4,128)} %bitcast.34, ...), custom_call_target="tpu_custom_call" | custom-call | bytes 2097152 | tf_op jit(solution)/shard_map/pallas_call | solution.py:89
  3.9 0.5 collective-permute-start.7
  4.5 3.7 %collective-permute-start = (bf16[944,128]{1,0:T(8,128)(2,1)}, bf16[944,128]{1,0:T(8,128)(2,1)S(1)}, u32[]{:S(2)}, u32[]{:S(2)}) collective-permute-start(bf16[944,128]{1,0:T(8,128)(2,1)} %get-tuple-element.18), channel_id=1, source_target_pairs={{0,8},{4,12},{8,0},{12,4},{1,9},{5,13},{9,1},{13,5},{2,10},{6,14},... | collective-permute-start | bytes 725000 | tf_op jit(solution)/shard_map/ppermute | solution.py:323
  8.1 1.6 %collective-permute-start.1 = (bf16[944,128]{1,0:T(8,128)(2,1)}, bf16[944,128]{1,0:T(8,128)(2,1)S(1)}, u32[]{:S(2)}, u32[]{:S(2)}) collective-permute-start(bf16[944,128]{1,0:T(8,128)(2,1)} %get-tuple-element.20), channel_id=1, source_target_pairs={{0,4},{4,8},{8,12},{12,0},{1,5},{5,9},{9,13},{13,1},{2,6},{6,10},{... | collective-permute-start | bytes 725000 | tf_op jit(solution)/shard_map/ppermute | solution.py:323
  9.7 2.2 %collective-permute-start.3 = (bf16[944,128]{1,0:T(8,128)(2,1)}, bf16[944,128]{1,0:T(8,128)(2,1)S(1)}, u32[]{:S(2)}, u32[]{:S(2)}) collective-permute-start(bf16[944,128]{1,0:T(8,128)(2,1)} %get-tuple-element.22), channel_id=1, source_target_pairs={{0,12},{4,0},{8,4},{12,8},{1,13},{5,1},{9,5},{13,9},{2,14},{6,2},{... | collective-permute-start | bytes 725000 | tf_op jit(solution)/shard_map/ppermute | solution.py:323
  12.0 1.5 %collective-permute-start.5 = (bf16[36,96,128]{2,1,0:T(8,128)(2,1)}, bf16[36,96,128]{2,1,0:T(8,128)(2,1)S(1)}, u32[]{:S(2)}, u32[]{:S(2)}) collective-permute-start(bf16[36,96,128]{2,1,0:T(8,128)(2,1)} %get-tuple-element.27), channel_id=1, source_target_pairs={{0,16},{16,0},{1,17},{17,1},{2,18},{18,2},{3,19},{19,3},{4,20},{20... | collective-permute-start | bytes 2654216 | tf_op jit(solution)/shard_map/ppermute | solution.py:270
  13.5 0.1 add_add_fusion.refs_1_.refs_11_
  13.5 0.1 add_add_fusion.1.refs_1_
  13.6 0.0 copy-done.7
  13.6 0.0 copy-done.6
  13.6 0.2 convert_reduce_fusion.1
  13.8 0.1 fusion.1
  13.9 0.1 select_reduce_fusion
  14.0 0.1 add_add_fusion.2.refs_1_
  14.1 0.1 reshape.97
  14.2 0.1 reshape.89
  14.3 0.1 pad_add_fusion.4.refs_1_.refs_7_
  14.4 7.3 %collective-permute-done.1.refs_2_.refs_12_ = bf16[944,128]{1,0:T(8,128)(2,1)S(1)} collective-permute-done((bf16[944,128]{1,0:T(8,128)(2,1)}, bf16[944,128]{1,0:T(8,128)(2,1)S(1)}, u32[]{:S(2)}, u32[]{:S(2)}) %collective-permute-start.1) | collective-permute-done | bytes 241696 | tf_op jit(solution)/shard_map/ppermute | solution.py:323
  21.7 1.5 %collective-permute-start.2 = (bf16[944,128]{1,0:T(8,128)(2,1)S(1)}, bf16[944,128]{1,0:T(8,128)(2,1)S(1)}, u32[]{:S(2)}, u32[]{:S(2)}) collective-permute-start(bf16[944,128]{1,0:T(8,128)(2,1)S(1)} %collective-permute-done.1.refs_2_.refs_12_), channel_id=1, source_target_pairs={{0,2},{2,0},{1,3},{3,1},{4,6},{6,4},{5,7},{7,5},{8,10},{10,8},{9,1... | collective-permute-start | bytes 725000 | tf_op jit(solution)/shard_map/ppermute | solution.py:270
  23.2 0.7 fusion.4
  23.8 0.7 slice_convert_fusion.2
  24.5 0.0 copy-done
  24.5 0.0 copy-start.2
  24.5 1.0 %copy-done.2 = bf16[1840,128]{1,0:T(8,128)(2,1)S(1)} copy-done((bf16[1840,128]{1,0:T(8,128)(2,1)S(1)}, bf16[1840,128]{1,0:T(8,128)(2,1)}, u32[]{:S(2)}) %copy-start.2) | copy-done | bytes 471064
  25.5 1.3 %shard_map.119.refs_6_ = bf16[4,2,2,32,3072]{4,3,2,1,0:T(8,128)(2,1)S(1)} custom-call(s32[3,14]{1,0:T(4,128)S(1)} %pad_add_fusion.1.refs_0_.refs_6_, s32[2]{0:T(128)S(1)} %pad_add_fusion.4.refs_1_.refs_7_, bf16[1840,128]{1,0:T(8,128)(2,1)S(1)} %copy-done.2, bf16[36,96,128]{2,1,0:T(8,128)(2,1)S(1)} %bitcast.20, bf16[36,96,128]{2,1,0:T(8,128)(2,1)S(1)} %bitcast.25), custom_call_target="tpu_custom_call" | custom-call | flops 44040192 | bytes 3145728 | tf_op jit(solution)/shard_map/pallas_call | solution.py:183
  26.9 0.0 collective-permute-done.3.refs_2_
  26.9 1.4 %collective-permute-start.6 = (bf16[944,128]{1,0:T(8,128)(2,1)S(1)}, bf16[944,128]{1,0:T(8,128)(2,1)S(1)}, u32[]{:S(2)}, u32[]{:S(2)}) collective-permute-start(bf16[944,128]{1,0:T(8,128)(2,1)S(1)} %collective-permute-done.3.refs_2_), channel_id=1, source_target_pairs={{0,2},{2,0},{1,3},{3,1},{4,6},{6,4},{5,7},{7,5},{8,10},{10,8},{9,1... | collective-permute-start | bytes 725000 | tf_op jit(solution)/shard_map/ppermute | solution.py:270
  28.3 0.0 copy-start.3
  28.3 0.3 collective-permute-done.2.refs_3_.refs_13_
  28.7 1.3 %shard_map.120.refs_14_ = bf16[4,2,2,32,3072]{4,3,2,1,0:T(8,128)(2,1)S(1)} custom-call(s32[3,14]{1,0:T(4,128)S(1)} %pad_add_fusion.refs_0_.refs_10_, s32[3]{0:T(128)S(1)} %add_add_fusion.refs_1_.refs_11_, bf16[944,128]{1,0:T(8,128)(2,1)S(1)} %collective-permute-done.1.refs_2_.refs_12_, ...), custom_call_target="tpu_custom_call", output_to_operand_aliasing={{}: (6, {})} | custom-call | flops 44040192 | bytes 3145728 | tf_op jit(solution)/shard_map/pallas_call | solution.py:183
  30.0 0.0 collective-permute-done.refs_2_
  30.0 1.6 %collective-permute-start.4 = (bf16[944,128]{1,0:T(8,128)(2,1)S(1)}, bf16[944,128]{1,0:T(8,128)(2,1)S(1)}, u32[]{:S(2)}, u32[]{:S(2)}) collective-permute-start(bf16[944,128]{1,0:T(8,128)(2,1)S(1)} %collective-permute-done.refs_2_), channel_id=1, source_target_pairs={{0,2},{2,0},{1,3},{3,1},{4,6},{6,4},{5,7},{7,5},{8,10},{10,8},{9,1... | collective-permute-start | bytes 725000 | tf_op jit(solution)/shard_map/ppermute | solution.py:270
  31.6 0.0 slice-start.1
  31.6 4.1 %collective-permute-done.6.refs_3_ = bf16[944,128]{1,0:T(8,128)(2,1)S(1)} collective-permute-done((bf16[944,128]{1,0:T(8,128)(2,1)S(1)}, bf16[944,128]{1,0:T(8,128)(2,1)S(1)}, u32[]{:S(2)}, u32[]{:S(2)}) %collective-permute-start.6) | collective-permute-done | bytes 241696 | tf_op jit(solution)/shard_map/ppermute | solution.py:270
  35.8 0.0 collective-permute-done.5.refs_9_.refs_6_
  35.8 3.3 %shard_map.121.refs_7_ = bf16[4,2,2,32,3072]{4,3,2,1,0:T(8,128)(2,1)S(1)} custom-call(s32[3,14]{1,0:T(4,128)S(1)} %pad_add_fusion.3.refs_0_, s32[3]{0:T(128)S(1)} %add_add_fusion.2.refs_1_, bf16[944,128]{1,0:T(8,128)(2,1)S(1)} %collective-permute-done.3.refs_2_, ...), custom_call_target="tpu_custom_call", output_to_operand_aliasing={{}: (14, {})} | custom-call | flops 176160768 | bytes 12582912 | tf_op jit(solution)/shard_map/pallas_call | solution.py:183
  39.0 0.0 collective-permute-done.4.refs_3_
  39.0 1.9 %shard_map.122.rows_x = bf16[4,2,2,32,3072]{4,3,2,1,0:T(8,128)(2,1)S(1)} custom-call(s32[3,14]{1,0:T(4,128)S(1)} %pad_add_fusion.2.refs_0_, s32[3]{0:T(128)S(1)} %add_add_fusion.1.refs_1_, bf16[944,128]{1,0:T(8,128)(2,1)S(1)} %collective-permute-done.refs_2_, bf16[944,128]{1,0:T(8,128)(2,1)S(1)} %collective-permute-done.4.refs_3_, ...), custom_call_target="tpu_custom_call", output_to_operand_aliasing={{}: (7, {})} | custom-call | flops 88080384 | bytes 3145728 | tf_op jit(solution)/shard_map/pallas_call | solution.py:183
  41.0 0.0 copy-start.4
  41.0 0.0 copy-start.5
  41.0 0.0 collective-permute-done.7.theirs
  41.0 7.2 %shard_map.123 = bf16[16,16,1024]{2,1,0:T(8,128)(2,1)S(1)} custom-call(bf16[4,2,2,32,3072]{4,3,2,1,0:T(8,128)(2,1)S(1)} %shard_map.122.rows_x, bf16[3072,1024]{1,0:T(8,128)(2,1)S(1)} %bitcast.30, bf16[3072,1024]{1,0:T(8,128)(2,1)} %collective-permute-done.7.theirs), custom_call_target="tpu_custom_call" | custom-call | flops 3221225472 | bytes 12582912 | tf_op jit(solution)/shard_map/pallas_call | solution.py:243
  48.3 29.7 %all_to_all.5 = bf16[16,16,1024]{2,1,0:T(8,128)(2,1)S(1)} all-to-all(bf16[16,16,1024]{2,1,0:T(8,128)(2,1)S(1)} %shard_map.123), channel_id=1, replica_groups=mesh['grp'=2,'band'=4,'var'=2,'sub'=2] {'grp','band','var'}, dimensions={0} | all-to-all | bytes 1048576 | tf_op jit(solution)/shard_map/all_to_all | solution.py:372
  78.0 0.1 convert_reduce_fusion
  78.1 0.1 multiply_reduce_fusion
  78.2 0.1 rsqrt.12
  78.3 0.1 fusion
  78.4 0.6 copy.18
  (25 shorter events, 0.1 us)
Async XLA Ops:
  0.0 24.5 %copy-start.1 = (bf16[36,4,24,128]{3,2,1,0:T(8,128)(2,1)S(1)}, bf16[36,4,24,128]{3,2,1,0:T(8,128)(2,1)}, u32[]{:S(2)}) copy-start(bf16[36,4,24,128]{3,2,1,0:T(8,128)(2,1)} %param.16) | copy-start | bytes 2654212
  0.0 24.5 %copy-start = (bf16[36,4,24,128]{3,2,1,0:T(8,128)(2,1)S(1)}, bf16[36,4,24,128]{3,2,1,0:T(8,128)(2,1)}, u32[]{:S(2)}) copy-start(bf16[36,4,24,128]{3,2,1,0:T(8,128)(2,1)} %param.12) | copy-start | bytes 2654212
  0.0 13.6 %copy-start.7 = (s32[36,1]{0,1:T(1,128)S(1)}, s32[36,1]{0,1:T(1,128)}, u32[]{:S(2)}) copy-start(s32[36,1]{0,1:T(1,128)} %param.17) | copy-start | bytes 436
  0.0 13.6 %copy-start.6 = (s32[36,1]{0,1:T(1,128)S(1)}, s32[36,1]{0,1:T(1,128)}, u32[]{:S(2)}) copy-start(s32[36,1]{0,1:T(1,128)} %param.13) | copy-start | bytes 436
  3.9 37.1 %collective-permute-start.7 = (bf16[3072,1024]{1,0:T(8,128)(2,1)}, bf16[3072,1024]{1,0:T(8,128)(2,1)}, u32[]{:S(2)}, u32[]{:S(2)}) collective-permute-start(bf16[3072,1024]{1,0:T(8,128)(2,1)} %mine.1), channel_id=1, source_target_pairs={{0,1},{1,0},{2,3},{3,2},{4,5},{5,4},{6,7},{7,6},{8,9},{9,8},{10,11... | collective-permute-start | bytes 18874376 | tf_op jit(solution)/shard_map/ppermute | solution.py:270
  4.5 25.5 %collective-permute-start = (bf16[944,128]{1,0:T(8,128)(2,1)}, bf16[944,128]{1,0:T(8,128)(2,1)S(1)}, u32[]{:S(2)}, u32[]{:S(2)}) collective-permute-start(bf16[944,128]{1,0:T(8,128)(2,1)} %get-tuple-element.18), channel_id=1, source_target_pairs={{0,8},{4,12},{8,0},{12,4},{1,9},{5,13},{9,1},{13,5},{2,10},{6,14},... | collective-permute-start | bytes 725000 | tf_op jit(solution)/shard_map/ppermute | solution.py:323
  8.1 13.5 %collective-permute-start.1 = (bf16[944,128]{1,0:T(8,128)(2,1)}, bf16[944,128]{1,0:T(8,128)(2,1)S(1)}, u32[]{:S(2)}, u32[]{:S(2)}) collective-permute-start(bf16[944,128]{1,0:T(8,128)(2,1)} %get-tuple-element.20), channel_id=1, source_target_pairs={{0,4},{4,8},{8,12},{12,0},{1,5},{5,9},{9,13},{13,1},{2,6},{6,10},{... | collective-permute-start | bytes 725000 | tf_op jit(solution)/shard_map/ppermute | solution.py:323
  9.7 17.2 %collective-permute-start.3 = (bf16[944,128]{1,0:T(8,128)(2,1)}, bf16[944,128]{1,0:T(8,128)(2,1)S(1)}, u32[]{:S(2)}, u32[]{:S(2)}) collective-permute-start(bf16[944,128]{1,0:T(8,128)(2,1)} %get-tuple-element.22), channel_id=1, source_target_pairs={{0,12},{4,0},{8,4},{12,8},{1,13},{5,1},{9,5},{13,9},{2,14},{6,2},{... | collective-permute-start | bytes 725000 | tf_op jit(solution)/shard_map/ppermute | solution.py:323
  12.0 23.8 %collective-permute-start.5 = (bf16[36,96,128]{2,1,0:T(8,128)(2,1)}, bf16[36,96,128]{2,1,0:T(8,128)(2,1)S(1)}, u32[]{:S(2)}, u32[]{:S(2)}) collective-permute-start(bf16[36,96,128]{2,1,0:T(8,128)(2,1)} %get-tuple-element.27), channel_id=1, source_target_pairs={{0,16},{16,0},{1,17},{17,1},{2,18},{18,2},{3,19},{19,3},{4,20},{20... | collective-permute-start | bytes 2654216 | tf_op jit(solution)/shard_map/ppermute | solution.py:270
  21.7 7.0 %collective-permute-start.2 = (bf16[944,128]{1,0:T(8,128)(2,1)S(1)}, bf16[944,128]{1,0:T(8,128)(2,1)S(1)}, u32[]{:S(2)}, u32[]{:S(2)}) collective-permute-start(bf16[944,128]{1,0:T(8,128)(2,1)S(1)} %collective-permute-done.1.refs_2_.refs_12_), channel_id=1, source_target_pairs={{0,2},{2,0},{1,3},{3,1},{4,6},{6,4},{5,7},{7,5},{8,10},{10,8},{9,1... | collective-permute-start | bytes 725000 | tf_op jit(solution)/shard_map/ppermute | solution.py:270
  24.5 1.0 %copy-start.2 = (bf16[1840,128]{1,0:T(8,128)(2,1)S(1)}, bf16[1840,128]{1,0:T(8,128)(2,1)}, u32[]{:S(2)}) copy-start(bf16[1840,128]{1,0:T(8,128)(2,1)} %get-tuple-element.23.refs_2_.refs_8_) | copy-start | bytes 1413124
  26.9 8.9 %collective-permute-start.6 = (bf16[944,128]{1,0:T(8,128)(2,1)S(1)}, bf16[944,128]{1,0:T(8,128)(2,1)S(1)}, u32[]{:S(2)}, u32[]{:S(2)}) collective-permute-start(bf16[944,128]{1,0:T(8,128)(2,1)S(1)} %collective-permute-done.3.refs_2_), channel_id=1, source_target_pairs={{0,2},{2,0},{1,3},{3,1},{4,6},{6,4},{5,7},{7,5},{8,10},{10,8},{9,1... | collective-permute-start | bytes 725000 | tf_op jit(solution)/shard_map/ppermute | solution.py:270
  28.3 7.4 %copy-start.3 = (bf16[1840,128]{1,0:T(8,128)(2,1)S(1)}, bf16[1840,128]{1,0:T(8,128)(2,1)}, u32[]{:S(2)}) copy-start(bf16[1840,128]{1,0:T(8,128)(2,1)} %get-tuple-element.23.refs_2_.refs_8_) | copy-start | bytes 1413124
  28.7 12.3 %slice-start = ((s8[6291456]{0:T(1024)(128)(4,1)}), s8[4194304]{0:T(1024)(128)(4,1)S(1)}, s32[]{:S(2)}) async-start(s8[6291456]{0:T(1024)(128)(4,1)} %bitcast.29), calls=%async_computation.1 | async-start | bytes 8388608
  30.0 9.0 %collective-permute-start.4 = (bf16[944,128]{1,0:T(8,128)(2,1)S(1)}, bf16[944,128]{1,0:T(8,128)(2,1)S(1)}, u32[]{:S(2)}, u32[]{:S(2)}) collective-permute-start(bf16[944,128]{1,0:T(8,128)(2,1)S(1)} %collective-permute-done.refs_2_), channel_id=1, source_target_pairs={{0,2},{2,0},{1,3},{3,1},{4,6},{6,4},{5,7},{7,5},{8,10},{10,8},{9,1... | collective-permute-start | bytes 725000 | tf_op jit(solution)/shard_map/ppermute | solution.py:270
  31.6 9.4 %slice-start.1 = ((s8[6291456]{0:T(1024)(128)(4,1)}), s8[2097152]{0:T(1024)(128)(4,1)S(1)}, s32[]{:S(2)}) async-start(s8[6291456]{0:T(1024)(128)(4,1)} %bitcast.29), calls=%async_computation.2 | async-start | bytes 4194304
  41.0 37.1 %copy-start.4 = (f32[1024]{0:T(1024)S(1)}, f32[1024]{0:T(1024)}, u32[]{:S(2)}) copy-start(f32[1024]{0:T(1024)} %param.22) | copy-start | bytes 12292
  41.0 37.3 %copy-start.5 = (f32[1024]{0:T(1024)S(1)}, f32[1024]{0:T(1024)}, u32[]{:S(2)}) copy-start(f32[1024]{0:T(1024)} %param.23) | copy-start | bytes 12292

commit v8 on v7

--- a/solution.py
+++ b/solution.py
@@ -197,9 +197,9 @@
     )(*operands)
 
 
-def embed_kernel(steps, halves, rows_x, mine, theirs, out, total):
+def embed_kernel(steps, halves, rows_x, first, second, out, total):
     at = pl.program_id(0)
-    sub, mine_group = lax.axis_index("sub"), lax.axis_index("grp")
+    mine_group = lax.axis_index("grp")
     bands, groups, _, row_count, width = rows_x.shape
     rows = bands * groups * row_count
 
@@ -207,10 +207,9 @@
     def _():
         total[...] = jnp.zeros_like(total)
 
-    left = rows_x[:, :, sub].reshape(rows, width)
-    right = rows_x[:, :, 1 - sub].reshape(rows, width)
-    total[...] += jnp.dot(left, mine[...], preferred_element_type=jnp.float32) + jnp.dot(
-        right, theirs[...], preferred_element_type=jnp.float32
+    left, right = (rows_x[:, :, half].reshape(rows, width) for half in range(2))
+    total[...] += jnp.dot(left, first[...], preferred_element_type=jnp.float32) + jnp.dot(
+        right, second[...], preferred_element_type=jnp.float32
     )
 
     @pl.when(at == pl.num_programs(0) - 1)
@@ -230,36 +229,38 @@
                     out[base + chunk] = jnp.concatenate(pieces, axis=0).astype(out.dtype)
 
 
-def embed(rows_x, mine, theirs, steps, halves):
+def embed(rows_x, weight, steps, halves):
     bands, groups, _, row_count, half_width = rows_x.shape
-    width = mine.shape[-1]
+    width = weight.shape[-1]
     grid = 6 if half_width % (6 * 256) == 0 else 3
     step_rows = half_width // grid
     rows = bands * groups * row_count
     chunks = groups * steps * halves
     share = row_count // (steps * halves)
     shape = (chunks, bands * share, width) if share % 4 == 0 else (rows, width)
-    weight_spec = pl.BlockSpec((step_rows, width), lambda i: (i, 0))
+    weight_specs = [
+        pl.BlockSpec((step_rows, width), lambda i: (i, 0)),
+        pl.BlockSpec((step_rows, width), lambda i: (i + grid, 0)),
+    ]
     out = pl.pallas_call(
         functools.partial(embed_kernel, steps, halves),
         out_shape=jax.ShapeDtypeStruct(shape, jnp.bfloat16),
         grid=(grid,),
         in_specs=[
             pl.BlockSpec((bands, groups, 2, row_count, step_rows), lambda i: (0, 0, 0, 0, i)),
-            weight_spec,
-            weight_spec,
+            *weight_specs,
         ],
         out_specs=pl.BlockSpec(shape, lambda i: (0,) * len(shape)),
         scratch_shapes=[pltpu.VMEM((rows, width), jnp.float32)],
         cost_estimate=pl.CostEstimate(
-            flops=4 * rows * mine.shape[0] * width,
-            bytes_accessed=4 * mine.shape[0] * width,
+            flops=2 * rows * weight.shape[0] * width,
+            bytes_accessed=2 * weight.shape[0] * width,
             transcendentals=0,
         ),
         compiler_params=pltpu.CompilerParams(
             vmem_limit_bytes=(48 if rows > 1024 else 16) << 20
         ),
-    )(rows_x, mine, theirs)
+    )(rows_x, weight, weight)
     if share % 4:
         out = out.reshape(bands, chunks, share, width).transpose(1, 0, 2, 3)
         out = out.reshape(chunks, bands * share, width)
@@ -299,6 +300,8 @@
     x, y = lax.axis_index("var"), lax.axis_index("grp")
     quarter = y * nv + x
 
+    embed_rows = lax.all_gather(embed_weight, "sub", axis=0, tiled=True)
+
     flat = (nb, cap * cells, cells)
     ocean_w, atmos_w = ocean_weights.reshape(flat), atmos_weights.reshape(flat)
     ocean_ids, atmos_ids = ocean_tiles.reshape(nb, cap), atmos_tiles.reshape(nb, cap)
@@ -313,18 +316,21 @@
 
     if ng == 2 and nv == 2 and cap % 2 == 0:
         each = cap // 2
+        head = (each + 1) // 2
         pieces = []
         for shift in order:
-            pieces.append((shift, 0, each, each))
+            if 2 * shift == nb:
+                pieces += [(shift, 0, head, each), (shift, head, each - head, each)]
+            else:
+                pieces.append((shift, 0, each, each))
         *packed, own_w, send = pack(
             pieces + [(0, 0, cap, None)], ocean_w, atmos_w, ocean_ids, atmos_ids, land, ocean_f, atmos_f
         )
-        sent = [
-            lax.ppermute(piece, "band", along(shift))
-            for piece, (shift, _, _, _) in zip(packed, pieces)
-        ]
-        embed_other, send = lax.optimization_barrier((embed_weight, send))
-        embed_other = swap(embed_other, "sub")
+        sent = []
+        for at, (piece, (shift, _, _, _)) in enumerate(zip(packed, pieces)):
+            if at >= 2:
+                piece, sent[at - 2] = lax.optimization_barrier((piece, sent[at - 2]))
+            sent.append(lax.ppermute(piece, "band", along(shift)))
         keep, theirs = (ocean_f, atmos_f), (swap(send, "grp"),)
         dest = jnp.where(y == 0, ocean_dest, atmos_dest)
         block_all, used_all = slot_tables(dest, nb, cap)
@@ -352,13 +358,12 @@
             return job_of((me - shift) % nb, parts, sizes, firsts, fields)
 
         ours, others = [(0, keep)], [(1, theirs)]
-        own_w, sent[0] = lax.optimization_barrier((own_w, sent[0]))
         jobs = [job_of(me, [own_w], [cap], [jnp.int32(0)], ours)]
         rows_x = call(jobs[:1], None, groups=2)
-        crossed = [swap(sent[0], "var")]
-        for at in range(1, len(sent)):
-            if at > 1:
-                jobs.append(job_at(order[at - 2], ours))
+        crossed = [swap(piece, "var") for piece in sent[:2]]
+        for at in range(2, len(sent)):
+            if at == 3:
+                jobs.append(job_at(order[0], ours))
                 rows_x = call(jobs[-1:], rows_x, groups=2)
             sent[at], rows_x = lax.optimization_barrier((sent[at], rows_x))
             crossed.append(swap(sent[at], "var"))
@@ -368,10 +373,9 @@
             jobs[done:-1] + [with_fields(job, others) for job in jobs[:-1]], rows_x, groups=2
         )
         rows_x = call([with_fields(jobs[-1], ours + others)], rows_x, groups=2)
-        sent = embed(rows_x, embed_weight, embed_other, steps, nv)
+        sent = embed(rows_x, embed_rows, steps, nv)
         got = lax.all_to_all(sent, ("grp", "band", "var"), split_axis=0, concat_axis=0, tiled=True)
     else:
-        embed_other = swap(embed_weight, "sub")
         both = jnp.concatenate([ocean_w, atmos_w], axis=1)
         fields = [(0, (jnp.concatenate([ocean_f, atmos_f], axis=0),))]
         ocean_block, ocean_used = slot_tables(ocean_dest, nb, cap)
@@ -409,7 +413,7 @@
             tile = meta[2 * tiles, :slots].astype(jnp.int32)
             parts = parts[:, :share_rows].reshape(slots * cells, cells)
             rows_x = call([job_of(band, tile, meta, parts)], rows_x, groups=1)
-        sent = embed(rows_x, embed_weight, embed_other, steps, nv)
+        sent = embed(rows_x, embed_rows, steps, nv)
         got = lax.all_to_all(sent, ("band", "var"), split_axis=0, concat_axis=0, tiled=True)
     shifted = jnp.sum(got.astype(jnp.float32), axis=0) + embed_bias
     inverse = lax.rsqrt(jnp.mean(shifted * shifted, axis=-1, keepdims=True) + 1e-05)

time: 79.4 us -> 84.9 us (1.069)
  between operations: 0.23 us -> 13.6 us
  blocking collectives: 29.7 us -> 18.5 us
  local copies, waits for them, and re-layouts: 1.98 us -> 9.58 us
  waiting for transfers between devices: 11.8 us -> 7.1 us
  Pallas kernels: 19 us -> 17.7 us
  other arithmetic: 2.38 us -> 3.58 us
    all_to_all x1, blocking collectives: 29.7 us -> 18.5 us  [per_device(): lax.all_to_all(sent, ('grp', 'band', 'var'), split_axis=0, concat_axis=0,...]
    unnamed x20, local copies, waits for them, and re-layouts: 1.06 us -> 8.56 us
    ppermute x3 -> x4, waiting for transfers between devices: 7.31 us -> 4.33 us  [per_device(): sent.append(lax.ppermute(piece, 'band', along(shift)))]
    pallas_call x1, Pallas kernels: 7.22 us -> 4.79 us  [embed(): pl.pallas_call(functools.partial(embed_kernel, steps, halves), out_shape=...]
    ppermute x5, waiting for transfers between devices: 4.45 us -> 2.04 us  [swap(): return lax.ppermute(x, axis, [(0, 1), (1, 0)])]
    pallas_call x4, Pallas kernels: 7.83 us -> 9.12 us  [regrid(): pl.pallas_call(functools.partial(regrid_kernel, steps, listed, len(operan...]
    ppermute x3 -> x4, starting transfers between devices: 7.49 us -> 8.35 us  [per_device(): sent.append(lax.ppermute(piece, 'band', along(shift)))]
  transfers between devices with their start and end apart: 8 -> 10, of which waited for: 3 -> 2; matrix products, arithmetic and copies ran while one was open for 3% -> 4% of each run, Pallas kernels for 10% -> 15%
where the time goes in v8:
time: 84.9 us; the launch traced here: 84.3 us
  blocking collectives  18.5 us (22%)
  Pallas kernels  17.7 us (21%)
  starting transfers between devices  14.2 us (17%)
  between operations  13.6 us (16%)
  local copies, waits for them, and re-layouts  9.58 us (11%)
  waiting for transfers between devices  7.1 us (8%)
  other arithmetic  3.58 us (4%)
    all_to_all x1, blocking collectives, per_device(): lax.all_to_all(sent, ('grp', 'band', 'var'), split_axis=0, concat_axis=0,...  18.5 us
    pallas_call x4, Pallas kernels, regrid(): pl.pallas_call(functools.partial(regrid_kernel, steps, listed, len(operan...  9.12 us
    unnamed x20, local copies, waits for them, and re-layouts  8.56 us
    ppermute x4, starting transfers between devices, per_device(): sent.append(lax.ppermute(piece, 'band', along(shift)))  8.35 us
    ppermute x5, starting transfers between devices, swap(): return lax.ppermute(x, axis, [(0, 1), (1, 0)])  5.87 us
    pallas_call x1, Pallas kernels, embed(): pl.pallas_call(functools.partial(embed_kernel, steps, halves), out_shape=...  4.79 us
    ppermute x4, waiting for transfers between devices, per_device(): sent.append(lax.ppermute(piece, 'band', along(shift)))  4.33 us
    pallas_call x1, Pallas kernels, pack(): pl.pallas_call(functools.partial(pack_kernel, pieces, len(fields) // 2),...  3.77 us
  transfers between devices with their start and end apart: 10, of which 2 were waited for; matrix products, arithmetic and copies ran while one was open for 4% of the time, Pallas kernels for 15%

profile of v8, /device:TPU:0, one launch (start us, length us, event | category | flops | bytes accessed | tf_op | source)
XLA Modules:
  0.0 84.3 jit_solution(15832531869166832755)
XLA Ops:
  6.5 0.7 all-gather.2.cloned.1.call-update
  7.3 3.8 %shard_map.118 = (bf16[944,128]{1,0:T(8,128)(2,1)}, bf16[944,128]{1,0:T(8,128)(2,1)}, bf16[560,128]{1,0:T(8,128)(2,1)}, bf16[384,128]{1,0:T(8,128)(2,1)}, bf16[1...) custom-call(bf16[4,1792,128]{2,1,0:T(8,128)(2,1)} %bitcast.31, bf16[4,1792,128]{2,1,0:T(8,128)(2,1)} %bitcast.32, ...), custom_call_target="tpu_custom_call" | custom-call | bytes 2097152 | tf_op jit(solution)/shard_map/pallas_call | solution.py:89
  11.1 3.1 %collective-permute-start = (bf16[944,128]{1,0:T(8,128)(2,1)}, bf16[944,128]{1,0:T(8,128)(2,1)S(1)}, u32[]{:S(2)}, u32[]{:S(2)}) collective-permute-start(bf16[944,128]{1,0:T(8,128)(2,1)} %get-tuple-element.20), channel_id=1, source_target_pairs={{0,4},{4,8},{8,12},{12,0},{1,5},{5,9},{9,13},{13,1},{2,6},{6,10},{... | collective-permute-start | bytes 725000 | tf_op jit(solution)/shard_map/ppermute | solution.py:333
  14.1 2.1 %collective-permute-start.3 = (bf16[944,128]{1,0:T(8,128)(2,1)}, bf16[944,128]{1,0:T(8,128)(2,1)}, u32[]{:S(2)}, u32[]{:S(2)}) collective-permute-start(bf16[944,128]{1,0:T(8,128)(2,1)} %get-tuple-element.25), channel_id=1, source_target_pairs={{0,12},{4,0},{8,4},{12,8},{1,13},{5,1},{9,5},{13,9},{2,14},{6,2},{... | collective-permute-start | bytes 725000 | tf_op jit(solution)/shard_map/ppermute | solution.py:333
  16.2 1.7 %collective-permute-start.7 = (bf16[36,96,128]{2,1,0:T(8,128)(2,1)}, bf16[36,96,128]{2,1,0:T(8,128)(2,1)}, u32[]{:S(2)}, u32[]{:S(2)}) collective-permute-start(bf16[36,96,128]{2,1,0:T(8,128)(2,1)} %get-tuple-element.30), channel_id=1, source_target_pairs={{0,16},{16,0},{1,17},{17,1},{2,18},{18,2},{3,19},{19,3},{4,20},{20... | collective-permute-start | bytes 2654216 | tf_op jit(solution)/shard_map/ppermute | solution.py:271
  17.9 0.2 convert_reduce_fusion.1
  18.1 0.1 select_reduce_fusion
  18.2 0.1 reshape.89
  18.3 0.1 fusion.1
  18.4 0.1 reshape.97
  18.5 0.6 slice_convert_fusion.3
  19.1 0.6 fusion.3
  19.8 0.1 pad_add_fusion.4.refs_1_.refs_7_
  19.8 0.1 stack.73.refs_1_
  19.9 1.4 %copy-done.1 = bf16[36,4,24,128]{3,2,1,0:T(8,128)(2,1)S(1)} copy-done((bf16[36,4,24,128]{3,2,1,0:T(8,128)(2,1)S(1)}, bf16[36,4,24,128]{3,2,1,0:T(8,128)(2,1)}, u32[]{:S(2)}) %copy-start.1) | copy-done | bytes 884760
  21.4 1.4 %copy-done.2 = bf16[36,4,24,128]{3,2,1,0:T(8,128)(2,1)S(1)} copy-done((bf16[36,4,24,128]{3,2,1,0:T(8,128)(2,1)S(1)}, bf16[36,4,24,128]{3,2,1,0:T(8,128)(2,1)}, u32[]{:S(2)}) %copy-start.2) | copy-done | bytes 884760
  22.8 1.1 %copy-done.3 = bf16[1840,128]{1,0:T(8,128)(2,1)S(1)} copy-done((bf16[1840,128]{1,0:T(8,128)(2,1)S(1)}, bf16[1840,128]{1,0:T(8,128)(2,1)}, u32[]{:S(2)}) %copy-start.3) | copy-done | bytes 471064
  23.9 1.3 %shard_map.119.refs_6_ = bf16[4,2,2,32,3072]{4,3,2,1,0:T(8,128)(2,1)S(1)} custom-call(s32[3,14]{1,0:T(4,128)S(1)} %pad_add_fusion.refs_0_.refs_6_, s32[2]{0:T(128)S(1)} %pad_add_fusion.4.refs_1_.refs_7_, bf16[1840,128]{1,0:T(8,128)(2,1)S(1)} %copy-done.3, bf16[36,96,128]{2,1,0:T(8,128)(2,1)S(1)} %bitcast.22, bf16[36,96,128]{2,1,0:T(8,128)(2,1)S(1)} %bitcast.27), custom_call_target="tpu_custom_call" | custom-call | flops 44040192 | bytes 3145728 | tf_op jit(solution)/shard_map/pallas_call | solution.py:183
  25.2 0.1 add_add_fusion.refs_1_.refs_11_
  25.3 0.1 add_add_fusion.1.refs_1_
  25.4 0.0 collective-permute-done.refs_2_.refs_12_
  25.4 2.8 %collective-permute-start.1 = (bf16[560,128]{1,0:T(8,128)(2,1)S(1)}, bf16[560,128]{1,0:T(8,128)(2,1)S(1)}, u32[]{:S(2)}, u32[]{:S(2)}) collective-permute-start(bf16[560,128]{1,0:T(8,128)(2,1)S(1)} %copy-done.8), channel_id=1, source_target_pairs={{0,8},{4,12},{8,0},{12,4},{1,9},{5,13},{9,1},{13,5},{2,10},{6,14},... | collective-permute-start | bytes 430088 | tf_op jit(solution)/shard_map/ppermute | solution.py:333
  28.2 0.0 collective-permute-done.3.refs_2_
  28.2 1.5 %collective-permute-start.5 = (bf16[944,128]{1,0:T(8,128)(2,1)S(1)}, bf16[944,128]{1,0:T(8,128)(2,1)S(1)}, u32[]{:S(2)}, u32[]{:S(2)}) collective-permute-start(bf16[944,128]{1,0:T(8,128)(2,1)S(1)} %collective-permute-done.refs_2_.refs_12_), channel_id=1, source_target_pairs={{0,2},{2,0},{1,3},{3,1},{4,6},{6,4},{5,7},{7,5},{8,10},{10,8},{9,1... | collective-permute-start | bytes 725000 | tf_op jit(solution)/shard_map/ppermute | solution.py:271
  29.7 0.7 slice_convert_fusion
  30.3 0.5 collective-permute-start.8
  30.9 0.4 collective-permute-start.4
  31.3 4.3 %collective-permute-done.1.refs_2_ = bf16[560,128]{1,0:T(8,128)(2,1)S(1)} collective-permute-done((bf16[560,128]{1,0:T(8,128)(2,1)S(1)}, bf16[560,128]{1,0:T(8,128)(2,1)S(1)}, u32[]{:S(2)}, u32[]{:S(2)}) %collective-permute-start.1) | collective-permute-done | bytes 143392 | tf_op jit(solution)/shard_map/ppermute | solution.py:333
  35.6 1.5 %collective-permute-start.2 = (bf16[560,128]{1,0:T(8,128)(2,1)S(1)}, bf16[560,128]{1,0:T(8,128)(2,1)S(1)}, u32[]{:S(2)}, u32[]{:S(2)}) collective-permute-start(bf16[560,128]{1,0:T(8,128)(2,1)S(1)} %collective-permute-done.1.refs_2_), channel_id=1, source_target_pairs={{0,2},{2,0},{1,3},{3,1},{4,6},{6,4},{5,7},{7,5},{8,10},{10,8},{9,1... | collective-permute-start | bytes 430088 | tf_op jit(solution)/shard_map/ppermute | solution.py:271
  37.1 0.7 fusion.6
  37.8 0.0 collective-permute-done.5.refs_3_.refs_13_
  37.8 1.3 %shard_map.120.refs_14_ = bf16[4,2,2,32,3072]{4,3,2,1,0:T(8,128)(2,1)S(1)} custom-call(s32[3,14]{1,0:T(4,128)S(1)} %pad_add_fusion.2.refs_0_.refs_10_, s32[3]{0:T(128)S(1)} %add_add_fusion.refs_1_.refs_11_, bf16[944,128]{1,0:T(8,128)(2,1)S(1)} %collective-permute-done.refs_2_.refs_12_, ...), custom_call_target="tpu_custom_call", output_to_operand_aliasing={{}: (6, {})} | custom-call | flops 44040192 | bytes 3145728 | tf_op jit(solution)/shard_map/pallas_call | solution.py:183
  39.2 0.7 collective-permute-start.6
  39.9 2.0 %collective-permute-done.8.refs_3_ = bf16[944,128]{1,0:T(8,128)(2,1)S(1)} collective-permute-done((bf16[944,128]{1,0:T(8,128)(2,1)}, bf16[944,128]{1,0:T(8,128)(2,1)S(1)}, u32[]{:S(2)}, u32[]{:S(2)}) %collective-permute-start.8) | collective-permute-done | bytes 241696 | tf_op jit(solution)/shard_map/ppermute | solution.py:271
  41.9 0.0 collective-permute-done.7.refs_9_.refs_8_
  41.9 3.9 %shard_map.121.refs_9_ = bf16[4,2,2,32,3072]{4,3,2,1,0:T(8,128)(2,1)S(1)} custom-call(s32[3,14]{1,0:T(4,128)S(1)} %pad_add_fusion.3.refs_0_, s32[3]{0:T(128)S(1)} %add_add_fusion.1.refs_1_, bf16[944,128]{1,0:T(8,128)(2,1)} %collective-permute-done.3.refs_2_, bf16[944,128]{1,0:T(8,128)(2,1)S(1)} %collective-permute-done.8.refs_3_, ...), custom_call_target="tpu_custom_call", output_to_operand_aliasing={{}: (14, {})} | custom-call | flops 176160768 | bytes 12582912 | tf_op jit(solution)/shard_map/pallas_call | solution.py:183
  45.8 0.0 collective-permute-done.2.refs_3_
  45.8 0.0 collective-permute-done.6.refs_5_
  45.9 2.5 %shard_map.122.rows_x = bf16[4,2,2,32,3072]{4,3,2,1,0:T(8,128)(2,1)S(1)} custom-call(s32[3,14]{1,0:T(4,128)S(1)} %pad_add_fusion.1.refs_0_, s32[5]{0:T(128)S(1)} %stack.73.refs_1_, bf16[560,128]{1,0:T(8,128)(2,1)S(1)} %collective-permute-done.1.refs_2_, bf16[560,128]{1,0:T(8,128)(2,1)S(1)} %collective-permute-done.2.refs_3_, ...), custom_call_target="tpu_custom_call", output_to_operand_aliasing={{}: (9, {})} | custom-call | flops 88080384 | bytes 3145728 | tf_op jit(solution)/shard_map/pallas_call | solution.py:183
  48.4 0.0 all-gather.2.cloned.1.call-done.first.second
  48.5 4.6 %copy-done = bf16[6144,1024]{1,0:T(8,128)(2,1)S(1)} copy-done((bf16[6144,1024]{1,0:T(8,128)(2,1)S(1)}, bf16[6144,1024]{1,0:T(8,128)(2,1)}, u32[]{:S(2)}) %copy-start) | copy-done | bytes 12582936
  53.0 4.8 %shard_map.123 = bf16[16,16,1024]{2,1,0:T(8,128)(2,1)S(1)} custom-call(bf16[4,2,2,32,3072]{4,3,2,1,0:T(8,128)(2,1)S(1)} %shard_map.122.rows_x, bf16[6144,1024]{1,0:T(8,128)(2,1)S(1)} %copy-done, bf16[6144,1024]{1,0:T(8,128)(2,1)S(1)} %copy-done), custom_call_target="tpu_custom_call" | custom-call | flops 3221225472 | bytes 12582912 | tf_op jit(solution)/shard_map/pallas_call | solution.py:245
  57.8 18.5 %all_to_all.5 = bf16[16,16,1024]{2,1,0:T(8,128)(2,1)S(1)} all-to-all(bf16[16,16,1024]{2,1,0:T(8,128)(2,1)S(1)} %shard_map.123), channel_id=1, replica_groups=mesh['grp'=2,'band'=4,'var'=2,'sub'=2] {'grp','band','var'}, dimensions={0} | all-to-all | bytes 1048576 | tf_op jit(solution)/shard_map/all_to_all | solution.py:377
  76.4 0.1 convert_reduce_fusion
  76.5 0.1 multiply_reduce_fusion
  76.6 0.1 rsqrt.12
  76.7 0.1 fusion
  76.8 0.6 copy.18
  (29 shorter events, 0.1 us)
Async XLA Ops:
  6.5 41.9 %all-gather.2.cloned.1.call-start = ((), (), s32[]{:S(2)}) async-start(), calls=%async_computation.1 | async-start | bytes 18874368 | tf_op jit(solution)/shard_map/all_gather | solution.py:303
  7.3 10.7 %copy-start.6 = (s32[36,1]{0,1:T(1,128)S(1)}, s32[36,1]{0,1:T(1,128)}, u32[]{:S(2)}) copy-start(s32[36,1]{0,1:T(1,128)} %param.13) | copy-start | bytes 436
  7.3 10.6 %copy-start.7 = (s32[36,1]{0,1:T(1,128)S(1)}, s32[36,1]{0,1:T(1,128)}, u32[]{:S(2)}) copy-start(s32[36,1]{0,1:T(1,128)} %param.17) | copy-start | bytes 436
  11.1 19.8 %copy-start.9 = (bf16[384,128]{1,0:T(8,128)(2,1)S(1)}, bf16[384,128]{1,0:T(8,128)(2,1)}, u32[]{:S(2)}) copy-start(bf16[384,128]{1,0:T(8,128)(2,1)} %get-tuple-element.26) | copy-start | bytes 294916
  11.1 14.3 %collective-permute-start = (bf16[944,128]{1,0:T(8,128)(2,1)}, bf16[944,128]{1,0:T(8,128)(2,1)S(1)}, u32[]{:S(2)}, u32[]{:S(2)}) collective-permute-start(bf16[944,128]{1,0:T(8,128)(2,1)} %get-tuple-element.20), channel_id=1, source_target_pairs={{0,4},{4,8},{8,12},{12,0},{1,5},{5,9},{9,13},{13,1},{2,6},{6,10},{... | collective-permute-start | bytes 725000 | tf_op jit(solution)/shard_map/ppermute | solution.py:333
  14.1 14.0 %collective-permute-start.3 = (bf16[944,128]{1,0:T(8,128)(2,1)}, bf16[944,128]{1,0:T(8,128)(2,1)}, u32[]{:S(2)}, u32[]{:S(2)}) collective-permute-start(bf16[944,128]{1,0:T(8,128)(2,1)} %get-tuple-element.25), channel_id=1, source_target_pairs={{0,12},{4,0},{8,4},{12,8},{1,13},{5,1},{9,5},{13,9},{2,14},{6,2},{... | collective-permute-start | bytes 725000 | tf_op jit(solution)/shard_map/ppermute | solution.py:333
  16.2 25.7 %collective-permute-start.7 = (bf16[36,96,128]{2,1,0:T(8,128)(2,1)}, bf16[36,96,128]{2,1,0:T(8,128)(2,1)}, u32[]{:S(2)}, u32[]{:S(2)}) collective-permute-start(bf16[36,96,128]{2,1,0:T(8,128)(2,1)} %get-tuple-element.30), channel_id=1, source_target_pairs={{0,16},{16,0},{1,17},{17,1},{2,18},{18,2},{3,19},{19,3},{4,20},{20... | collective-permute-start | bytes 2654216 | tf_op jit(solution)/shard_map/ppermute | solution.py:271
  19.9 1.4 %copy-start.1 = (bf16[36,4,24,128]{3,2,1,0:T(8,128)(2,1)S(1)}, bf16[36,4,24,128]{3,2,1,0:T(8,128)(2,1)}, u32[]{:S(2)}) copy-start(bf16[36,4,24,128]{3,2,1,0:T(8,128)(2,1)} %param.12) | copy-start | bytes 2654212
  21.4 1.4 %copy-start.2 = (bf16[36,4,24,128]{3,2,1,0:T(8,128)(2,1)S(1)}, bf16[36,4,24,128]{3,2,1,0:T(8,128)(2,1)}, u32[]{:S(2)}) copy-start(bf16[36,4,24,128]{3,2,1,0:T(8,128)(2,1)} %param.16) | copy-start | bytes 2654212
  22.8 1.1 %copy-start.3 = (bf16[1840,128]{1,0:T(8,128)(2,1)S(1)}, bf16[1840,128]{1,0:T(8,128)(2,1)}, u32[]{:S(2)}) copy-start(bf16[1840,128]{1,0:T(8,128)(2,1)} %get-tuple-element.22.refs_2_.refs_8_) | copy-start | bytes 1413124
  23.9 1.5 %copy-start.8 = (bf16[560,128]{1,0:T(8,128)(2,1)S(1)}, bf16[560,128]{1,0:T(8,128)(2,1)}, u32[]{:S(2)}) copy-start(bf16[560,128]{1,0:T(8,128)(2,1)} %get-tuple-element.21) | copy-start | bytes 430084
  25.4 10.2 %collective-permute-start.1 = (bf16[560,128]{1,0:T(8,128)(2,1)S(1)}, bf16[560,128]{1,0:T(8,128)(2,1)S(1)}, u32[]{:S(2)}, u32[]{:S(2)}) collective-permute-start(bf16[560,128]{1,0:T(8,128)(2,1)S(1)} %copy-done.8), channel_id=1, source_target_pairs={{0,8},{4,12},{8,0},{12,4},{1,9},{5,13},{9,1},{13,5},{2,10},{6,14},... | collective-permute-start | bytes 430088 | tf_op jit(solution)/shard_map/ppermute | solution.py:333
  28.2 9.7 %collective-permute-start.5 = (bf16[944,128]{1,0:T(8,128)(2,1)S(1)}, bf16[944,128]{1,0:T(8,128)(2,1)S(1)}, u32[]{:S(2)}, u32[]{:S(2)}) collective-permute-start(bf16[944,128]{1,0:T(8,128)(2,1)S(1)} %collective-permute-done.refs_2_.refs_12_), channel_id=1, source_target_pairs={{0,2},{2,0},{1,3},{3,1},{4,6},{6,4},{5,7},{7,5},{8,10},{10,8},{9,1... | collective-permute-start | bytes 725000 | tf_op jit(solution)/shard_map/ppermute | solution.py:271
  30.3 11.6 %collective-permute-start.8 = (bf16[944,128]{1,0:T(8,128)(2,1)}, bf16[944,128]{1,0:T(8,128)(2,1)S(1)}, u32[]{:S(2)}, u32[]{:S(2)}) collective-permute-start(bf16[944,128]{1,0:T(8,128)(2,1)} %collective-permute-done.3.refs_2_), channel_id=1, source_target_pairs={{0,2},{2,0},{1,3},{3,1},{4,6},{6,4},{5,7},{7,5},{8,10},{10,8},{9,1... | collective-permute-start | bytes 725000 | tf_op jit(solution)/shard_map/ppermute | solution.py:271
  30.9 8.3 %collective-permute-start.4 = (bf16[384,128]{1,0:T(8,128)(2,1)S(1)}, bf16[384,128]{1,0:T(8,128)(2,1)S(1)}, u32[]{:S(2)}, u32[]{:S(2)}) collective-permute-start(bf16[384,128]{1,0:T(8,128)(2,1)S(1)} %copy-done.9), channel_id=1, source_target_pairs={{0,8},{4,12},{8,0},{12,4},{1,9},{5,13},{9,1},{13,5},{2,10},{6,14},... | collective-permute-start | bytes 294920 | tf_op jit(solution)/shard_map/ppermute | solution.py:333
  35.6 10.2 %collective-permute-start.2 = (bf16[560,128]{1,0:T(8,128)(2,1)S(1)}, bf16[560,128]{1,0:T(8,128)(2,1)S(1)}, u32[]{:S(2)}, u32[]{:S(2)}) collective-permute-start(bf16[560,128]{1,0:T(8,128)(2,1)S(1)} %collective-permute-done.1.refs_2_), channel_id=1, source_target_pairs={{0,2},{2,0},{1,3},{3,1},{4,6},{6,4},{5,7},{7,5},{8,10},{10,8},{9,1... | collective-permute-start | bytes 430088 | tf_op jit(solution)/shard_map/ppermute | solution.py:271
  39.2 6.7 %collective-permute-start.6 = (bf16[384,128]{1,0:T(8,128)(2,1)S(1)}, bf16[384,128]{1,0:T(8,128)(2,1)S(1)}, u32[]{:S(2)}, u32[]{:S(2)}) collective-permute-start(bf16[384,128]{1,0:T(8,128)(2,1)S(1)} %collective-permute-done.4.refs_4_), channel_id=1, source_target_pairs={{0,2},{2,0},{1,3},{3,1},{4,6},{6,4},{5,7},{7,5},{8,10},{10,8},{9,1... | collective-permute-start | bytes 294920 | tf_op jit(solution)/shard_map/ppermute | solution.py:271
  48.4 4.6 %copy-start = (bf16[6144,1024]{1,0:T(8,128)(2,1)S(1)}, bf16[6144,1024]{1,0:T(8,128)(2,1)}, u32[]{:S(2)}) copy-start(bf16[6144,1024]{1,0:T(8,128)(2,1)} %all-gather.2.cloned.1.call-done.first.second) | copy-start | bytes 37748740
  53.0 23.5 %copy-start.4 = (f32[1024]{0:T(1024)S(1)}, f32[1024]{0:T(1024)}, u32[]{:S(2)}) copy-start(f32[1024]{0:T(1024)} %param.22) | copy-start | bytes 12292
  53.0 23.7 %copy-start.5 = (f32[1024]{0:T(1024)S(1)}, f32[1024]{0:T(1024)}, u32[]{:S(2)}) copy-start(f32[1024]{0:T(1024)} %param.23) | copy-start | bytes 12292
Sparse Core Ops, SparseCore 0:
  8.9 27.5 all-gather.1

commit v9 on v7

--- a/solution.py
+++ b/solution.py
@@ -9,6 +9,7 @@
 
 REPL = ("grp", "var")
 PACK_LIMIT = 60 << 20
+FINISH_LIMIT = 36 << 20
 
 
 def slot_tables(dest, band_count, cap):
@@ -97,8 +98,7 @@
     )(ocean_w, atmos_w, ocean_ids, atmos_ids, land, *fields)
 
 
-def regrid_kernel(steps, jobs, count, *refs):
-    out, acc, scale = refs[-3:]
+def run_jobs(steps, jobs, refs, out, acc, scale):
     local_rows, cells = acc.shape[1] // (scale.shape[0] // 2 - 4), acc.shape[2]
     tiles = acc.shape[1] // local_rows
     local_vars = local_rows // steps
@@ -150,7 +150,60 @@
                     ).astype(out.dtype)
 
 
-def regrid(jobs, previous, bands, groups, steps, tiles, rows, cells):
+def regrid_kernel(steps, jobs, *refs):
+    run_jobs(steps, jobs, refs, *refs[-3:])
+
+
+def finish_kernel(steps, halves, jobs, count, *refs):
+    theirs, mine, rows_x, out, acc, scale, weight, total, sem = refs[count:]
+    sub, mine_group = lax.axis_index("sub"), lax.axis_index("grp")
+    chunks = sem.shape[0]
+    height = mine.shape[0] // chunks
+
+    def span(chunk):
+        return pl.ds(pl.multiple_of(chunk * height, height), height)
+
+    def copy(chunk):
+        return pltpu.make_async_copy(
+            mine.at[span(chunk), :], weight.at[span(chunk), :], sem.at[chunk]
+        )
+
+    def add(chunk, place, source):
+        left = rows_x[:, :, place, :, span(chunk)].reshape(total.shape[0], height)
+        total[...] += jnp.dot(left, source[span(chunk), :], preferred_element_type=jnp.float32)
+
+    for chunk in range(chunks):
+        copy(chunk).start()
+    run_jobs(steps, jobs, refs, rows_x, acc, scale)
+    total[...] = jnp.zeros_like(total)
+
+    @pl.loop(0, chunks)
+    def _(chunk):
+        add(chunk, 1 - sub, theirs)
+
+    @pl.loop(0, chunks)
+    def _(chunk):
+        copy(chunk).wait()
+        add(chunk, sub, weight)
+
+    send_rows(steps, halves, rows_x.shape, mine_group, total, out)
+
+
+def send_rows(steps, halves, shape, mine_group, total, out):
+    bands, groups, _, row_count, _ = shape
+    count = steps * halves
+    share = row_count // count
+    for g in range(groups):
+        base = (mine_group if g == 0 else 1 - mine_group) * count if groups > 1 else 0
+        for chunk in range(count):
+            pieces = [
+                total[pl.ds((b * groups + g) * row_count + chunk * share, share), :]
+                for b in range(bands)
+            ]
+            out[base + chunk] = jnp.concatenate(pieces, axis=0).astype(out.dtype)
+
+
+def regrid(jobs, previous, bands, groups, steps, tiles, rows, cells, last=None):
     operands, specs, places = [], [], {}
 
     def place(array, space):
@@ -175,26 +228,47 @@
         flops += 2 * sum(sizes) * len(fields) * rows * cells * cells
         most = max(most, len(fields))
     aliases = {}
+    vmem = pl.BlockSpec(memory_space=pltpu.VMEM)
     if previous is not None:
         aliases = {len(operands): 0}
         operands.append(previous)
-        specs.append(pl.BlockSpec(memory_space=pltpu.VMEM))
+        specs.append(vmem)
     shape = (bands, groups, 2, steps * tiles // 2, rows // steps // 2 * 2 * cells)
-    return pl.pallas_call(
-        functools.partial(regrid_kernel, steps, listed, len(operands)),
-        out_shape=jax.ShapeDtypeStruct(shape, jnp.bfloat16),
+    shapes = [jax.ShapeDtypeStruct(shape, jnp.bfloat16)]
+    scratch = [
+        pltpu.VMEM((most, tiles * rows, cells), jnp.float32),
+        pltpu.VMEM((2 * tiles + 8, cells), jnp.float32),
+    ]
+    if last is None:
+        body = functools.partial(regrid_kernel, steps, listed)
+        limit, moved = 12 << 20, len(jobs) * 3 << 20
+    else:
+        mine, theirs, halves = last
+        height, width = mine.shape
+        total = bands * groups * shape[3]
+        body = functools.partial(finish_kernel, steps, halves, listed, len(operands))
+        operands += [theirs, mine]
+        specs += [vmem, pl.BlockSpec(memory_space=pl.ANY)]
+        count = groups * steps * halves
+        shapes.append(jax.ShapeDtypeStruct((count, total // count, width), jnp.bfloat16))
+        scratch += [
+            pltpu.VMEM((height, width), jnp.bfloat16),
+            pltpu.VMEM((total, width), jnp.float32),
+            pltpu.SemaphoreType.DMA((6,)),
+        ]
+        limit, moved = FINISH_LIMIT, 4 * height * width
+        flops += 4 * total * height * width
+    done = pl.pallas_call(
+        body,
+        out_shape=shapes,
         in_specs=specs,
-        out_specs=pl.BlockSpec(memory_space=pltpu.VMEM),
-        scratch_shapes=[
-            pltpu.VMEM((most, tiles * rows, cells), jnp.float32),
-            pltpu.VMEM((2 * tiles + 8, cells), jnp.float32),
-        ],
+        out_specs=[vmem] * len(shapes),
+        scratch_shapes=scratch,
         input_output_aliases=aliases,
-        cost_estimate=pl.CostEstimate(
-            flops=flops, bytes_accessed=len(jobs) * 3 << 20, transcendentals=0
-        ),
-        compiler_params=pltpu.CompilerParams(vmem_limit_bytes=28 << 20),
+        cost_estimate=pl.CostEstimate(flops=flops, bytes_accessed=moved, transcendentals=0),
+        compiler_params=pltpu.CompilerParams(vmem_limit_bytes=limit),
     )(*operands)
+    return done[-1]
 
 
 def embed_kernel(steps, halves, rows_x, mine, theirs, out, total):
@@ -218,16 +292,7 @@
         if out.ndim == 2:
             out[...] = total[...].astype(out.dtype)
         else:
-            count = steps * halves
-            share = row_count // count
-            for g in range(groups):
-                base = (mine_group if g == 0 else 1 - mine_group) * count if groups > 1 else 0
-                for chunk in range(count):
-                    pieces = [
-                        total[pl.ds((b * groups + g) * row_count + chunk * share, share), :]
-                        for b in range(bands)
-                    ]
-                    out[base + chunk] = jnp.concatenate(pieces, axis=0).astype(out.dtype)
+            send_rows(steps, halves, rows_x.shape, mine_group, total, out)
 
 
 def embed(rows_x, mine, theirs, steps, halves):
@@ -319,10 +384,11 @@
         *packed, own_w, send = pack(
             pieces + [(0, 0, cap, None)], ocean_w, atmos_w, ocean_ids, atmos_ids, land, ocean_f, atmos_f
         )
-        sent = [
-            lax.ppermute(piece, "band", along(shift))
-            for piece, (shift, _, _, _) in zip(packed, pieces)
-        ]
+        sent = []
+        for at, (piece, (shift, _, _, _)) in enumerate(zip(packed, pieces)):
+            if at >= 2:
+                piece, sent[at - 2] = lax.optimization_barrier((piece, sent[at - 2]))
+            sent.append(lax.ppermute(piece, "band", along(shift)))
         embed_other, send = lax.optimization_barrier((embed_weight, send))
         embed_other = swap(embed_other, "sub")
         keep, theirs = (ocean_f, atmos_f), (swap(send, "grp"),)
@@ -352,14 +418,12 @@
             return job_of((me - shift) % nb, parts, sizes, firsts, fields)
 
         ours, others = [(0, keep)], [(1, theirs)]
-        own_w, sent[0] = lax.optimization_barrier((own_w, sent[0]))
         jobs = [job_of(me, [own_w], [cap], [jnp.int32(0)], ours)]
         rows_x = call(jobs[:1], None, groups=2)
-        crossed = [swap(sent[0], "var")]
-        for at in range(1, len(sent)):
-            if at > 1:
-                jobs.append(job_at(order[at - 2], ours))
-                rows_x = call(jobs[-1:], rows_x, groups=2)
+        crossed = [swap(piece, "var") for piece in sent[:2]]
+        for at in range(2, len(sent)):
+            jobs.append(job_at(order[at - 2], ours))
+            rows_x = call(jobs[-1:], rows_x, groups=2)
             sent[at], rows_x = lax.optimization_barrier((sent[at], rows_x))
             crossed.append(swap(sent[at], "var"))
         done = len(jobs)
@@ -367,8 +431,12 @@
         rows_x = call(
             jobs[done:-1] + [with_fields(job, others) for job in jobs[:-1]], rows_x, groups=2
         )
-        rows_x = call([with_fields(jobs[-1], ours + others)], rows_x, groups=2)
-        sent = embed(rows_x, embed_weight, embed_other, steps, nv)
+        sent = call(
+            [with_fields(jobs[-1], ours + others)],
+            rows_x,
+            groups=2,
+            last=(embed_weight, embed_other, nv),
+        )
         got = lax.all_to_all(sent, ("grp", "band", "var"), split_axis=0, concat_axis=0, tiled=True)
     else:
         embed_other = swap(embed_weight, "sub")

time: 79.4 us -> 66.7 us (0.84)
  blocking collectives: 29.7 us -> 17 us
  waiting for transfers between devices: 11.8 us -> 6.5 us
  starting transfers between devices: 14 us -> 18.8 us
    all_to_all x1, blocking collectives: 29.7 us -> 17 us  [per_device(): lax.all_to_all(sent, ('grp', 'band', 'var'), split_axis=0, concat_axis=0,...]
    ppermute x3, starting transfers between devices: 7.49 us -> 13 us  [per_device(): sent.append(lax.ppermute(piece, 'band', along(shift)))]
    ppermute x3, waiting for transfers between devices: 7.31 us -> 3.66 us  [per_device(): sent.append(lax.ppermute(piece, 'band', along(shift)))]
    ppermute x5, waiting for transfers between devices: 4.45 us -> 2.84 us  [swap(): return lax.ppermute(x, axis, [(0, 1), (1, 0)])]
    pallas_call x5 -> x4, Pallas kernels: 15.1 us -> 15.6 us  [regrid(): pl.pallas_call(body, out_shape=shapes, in_specs=specs, out_specs=[vmem] *...]
  transfers between devices with their start and end apart: 8 -> 8, of which waited for: 3 -> 3; matrix products, arithmetic and copies ran while one was open for 3% -> 3% of each run, Pallas kernels for 10% -> 9%
where the time goes in v9:
time: 66.7 us; the launch traced here: 66.4 us
  Pallas kernels  19.5 us (29%)
  starting transfers between devices  18.8 us (28%)
  blocking collectives  17 us (25%)
  waiting for transfers between devices  6.5 us (10%)
  other arithmetic  2.41 us (4%)
  local copies, waits for them, and re-layouts  1.98 us (3%)
    all_to_all x1, blocking collectives, per_device(): lax.all_to_all(sent, ('grp', 'band', 'var'), split_axis=0, concat_axis=0,...  17 us
    pallas_call x4, Pallas kernels, regrid(): pl.pallas_call(body, out_shape=shapes, in_specs=specs, out_specs=[vmem] *...  15.6 us
    ppermute x3, starting transfers between devices, per_device(): sent.append(lax.ppermute(piece, 'band', along(shift)))  13 us
    ppermute x5, starting transfers between devices, swap(): return lax.ppermute(x, axis, [(0, 1), (1, 0)])  5.84 us
    pallas_call x1, Pallas kernels, pack(): pl.pallas_call(functools.partial(pack_kernel, pieces, len(fields) // 2),...  3.88 us
    ppermute x3, waiting for transfers between devices, per_device(): sent.append(lax.ppermute(piece, 'band', along(shift)))  3.66 us
    ppermute x5, waiting for transfers between devices, swap(): return lax.ppermute(x, axis, [(0, 1), (1, 0)])  2.84 us
  transfers between devices with their start and end apart: 8, of which 3 were waited for; matrix products, arithmetic and copies ran while one was open for 3% of the time, Pallas kernels for 9%

profile of v9, /device:TPU:0, one launch (start us, length us, event | category | flops | bytes accessed | tf_op | source)
XLA Modules:
  0.0 66.4 jit_solution(6119995351292014310)
XLA Ops:
  0.0 0.0 copy-start.1
  0.0 3.9 %shard_map.118 = (bf16[944,128]{1,0:T(8,128)(2,1)}, bf16[944,128]{1,0:T(8,128)(2,1)}, bf16[944,128]{1,0:T(8,128)(2,1)}, bf16[1840,128]{1,0:T(8,128)(2,1)}, bf16[36,96,128]{2,1,0:T(8,128)(2,1)}) custom-call(bf16[4,1792,128]{2,1,0:T(8,128)(2,1)} %bitcast.29, bf16[4,1792,128]{2,1,0:T(8,128)(2,1)} %bitcast.30, s32[4,14]{1,0:T(4,128)} %bitcast.32, ...), custom_call_target="tpu_custom_call" | custom-call | bytes 2097152 | tf_op jit(solution)/shard_map/pallas_call | solution.py:90
  3.9 0.5 collective-permute-start.7
  4.4 2.6 %collective-permute-start = (bf16[944,128]{1,0:T(8,128)(2,1)}, bf16[944,128]{1,0:T(8,128)(2,1)S(1)}, u32[]{:S(2)}, u32[]{:S(2)}) collective-permute-start(bf16[944,128]{1,0:T(8,128)(2,1)} %get-tuple-element.18), channel_id=1, source_target_pairs={{0,4},{4,8},{8,12},{12,0},{1,5},{5,9},{9,13},{13,1},{2,6},{6,10},{... | collective-permute-start | bytes 725000 | tf_op jit(solution)/shard_map/ppermute | solution.py:391
  7.1 2.1 %collective-permute-start.5 = (bf16[944,128]{1,0:T(8,128)(2,1)}, bf16[944,128]{1,0:T(8,128)(2,1)S(1)}, u32[]{:S(2)}, u32[]{:S(2)}) collective-permute-start(bf16[944,128]{1,0:T(8,128)(2,1)} %get-tuple-element.25), channel_id=1, source_target_pairs={{0,12},{4,0},{8,4},{12,8},{1,13},{5,1},{9,5},{13,9},{2,14},{6,2},{... | collective-permute-start | bytes 725000 | tf_op jit(solution)/shard_map/ppermute | solution.py:391
  9.2 1.7 %collective-permute-start.4 = (bf16[36,96,128]{2,1,0:T(8,128)(2,1)}, bf16[36,96,128]{2,1,0:T(8,128)(2,1)S(1)}, u32[]{:S(2)}, u32[]{:S(2)}) collective-permute-start(bf16[36,96,128]{2,1,0:T(8,128)(2,1)} %get-tuple-element.24), channel_id=1, source_target_pairs={{0,16},{16,0},{1,17},{17,1},{2,18},{18,2},{3,19},{19,3},{4,20},{20... | collective-permute-start | bytes 2654216 | tf_op jit(solution)/shard_map/ppermute | solution.py:335
  10.8 0.0 copy-done.6
  10.8 0.0 copy-done.5
  10.8 0.2 convert_reduce_fusion.1
  11.0 0.1 select_reduce_fusion
  11.1 0.1 reshape.89
  11.2 0.1 add_add_fusion.refs_1_.refs_11_
  11.3 0.1 add_add_fusion.1.refs_1_
  11.4 0.1 add_add_fusion.2.refs_1_
  11.5 0.1 fusion.1
  11.6 0.1 pad_add_fusion.4.refs_1_.refs_7_
  11.6 0.1 reshape.97
  11.7 0.7 %slice_convert_fusion.2 = s32[1,14]{1,0:T(1,128)S(1)} fusion(bf16[1840,128]{1,0:T(8,128)(2,1)} %get-tuple-element.21.refs_2_.refs_8_), kind=kLoop, calls=%fused_computation.35 | loop fusion | flops 14 | bytes 84 | tf_op jit(solution)/shard_map/convert_element_type | solution.py:400
  12.4 3.7 %collective-permute-done.refs_2_.refs_12_ = bf16[944,128]{1,0:T(8,128)(2,1)S(1)} collective-permute-done((bf16[944,128]{1,0:T(8,128)(2,1)}, bf16[944,128]{1,0:T(8,128)(2,1)S(1)}, u32[]{:S(2)}, u32[]{:S(2)}) %collective-permute-start) | collective-permute-done | bytes 241696 | tf_op jit(solution)/shard_map/ppermute | solution.py:391
  16.1 8.2 %collective-permute-start.1 = (bf16[944,128]{1,0:T(8,128)(2,1)}, bf16[944,128]{1,0:T(8,128)(2,1)S(1)}, u32[]{:S(2)}, u32[]{:S(2)}) collective-permute-start(bf16[944,128]{1,0:T(8,128)(2,1)} %get-tuple-element.19), channel_id=1, source_target_pairs={{0,8},{4,12},{8,0},{12,4},{1,9},{5,13},{9,1},{13,5},{2,10},{6,14},... | collective-permute-start | bytes 725000 | tf_op jit(solution)/shard_map/ppermute | solution.py:391
  24.3 1.5 %collective-permute-start.2 = (bf16[944,128]{1,0:T(8,128)(2,1)S(1)}, bf16[944,128]{1,0:T(8,128)(2,1)S(1)}, u32[]{:S(2)}, u32[]{:S(2)}) collective-permute-start(bf16[944,128]{1,0:T(8,128)(2,1)S(1)} %collective-permute-done.refs_2_.refs_12_), channel_id=1, source_target_pairs={{0,2},{2,0},{1,3},{3,1},{4,6},{6,4},{5,7},{7,5},{8,10},{10,8},{9,1... | collective-permute-start | bytes 725000 | tf_op jit(solution)/shard_map/ppermute | solution.py:335
  25.8 0.7 %fusion.4 = (s32[1,14]{1,0:T(1,128)S(1)}, s32[1,14]{1,0:T(1,128)S(1)}) fusion(pred[4,14]{1,0:T(4,128)(4,1)S(1)} %reshape.97, s32[]{:T(128)S(6)} %select_n.70, s32[]{:T(128)S(6)} %mul.61, bf16[1840,128]{1,0:T(8,128)(2,1)} %get-tuple-element.21.refs_2_.refs_8_, bf16[944,128]{1,0:T(8,128)(2,1)S(1)} %collective-permute-done.refs_2_.refs_12_, s32[]{:T(128)S(6)} %select_n.68), kind=kLoop, calls=%fused_computation.23 | loop fusion | flops 84 | bytes 208 | tf_op jit(solution)/shard_map/jit(_where)/select_n | solution.py:403
  26.5 0.0 collective-permute-done.5.refs_2_
  26.5 0.6 collective-permute-start.6
  27.1 0.0 copy-done.1
  27.1 0.0 copy-done
  27.1 1.0 %copy-done.2 = bf16[1840,128]{1,0:T(8,128)(2,1)S(1)} copy-done((bf16[1840,128]{1,0:T(8,128)(2,1)S(1)}, bf16[1840,128]{1,0:T(8,128)(2,1)}, u32[]{:S(2)}) %copy-start.2) | copy-done | bytes 471064
  28.1 1.3 %shard_map.119.refs_6_ = bf16[4,2,2,32,3072]{4,3,2,1,0:T(8,128)(2,1)S(1)} custom-call(s32[3,14]{1,0:T(4,128)S(1)} %get-tuple-element.38.refs_0_.refs_6_, s32[2]{0:T(128)S(1)} %pad_add_fusion.4.refs_1_.refs_7_, bf16[1840,128]{1,0:T(8,128)(2,1)S(1)} %copy-done.2, bf16[36,96,128]{2,1,0:T(8,128)(2,1)S(1)} %bitcast.20, bf16[36,96,128]{2,1,0:T(8,128)(2,1)S(1)} %bitcast.25), custom_call_target="tpu_custom_call" | custom-call | flops 44040192 | bytes 3145728 | tf_op jit(solution)/shard_map/pallas_call | solution.py:261
  29.5 1.0 %collective-permute-done.2.refs_3_.refs_13_ = bf16[944,128]{1,0:T(8,128)(2,1)S(1)} collective-permute-done((bf16[944,128]{1,0:T(8,128)(2,1)S(1)}, bf16[944,128]{1,0:T(8,128)(2,1)S(1)}, u32[]{:S(2)}, u32[]{:S(2)}) %collective-permute-start.2) | collective-permute-done | bytes 241696 | tf_op jit(solution)/shard_map/ppermute | solution.py:335
  30.4 1.3 %shard_map.120.refs_14_ = bf16[4,2,2,32,3072]{4,3,2,1,0:T(8,128)(2,1)S(1)} custom-call(s32[3,14]{1,0:T(4,128)S(1)} %get-tuple-element.37.refs_0_.refs_10_, s32[3]{0:T(128)S(1)} %add_add_fusion.refs_1_.refs_11_, bf16[944,128]{1,0:T(8,128)(2,1)S(1)} %collective-permute-done.refs_2_.refs_12_, ...), custom_call_target="tpu_custom_call", output_to_operand_aliasing={{}: (6, {})} | custom-call | flops 44040192 | bytes 3145728 | tf_op jit(solution)/shard_map/pallas_call | solution.py:261
  31.8 0.0 collective-permute-done.1.refs_2_
  31.8 1.6 %collective-permute-start.3 = (bf16[944,128]{1,0:T(8,128)(2,1)S(1)}, bf16[944,128]{1,0:T(8,128)(2,1)S(1)}, u32[]{:S(2)}, u32[]{:S(2)}) collective-permute-start(bf16[944,128]{1,0:T(8,128)(2,1)S(1)} %collective-permute-done.1.refs_2_), channel_id=1, source_target_pairs={{0,2},{2,0},{1,3},{3,1},{4,6},{6,4},{5,7},{7,5},{8,10},{10,8},{9,1... | collective-permute-start | bytes 725000 | tf_op jit(solution)/shard_map/ppermute | solution.py:335
  33.4 0.0 collective-permute-done.6.refs_3_
  33.4 0.0 collective-permute-done.4.refs_9_.refs_6_
  33.4 3.3 %shard_map.121.refs_7_ = bf16[4,2,2,32,3072]{4,3,2,1,0:T(8,128)(2,1)S(1)} custom-call(s32[3,14]{1,0:T(4,128)S(1)} %pad_add_fusion.3.refs_0_, s32[3]{0:T(128)S(1)} %add_add_fusion.2.refs_1_, bf16[944,128]{1,0:T(8,128)(2,1)S(1)} %collective-permute-done.5.refs_2_, ...), custom_call_target="tpu_custom_call", output_to_operand_aliasing={{}: (14, {})} | custom-call | flops 176160768 | bytes 12582912 | tf_op jit(solution)/shard_map/pallas_call | solution.py:261
  36.7 0.0 copy-start.3
  36.7 0.0 copy-start.4
  36.7 1.9 %collective-permute-done.3.refs_3_ = bf16[944,128]{1,0:T(8,128)(2,1)S(1)} collective-permute-done((bf16[944,128]{1,0:T(8,128)(2,1)S(1)}, bf16[944,128]{1,0:T(8,128)(2,1)S(1)}, u32[]{:S(2)}, u32[]{:S(2)}) %collective-permute-start.3) | collective-permute-done | bytes 241696 | tf_op jit(solution)/shard_map/ppermute | solution.py:335
  38.6 0.0 collective-permute-done.7.refs_8_
  38.6 9.7 %shard_map.122 = (bf16[4,2,2,32,3072]{4,3,2,1,0:T(8,128)(2,1)S(1)}, bf16[16,16,1024]{2,1,0:T(8,128)(2,1)S(1)}) custom-call(s32[3,14]{1,0:T(4,128)S(1)} %pad_add_fusion.2.refs_0_, s32[3]{0:T(128)S(1)} %add_add_fusion.1.refs_1_, bf16[944,128]{1,0:T(8,128)(2,1)S(1)} %collective-permute-done.1.refs_2_, ...), custom_call_target="tpu_custom_call", output_to_operand_aliasing={{0}: (7, {})} | custom-call | flops 3309305856 | bytes 12582912 | tf_op jit(solution)/shard_map/pallas_call | solution.py:261
  48.3 17.0 %all_to_all.5 = bf16[16,16,1024]{2,1,0:T(8,128)(2,1)S(1)} all-to-all(bf16[16,16,1024]{2,1,0:T(8,128)(2,1)S(1)} %get-tuple-element.28), channel_id=1, replica_groups=mesh['grp'=2,'band'=4,'var'=2,'sub'=2] {'grp','band','var'}, dimensions={0} | all-to-all | bytes 1048576 | tf_op jit(solution)/shard_map/all_to_all | solution.py:440
  65.3 0.1 convert_reduce_fusion
  65.4 0.0 copy-done.3
  65.4 0.1 multiply_reduce_fusion
  65.5 0.1 rsqrt.12
  65.6 0.0 copy-done.4
  65.6 0.1 fusion
  65.7 0.6 copy.18
  (16 shorter events, 0.1 us)
Async XLA Ops:
  0.0 27.1 %copy-start.1 = (bf16[36,4,24,128]{3,2,1,0:T(8,128)(2,1)S(1)}, bf16[36,4,24,128]{3,2,1,0:T(8,128)(2,1)}, u32[]{:S(2)}) copy-start(bf16[36,4,24,128]{3,2,1,0:T(8,128)(2,1)} %param.16) | copy-start | bytes 2654212
  0.0 27.1 %copy-start = (bf16[36,4,24,128]{3,2,1,0:T(8,128)(2,1)S(1)}, bf16[36,4,24,128]{3,2,1,0:T(8,128)(2,1)}, u32[]{:S(2)}) copy-start(bf16[36,4,24,128]{3,2,1,0:T(8,128)(2,1)} %param.12) | copy-start | bytes 2654212
  0.0 10.8 %copy-start.6 = (s32[36,1]{0,1:T(1,128)S(1)}, s32[36,1]{0,1:T(1,128)}, u32[]{:S(2)}) copy-start(s32[36,1]{0,1:T(1,128)} %param.17) | copy-start | bytes 436
  0.0 10.8 %copy-start.5 = (s32[36,1]{0,1:T(1,128)S(1)}, s32[36,1]{0,1:T(1,128)}, u32[]{:S(2)}) copy-start(s32[36,1]{0,1:T(1,128)} %param.13) | copy-start | bytes 436
  3.9 34.7 %collective-permute-start.7 = (bf16[3072,1024]{1,0:T(8,128)(2,1)}, bf16[3072,1024]{1,0:T(8,128)(2,1)}, u32[]{:S(2)}, u32[]{:S(2)}) collective-permute-start(bf16[3072,1024]{1,0:T(8,128)(2,1)} %refs_9_.1), channel_id=1, source_target_pairs={{0,1},{1,0},{2,3},{3,2},{4,5},{5,4},{6,7},{7,6},{8,9},{9,8},{10,11... | collective-permute-start | bytes 18874376 | tf_op jit(solution)/shard_map/ppermute | solution.py:335
  4.4 11.6 %collective-permute-start = (bf16[944,128]{1,0:T(8,128)(2,1)}, bf16[944,128]{1,0:T(8,128)(2,1)S(1)}, u32[]{:S(2)}, u32[]{:S(2)}) collective-permute-start(bf16[944,128]{1,0:T(8,128)(2,1)} %get-tuple-element.18), channel_id=1, source_target_pairs={{0,4},{4,8},{8,12},{12,0},{1,5},{5,9},{9,13},{13,1},{2,6},{6,10},{... | collective-permute-start | bytes 725000 | tf_op jit(solution)/shard_map/ppermute | solution.py:391
  7.1 19.4 %collective-permute-start.5 = (bf16[944,128]{1,0:T(8,128)(2,1)}, bf16[944,128]{1,0:T(8,128)(2,1)S(1)}, u32[]{:S(2)}, u32[]{:S(2)}) collective-permute-start(bf16[944,128]{1,0:T(8,128)(2,1)} %get-tuple-element.25), channel_id=1, source_target_pairs={{0,12},{4,0},{8,4},{12,8},{1,13},{5,1},{9,5},{13,9},{2,14},{6,2},{... | collective-permute-start | bytes 725000 | tf_op jit(solution)/shard_map/ppermute | solution.py:391
  9.2 24.2 %collective-permute-start.4 = (bf16[36,96,128]{2,1,0:T(8,128)(2,1)}, bf16[36,96,128]{2,1,0:T(8,128)(2,1)S(1)}, u32[]{:S(2)}, u32[]{:S(2)}) collective-permute-start(bf16[36,96,128]{2,1,0:T(8,128)(2,1)} %get-tuple-element.24), channel_id=1, source_target_pairs={{0,16},{16,0},{1,17},{17,1},{2,18},{18,2},{3,19},{19,3},{4,20},{20... | collective-permute-start | bytes 2654216 | tf_op jit(solution)/shard_map/ppermute | solution.py:335
  16.1 15.7 %collective-permute-start.1 = (bf16[944,128]{1,0:T(8,128)(2,1)}, bf16[944,128]{1,0:T(8,128)(2,1)S(1)}, u32[]{:S(2)}, u32[]{:S(2)}) collective-permute-start(bf16[944,128]{1,0:T(8,128)(2,1)} %get-tuple-element.19), channel_id=1, source_target_pairs={{0,8},{4,12},{8,0},{12,4},{1,9},{5,13},{9,1},{13,5},{2,10},{6,14},... | collective-permute-start | bytes 725000 | tf_op jit(solution)/shard_map/ppermute | solution.py:391
  24.3 6.2 %collective-permute-start.2 = (bf16[944,128]{1,0:T(8,128)(2,1)S(1)}, bf16[944,128]{1,0:T(8,128)(2,1)S(1)}, u32[]{:S(2)}, u32[]{:S(2)}) collective-permute-start(bf16[944,128]{1,0:T(8,128)(2,1)S(1)} %collective-permute-done.refs_2_.refs_12_), channel_id=1, source_target_pairs={{0,2},{2,0},{1,3},{3,1},{4,6},{6,4},{5,7},{7,5},{8,10},{10,8},{9,1... | collective-permute-start | bytes 725000 | tf_op jit(solution)/shard_map/ppermute | solution.py:335
  26.5 6.9 %collective-permute-start.6 = (bf16[944,128]{1,0:T(8,128)(2,1)S(1)}, bf16[944,128]{1,0:T(8,128)(2,1)S(1)}, u32[]{:S(2)}, u32[]{:S(2)}) collective-permute-start(bf16[944,128]{1,0:T(8,128)(2,1)S(1)} %collective-permute-done.5.refs_2_), channel_id=1, source_target_pairs={{0,2},{2,0},{1,3},{3,1},{4,6},{6,4},{5,7},{7,5},{8,10},{10,8},{9,1... | collective-permute-start | bytes 725000 | tf_op jit(solution)/shard_map/ppermute | solution.py:335
  27.1 1.0 %copy-start.2 = (bf16[1840,128]{1,0:T(8,128)(2,1)S(1)}, bf16[1840,128]{1,0:T(8,128)(2,1)}, u32[]{:S(2)}) copy-start(bf16[1840,128]{1,0:T(8,128)(2,1)} %get-tuple-element.21.refs_2_.refs_8_) | copy-start | bytes 1413124
  31.8 6.8 %collective-permute-start.3 = (bf16[944,128]{1,0:T(8,128)(2,1)S(1)}, bf16[944,128]{1,0:T(8,128)(2,1)S(1)}, u32[]{:S(2)}, u32[]{:S(2)}) collective-permute-start(bf16[944,128]{1,0:T(8,128)(2,1)S(1)} %collective-permute-done.1.refs_2_), channel_id=1, source_target_pairs={{0,2},{2,0},{1,3},{3,1},{4,6},{6,4},{5,7},{7,5},{8,10},{10,8},{9,1... | collective-permute-start | bytes 725000 | tf_op jit(solution)/shard_map/ppermute | solution.py:335
  36.7 28.7 %copy-start.3 = (f32[1024]{0:T(1024)S(1)}, f32[1024]{0:T(1024)}, u32[]{:S(2)}) copy-start(f32[1024]{0:T(1024)} %param.22) | copy-start | bytes 12292
  36.7 28.9 %copy-start.4 = (f32[1024]{0:T(1024)S(1)}, f32[1024]{0:T(1024)}, u32[]{:S(2)}) copy-start(f32[1024]{0:T(1024)} %param.23) | copy-start | bytes 12292

commit v10 on v9

--- a/solution.py
+++ b/solution.py
@@ -8,8 +8,6 @@
 from jax.sharding import PartitionSpec as P
 
 REPL = ("grp", "var")
-PACK_LIMIT = 60 << 20
-FINISH_LIMIT = 36 << 20
 
 
 def slot_tables(dest, band_count, cap):
@@ -81,7 +79,7 @@
         load.wait()
 
 
-def pack(pieces, ocean_w, atmos_w, ocean_ids, atmos_ids, land, *fields):
+def pack(limit, pieces, ocean_w, atmos_w, ocean_ids, atmos_ids, land, *fields):
     cells, tiles = land.shape[-1], land.shape[0]
     any_spec = pl.BlockSpec(memory_space=pl.ANY)
     vmem = pl.BlockSpec(memory_space=pltpu.VMEM)
@@ -94,7 +92,7 @@
         out_specs=[vmem] * len(shapes),
         scratch_shapes=[pltpu.SemaphoreType.DMA((len(shapes),))],
         cost_estimate=pl.CostEstimate(flops=0, bytes_accessed=2 << 20, transcendentals=0),
-        compiler_params=pltpu.CompilerParams(vmem_limit_bytes=PACK_LIMIT),
+        compiler_params=pltpu.CompilerParams(vmem_limit_bytes=limit << 20),
     )(ocean_w, atmos_w, ocean_ids, atmos_ids, land, *fields)
 
 
@@ -157,35 +155,26 @@
 def finish_kernel(steps, halves, jobs, count, *refs):
     theirs, mine, rows_x, out, acc, scale, weight, total, sem = refs[count:]
     sub, mine_group = lax.axis_index("sub"), lax.axis_index("grp")
-    chunks = sem.shape[0]
-    height = mine.shape[0] // chunks
-
-    def span(chunk):
-        return pl.ds(pl.multiple_of(chunk * height, height), height)
-
-    def copy(chunk):
-        return pltpu.make_async_copy(
-            mine.at[span(chunk), :], weight.at[span(chunk), :], sem.at[chunk]
-        )
-
-    def add(chunk, place, source):
-        left = rows_x[:, :, place, :, span(chunk)].reshape(total.shape[0], height)
-        total[...] += jnp.dot(left, source[span(chunk), :], preferred_element_type=jnp.float32)
-
-    for chunk in range(chunks):
-        copy(chunk).start()
+    blocks = sem.shape[0]
+    width = mine.shape[1] // blocks
+
+    def copy(block):
+        span = pl.ds(block * width, width)
+        return pltpu.make_async_copy(mine.at[:, span], weight.at[:, span], sem.at[block])
+
+    for block in range(blocks):
+        copy(block).start()
     run_jobs(steps, jobs, refs, rows_x, acc, scale)
-    total[...] = jnp.zeros_like(total)
-
-    @pl.loop(0, chunks)
-    def _(chunk):
-        add(chunk, 1 - sub, theirs)
-
-    @pl.loop(0, chunks)
-    def _(chunk):
-        copy(chunk).wait()
-        add(chunk, sub, weight)
-
+    for block in range(blocks):
+        span = pl.ds(block * width, width)
+        left, right = (
+            rows_x[:, :, place].reshape(total.shape[0], mine.shape[0]) for place in (1 - sub, sub)
+        )
+        some = jnp.dot(left, theirs[:, span], preferred_element_type=jnp.float32)
+        copy(block).wait()
+        total[:, span] = some + jnp.dot(
+            right, weight[:, span], preferred_element_type=jnp.float32
+        )
     send_rows(steps, halves, rows_x.shape, mine_group, total, out)
 
 
@@ -254,9 +243,9 @@
         scratch += [
             pltpu.VMEM((height, width), jnp.bfloat16),
             pltpu.VMEM((total, width), jnp.float32),
-            pltpu.SemaphoreType.DMA((6,)),
+            pltpu.SemaphoreType.DMA((4,)),
         ]
-        limit, moved = FINISH_LIMIT, 4 * height * width
+        limit, moved = 36 << 20, 4 * height * width
         flops += 4 * total * height * width
     done = pl.pallas_call(
         body,
@@ -381,20 +370,20 @@
         pieces = []
         for shift in order:
             pieces.append((shift, 0, each, each))
-        *packed, own_w, send = pack(
-            pieces + [(0, 0, cap, None)], ocean_w, atmos_w, ocean_ids, atmos_ids, land, ocean_f, atmos_f
+        *packed, send = pack(
+            60, pieces, ocean_w, atmos_w, ocean_ids, atmos_ids, land, ocean_f, atmos_f
         )
         sent = []
         for at, (piece, (shift, _, _, _)) in enumerate(zip(packed, pieces)):
             if at >= 2:
                 piece, sent[at - 2] = lax.optimization_barrier((piece, sent[at - 2]))
             sent.append(lax.ppermute(piece, "band", along(shift)))
-        embed_other, send = lax.optimization_barrier((embed_weight, send))
+        embed_other, own_land, send = lax.optimization_barrier((embed_weight, land, send))
+        own_w = pack(54, [(0, 0, cap, None)], ocean_w, atmos_w, ocean_ids, atmos_ids, own_land)[0]
         embed_other = swap(embed_other, "sub")
         keep, theirs = (ocean_f, atmos_f), (swap(send, "grp"),)
         dest = jnp.where(y == 0, ocean_dest, atmos_dest)
         block_all, used_all = slot_tables(dest, nb, cap)
-
         def job_of(band, parts, sizes, firsts, fields):
             meta_at = sizes[0] * cells
             tile = parts[0][meta_at + 2 * tiles, :cap].astype(jnp.int32)

time: 66.7 us -> 71.2 us (1.067)
  Pallas kernels: 19.5 us -> 26 us
  waiting for transfers between devices: 6.5 us -> 4.15 us
    pallas_call x4, Pallas kernels: 15.6 us -> 20 us  [regrid(): pl.pallas_call(body, out_shape=shapes, in_specs=specs, out_specs=[vmem] *...]
    ppermute x3, waiting for transfers between devices: 3.66 us -> 1.12 us  [per_device(): sent.append(lax.ppermute(piece, 'band', along(shift)))]
    pallas_call x1 -> x2, Pallas kernels: 3.88 us -> 6.04 us  [pack(): pl.pallas_call(functools.partial(pack_kernel, pieces, len(fields) // 2),...]
  transfers between devices with their start and end apart: 8 -> 8, of which waited for: 3 -> 3; matrix products, arithmetic and copies ran while one was open for 3% -> 3% of each run, Pallas kernels for 9% -> 12%
where the time goes in v10:
time: 71.2 us; the launch traced here: 70.7 us
  Pallas kernels  26 us (37%)
  starting transfers between devices  18.8 us (26%)
  blocking collectives  17.2 us (24%)
  waiting for transfers between devices  4.15 us (6%)
  other arithmetic  2.39 us (3%)
  local copies, waits for them, and re-layouts  1.99 us (3%)
    pallas_call x4, Pallas kernels, regrid(): pl.pallas_call(body, out_shape=shapes, in_specs=specs, out_specs=[vmem] *...  20 us
    all_to_all x1, blocking collectives, per_device(): lax.all_to_all(sent, ('grp', 'band', 'var'), split_axis=0, concat_axis=0,...  17.2 us
    ppermute x3, starting transfers between devices, per_device(): sent.append(lax.ppermute(piece, 'band', along(shift)))  13 us
    pallas_call x2, Pallas kernels, pack(): pl.pallas_call(functools.partial(pack_kernel, pieces, len(fields) // 2),...  6.04 us
    ppermute x5, starting transfers between devices, swap(): return lax.ppermute(x, axis, [(0, 1), (1, 0)])  5.83 us
    ppermute x5, waiting for transfers between devices, swap(): return lax.ppermute(x, axis, [(0, 1), (1, 0)])  3.03 us
  transfers between devices with their start and end apart: 8, of which 3 were waited for; matrix products, arithmetic and copies ran while one was open for 3% of the time, Pallas kernels for 12%

profile of v10, /device:TPU:0, one launch (start us, length us, event | category | flops | bytes accessed | tf_op | source)
XLA Modules:
  0.0 70.7 jit_solution(14608403942963149812)
XLA Ops:
  0.0 3.5 %shard_map.118 = (bf16[944,128]{1,0:T(8,128)(2,1)}, bf16[944,128]{1,0:T(8,128)(2,1)}, bf16[944,128]{1,0:T(8,128)(2,1)}, bf16[36,96,128]{2,1,0:T(8,128)(2,1)}) custom-call(bf16[4,1792,128]{2,1,0:T(8,128)(2,1)} %bitcast.29, bf16[4,1792,128]{2,1,0:T(8,128)(2,1)} %bitcast.31, s32[4,14]{1,0:T(4,128)} %bitcast.35, s32[4,14]{1,0:T(4,128)} %bitcast.37, ...), custom_call_target="tpu_custom_call" | custom-call | bytes 2097152 | tf_op jit(solution)/shard_map/pallas_call | solution.py:88
  3.5 0.0 copy-start.8
  3.5 0.0 copy-start
  3.5 0.0 copy-start.1
  3.5 0.5 collective-permute-start.7
  4.1 2.6 %collective-permute-start = (bf16[944,128]{1,0:T(8,128)(2,1)}, bf16[944,128]{1,0:T(8,128)(2,1)S(1)}, u32[]{:S(2)}, u32[]{:S(2)}) collective-permute-start(bf16[944,128]{1,0:T(8,128)(2,1)} %get-tuple-element.18), channel_id=1, source_target_pairs={{0,4},{4,8},{8,12},{12,0},{1,5},{5,9},{9,13},{13,1},{2,6},{6,10},{... | collective-permute-start | bytes 725000 | tf_op jit(solution)/shard_map/ppermute | solution.py:380
  6.7 2.1 %collective-permute-start.5 = (bf16[944,128]{1,0:T(8,128)(2,1)}, bf16[944,128]{1,0:T(8,128)(2,1)S(1)}, u32[]{:S(2)}, u32[]{:S(2)}) collective-permute-start(bf16[944,128]{1,0:T(8,128)(2,1)} %get-tuple-element.25), channel_id=1, source_target_pairs={{0,12},{4,0},{8,4},{12,8},{1,13},{5,1},{9,5},{13,9},{2,14},{6,2},{... | collective-permute-start | bytes 725000 | tf_op jit(solution)/shard_map/ppermute | solution.py:380
  8.8 1.7 %collective-permute-start.4 = (bf16[36,96,128]{2,1,0:T(8,128)(2,1)}, bf16[36,96,128]{2,1,0:T(8,128)(2,1)S(1)}, u32[]{:S(2)}, u32[]{:S(2)}) collective-permute-start(bf16[36,96,128]{2,1,0:T(8,128)(2,1)} %get-tuple-element.24), channel_id=1, source_target_pairs={{0,16},{16,0},{1,17},{17,1},{2,18},{18,2},{3,19},{19,3},{4,20},{20... | collective-permute-start | bytes 2654216 | tf_op jit(solution)/shard_map/ppermute | solution.py:324
  10.5 0.0 copy-done.7
  10.5 0.2 convert_reduce_fusion.1
  10.7 0.1 select_reduce_fusion
  10.8 0.1 reshape.89
  10.9 0.1 add_add_fusion.refs_1_.refs_11_
  10.9 0.1 add_add_fusion.1.refs_1_
  11.0 0.1 add_add_fusion.2.refs_1_
  11.1 0.1 fusion.1
  11.2 0.1 pad_add_fusion.4.refs_1_.refs_7_
  11.3 0.1 reshape.97
  11.4 2.5 %shard_map.119.refs_2_.refs_8_ = bf16[1840,128]{1,0:T(8,128)(2,1)} custom-call(bf16[4,1792,128]{2,1,0:T(8,128)(2,1)} %bitcast.30, bf16[4,1792,128]{2,1,0:T(8,128)(2,1)} %bitcast.32, s32[4,14]{1,0:T(4,128)} %bitcast.36, s32[4,14]{1,0:T(4,128)} %bitcast.38, f32[16,128]{1,0:T(8,128)} %bitcast.34), custom_call_target="tpu_custom_call" | custom-call | bytes 2097152 | tf_op jit(solution)/shard_map/pallas_call | solution.py:88
  13.9 0.7 slice_convert_fusion.1
  14.6 1.1 %collective-permute-done.refs_2_.refs_12_ = bf16[944,128]{1,0:T(8,128)(2,1)S(1)} collective-permute-done((bf16[944,128]{1,0:T(8,128)(2,1)}, bf16[944,128]{1,0:T(8,128)(2,1)S(1)}, u32[]{:S(2)}, u32[]{:S(2)}) %collective-permute-start) | collective-permute-done | bytes 241696 | tf_op jit(solution)/shard_map/ppermute | solution.py:380
  15.7 0.0 copy-done.8
  15.7 8.2 %collective-permute-start.1 = (bf16[944,128]{1,0:T(8,128)(2,1)S(1)}, bf16[944,128]{1,0:T(8,128)(2,1)S(1)}, u32[]{:S(2)}, u32[]{:S(2)}) collective-permute-start(bf16[944,128]{1,0:T(8,128)(2,1)S(1)} %copy-done.8), channel_id=1, source_target_pairs={{0,8},{4,12},{8,0},{12,4},{1,9},{5,13},{9,1},{13,5},{2,10},{6,14},... | collective-permute-start | bytes 725000 | tf_op jit(solution)/shard_map/ppermute | solution.py:380
  23.9 1.5 %collective-permute-start.2 = (bf16[944,128]{1,0:T(8,128)(2,1)S(1)}, bf16[944,128]{1,0:T(8,128)(2,1)S(1)}, u32[]{:S(2)}, u32[]{:S(2)}) collective-permute-start(bf16[944,128]{1,0:T(8,128)(2,1)S(1)} %collective-permute-done.refs_2_.refs_12_), channel_id=1, source_target_pairs={{0,2},{2,0},{1,3},{3,1},{4,6},{6,4},{5,7},{7,5},{8,10},{10,8},{9,1... | collective-permute-start | bytes 725000 | tf_op jit(solution)/shard_map/ppermute | solution.py:324
  25.4 0.7 fusion.4
  26.1 0.0 collective-permute-done.5.refs_2_
  26.1 0.6 collective-permute-start.6
  26.7 1.0 %copy-done.2 = bf16[1840,128]{1,0:T(8,128)(2,1)S(1)} copy-done((bf16[1840,128]{1,0:T(8,128)(2,1)S(1)}, bf16[1840,128]{1,0:T(8,128)(2,1)}, u32[]{:S(2)}) %copy-start.2) | copy-done | bytes 471064
  27.8 1.3 %shard_map.120.refs_6_ = bf16[4,2,2,32,3072]{4,3,2,1,0:T(8,128)(2,1)S(1)} custom-call(s32[3,14]{1,0:T(4,128)S(1)} %get-tuple-element.38.refs_0_.refs_6_, s32[2]{0:T(128)S(1)} %pad_add_fusion.4.refs_1_.refs_7_, bf16[1840,128]{1,0:T(8,128)(2,1)S(1)} %copy-done.2, bf16[36,96,128]{2,1,0:T(8,128)(2,1)S(1)} %bitcast.20, bf16[36,96,128]{2,1,0:T(8,128)(2,1)S(1)} %bitcast.25), custom_call_target="tpu_custom_call" | custom-call | flops 44040192 | bytes 3145728 | tf_op jit(solution)/shard_map/pallas_call | solution.py:250
  29.1 1.0 %collective-permute-done.2.refs_3_.refs_13_ = bf16[944,128]{1,0:T(8,128)(2,1)S(1)} collective-permute-done((bf16[944,128]{1,0:T(8,128)(2,1)S(1)}, bf16[944,128]{1,0:T(8,128)(2,1)S(1)}, u32[]{:S(2)}, u32[]{:S(2)}) %collective-permute-start.2) | collective-permute-done | bytes 241696 | tf_op jit(solution)/shard_map/ppermute | solution.py:324
  30.1 1.3 %shard_map.121.refs_14_ = bf16[4,2,2,32,3072]{4,3,2,1,0:T(8,128)(2,1)S(1)} custom-call(s32[3,14]{1,0:T(4,128)S(1)} %get-tuple-element.37.refs_0_.refs_10_, s32[3]{0:T(128)S(1)} %add_add_fusion.refs_1_.refs_11_, bf16[944,128]{1,0:T(8,128)(2,1)S(1)} %collective-permute-done.refs_2_.refs_12_, ...), custom_call_target="tpu_custom_call", output_to_operand_aliasing={{}: (6, {})} | custom-call | flops 44040192 | bytes 3145728 | tf_op jit(solution)/shard_map/pallas_call | solution.py:250
  31.4 0.0 collective-permute-done.1.refs_2_
  31.4 1.6 %collective-permute-start.3 = (bf16[944,128]{1,0:T(8,128)(2,1)S(1)}, bf16[944,128]{1,0:T(8,128)(2,1)S(1)}, u32[]{:S(2)}, u32[]{:S(2)}) collective-permute-start(bf16[944,128]{1,0:T(8,128)(2,1)S(1)} %collective-permute-done.1.refs_2_), channel_id=1, source_target_pairs={{0,2},{2,0},{1,3},{3,1},{4,6},{6,4},{5,7},{7,5},{8,10},{10,8},{9,1... | collective-permute-start | bytes 725000 | tf_op jit(solution)/shard_map/ppermute | solution.py:324
  33.0 0.0 collective-permute-done.6.refs_3_
  33.0 0.0 collective-permute-done.4.refs_9_.refs_6_
  33.1 3.3 %shard_map.122.refs_7_ = bf16[4,2,2,32,3072]{4,3,2,1,0:T(8,128)(2,1)S(1)} custom-call(s32[3,14]{1,0:T(4,128)S(1)} %pad_add_fusion.3.refs_0_, s32[3]{0:T(128)S(1)} %add_add_fusion.2.refs_1_, bf16[944,128]{1,0:T(8,128)(2,1)S(1)} %collective-permute-done.5.refs_2_, ...), custom_call_target="tpu_custom_call", output_to_operand_aliasing={{}: (14, {})} | custom-call | flops 176160768 | bytes 12582912 | tf_op jit(solution)/shard_map/pallas_call | solution.py:250
  36.3 0.0 copy-start.4
  36.4 0.0 copy-start.5
  36.4 2.0 %collective-permute-done.3.refs_3_ = bf16[944,128]{1,0:T(8,128)(2,1)S(1)} collective-permute-done((bf16[944,128]{1,0:T(8,128)(2,1)S(1)}, bf16[944,128]{1,0:T(8,128)(2,1)S(1)}, u32[]{:S(2)}, u32[]{:S(2)}) %collective-permute-start.3) | collective-permute-done | bytes 241696 | tf_op jit(solution)/shard_map/ppermute | solution.py:324
  38.4 0.0 collective-permute-done.7.refs_8_
  38.4 14.1 %shard_map.123 = (bf16[4,2,2,32,3072]{4,3,2,1,0:T(8,128)(2,1)S(1)}, bf16[16,16,1024]{2,1,0:T(8,128)(2,1)S(1)}) custom-call(s32[3,14]{1,0:T(4,128)S(1)} %pad_add_fusion.2.refs_0_, s32[3]{0:T(128)S(1)} %add_add_fusion.1.refs_1_, bf16[944,128]{1,0:T(8,128)(2,1)S(1)} %collective-permute-done.1.refs_2_, ...), custom_call_target="tpu_custom_call", output_to_operand_aliasing={{0}: (7, {})} | custom-call | flops 3309305856 | bytes 12582912 | tf_op jit(solution)/shard_map/pallas_call | solution.py:250
  52.5 17.2 %all_to_all.5 = bf16[16,16,1024]{2,1,0:T(8,128)(2,1)S(1)} all-to-all(bf16[16,16,1024]{2,1,0:T(8,128)(2,1)S(1)} %get-tuple-element.28), channel_id=1, replica_groups=mesh['grp'=2,'band'=4,'var'=2,'sub'=2] {'grp','band','var'}, dimensions={0} | all-to-all | bytes 1048576 | tf_op jit(solution)/shard_map/all_to_all | solution.py:429
  69.7 0.1 convert_reduce_fusion
  69.8 0.1 multiply_reduce_fusion
  69.9 0.1 rsqrt.12
  70.0 0.0 copy-done.5
  70.0 0.1 fusion
  70.1 0.6 copy.18
  (21 shorter events, 0.1 us)
Async XLA Ops:
  0.0 10.5 %copy-start.7 = (s32[36,1]{0,1:T(1,128)S(1)}, s32[36,1]{0,1:T(1,128)}, u32[]{:S(2)}) copy-start(s32[36,1]{0,1:T(1,128)} %param.17) | copy-start | bytes 436
  0.0 10.5 %copy-start.6 = (s32[36,1]{0,1:T(1,128)S(1)}, s32[36,1]{0,1:T(1,128)}, u32[]{:S(2)}) copy-start(s32[36,1]{0,1:T(1,128)} %param.13) | copy-start | bytes 436
  3.5 12.2 %copy-start.8 = (bf16[944,128]{1,0:T(8,128)(2,1)S(1)}, bf16[944,128]{1,0:T(8,128)(2,1)}, u32[]{:S(2)}) copy-start(bf16[944,128]{1,0:T(8,128)(2,1)} %get-tuple-element.19) | copy-start | bytes 724996
  3.5 23.2 %copy-start = (bf16[36,4,24,128]{3,2,1,0:T(8,128)(2,1)S(1)}, bf16[36,4,24,128]{3,2,1,0:T(8,128)(2,1)}, u32[]{:S(2)}) copy-start(bf16[36,4,24,128]{3,2,1,0:T(8,128)(2,1)} %param.12) | copy-start | bytes 2654212
  3.5 23.2 %copy-start.1 = (bf16[36,4,24,128]{3,2,1,0:T(8,128)(2,1)S(1)}, bf16[36,4,24,128]{3,2,1,0:T(8,128)(2,1)}, u32[]{:S(2)}) copy-start(bf16[36,4,24,128]{3,2,1,0:T(8,128)(2,1)} %param.16) | copy-start | bytes 2654212
  3.5 34.9 %collective-permute-start.7 = (bf16[3072,1024]{1,0:T(8,128)(2,1)}, bf16[3072,1024]{1,0:T(8,128)(2,1)}, u32[]{:S(2)}, u32[]{:S(2)}) collective-permute-start(bf16[3072,1024]{1,0:T(8,128)(2,1)} %refs_9_.1), channel_id=1, source_target_pairs={{0,1},{1,0},{2,3},{3,2},{4,5},{5,4},{6,7},{7,6},{8,9},{9,8},{10,11... | collective-permute-start | bytes 18874376 | tf_op jit(solution)/shard_map/ppermute | solution.py:324
  4.1 11.6 %collective-permute-start = (bf16[944,128]{1,0:T(8,128)(2,1)}, bf16[944,128]{1,0:T(8,128)(2,1)S(1)}, u32[]{:S(2)}, u32[]{:S(2)}) collective-permute-start(bf16[944,128]{1,0:T(8,128)(2,1)} %get-tuple-element.18), channel_id=1, source_target_pairs={{0,4},{4,8},{8,12},{12,0},{1,5},{5,9},{9,13},{13,1},{2,6},{6,10},{... | collective-permute-start | bytes 725000 | tf_op jit(solution)/shard_map/ppermute | solution.py:380
  6.7 19.4 %collective-permute-start.5 = (bf16[944,128]{1,0:T(8,128)(2,1)}, bf16[944,128]{1,0:T(8,128)(2,1)S(1)}, u32[]{:S(2)}, u32[]{:S(2)}) collective-permute-start(bf16[944,128]{1,0:T(8,128)(2,1)} %get-tuple-element.25), channel_id=1, source_target_pairs={{0,12},{4,0},{8,4},{12,8},{1,13},{5,1},{9,5},{13,9},{2,14},{6,2},{... | collective-permute-start | bytes 725000 | tf_op jit(solution)/shard_map/ppermute | solution.py:380
  8.8 24.2 %collective-permute-start.4 = (bf16[36,96,128]{2,1,0:T(8,128)(2,1)}, bf16[36,96,128]{2,1,0:T(8,128)(2,1)S(1)}, u32[]{:S(2)}, u32[]{:S(2)}) collective-permute-start(bf16[36,96,128]{2,1,0:T(8,128)(2,1)} %get-tuple-element.24), channel_id=1, source_target_pairs={{0,16},{16,0},{1,17},{17,1},{2,18},{18,2},{3,19},{19,3},{4,20},{20... | collective-permute-start | bytes 2654216 | tf_op jit(solution)/shard_map/ppermute | solution.py:324
  15.7 15.7 %collective-permute-start.1 = (bf16[944,128]{1,0:T(8,128)(2,1)S(1)}, bf16[944,128]{1,0:T(8,128)(2,1)S(1)}, u32[]{:S(2)}, u32[]{:S(2)}) collective-permute-start(bf16[944,128]{1,0:T(8,128)(2,1)S(1)} %copy-done.8), channel_id=1, source_target_pairs={{0,8},{4,12},{8,0},{12,4},{1,9},{5,13},{9,1},{13,5},{2,10},{6,14},... | collective-permute-start | bytes 725000 | tf_op jit(solution)/shard_map/ppermute | solution.py:380
  23.9 6.2 %collective-permute-start.2 = (bf16[944,128]{1,0:T(8,128)(2,1)S(1)}, bf16[944,128]{1,0:T(8,128)(2,1)S(1)}, u32[]{:S(2)}, u32[]{:S(2)}) collective-permute-start(bf16[944,128]{1,0:T(8,128)(2,1)S(1)} %collective-permute-done.refs_2_.refs_12_), channel_id=1, source_target_pairs={{0,2},{2,0},{1,3},{3,1},{4,6},{6,4},{5,7},{7,5},{8,10},{10,8},{9,1... | collective-permute-start | bytes 725000 | tf_op jit(solution)/shard_map/ppermute | solution.py:324
  26.1 6.9 %collective-permute-start.6 = (bf16[944,128]{1,0:T(8,128)(2,1)S(1)}, bf16[944,128]{1,0:T(8,128)(2,1)S(1)}, u32[]{:S(2)}, u32[]{:S(2)}) collective-permute-start(bf16[944,128]{1,0:T(8,128)(2,1)S(1)} %collective-permute-done.5.refs_2_), channel_id=1, source_target_pairs={{0,2},{2,0},{1,3},{3,1},{4,6},{6,4},{5,7},{7,5},{8,10},{10,8},{9,1... | collective-permute-start | bytes 725000 | tf_op jit(solution)/shard_map/ppermute | solution.py:324
  26.7 1.0 %copy-start.2 = (bf16[1840,128]{1,0:T(8,128)(2,1)S(1)}, bf16[1840,128]{1,0:T(8,128)(2,1)}, u32[]{:S(2)}) copy-start(bf16[1840,128]{1,0:T(8,128)(2,1)} %shard_map.119.refs_2_.refs_8_) | copy-start | bytes 1413124
  30.1 3.0 %copy-start.3 = (bf16[1840,128]{1,0:T(8,128)(2,1)S(1)}, bf16[1840,128]{1,0:T(8,128)(2,1)}, u32[]{:S(2)}) copy-start(bf16[1840,128]{1,0:T(8,128)(2,1)} %shard_map.119.refs_2_.refs_8_) | copy-start | bytes 1413124
  31.4 7.0 %collective-permute-start.3 = (bf16[944,128]{1,0:T(8,128)(2,1)S(1)}, bf16[944,128]{1,0:T(8,128)(2,1)S(1)}, u32[]{:S(2)}, u32[]{:S(2)}) collective-permute-start(bf16[944,128]{1,0:T(8,128)(2,1)S(1)} %collective-permute-done.1.refs_2_), channel_id=1, source_target_pairs={{0,2},{2,0},{1,3},{3,1},{4,6},{6,4},{5,7},{7,5},{8,10},{10,8},{9,1... | collective-permute-start | bytes 725000 | tf_op jit(solution)/shard_map/ppermute | solution.py:324
  36.3 33.4 %copy-start.4 = (f32[1024]{0:T(1024)S(1)}, f32[1024]{0:T(1024)}, u32[]{:S(2)}) copy-start(f32[1024]{0:T(1024)} %param.22) | copy-start | bytes 12292
  36.4 33.6 %copy-start.5 = (f32[1024]{0:T(1024)S(1)}, f32[1024]{0:T(1024)}, u32[]{:S(2)}) copy-start(f32[1024]{0:T(1024)} %param.23) | copy-start | bytes 12292

commit v11 on v10

--- a/solution.py
+++ b/solution.py
@@ -155,26 +155,29 @@
 def finish_kernel(steps, halves, jobs, count, *refs):
     theirs, mine, rows_x, out, acc, scale, weight, total, sem = refs[count:]
     sub, mine_group = lax.axis_index("sub"), lax.axis_index("grp")
-    blocks = sem.shape[0]
-    width = mine.shape[1] // blocks
-
-    def copy(block):
-        span = pl.ds(block * width, width)
-        return pltpu.make_async_copy(mine.at[:, span], weight.at[:, span], sem.at[block])
-
-    for block in range(blocks):
-        copy(block).start()
+    chunks = sem.shape[0]
+    height = mine.shape[0] // chunks
+
+    def copy(chunk):
+        span = pl.ds(pl.multiple_of(chunk * height, height), height)
+        return pltpu.make_async_copy(mine.at[span, :], weight.at[span, :], sem.at[chunk])
+
+    for chunk in range(chunks):
+        copy(chunk).start()
     run_jobs(steps, jobs, refs, rows_x, acc, scale)
-    for block in range(blocks):
-        span = pl.ds(block * width, width)
+    total[...] = jnp.zeros_like(total)
+
+    @pl.loop(0, chunks)
+    def _(chunk):
+        span = pl.ds(pl.multiple_of(chunk * height, height), height)
         left, right = (
-            rows_x[:, :, place].reshape(total.shape[0], mine.shape[0]) for place in (1 - sub, sub)
+            rows_x[:, :, place, :, span].reshape(total.shape[0], height) for place in (sub, 1 - sub)
         )
-        some = jnp.dot(left, theirs[:, span], preferred_element_type=jnp.float32)
-        copy(block).wait()
-        total[:, span] = some + jnp.dot(
-            right, weight[:, span], preferred_element_type=jnp.float32
-        )
+        copy(chunk).wait()
+        total[...] += jnp.dot(
+            left, weight[span, :], preferred_element_type=jnp.float32
+        ) + jnp.dot(right, theirs[span, :], preferred_element_type=jnp.float32)
+
     send_rows(steps, halves, rows_x.shape, mine_group, total, out)
 
 
@@ -243,7 +246,7 @@
         scratch += [
             pltpu.VMEM((height, width), jnp.bfloat16),
             pltpu.VMEM((total, width), jnp.float32),
-            pltpu.SemaphoreType.DMA((4,)),
+            pltpu.SemaphoreType.DMA((6,)),
         ]
         limit, moved = 36 << 20, 4 * height * width
         flops += 4 * total * height * width
@@ -373,11 +376,10 @@
         *packed, send = pack(
             60, pieces, ocean_w, atmos_w, ocean_ids, atmos_ids, land, ocean_f, atmos_f
         )
-        sent = []
-        for at, (piece, (shift, _, _, _)) in enumerate(zip(packed, pieces)):
-            if at >= 2:
-                piece, sent[at - 2] = lax.optimization_barrier((piece, sent[at - 2]))
-            sent.append(lax.ppermute(piece, "band", along(shift)))
+        sent = [
+            lax.ppermute(piece, "band", along(shift))
+            for piece, (shift, _, _, _) in zip(packed[:2], pieces)
+        ]
         embed_other, own_land, send = lax.optimization_barrier((embed_weight, land, send))
         own_w = pack(54, [(0, 0, cap, None)], ocean_w, atmos_w, ocean_ids, atmos_ids, own_land)[0]
         embed_other = swap(embed_other, "sub")
@@ -408,17 +410,14 @@
 
         ours, others = [(0, keep)], [(1, theirs)]
         jobs = [job_of(me, [own_w], [cap], [jnp.int32(0)], ours)]
-        rows_x = call(jobs[:1], None, groups=2)
-        crossed = [swap(piece, "var") for piece in sent[:2]]
-        for at in range(2, len(sent)):
-            jobs.append(job_at(order[at - 2], ours))
-            rows_x = call(jobs[-1:], rows_x, groups=2)
-            sent[at], rows_x = lax.optimization_barrier((sent[at], rows_x))
-            crossed.append(swap(sent[at], "var"))
-        done = len(jobs)
-        jobs += [job_at(shift, ours) for shift in order[done - 1 :]]
+        rows_x = call(jobs, None, groups=2)
+        for at, (piece, (shift, _, _, _)) in enumerate(zip(packed[2:], pieces[2:])):
+            piece, sent[at], rows_x = lax.optimization_barrier((piece, sent[at], rows_x))
+            sent.append(lax.ppermute(piece, "band", along(shift)))
+        crossed = [swap(piece, "var") for piece in sent]
+        jobs += [job_at(shift, ours) for shift in order]
         rows_x = call(
-            jobs[done:-1] + [with_fields(job, others) for job in jobs[:-1]], rows_x, groups=2
+            jobs[1:-1] + [with_fields(job, others) for job in jobs[:-1]], rows_x, groups=2
         )
         sent = call(
             [with_fields(jobs[-1], ours + others)],

time: 71.2 us -> 67.4 us (0.947)
  waiting for transfers between devices: 4.15 us -> 10 us
  Pallas kernels: 26 us -> 21 us
  starting transfers between devices: 18.8 us -> 14.1 us
    ppermute x3 -> x1, starting transfers between devices: 13 us -> 3.66 us  [per_device(): sent.append(lax.ppermute(piece, 'band', along(shift)))]
    ppermute x3 -> x1, waiting for transfers between devices: 1.12 us -> 7.62 us  [per_device(): sent.append(lax.ppermute(piece, 'band', along(shift)))]
    pallas_call x4 -> x3, Pallas kernels: 20 us -> 14.9 us  [regrid(): pl.pallas_call(body, out_shape=shapes, in_specs=specs, out_specs=[vmem] *...]
    ppermute x0 -> x2, starting transfers between devices: none -> 4.75 us  [per_device(): lax.ppermute(piece, 'band', along(shift))]
  transfers between devices with their start and end apart: 8 -> 8, of which waited for: 3 -> 2; matrix products, arithmetic and copies ran while one was open for 3% -> 3% of each run, Pallas kernels for 12% -> 12%
where the time goes in v11:
time: 67.4 us; the launch traced here: 67 us
  Pallas kernels  21 us (31%)
  blocking collectives  17.4 us (26%)
  starting transfers between devices  14.1 us (21%)
  waiting for transfers between devices  10 us (15%)
  other arithmetic  2.34 us (3%)
  local copies, waits for them, and re-layouts  1.98 us (3%)
    all_to_all x1, blocking collectives, per_device(): lax.all_to_all(sent, ('grp', 'band', 'var'), split_axis=0, concat_axis=0,...  17.4 us
    pallas_call x3, Pallas kernels, regrid(): pl.pallas_call(body, out_shape=shapes, in_specs=specs, out_specs=[vmem] *...  14.9 us
    ppermute x1, waiting for transfers between devices, per_device(): sent.append(lax.ppermute(piece, 'band', along(shift)))  7.62 us
    pallas_call x2, Pallas kernels, pack(): pl.pallas_call(functools.partial(pack_kernel, pieces, len(fields) // 2),...  6.1 us
    ppermute x5, starting transfers between devices, swap(): return lax.ppermute(x, axis, [(0, 1), (1, 0)])  5.72 us
    ppermute x2, starting transfers between devices, per_device(): lax.ppermute(piece, 'band', along(shift))  4.75 us
    ppermute x1, starting transfers between devices, per_device(): sent.append(lax.ppermute(piece, 'band', along(shift)))  3.66 us
    ppermute x5, waiting for transfers between devices, swap(): return lax.ppermute(x, axis, [(0, 1), (1, 0)])  2.37 us
  transfers between devices with their start and end apart: 8, of which 2 were waited for; matrix products, arithmetic and copies ran while one was open for 3% of the time, Pallas kernels for 12%

profile of v11, /device:TPU:0, one launch (start us, length us, event | category | flops | bytes accessed | tf_op | source)
XLA Modules:
  0.0 67.0 jit_solution(12093148524928458470)
XLA Ops:
  0.0 0.0 copy-start.6
  0.0 3.5 %shard_map.118 = (bf16[944,128]{1,0:T(8,128)(2,1)}, bf16[944,128]{1,0:T(8,128)(2,1)}, bf16[944,128]{1,0:T(8,128)(2,1)}, bf16[36,96,128]{2,1,0:T(8,128)(2,1)}) custom-call(bf16[4,1792,128]{2,1,0:T(8,128)(2,1)} %bitcast.27, bf16[4,1792,128]{2,1,0:T(8,128)(2,1)} %bitcast.29, s32[4,14]{1,0:T(4,128)} %bitcast.33, s32[4,14]{1,0:T(4,128)} %bitcast.35, ...), custom_call_target="tpu_custom_call" | custom-call | bytes 2097152 | tf_op jit(solution)/shard_map/pallas_call | solution.py:88
  3.5 0.0 copy-start
  3.5 0.0 copy-start.1
  3.5 0.5 collective-permute-start.7
  4.1 2.6 %collective-permute-start = (bf16[944,128]{1,0:T(8,128)(2,1)}, bf16[944,128]{1,0:T(8,128)(2,1)S(1)}, u32[]{:S(2)}, u32[]{:S(2)}) collective-permute-start(bf16[944,128]{1,0:T(8,128)(2,1)} %get-tuple-element.17), channel_id=1, source_target_pairs={{0,4},{4,8},{8,12},{12,0},{1,5},{5,9},{9,13},{13,1},{2,6},{6,10},{... | collective-permute-start | bytes 725000 | tf_op jit(solution)/shard_map/ppermute | solution.py:380
  6.7 2.1 %collective-permute-start.5 = (bf16[944,128]{1,0:T(8,128)(2,1)}, bf16[944,128]{1,0:T(8,128)(2,1)S(1)}, u32[]{:S(2)}, u32[]{:S(2)}) collective-permute-start(bf16[944,128]{1,0:T(8,128)(2,1)} %get-tuple-element.23), channel_id=1, source_target_pairs={{0,12},{4,0},{8,4},{12,8},{1,13},{5,1},{9,5},{13,9},{2,14},{6,2},{... | collective-permute-start | bytes 725000 | tf_op jit(solution)/shard_map/ppermute | solution.py:380
  8.8 1.7 %collective-permute-start.3 = (bf16[36,96,128]{2,1,0:T(8,128)(2,1)}, bf16[36,96,128]{2,1,0:T(8,128)(2,1)S(1)}, u32[]{:S(2)}, u32[]{:S(2)}) collective-permute-start(bf16[36,96,128]{2,1,0:T(8,128)(2,1)} %get-tuple-element.21), channel_id=1, source_target_pairs={{0,16},{16,0},{1,17},{17,1},{2,18},{18,2},{3,19},{19,3},{4,20},{20... | collective-permute-start | bytes 2654216 | tf_op jit(solution)/shard_map/ppermute | solution.py:327
  10.5 0.0 copy-done.6
  10.5 0.0 copy-done.5
  10.5 0.2 convert_reduce_fusion.1
  10.7 0.1 fusion.1
  10.8 0.1 reshape.97
  10.9 0.1 select_reduce_fusion
  11.0 0.1 reshape.89
  11.0 2.6 %shard_map.119.refs_2_.refs_12_ = bf16[1840,128]{1,0:T(8,128)(2,1)} custom-call(bf16[4,1792,128]{2,1,0:T(8,128)(2,1)} %bitcast.28, bf16[4,1792,128]{2,1,0:T(8,128)(2,1)} %bitcast.30, s32[4,14]{1,0:T(4,128)} %bitcast.34, s32[4,14]{1,0:T(4,128)} %bitcast.36, f32[16,128]{1,0:T(8,128)} %bitcast.32), custom_call_target="tpu_custom_call" | custom-call | bytes 2097152 | tf_op jit(solution)/shard_map/pallas_call | solution.py:88
  13.7 0.1 add_add_fusion
  13.7 0.7 %slice_convert_fusion.2 = s32[1,14]{1,0:T(1,128)S(1)} fusion(bf16[1840,128]{1,0:T(8,128)(2,1)} %shard_map.119.refs_2_.refs_12_), kind=kLoop, calls=%fused_computation.30 | loop fusion | flops 14 | bytes 84 | tf_op jit(solution)/shard_map/convert_element_type | solution.py:391
  14.4 0.7 %fusion.3 = s32[1,14]{1,0:T(1,128)S(1)} fusion(pred[4,14]{1,0:T(4,128)(4,1)S(1)} %reshape.97, s32[]{:T(128)S(6)} %select_n.67, s32[]{:T(128)S(6)} %mul.61, bf16[1840,128]{1,0:T(8,128)(2,1)} %shard_map.119.refs_2_.refs_12_), kind=kLoop, calls=%fused_computation.22 | loop fusion | flops 42 | bytes 106 | tf_op jit(solution)/shard_map/jit(_where)/select_n | solution.py:394
  15.1 0.1 add_add_fusion.2.refs_7_
  15.2 0.1 pad_add_fusion.4.refs_1_.refs_11_
  15.3 0.0 copy-done
  15.3 0.0 copy-done.1
  15.3 1.0 %copy-done.2 = bf16[1840,128]{1,0:T(8,128)(2,1)S(1)} copy-done((bf16[1840,128]{1,0:T(8,128)(2,1)S(1)}, bf16[1840,128]{1,0:T(8,128)(2,1)}, u32[]{:S(2)}) %copy-start.2) | copy-done | bytes 471064
  16.3 1.3 %shard_map.120.refs_14_ = bf16[4,2,2,32,3072]{4,3,2,1,0:T(8,128)(2,1)S(1)} custom-call(s32[3,14]{1,0:T(4,128)S(1)} %pad_add_fusion.refs_0_.refs_10_, s32[2]{0:T(128)S(1)} %pad_add_fusion.4.refs_1_.refs_11_, bf16[1840,128]{1,0:T(8,128)(2,1)S(1)} %copy-done.2, bf16[36,96,128]{2,1,0:T(8,128)(2,1)S(1)} %bitcast.20, bf16[36,96,128]{2,1,0:T(8,128)(2,1)S(1)} %bitcast.24), custom_call_target="tpu_custom_call" | custom-call | flops 44040192 | bytes 3145728 | tf_op jit(solution)/shard_map/pallas_call | solution.py:253
  17.6 0.0 collective-permute-done.refs_2_
  17.7 0.0 copy-done.7
  17.7 3.7 %collective-permute-start.1 = (bf16[944,128]{1,0:T(8,128)(2,1)S(1)}, bf16[944,128]{1,0:T(8,128)(2,1)S(1)}, u32[]{:S(2)}, u32[]{:S(2)}) collective-permute-start(bf16[944,128]{1,0:T(8,128)(2,1)S(1)} %copy-done.7), channel_id=1, source_target_pairs={{0,8},{4,12},{8,0},{12,4},{1,9},{5,13},{9,1},{13,5},{2,10},{6,14},... | collective-permute-start | bytes 725000 | tf_op jit(solution)/shard_map/ppermute | solution.py:416
  21.3 1.5 %collective-permute-start.4 = (bf16[944,128]{1,0:T(8,128)(2,1)S(1)}, bf16[944,128]{1,0:T(8,128)(2,1)S(1)}, u32[]{:S(2)}, u32[]{:S(2)}) collective-permute-start(bf16[944,128]{1,0:T(8,128)(2,1)S(1)} %collective-permute-done.refs_2_), channel_id=1, source_target_pairs={{0,2},{2,0},{1,3},{3,1},{4,6},{6,4},{5,7},{7,5},{8,10},{10,8},{9,1... | collective-permute-start | bytes 725000 | tf_op jit(solution)/shard_map/ppermute | solution.py:327
  22.8 0.0 collective-permute-done.5.refs_8_
  22.8 0.5 collective-permute-start.6
  23.4 7.6 %collective-permute-done.1.refs_2_ = bf16[944,128]{1,0:T(8,128)(2,1)S(1)} collective-permute-done((bf16[944,128]{1,0:T(8,128)(2,1)S(1)}, bf16[944,128]{1,0:T(8,128)(2,1)S(1)}, u32[]{:S(2)}, u32[]{:S(2)}) %collective-permute-start.1) | collective-permute-done | bytes 241696 | tf_op jit(solution)/shard_map/ppermute | solution.py:416
  31.0 1.5 %collective-permute-start.2 = (bf16[944,128]{1,0:T(8,128)(2,1)S(1)}, bf16[944,128]{1,0:T(8,128)(2,1)S(1)}, u32[]{:S(2)}, u32[]{:S(2)}) collective-permute-start(bf16[944,128]{1,0:T(8,128)(2,1)S(1)} %collective-permute-done.1.refs_2_), channel_id=1, source_target_pairs={{0,2},{2,0},{1,3},{3,1},{4,6},{6,4},{5,7},{7,5},{8,10},{10,8},{9,1... | collective-permute-start | bytes 725000 | tf_op jit(solution)/shard_map/ppermute | solution.py:327
  32.6 0.0 collective-permute-done.6.refs_9_
  32.6 0.0 collective-permute-done.4.refs_3_
  32.6 0.0 collective-permute-done.3.refs_13_.refs_6_
  32.6 3.9 %shard_map.121.refs_7_ = bf16[4,2,2,32,3072]{4,3,2,1,0:T(8,128)(2,1)S(1)} custom-call(s32[3,14]{1,0:T(4,128)S(1)} %get-tuple-element.37.refs_0_, s32[3]{0:T(128)S(1)} %get-tuple-element.35.refs_1_, bf16[944,128]{1,0:T(8,128)(2,1)S(1)} %collective-permute-done.refs_2_, ...), custom_call_target="tpu_custom_call", output_to_operand_aliasing={{}: (14, {})} | custom-call | flops 220200960 | bytes 15728640 | tf_op jit(solution)/shard_map/pallas_call | solution.py:253
  36.5 2.4 %collective-permute-done.2.refs_3_ = bf16[944,128]{1,0:T(8,128)(2,1)S(1)} collective-permute-done((bf16[944,128]{1,0:T(8,128)(2,1)S(1)}, bf16[944,128]{1,0:T(8,128)(2,1)S(1)}, u32[]{:S(2)}, u32[]{:S(2)}) %collective-permute-start.2) | collective-permute-done | bytes 241696 | tf_op jit(solution)/shard_map/ppermute | solution.py:327
  38.9 0.0 collective-permute-done.7.refs_8_
  38.9 9.7 %shard_map.122 = (bf16[4,2,2,32,3072]{4,3,2,1,0:T(8,128)(2,1)S(1)}, bf16[16,16,1024]{2,1,0:T(8,128)(2,1)S(1)}) custom-call(s32[3,14]{1,0:T(4,128)S(1)} %get-tuple-element.36.refs_0_, s32[3]{0:T(128)S(1)} %get-tuple-element.34.refs_1_, bf16[944,128]{1,0:T(8,128)(2,1)S(1)} %collective-permute-done.1.refs_2_, ...), custom_call_target="tpu_custom_call", output_to_operand_aliasing={{0}: (7, {})} | custom-call | flops 3309305856 | bytes 12582912 | tf_op jit(solution)/shard_map/pallas_call | solution.py:253
  48.6 17.4 %all_to_all.5 = bf16[16,16,1024]{2,1,0:T(8,128)(2,1)S(1)} all-to-all(bf16[16,16,1024]{2,1,0:T(8,128)(2,1)S(1)} %get-tuple-element.26), channel_id=1, replica_groups=mesh['grp'=2,'band'=4,'var'=2,'sub'=2] {'grp','band','var'}, dimensions={0} | all-to-all | bytes 1048576 | tf_op jit(solution)/shard_map/all_to_all | solution.py:428
  66.0 0.1 convert_reduce_fusion
  66.1 0.0 copy-done.3
  66.1 0.1 multiply_reduce_fusion
  66.2 0.1 rsqrt.12
  66.3 0.0 copy-done.4
  66.3 0.1 fusion
  66.4 0.6 copy.17
  (17 shorter events, 0.1 us)
Async XLA Ops:
  0.0 10.5 %copy-start.6 = (s32[36,1]{0,1:T(1,128)S(1)}, s32[36,1]{0,1:T(1,128)}, u32[]{:S(2)}) copy-start(s32[36,1]{0,1:T(1,128)} %param.17) | copy-start | bytes 436
  0.0 10.5 %copy-start.5 = (s32[36,1]{0,1:T(1,128)S(1)}, s32[36,1]{0,1:T(1,128)}, u32[]{:S(2)}) copy-start(s32[36,1]{0,1:T(1,128)} %param.13) | copy-start | bytes 436
  3.5 11.8 %copy-start = (bf16[36,4,24,128]{3,2,1,0:T(8,128)(2,1)S(1)}, bf16[36,4,24,128]{3,2,1,0:T(8,128)(2,1)}, u32[]{:S(2)}) copy-start(bf16[36,4,24,128]{3,2,1,0:T(8,128)(2,1)} %param.12) | copy-start | bytes 2654212
  3.5 11.8 %copy-start.1 = (bf16[36,4,24,128]{3,2,1,0:T(8,128)(2,1)S(1)}, bf16[36,4,24,128]{3,2,1,0:T(8,128)(2,1)}, u32[]{:S(2)}) copy-start(bf16[36,4,24,128]{3,2,1,0:T(8,128)(2,1)} %param.16) | copy-start | bytes 2654212
  3.5 35.3 %collective-permute-start.7 = (bf16[3072,1024]{1,0:T(8,128)(2,1)}, bf16[3072,1024]{1,0:T(8,128)(2,1)}, u32[]{:S(2)}, u32[]{:S(2)}) collective-permute-start(bf16[3072,1024]{1,0:T(8,128)(2,1)} %refs_9_.1), channel_id=1, source_target_pairs={{0,1},{1,0},{2,3},{3,2},{4,5},{5,4},{6,7},{7,6},{8,9},{9,8},{10,11... | collective-permute-start | bytes 18874376 | tf_op jit(solution)/shard_map/ppermute | solution.py:327
  4.1 13.6 %collective-permute-start = (bf16[944,128]{1,0:T(8,128)(2,1)}, bf16[944,128]{1,0:T(8,128)(2,1)S(1)}, u32[]{:S(2)}, u32[]{:S(2)}) collective-permute-start(bf16[944,128]{1,0:T(8,128)(2,1)} %get-tuple-element.17), channel_id=1, source_target_pairs={{0,4},{4,8},{8,12},{12,0},{1,5},{5,9},{9,13},{13,1},{2,6},{6,10},{... | collective-permute-start | bytes 725000 | tf_op jit(solution)/shard_map/ppermute | solution.py:380
  6.7 16.1 %collective-permute-start.5 = (bf16[944,128]{1,0:T(8,128)(2,1)}, bf16[944,128]{1,0:T(8,128)(2,1)S(1)}, u32[]{:S(2)}, u32[]{:S(2)}) collective-permute-start(bf16[944,128]{1,0:T(8,128)(2,1)} %get-tuple-element.23), channel_id=1, source_target_pairs={{0,12},{4,0},{8,4},{12,8},{1,13},{5,1},{9,5},{13,9},{2,14},{6,2},{... | collective-permute-start | bytes 725000 | tf_op jit(solution)/shard_map/ppermute | solution.py:380
  8.8 23.8 %collective-permute-start.3 = (bf16[36,96,128]{2,1,0:T(8,128)(2,1)}, bf16[36,96,128]{2,1,0:T(8,128)(2,1)S(1)}, u32[]{:S(2)}, u32[]{:S(2)}) collective-permute-start(bf16[36,96,128]{2,1,0:T(8,128)(2,1)} %get-tuple-element.21), channel_id=1, source_target_pairs={{0,16},{16,0},{1,17},{17,1},{2,18},{18,2},{3,19},{19,3},{4,20},{20... | collective-permute-start | bytes 2654216 | tf_op jit(solution)/shard_map/ppermute | solution.py:327
  11.0 6.6 %copy-start.7 = (bf16[944,128]{1,0:T(8,128)(2,1)S(1)}, bf16[944,128]{1,0:T(8,128)(2,1)}, u32[]{:S(2)}) copy-start(bf16[944,128]{1,0:T(8,128)(2,1)} %get-tuple-element.20) | copy-start | bytes 724996
  15.3 1.0 %copy-start.2 = (bf16[1840,128]{1,0:T(8,128)(2,1)S(1)}, bf16[1840,128]{1,0:T(8,128)(2,1)}, u32[]{:S(2)}) copy-start(bf16[1840,128]{1,0:T(8,128)(2,1)} %shard_map.119.refs_2_.refs_12_) | copy-start | bytes 1413124
  17.7 13.3 %collective-permute-start.1 = (bf16[944,128]{1,0:T(8,128)(2,1)S(1)}, bf16[944,128]{1,0:T(8,128)(2,1)S(1)}, u32[]{:S(2)}, u32[]{:S(2)}) collective-permute-start(bf16[944,128]{1,0:T(8,128)(2,1)S(1)} %copy-done.7), channel_id=1, source_target_pairs={{0,8},{4,12},{8,0},{12,4},{1,9},{5,13},{9,1},{13,5},{2,10},{6,14},... | collective-permute-start | bytes 725000 | tf_op jit(solution)/shard_map/ppermute | solution.py:416
  21.3 11.2 %collective-permute-start.4 = (bf16[944,128]{1,0:T(8,128)(2,1)S(1)}, bf16[944,128]{1,0:T(8,128)(2,1)S(1)}, u32[]{:S(2)}, u32[]{:S(2)}) collective-permute-start(bf16[944,128]{1,0:T(8,128)(2,1)S(1)} %collective-permute-done.refs_2_), channel_id=1, source_target_pairs={{0,2},{2,0},{1,3},{3,1},{4,6},{6,4},{5,7},{7,5},{8,10},{10,8},{9,1... | collective-permute-start | bytes 725000 | tf_op jit(solution)/shard_map/ppermute | solution.py:327
  22.8 9.7 %collective-permute-start.6 = (bf16[944,128]{1,0:T(8,128)(2,1)S(1)}, bf16[944,128]{1,0:T(8,128)(2,1)S(1)}, u32[]{:S(2)}, u32[]{:S(2)}) collective-permute-start(bf16[944,128]{1,0:T(8,128)(2,1)S(1)} %collective-permute-done.5.refs_8_), channel_id=1, source_target_pairs={{0,2},{2,0},{1,3},{3,1},{4,6},{6,4},{5,7},{7,5},{8,10},{10,8},{9,1... | collective-permute-start | bytes 725000 | tf_op jit(solution)/shard_map/ppermute | solution.py:327
  31.0 7.9 %collective-permute-start.2 = (bf16[944,128]{1,0:T(8,128)(2,1)S(1)}, bf16[944,128]{1,0:T(8,128)(2,1)S(1)}, u32[]{:S(2)}, u32[]{:S(2)}) collective-permute-start(bf16[944,128]{1,0:T(8,128)(2,1)S(1)} %collective-permute-done.1.refs_2_), channel_id=1, source_target_pairs={{0,2},{2,0},{1,3},{3,1},{4,6},{6,4},{5,7},{7,5},{8,10},{10,8},{9,1... | collective-permute-start | bytes 725000 | tf_op jit(solution)/shard_map/ppermute | solution.py:327
  38.9 27.2 %copy-start.3 = (f32[1024]{0:T(1024)S(1)}, f32[1024]{0:T(1024)}, u32[]{:S(2)}) copy-start(f32[1024]{0:T(1024)} %param.22) | copy-start | bytes 12292
  38.9 27.4 %copy-start.4 = (f32[1024]{0:T(1024)S(1)}, f32[1024]{0:T(1024)}, u32[]{:S(2)}) copy-start(f32[1024]{0:T(1024)} %param.23) | copy-start | bytes 12292

commit v12 on v11

--- a/solution.py
+++ b/solution.py
@@ -153,32 +153,112 @@
 
 
 def finish_kernel(steps, halves, jobs, count, *refs):
-    theirs, mine, rows_x, out, acc, scale, weight, total, sem = refs[count:]
-    sub, mine_group = lax.axis_index("sub"), lax.axis_index("grp")
-    chunks = sem.shape[0]
-    height = mine.shape[0] // chunks
-
-    def copy(chunk):
+    sources, refs, outs = refs[count : count + 2], refs[:count], refs[count + 2 :]
+    rows_x, keep_x, send_x, keep_y, send_y, acc, scale, weight, total, sem = outs
+    sub = lax.axis_index("sub")
+    chunks = sem.shape[1]
+    height = weight.shape[1] // chunks
+
+    def copy(half, chunk):
         span = pl.ds(pl.multiple_of(chunk * height, height), height)
-        return pltpu.make_async_copy(mine.at[span, :], weight.at[span, :], sem.at[chunk])
+        return pltpu.make_async_copy(
+            sources[half].at[span, :], weight.at[half, span, :], sem.at[half, chunk]
+        )
 
     for chunk in range(chunks):
-        copy(chunk).start()
+        for half in range(2):
+            copy(half, chunk).start()
     run_jobs(steps, jobs, refs, rows_x, acc, scale)
     total[...] = jnp.zeros_like(total)
 
     @pl.loop(0, chunks)
     def _(chunk):
         span = pl.ds(pl.multiple_of(chunk * height, height), height)
-        left, right = (
-            rows_x[:, :, place, :, span].reshape(total.shape[0], height) for place in (sub, 1 - sub)
-        )
-        copy(chunk).wait()
-        total[...] += jnp.dot(
-            left, weight[span, :], preferred_element_type=jnp.float32
-        ) + jnp.dot(right, theirs[span, :], preferred_element_type=jnp.float32)
-
-    send_rows(steps, halves, rows_x.shape, mine_group, total, out)
+        terms = []
+        for half, place in enumerate((sub, 1 - sub)):
+            left = rows_x[:, :, place, :, span].reshape(total.shape[0], height)
+            copy(half, chunk).wait()
+            terms.append(
+                jnp.dot(left, weight[half, span, :], preferred_element_type=jnp.float32)
+            )
+        total[...] += terms[0] + terms[1]
+
+    x = lax.axis_index("var")
+    bands, groups, _, row_count, _ = rows_x.shape
+    share = row_count // (steps * halves)
+    width = total.shape[1] // 2
+    size = bands * share
+    for g in range(groups):
+        for t in range(steps):
+            for h in range(halves):
+                starts = [
+                    (b * groups + g) * row_count + (t * halves + h) * share for b in range(bands)
+                ]
+                first, second = (
+                    jnp.concatenate(
+                        [total[pl.ds(at, share), pl.ds(c * width, width)] for at in starts], axis=0
+                    )
+                    for c in range(2)
+                )
+                place = pl.ds((g * steps + t) * size, size)
+
+                @pl.when(x == h)
+                def _(place=place, first=first):
+                    keep_x[place, :] = first
+
+                @pl.when(x != h)
+                def _(place=place, first=first):
+                    send_x[place, :] = first.astype(send_x.dtype)
+
+                place = pl.multiple_of((lax.rem(x + h, 2) * steps + t) * size, size)
+                if g == 0:
+                    keep_y[pl.ds(place, size), :] = second
+                else:
+                    send_y[pl.ds(place, size), :] = second.astype(send_y.dtype)
+
+
+def add_kernel(keep_x, got_x, keep_y, got_y, sum_x, send_x, sum_y, send_y):
+    half = sum_x.shape[0]
+    for keep, got, out, send in (
+        (keep_x, got_x, sum_x, send_x),
+        (keep_y, got_y, sum_y, send_y),
+    ):
+        out[...] = keep[:half, :] + got[:half, :].astype(jnp.float32)
+        send[...] = (keep[half:, :] + got[half:, :].astype(jnp.float32)).astype(send.dtype)
+
+
+def split_kernel(shifts, keep_x, got_x, keep_y, got_y, *outs):
+    size, width = outs[0].shape[0], keep_x.shape[1]
+    me, bands = lax.axis_index("band"), keep_x.shape[0] // size
+    for out, shift in zip(outs, (0,) + tuple(shifts)):
+        span = pl.ds(pl.multiple_of(lax.rem(me + shift, bands) * size, size), size)
+        for c, (keep, got) in enumerate(((keep_x, got_x), (keep_y, got_y))):
+            some = keep[span, :] + got[span, :].astype(jnp.float32)
+            out[:, pl.ds(c * width, width)] = some.astype(out.dtype)
+
+
+def norm_kernel(bands, own, *refs):
+    parts, bias, gain, out = refs[:-3], refs[-3], refs[-2], refs[-1]
+    summed = own[...] + bias[...]
+    for part in parts:
+        summed += part[...].astype(jnp.float32)
+    inverse = lax.rsqrt(jnp.mean(summed * summed, axis=-1, keepdims=True) + 1e-05)
+    done = summed * inverse * gain[...]
+    share = done.shape[0] // bands
+    rows = [done[b * share + p : b * share + p + 1] for p in range(share) for b in range(bands)]
+    out[...] = jnp.concatenate(rows, axis=0).astype(out.dtype)
+
+
+def small(body, shapes, *operands):
+    vmem = pl.BlockSpec(memory_space=pltpu.VMEM)
+    return pl.pallas_call(
+        body,
+        out_shape=[jax.ShapeDtypeStruct(shape, kind) for shape, kind in shapes],
+        in_specs=[vmem] * len(operands),
+        out_specs=[vmem] * len(shapes),
+        cost_estimate=pl.CostEstimate(flops=1 << 18, bytes_accessed=1 << 20, transcendentals=0),
+        compiler_params=pltpu.CompilerParams(vmem_limit_bytes=12 << 20),
+    )(*operands)
 
 
 def send_rows(steps, halves, shape, mine_group, total, out):
@@ -239,16 +319,16 @@
         height, width = mine.shape
         total = bands * groups * shape[3]
         body = functools.partial(finish_kernel, steps, halves, listed, len(operands))
-        operands += [theirs, mine]
-        specs += [vmem, pl.BlockSpec(memory_space=pl.ANY)]
-        count = groups * steps * halves
-        shapes.append(jax.ShapeDtypeStruct((count, total // count, width), jnp.bfloat16))
+        operands += [mine, theirs]
+        specs += [pl.BlockSpec(memory_space=pl.ANY)] * 2
+        half = (total // 2, width // 2)
+        shapes += [jax.ShapeDtypeStruct(half, kind) for kind in (jnp.float32, jnp.bfloat16) * 2]
         scratch += [
-            pltpu.VMEM((height, width), jnp.bfloat16),
+            pltpu.VMEM((2, height, width), jnp.bfloat16),
             pltpu.VMEM((total, width), jnp.float32),
-            pltpu.SemaphoreType.DMA((6,)),
+            pltpu.SemaphoreType.DMA((2, 6)),
         ]
-        limit, moved = 36 << 20, 4 * height * width
+        limit, moved = 44 << 20, 4 * height * width
         flops += 4 * total * height * width
     done = pl.pallas_call(
         body,
@@ -260,7 +340,7 @@
         cost_estimate=pl.CostEstimate(flops=flops, bytes_accessed=moved, transcendentals=0),
         compiler_params=pltpu.CompilerParams(vmem_limit_bytes=limit),
     )(*operands)
-    return done[-1]
+    return done[0] if last is None else done[1:]
 
 
 def embed_kernel(steps, halves, rows_x, mine, theirs, out, total):
@@ -368,7 +448,7 @@
         regrid, bands=nb, steps=steps, tiles=tiles, rows=steps * local_vars, cells=cells
     )
 
-    if ng == 2 and nv == 2 and cap % 2 == 0:
+    if ng == 2 and nv == 2 and cap % 2 == 0 and steps == nb:
         each = cap // 2
         pieces = []
         for shift in order:
@@ -381,7 +461,7 @@
             for piece, (shift, _, _, _) in zip(packed[:2], pieces)
         ]
         embed_other, own_land, send = lax.optimization_barrier((embed_weight, land, send))
-        own_w = pack(54, [(0, 0, cap, None)], ocean_w, atmos_w, ocean_ids, atmos_ids, own_land)[0]
+        own_w = pack(60, [(0, 0, cap, None)], ocean_w, atmos_w, ocean_ids, atmos_ids, own_land)[0]
         embed_other = swap(embed_other, "sub")
         keep, theirs = (ocean_f, atmos_f), (swap(send, "grp"),)
         dest = jnp.where(y == 0, ocean_dest, atmos_dest)
@@ -419,13 +499,36 @@
         rows_x = call(
             jobs[1:-1] + [with_fields(job, others) for job in jobs[:-1]], rows_x, groups=2
         )
-        sent = call(
+        keep_x, send_x, keep_y, send_y = call(
             [with_fields(jobs[-1], ours + others)],
             rows_x,
             groups=2,
             last=(embed_weight, embed_other, nv),
         )
-        got = lax.all_to_all(sent, ("grp", "band", "var"), split_axis=0, concat_axis=0, tiled=True)
+        whole, width = keep_x.shape
+        part = ((whole // 2, width), jnp.float32), ((whole // 2, width), jnp.bfloat16)
+        sum_x, send_x, sum_y, send_y = small(
+            add_kernel, part * 2, keep_x, swap(send_x, "var"), keep_y, swap(send_y, "grp")
+        )
+        own = (whole // 2 // nb, 2 * width)
+        own, *send = small(
+            functools.partial(split_kernel, order),
+            [(own, jnp.float32)] + [(own, jnp.bfloat16)] * len(order),
+            sum_x,
+            swap(send_x, "grp"),
+            sum_y,
+            swap(send_y, "var"),
+        )
+        got = [lax.ppermute(part, "band", along(shift)) for part, shift in zip(send, order)]
+        finished = small(
+            functools.partial(norm_kernel, nb),
+            [(own.shape, jnp.bfloat16)],
+            own,
+            *got,
+            embed_bias.reshape(1, -1),
+            embed_gain.reshape(1, -1),
+        )[0]
+        return finished.reshape(1, share, nb, steps // nb, 2 * width)
     else:
         embed_other = swap(embed_weight, "sub")
         both = jnp.concatenate([ocean_w, atmos_w], axis=1)

time: 67.4 us -> 69.1 us (1.025)
  blocking collectives: 17.4 us -> 0 us
  waiting for transfers between devices: 10 us -> 22.2 us
  starting transfers between devices: 14.1 us -> 22.6 us
  Pallas kernels: 21 us -> 19.8 us
    all_to_all x1 -> x0, blocking collectives: 17.4 us -> none  [per_device(): lax.all_to_all(sent, ('grp', 'band', 'var'), split_axis=0, concat_axis=0,...]
    ppermute x5 -> x9, waiting for transfers between devices: 2.37 us -> 9.8 us  [swap(): return lax.ppermute(x, axis, [(0, 1), (1, 0)])]
    ppermute x0 -> x3, waiting for transfers between devices: none -> 4.81 us  [per_device(): lax.ppermute(part, 'band', along(shift))]
    ppermute x5 -> x9, starting transfers between devices: 5.72 us -> 10.3 us  [swap(): return lax.ppermute(x, axis, [(0, 1), (1, 0)])]
    ppermute x0 -> x3, starting transfers between devices: none -> 3.88 us  [per_device(): lax.ppermute(part, 'band', along(shift))]
    pallas_call x3, Pallas kernels: 14.9 us -> 13.5 us  [regrid(): pl.pallas_call(body, out_shape=shapes, in_specs=specs, out_specs=[vmem] *...]
  transfers between devices with their start and end apart: 8 -> 15, of which waited for: 2 -> 8; matrix products, arithmetic and copies ran while one was open for 3% -> 3% of each run, Pallas kernels for 12% -> 11%
where the time goes in v12:
time: 69.1 us; the launch traced here: 68.7 us
  starting transfers between devices  22.6 us (33%)
  waiting for transfers between devices  22.2 us (32%)
  Pallas kernels  19.8 us (29%)
  other arithmetic  2.04 us (3%)
  local copies, waits for them, and re-layouts  1.87 us (3%)
    pallas_call x3, Pallas kernels, regrid(): pl.pallas_call(body, out_shape=shapes, in_specs=specs, out_specs=[vmem] *...  13.5 us
    ppermute x9, starting transfers between devices, swap(): return lax.ppermute(x, axis, [(0, 1), (1, 0)])  10.3 us
    ppermute x9, waiting for transfers between devices, swap(): return lax.ppermute(x, axis, [(0, 1), (1, 0)])  9.8 us
    ppermute x1, waiting for transfers between devices, per_device(): sent.append(lax.ppermute(piece, 'band', along(shift)))  7.62 us
    pallas_call x2, Pallas kernels, pack(): pl.pallas_call(functools.partial(pack_kernel, pieces, len(fields) // 2),...  6.1 us
    ppermute x3, waiting for transfers between devices, per_device(): lax.ppermute(part, 'band', along(shift))  4.81 us
    ppermute x2, starting transfers between devices, per_device(): lax.ppermute(piece, 'band', along(shift))  4.75 us
    ppermute x3, starting transfers between devices, per_device(): lax.ppermute(part, 'band', along(shift))  3.88 us
  transfers between devices with their start and end apart: 15, of which 8 were waited for; matrix products, arithmetic and copies ran while one was open for 3% of the time, Pallas kernels for 11%

profile of v12, /device:TPU:0, one launch (start us, length us, event | category | flops | bytes accessed | tf_op | source)
XLA Modules:
  0.0 68.7 jit_solution(1921092278577806682)
XLA Ops:
  0.0 3.5 %shard_map.118 = (bf16[944,128]{1,0:T(8,128)(2,1)}, bf16[944,128]{1,0:T(8,128)(2,1)}, bf16[944,128]{1,0:T(8,128)(2,1)}, bf16[36,96,128]{2,1,0:T(8,128)(2,1)}) custom-call(bf16[4,1792,128]{2,1,0:T(8,128)(2,1)} %bitcast.28, bf16[4,1792,128]{2,1,0:T(8,128)(2,1)} %bitcast.30, s32[4,14]{1,0:T(4,128)} %bitcast.34, s32[4,14]{1,0:T(4,128)} %bitcast.36, ...), custom_call_target="tpu_custom_call" | custom-call | bytes 2097152 | tf_op jit(solution)/shard_map/pallas_call | solution.py:88
  3.5 0.0 copy-start
  3.5 0.0 copy-start.1
  3.6 0.5 collective-permute-start.7
  4.1 2.6 %collective-permute-start = (bf16[944,128]{1,0:T(8,128)(2,1)}, bf16[944,128]{1,0:T(8,128)(2,1)S(1)}, u32[]{:S(2)}, u32[]{:S(2)}) collective-permute-start(bf16[944,128]{1,0:T(8,128)(2,1)} %get-tuple-element.28), channel_id=1, source_target_pairs={{0,4},{4,8},{8,12},{12,0},{1,5},{5,9},{9,13},{13,1},{2,6},{6,10},{... | collective-permute-start | bytes 725000 | tf_op jit(solution)/shard_map/ppermute | solution.py:460
  6.7 2.1 %collective-permute-start.5 = (bf16[944,128]{1,0:T(8,128)(2,1)}, bf16[944,128]{1,0:T(8,128)(2,1)S(1)}, u32[]{:S(2)}, u32[]{:S(2)}) collective-permute-start(bf16[944,128]{1,0:T(8,128)(2,1)} %get-tuple-element.34), channel_id=1, source_target_pairs={{0,12},{4,0},{8,4},{12,8},{1,13},{5,1},{9,5},{13,9},{2,14},{6,2},{... | collective-permute-start | bytes 725000 | tf_op jit(solution)/shard_map/ppermute | solution.py:460
  8.8 1.7 %collective-permute-start.3 = (bf16[36,96,128]{2,1,0:T(8,128)(2,1)}, bf16[36,96,128]{2,1,0:T(8,128)(2,1)S(1)}, u32[]{:S(2)}, u32[]{:S(2)}) collective-permute-start(bf16[36,96,128]{2,1,0:T(8,128)(2,1)} %get-tuple-element.32), channel_id=1, source_target_pairs={{0,16},{16,0},{1,17},{17,1},{2,18},{18,2},{3,19},{19,3},{4,20},{20... | collective-permute-start | bytes 2654216 | tf_op jit(solution)/shard_map/ppermute | solution.py:407
  10.5 0.2 convert_reduce_fusion
  10.7 0.1 fusion
  10.8 0.1 reshape.53
  10.9 0.1 select_reduce_fusion
  11.0 0.1 reshape.45
  11.1 2.6 %shard_map.119.refs_2_.refs_12_ = bf16[1840,128]{1,0:T(8,128)(2,1)} custom-call(bf16[4,1792,128]{2,1,0:T(8,128)(2,1)} %bitcast.29, bf16[4,1792,128]{2,1,0:T(8,128)(2,1)} %bitcast.31, s32[4,14]{1,0:T(4,128)} %bitcast.35, s32[4,14]{1,0:T(4,128)} %bitcast.37, f32[16,128]{1,0:T(8,128)} %bitcast.33), custom_call_target="tpu_custom_call" | custom-call | bytes 2097152 | tf_op jit(solution)/shard_map/pallas_call | solution.py:88
  13.7 0.1 add_add_fusion
  13.8 0.7 slice_convert_fusion.2
  14.4 0.7 %fusion.2 = s32[1,14]{1,0:T(1,128)S(1)} fusion(pred[4,14]{1,0:T(4,128)(4,1)S(1)} %reshape.53, s32[]{:T(128)S(6)} %select_n.67, s32[]{:T(128)S(6)} %mul.28, bf16[1840,128]{1,0:T(8,128)(2,1)} %shard_map.119.refs_2_.refs_12_), kind=kLoop, calls=%fused_computation.18 | loop fusion | flops 42 | bytes 106 | tf_op jit(solution)/shard_map/jit(_where)/select_n | solution.py:474
  15.1 0.1 add_add_fusion.2.refs_7_
  15.2 0.1 pad_add_fusion.4.refs_1_.refs_11_
  15.3 1.0 %copy-done.2 = bf16[1840,128]{1,0:T(8,128)(2,1)S(1)} copy-done((bf16[1840,128]{1,0:T(8,128)(2,1)S(1)}, bf16[1840,128]{1,0:T(8,128)(2,1)}, u32[]{:S(2)}) %copy-start.2) | copy-done | bytes 471064
  16.3 1.3 %shard_map.120.refs_14_ = bf16[4,2,2,32,3072]{4,3,2,1,0:T(8,128)(2,1)S(1)} custom-call(s32[3,14]{1,0:T(4,128)S(1)} %pad_add_fusion.refs_0_.refs_10_, s32[2]{0:T(128)S(1)} %pad_add_fusion.4.refs_1_.refs_11_, bf16[1840,128]{1,0:T(8,128)(2,1)S(1)} %copy-done.2, bf16[36,96,128]{2,1,0:T(8,128)(2,1)S(1)} %bitcast.19, bf16[36,96,128]{2,1,0:T(8,128)(2,1)S(1)} %bitcast.23), custom_call_target="tpu_custom_call" | custom-call | flops 44040192 | bytes 3145728 | tf_op jit(solution)/shard_map/pallas_call | solution.py:333
  17.7 3.7 %collective-permute-start.1 = (bf16[944,128]{1,0:T(8,128)(2,1)S(1)}, bf16[944,128]{1,0:T(8,128)(2,1)S(1)}, u32[]{:S(2)}, u32[]{:S(2)}) collective-permute-start(bf16[944,128]{1,0:T(8,128)(2,1)S(1)} %copy-done.7), channel_id=1, source_target_pairs={{0,8},{4,12},{8,0},{12,4},{1,9},{5,13},{9,1},{13,5},{2,10},{6,14},... | collective-permute-start | bytes 725000 | tf_op jit(solution)/shard_map/ppermute | solution.py:496
  21.3 1.5 %collective-permute-start.4 = (bf16[944,128]{1,0:T(8,128)(2,1)S(1)}, bf16[944,128]{1,0:T(8,128)(2,1)S(1)}, u32[]{:S(2)}, u32[]{:S(2)}) collective-permute-start(bf16[944,128]{1,0:T(8,128)(2,1)S(1)} %collective-permute-done.refs_2_), channel_id=1, source_target_pairs={{0,2},{2,0},{1,3},{3,1},{4,6},{6,4},{5,7},{7,5},{8,10},{10,8},{9,1... | collective-permute-start | bytes 725000 | tf_op jit(solution)/shard_map/ppermute | solution.py:407
  22.8 0.5 collective-permute-start.6
  23.4 7.6 %collective-permute-done.1.refs_2_ = bf16[944,128]{1,0:T(8,128)(2,1)S(1)} collective-permute-done((bf16[944,128]{1,0:T(8,128)(2,1)S(1)}, bf16[944,128]{1,0:T(8,128)(2,1)S(1)}, u32[]{:S(2)}, u32[]{:S(2)}) %collective-permute-start.1) | collective-permute-done | bytes 241696 | tf_op jit(solution)/shard_map/ppermute | solution.py:496
  31.0 1.5 %collective-permute-start.2 = (bf16[944,128]{1,0:T(8,128)(2,1)S(1)}, bf16[944,128]{1,0:T(8,128)(2,1)S(1)}, u32[]{:S(2)}, u32[]{:S(2)}) collective-permute-start(bf16[944,128]{1,0:T(8,128)(2,1)S(1)} %collective-permute-done.1.refs_2_), channel_id=1, source_target_pairs={{0,2},{2,0},{1,3},{3,1},{4,6},{6,4},{5,7},{7,5},{8,10},{10,8},{9,1... | collective-permute-start | bytes 725000 | tf_op jit(solution)/shard_map/ppermute | solution.py:407
  32.6 0.0 collective-permute-done.6.refs_9_
  32.6 0.0 collective-permute-done.3.refs_13_.refs_6_
  32.6 3.9 %shard_map.121.refs_7_ = bf16[4,2,2,32,3072]{4,3,2,1,0:T(8,128)(2,1)S(1)} custom-call(s32[3,14]{1,0:T(4,128)S(1)} %get-tuple-element.59.refs_0_, s32[3]{0:T(128)S(1)} %get-tuple-element.57.refs_1_, bf16[944,128]{1,0:T(8,128)(2,1)S(1)} %collective-permute-done.refs_2_, ...), custom_call_target="tpu_custom_call", output_to_operand_aliasing={{}: (14, {})} | custom-call | flops 220200960 | bytes 15728640 | tf_op jit(solution)/shard_map/pallas_call | solution.py:333
  36.5 2.3 %collective-permute-done.2.refs_3_ = bf16[944,128]{1,0:T(8,128)(2,1)S(1)} collective-permute-done((bf16[944,128]{1,0:T(8,128)(2,1)S(1)}, bf16[944,128]{1,0:T(8,128)(2,1)S(1)}, u32[]{:S(2)}, u32[]{:S(2)}) %collective-permute-start.2) | collective-permute-done | bytes 241696 | tf_op jit(solution)/shard_map/ppermute | solution.py:407
  38.9 0.0 collective-permute-done.7.refs_9_
  38.9 8.2 %shard_map.122 = (bf16[4,2,2,32,3072]{4,3,2,1,0:T(8,128)(2,1)S(1)}, f32[128,512]{1,0:T(8,128)S(1)}, bf16[128,512]{1,0:T(8,128)(2,1)S(1)}, f32[128,512]{1,0:T(8,128)S(1)}, bf16[128,512]{1,0:T(8,128)(2,1)S(1)}) custom-call(s32[3,14]{1,0:T(4,128)S(1)} %get-tuple-element.58.refs_0_, s32[3]{0:T(128)S(1)} %get-tuple-element.56.refs_1_, ...), custom_call_target="tpu_custom_call", output_to_operand_aliasing={{0}: (7, {})} | custom-call | flops 3309305856 | bytes 12582912 | tf_op jit(solution)/shard_map/pallas_call | solution.py:333
  47.1 1.5 %collective-permute-start.8 = (bf16[128,512]{1,0:T(8,128)(2,1)S(1)}, bf16[128,512]{1,0:T(8,128)(2,1)S(1)}, u32[]{:S(2)}, u32[]{:S(2)}) collective-permute-start(bf16[128,512]{1,0:T(8,128)(2,1)S(1)} %get-tuple-element.38), channel_id=1, source_target_pairs={{0,2},{2,0},{1,3},{3,1},{4,6},{6,4},{5,7},{7,5},{8,10},{10,8},{9,1... | collective-permute-start | bytes 393224 | tf_op jit(solution)/shard_map/ppermute | solution.py:407
  48.6 1.2 %collective-permute-start.9 = (bf16[128,512]{1,0:T(8,128)(2,1)S(1)}, bf16[128,512]{1,0:T(8,128)(2,1)S(1)}, u32[]{:S(2)}, u32[]{:S(2)}) collective-permute-start(bf16[128,512]{1,0:T(8,128)(2,1)S(1)} %get-tuple-element.40), channel_id=1, source_target_pairs={{0,16},{16,0},{1,17},{17,1},{2,18},{18,2},{3,19},{19,3},{4,20},{20... | collective-permute-start | bytes 393224 | tf_op jit(solution)/shard_map/ppermute | solution.py:407
  49.9 2.3 %collective-permute-done.8.got_x = bf16[128,512]{1,0:T(8,128)(2,1)S(1)} collective-permute-done((bf16[128,512]{1,0:T(8,128)(2,1)S(1)}, bf16[128,512]{1,0:T(8,128)(2,1)S(1)}, u32[]{:S(2)}, u32[]{:S(2)}) %collective-permute-start.8) | collective-permute-done | bytes 131104 | tf_op jit(solution)/shard_map/ppermute | solution.py:407
  52.2 1.4 %collective-permute-done.9.got_y = bf16[128,512]{1,0:T(8,128)(2,1)S(1)} collective-permute-done((bf16[128,512]{1,0:T(8,128)(2,1)S(1)}, bf16[128,512]{1,0:T(8,128)(2,1)S(1)}, u32[]{:S(2)}, u32[]{:S(2)}) %collective-permute-start.9) | collective-permute-done | bytes 131104 | tf_op jit(solution)/shard_map/ppermute | solution.py:407
  53.6 0.1 shard_map.123
  53.7 1.3 %collective-permute-start.10 = (bf16[64,512]{1,0:T(8,128)(2,1)S(1)}, bf16[64,512]{1,0:T(8,128)(2,1)S(1)}, u32[]{:S(2)}, u32[]{:S(2)}) collective-permute-start(bf16[64,512]{1,0:T(8,128)(2,1)S(1)} %get-tuple-element.42), channel_id=1, source_target_pairs={{0,16},{16,0},{1,17},{17,1},{2,18},{18,2},{3,19},{19,3},{4,20},{20... | collective-permute-start | bytes 196616 | tf_op jit(solution)/shard_map/ppermute | solution.py:407
  55.0 0.5 collective-permute-start.11
  55.5 2.5 %collective-permute-done.10.got_x = bf16[64,512]{1,0:T(8,128)(2,1)S(1)} collective-permute-done((bf16[64,512]{1,0:T(8,128)(2,1)S(1)}, bf16[64,512]{1,0:T(8,128)(2,1)S(1)}, u32[]{:S(2)}, u32[]{:S(2)}) %collective-permute-start.10) | collective-permute-done | bytes 65568 | tf_op jit(solution)/shard_map/ppermute | solution.py:407
  58.0 1.2 %collective-permute-done.11.got_y = bf16[64,512]{1,0:T(8,128)(2,1)S(1)} collective-permute-done((bf16[64,512]{1,0:T(8,128)(2,1)S(1)}, bf16[64,512]{1,0:T(8,128)(2,1)S(1)}, u32[]{:S(2)}, u32[]{:S(2)}) %collective-permute-start.11) | collective-permute-done | bytes 65568 | tf_op jit(solution)/shard_map/ppermute | solution.py:407
  59.3 0.3 collective-permute-start.12
  59.5 3.6 %collective-permute-start.13 = (bf16[16,1024]{1,0:T(8,128)(2,1)S(1)}, bf16[16,1024]{1,0:T(8,128)(2,1)S(1)}, u32[]{:S(2)}, u32[]{:S(2)}) collective-permute-start(bf16[16,1024]{1,0:T(8,128)(2,1)S(1)} %get-tuple-element.47), channel_id=1, source_target_pairs={{0,12},{4,0},{8,4},{12,8},{1,13},{5,1},{9,5},{13,9},{2,14},{6,2},{... | collective-permute-start | bytes 98312 | tf_op jit(solution)/shard_map/ppermute | solution.py:522
  63.1 0.0 collective-permute-start.14
  63.1 1.9 %collective-permute-done.12.refs_0_ = bf16[16,1024]{1,0:T(8,128)(2,1)S(1)} collective-permute-done((bf16[16,1024]{1,0:T(8,128)(2,1)S(1)}, bf16[16,1024]{1,0:T(8,128)(2,1)S(1)}, u32[]{:S(2)}, u32[]{:S(2)}) %collective-permute-start.12) | collective-permute-done | bytes 32800 | tf_op jit(solution)/shard_map/ppermute | solution.py:522
  65.0 0.0 collective-permute-done.13.refs_1_
  65.0 2.9 %collective-permute-done.14.refs_2_ = bf16[16,1024]{1,0:T(8,128)(2,1)S(1)} collective-permute-done((bf16[16,1024]{1,0:T(8,128)(2,1)S(1)}, bf16[16,1024]{1,0:T(8,128)(2,1)S(1)}, u32[]{:S(2)}, u32[]{:S(2)}) %collective-permute-start.14) | collective-permute-done | bytes 32800 | tf_op jit(solution)/shard_map/ppermute | solution.py:522
  68.0 0.1 shard_map.125
  68.1 0.6 reshape.56
  (27 shorter events, 0.1 us)
Async XLA Ops:
  0.0 10.5 %copy-start.6 = (s32[36,1]{0,1:T(1,128)S(1)}, s32[36,1]{0,1:T(1,128)}, u32[]{:S(2)}) copy-start(s32[36,1]{0,1:T(1,128)} %param.17) | copy-start | bytes 436
  0.0 10.5 %copy-start.5 = (s32[36,1]{0,1:T(1,128)S(1)}, s32[36,1]{0,1:T(1,128)}, u32[]{:S(2)}) copy-start(s32[36,1]{0,1:T(1,128)} %param.13) | copy-start | bytes 436
  3.5 11.8 %copy-start = (bf16[36,4,24,128]{3,2,1,0:T(8,128)(2,1)S(1)}, bf16[36,4,24,128]{3,2,1,0:T(8,128)(2,1)}, u32[]{:S(2)}) copy-start(bf16[36,4,24,128]{3,2,1,0:T(8,128)(2,1)} %param.12) | copy-start | bytes 2654212
  3.5 11.8 %copy-start.1 = (bf16[36,4,24,128]{3,2,1,0:T(8,128)(2,1)S(1)}, bf16[36,4,24,128]{3,2,1,0:T(8,128)(2,1)}, u32[]{:S(2)}) copy-start(bf16[36,4,24,128]{3,2,1,0:T(8,128)(2,1)} %param.16) | copy-start | bytes 2654212
  3.6 35.3 %collective-permute-start.7 = (bf16[3072,1024]{1,0:T(8,128)(2,1)}, bf16[3072,1024]{1,0:T(8,128)(2,1)}, u32[]{:S(2)}, u32[]{:S(2)}) collective-permute-start(bf16[3072,1024]{1,0:T(8,128)(2,1)} %refs_8_.1), channel_id=1, source_target_pairs={{0,1},{1,0},{2,3},{3,2},{4,5},{5,4},{6,7},{7,6},{8,9},{9,8},{10,11... | collective-permute-start | bytes 18874376 | tf_op jit(solution)/shard_map/ppermute | solution.py:407
  4.1 13.6 %collective-permute-start = (bf16[944,128]{1,0:T(8,128)(2,1)}, bf16[944,128]{1,0:T(8,128)(2,1)S(1)}, u32[]{:S(2)}, u32[]{:S(2)}) collective-permute-start(bf16[944,128]{1,0:T(8,128)(2,1)} %get-tuple-element.28), channel_id=1, source_target_pairs={{0,4},{4,8},{8,12},{12,0},{1,5},{5,9},{9,13},{13,1},{2,6},{6,10},{... | collective-permute-start | bytes 725000 | tf_op jit(solution)/shard_map/ppermute | solution.py:460
  6.7 16.1 %collective-permute-start.5 = (bf16[944,128]{1,0:T(8,128)(2,1)}, bf16[944,128]{1,0:T(8,128)(2,1)S(1)}, u32[]{:S(2)}, u32[]{:S(2)}) collective-permute-start(bf16[944,128]{1,0:T(8,128)(2,1)} %get-tuple-element.34), channel_id=1, source_target_pairs={{0,12},{4,0},{8,4},{12,8},{1,13},{5,1},{9,5},{13,9},{2,14},{6,2},{... | collective-permute-start | bytes 725000 | tf_op jit(solution)/shard_map/ppermute | solution.py:460
  8.8 23.8 %collective-permute-start.3 = (bf16[36,96,128]{2,1,0:T(8,128)(2,1)}, bf16[36,96,128]{2,1,0:T(8,128)(2,1)S(1)}, u32[]{:S(2)}, u32[]{:S(2)}) collective-permute-start(bf16[36,96,128]{2,1,0:T(8,128)(2,1)} %get-tuple-element.32), channel_id=1, source_target_pairs={{0,16},{16,0},{1,17},{17,1},{2,18},{18,2},{3,19},{19,3},{4,20},{20... | collective-permute-start | bytes 2654216 | tf_op jit(solution)/shard_map/ppermute | solution.py:407
  11.1 6.6 %copy-start.7 = (bf16[944,128]{1,0:T(8,128)(2,1)S(1)}, bf16[944,128]{1,0:T(8,128)(2,1)}, u32[]{:S(2)}) copy-start(bf16[944,128]{1,0:T(8,128)(2,1)} %get-tuple-element.31) | copy-start | bytes 724996
  15.3 1.0 %copy-start.2 = (bf16[1840,128]{1,0:T(8,128)(2,1)S(1)}, bf16[1840,128]{1,0:T(8,128)(2,1)}, u32[]{:S(2)}) copy-start(bf16[1840,128]{1,0:T(8,128)(2,1)} %shard_map.119.refs_2_.refs_12_) | copy-start | bytes 1413124
  17.7 13.3 %collective-permute-start.1 = (bf16[944,128]{1,0:T(8,128)(2,1)S(1)}, bf16[944,128]{1,0:T(8,128)(2,1)S(1)}, u32[]{:S(2)}, u32[]{:S(2)}) collective-permute-start(bf16[944,128]{1,0:T(8,128)(2,1)S(1)} %copy-done.7), channel_id=1, source_target_pairs={{0,8},{4,12},{8,0},{12,4},{1,9},{5,13},{9,1},{13,5},{2,10},{6,14},... | collective-permute-start | bytes 725000 | tf_op jit(solution)/shard_map/ppermute | solution.py:496
  21.3 11.2 %collective-permute-start.4 = (bf16[944,128]{1,0:T(8,128)(2,1)S(1)}, bf16[944,128]{1,0:T(8,128)(2,1)S(1)}, u32[]{:S(2)}, u32[]{:S(2)}) collective-permute-start(bf16[944,128]{1,0:T(8,128)(2,1)S(1)} %collective-permute-done.refs_2_), channel_id=1, source_target_pairs={{0,2},{2,0},{1,3},{3,1},{4,6},{6,4},{5,7},{7,5},{8,10},{10,8},{9,1... | collective-permute-start | bytes 725000 | tf_op jit(solution)/shard_map/ppermute | solution.py:407
  22.8 9.7 %collective-permute-start.6 = (bf16[944,128]{1,0:T(8,128)(2,1)S(1)}, bf16[944,128]{1,0:T(8,128)(2,1)S(1)}, u32[]{:S(2)}, u32[]{:S(2)}) collective-permute-start(bf16[944,128]{1,0:T(8,128)(2,1)S(1)} %collective-permute-done.5.refs_8_), channel_id=1, source_target_pairs={{0,2},{2,0},{1,3},{3,1},{4,6},{6,4},{5,7},{7,5},{8,10},{10,8},{9,1... | collective-permute-start | bytes 725000 | tf_op jit(solution)/shard_map/ppermute | solution.py:407
  31.0 7.8 %collective-permute-start.2 = (bf16[944,128]{1,0:T(8,128)(2,1)S(1)}, bf16[944,128]{1,0:T(8,128)(2,1)S(1)}, u32[]{:S(2)}, u32[]{:S(2)}) collective-permute-start(bf16[944,128]{1,0:T(8,128)(2,1)S(1)} %collective-permute-done.1.refs_2_), channel_id=1, source_target_pairs={{0,2},{2,0},{1,3},{3,1},{4,6},{6,4},{5,7},{7,5},{8,10},{10,8},{9,1... | collective-permute-start | bytes 725000 | tf_op jit(solution)/shard_map/ppermute | solution.py:407
  38.9 29.1 %copy-start.3 = (f32[1024]{0:T(1024)S(1)}, f32[1024]{0:T(1024)}, u32[]{:S(2)}) copy-start(f32[1024]{0:T(1024)} %param.22) | copy-start | bytes 12292
  38.9 29.1 %copy-start.4 = (f32[1024]{0:T(1024)S(1)}, f32[1024]{0:T(1024)}, u32[]{:S(2)}) copy-start(f32[1024]{0:T(1024)} %param.23) | copy-start | bytes 12292
  47.1 5.0 %collective-permute-start.8 = (bf16[128,512]{1,0:T(8,128)(2,1)S(1)}, bf16[128,512]{1,0:T(8,128)(2,1)S(1)}, u32[]{:S(2)}, u32[]{:S(2)}) collective-permute-start(bf16[128,512]{1,0:T(8,128)(2,1)S(1)} %get-tuple-element.38), channel_id=1, source_target_pairs={{0,2},{2,0},{1,3},{3,1},{4,6},{6,4},{5,7},{7,5},{8,10},{10,8},{9,1... | collective-permute-start | bytes 393224 | tf_op jit(solution)/shard_map/ppermute | solution.py:407
  48.6 5.0 %collective-permute-start.9 = (bf16[128,512]{1,0:T(8,128)(2,1)S(1)}, bf16[128,512]{1,0:T(8,128)(2,1)S(1)}, u32[]{:S(2)}, u32[]{:S(2)}) collective-permute-start(bf16[128,512]{1,0:T(8,128)(2,1)S(1)} %get-tuple-element.40), channel_id=1, source_target_pairs={{0,16},{16,0},{1,17},{17,1},{2,18},{18,2},{3,19},{19,3},{4,20},{20... | collective-permute-start | bytes 393224 | tf_op jit(solution)/shard_map/ppermute | solution.py:407
  53.7 4.3 %collective-permute-start.10 = (bf16[64,512]{1,0:T(8,128)(2,1)S(1)}, bf16[64,512]{1,0:T(8,128)(2,1)S(1)}, u32[]{:S(2)}, u32[]{:S(2)}) collective-permute-start(bf16[64,512]{1,0:T(8,128)(2,1)S(1)} %get-tuple-element.42), channel_id=1, source_target_pairs={{0,16},{16,0},{1,17},{17,1},{2,18},{18,2},{3,19},{19,3},{4,20},{20... | collective-permute-start | bytes 196616 | tf_op jit(solution)/shard_map/ppermute | solution.py:407
  55.0 4.3 %collective-permute-start.11 = (bf16[64,512]{1,0:T(8,128)(2,1)S(1)}, bf16[64,512]{1,0:T(8,128)(2,1)S(1)}, u32[]{:S(2)}, u32[]{:S(2)}) collective-permute-start(bf16[64,512]{1,0:T(8,128)(2,1)S(1)} %get-tuple-element.44), channel_id=1, source_target_pairs={{0,2},{2,0},{1,3},{3,1},{4,6},{6,4},{5,7},{7,5},{8,10},{10,8},{9,1... | collective-permute-start | bytes 196616 | tf_op jit(solution)/shard_map/ppermute | solution.py:407
  59.3 5.8 %collective-permute-start.12 = (bf16[16,1024]{1,0:T(8,128)(2,1)S(1)}, bf16[16,1024]{1,0:T(8,128)(2,1)S(1)}, u32[]{:S(2)}, u32[]{:S(2)}) collective-permute-start(bf16[16,1024]{1,0:T(8,128)(2,1)S(1)} %get-tuple-element.46), channel_id=1, source_target_pairs={{0,4},{4,8},{8,12},{12,0},{1,5},{5,9},{9,13},{13,1},{2,6},{6,10},{... | collective-permute-start | bytes 98312 | tf_op jit(solution)/shard_map/ppermute | solution.py:522
  59.5 5.5 %collective-permute-start.13 = (bf16[16,1024]{1,0:T(8,128)(2,1)S(1)}, bf16[16,1024]{1,0:T(8,128)(2,1)S(1)}, u32[]{:S(2)}, u32[]{:S(2)}) collective-permute-start(bf16[16,1024]{1,0:T(8,128)(2,1)S(1)} %get-tuple-element.47), channel_id=1, source_target_pairs={{0,12},{4,0},{8,4},{12,8},{1,13},{5,1},{9,5},{13,9},{2,14},{6,2},{... | collective-permute-start | bytes 98312 | tf_op jit(solution)/shard_map/ppermute | solution.py:522
  63.1 4.8 %collective-permute-start.14 = (bf16[16,1024]{1,0:T(8,128)(2,1)S(1)}, bf16[16,1024]{1,0:T(8,128)(2,1)S(1)}, u32[]{:S(2)}, u32[]{:S(2)}) collective-permute-start(bf16[16,1024]{1,0:T(8,128)(2,1)S(1)} %get-tuple-element.48), channel_id=1, source_target_pairs={{0,8},{4,12},{8,0},{12,4},{1,9},{5,13},{9,1},{13,5},{2,10},{6,14},... | collective-permute-start | bytes 98312 | tf_op jit(solution)/shard_map/ppermute | solution.py:522

commit v13 on v11

--- a/solution.py
+++ b/solution.py
@@ -153,14 +153,14 @@
 
 
 def finish_kernel(steps, halves, jobs, count, *refs):
-    theirs, mine, rows_x, out, acc, scale, weight, total, sem = refs[count:]
+    mine, theirs, rows_x, out, acc, scale, weight, total, sem = refs[count:]
     sub, mine_group = lax.axis_index("sub"), lax.axis_index("grp")
     chunks = sem.shape[0]
     height = mine.shape[0] // chunks
 
     def copy(chunk):
         span = pl.ds(pl.multiple_of(chunk * height, height), height)
-        return pltpu.make_async_copy(mine.at[span, :], weight.at[span, :], sem.at[chunk])
+        return pltpu.make_async_copy(theirs.at[span, :], weight.at[span, :], sem.at[chunk])
 
     for chunk in range(chunks):
         copy(chunk).start()
@@ -175,8 +175,8 @@
         )
         copy(chunk).wait()
         total[...] += jnp.dot(
-            left, weight[span, :], preferred_element_type=jnp.float32
-        ) + jnp.dot(right, theirs[span, :], preferred_element_type=jnp.float32)
+            left, mine[span, :], preferred_element_type=jnp.float32
+        ) + jnp.dot(right, weight[span, :], preferred_element_type=jnp.float32)
 
     send_rows(steps, halves, rows_x.shape, mine_group, total, out)
 
@@ -239,7 +239,7 @@
         height, width = mine.shape
         total = bands * groups * shape[3]
         body = functools.partial(finish_kernel, steps, halves, listed, len(operands))
-        operands += [theirs, mine]
+        operands += [mine, theirs]
         specs += [vmem, pl.BlockSpec(memory_space=pl.ANY)]
         count = groups * steps * halves
         shapes.append(jax.ShapeDtypeStruct((count, total // count, width), jnp.bfloat16))
@@ -248,7 +248,7 @@
             pltpu.VMEM((total, width), jnp.float32),
             pltpu.SemaphoreType.DMA((6,)),
         ]
-        limit, moved = 36 << 20, 4 * height * width
+        limit, moved = 24 << 20, 4 * height * width
         flops += 4 * total * height * width
     done = pl.pallas_call(
         body,
@@ -368,7 +368,7 @@
         regrid, bands=nb, steps=steps, tiles=tiles, rows=steps * local_vars, cells=cells
     )
 
-    if ng == 2 and nv == 2 and cap % 2 == 0:
+    if ng == 2 and nv == 2 and cap % 2 == 0 and steps == nb:
         each = cap // 2
         pieces = []
         for shift in order:
@@ -381,7 +381,7 @@
             for piece, (shift, _, _, _) in zip(packed[:2], pieces)
         ]
         embed_other, own_land, send = lax.optimization_barrier((embed_weight, land, send))
-        own_w = pack(54, [(0, 0, cap, None)], ocean_w, atmos_w, ocean_ids, atmos_ids, own_land)[0]
+        own_w = pack(60, [(0, 0, cap, None)], ocean_w, atmos_w, ocean_ids, atmos_ids, own_land)[0]
         embed_other = swap(embed_other, "sub")
         keep, theirs = (ocean_f, atmos_f), (swap(send, "grp"),)
         dest = jnp.where(y == 0, ocean_dest, atmos_dest)

time: 67.4 us -> 65.2 us (0.967)
  Pallas kernels: 21 us -> 18.8 us
    pallas_call x3, Pallas kernels: 14.9 us -> 12.7 us  [regrid(): pl.pallas_call(body, out_shape=shapes, in_specs=specs, out_specs=[vmem] *...]
where the time goes in v13:
time: 65.2 us; the launch traced here: 64.8 us
  Pallas kernels  18.8 us (29%)
  blocking collectives  17.4 us (27%)
  starting transfers between devices  14.1 us (22%)
  waiting for transfers between devices  9.98 us (15%)
  other arithmetic  2.34 us (4%)
  local copies, waits for them, and re-layouts  2 us (3%)
    all_to_all x1, blocking collectives, per_device(): lax.all_to_all(sent, ('grp', 'band', 'var'), split_axis=0, concat_axis=0,...  17.4 us
    pallas_call x3, Pallas kernels, regrid(): pl.pallas_call(body, out_shape=shapes, in_specs=specs, out_specs=[vmem] *...  12.7 us
    ppermute x1, waiting for transfers between devices, per_device(): sent.append(lax.ppermute(piece, 'band', along(shift)))  7.62 us
    pallas_call x2, Pallas kernels, pack(): pl.pallas_call(functools.partial(pack_kernel, pieces, len(fields) // 2),...  6.1 us
    ppermute x5, starting transfers between devices, swap(): return lax.ppermute(x, axis, [(0, 1), (1, 0)])  5.72 us
    ppermute x2, starting transfers between devices, per_device(): lax.ppermute(piece, 'band', along(shift))  4.75 us
    ppermute x1, starting transfers between devices, per_device(): sent.append(lax.ppermute(piece, 'band', along(shift)))  3.65 us
    ppermute x5, waiting for transfers between devices, swap(): return lax.ppermute(x, axis, [(0, 1), (1, 0)])  2.35 us
  transfers between devices with their start and end apart: 8, of which 2 were waited for; matrix products, arithmetic and copies ran while one was open for 3% of the time, Pallas kernels for 12%

profile of v13, /device:TPU:0, one launch (start us, length us, event | category | flops | bytes accessed | tf_op | source)
XLA Modules:
  0.0 64.8 jit_solution(12515129621883363461)
XLA Ops:
  0.0 3.5 %shard_map.118 = (bf16[944,128]{1,0:T(8,128)(2,1)}, bf16[944,128]{1,0:T(8,128)(2,1)}, bf16[944,128]{1,0:T(8,128)(2,1)}, bf16[36,96,128]{2,1,0:T(8,128)(2,1)}) custom-call(bf16[4,1792,128]{2,1,0:T(8,128)(2,1)} %bitcast.29, bf16[4,1792,128]{2,1,0:T(8,128)(2,1)} %bitcast.31, s32[4,14]{1,0:T(4,128)} %bitcast.35, s32[4,14]{1,0:T(4,128)} %bitcast.37, ...), custom_call_target="tpu_custom_call" | custom-call | bytes 2097152 | tf_op jit(solution)/shard_map/pallas_call | solution.py:88
  3.5 0.0 copy-start
  3.5 0.0 copy-start.1
  3.6 0.5 collective-permute-start.7
  4.1 2.6 %collective-permute-start = (bf16[944,128]{1,0:T(8,128)(2,1)}, bf16[944,128]{1,0:T(8,128)(2,1)S(1)}, u32[]{:S(2)}, u32[]{:S(2)}) collective-permute-start(bf16[944,128]{1,0:T(8,128)(2,1)} %get-tuple-element.17), channel_id=1, source_target_pairs={{0,4},{4,8},{8,12},{12,0},{1,5},{5,9},{9,13},{13,1},{2,6},{6,10},{... | collective-permute-start | bytes 725000 | tf_op jit(solution)/shard_map/ppermute | solution.py:380
  6.7 2.1 %collective-permute-start.5 = (bf16[944,128]{1,0:T(8,128)(2,1)}, bf16[944,128]{1,0:T(8,128)(2,1)S(1)}, u32[]{:S(2)}, u32[]{:S(2)}) collective-permute-start(bf16[944,128]{1,0:T(8,128)(2,1)} %get-tuple-element.23), channel_id=1, source_target_pairs={{0,12},{4,0},{8,4},{12,8},{1,13},{5,1},{9,5},{13,9},{2,14},{6,2},{... | collective-permute-start | bytes 725000 | tf_op jit(solution)/shard_map/ppermute | solution.py:380
  8.8 1.7 %collective-permute-start.3 = (bf16[36,96,128]{2,1,0:T(8,128)(2,1)}, bf16[36,96,128]{2,1,0:T(8,128)(2,1)S(1)}, u32[]{:S(2)}, u32[]{:S(2)}) collective-permute-start(bf16[36,96,128]{2,1,0:T(8,128)(2,1)} %get-tuple-element.21), channel_id=1, source_target_pairs={{0,16},{16,0},{1,17},{17,1},{2,18},{18,2},{3,19},{19,3},{4,20},{20... | collective-permute-start | bytes 2654216 | tf_op jit(solution)/shard_map/ppermute | solution.py:327
  10.5 0.0 copy-done.7
  10.5 0.0 copy-done.6
  10.5 0.2 convert_reduce_fusion.1
  10.7 0.1 fusion.1
  10.8 0.1 reshape.97
  10.9 0.1 select_reduce_fusion
  11.0 0.1 reshape.89
  11.0 2.6 %shard_map.119.refs_2_.refs_12_ = bf16[1840,128]{1,0:T(8,128)(2,1)} custom-call(bf16[4,1792,128]{2,1,0:T(8,128)(2,1)} %bitcast.30, bf16[4,1792,128]{2,1,0:T(8,128)(2,1)} %bitcast.32, s32[4,14]{1,0:T(4,128)} %bitcast.36, s32[4,14]{1,0:T(4,128)} %bitcast.38, f32[16,128]{1,0:T(8,128)} %bitcast.34), custom_call_target="tpu_custom_call" | custom-call | bytes 2097152 | tf_op jit(solution)/shard_map/pallas_call | solution.py:88
  13.7 0.1 add_add_fusion
  13.8 0.7 %slice_convert_fusion.2 = s32[1,14]{1,0:T(1,128)S(1)} fusion(bf16[1840,128]{1,0:T(8,128)(2,1)} %shard_map.119.refs_2_.refs_12_), kind=kLoop, calls=%fused_computation.30 | loop fusion | flops 14 | bytes 84 | tf_op jit(solution)/shard_map/convert_element_type | solution.py:391
  14.4 0.7 %fusion.3 = s32[1,14]{1,0:T(1,128)S(1)} fusion(pred[4,14]{1,0:T(4,128)(4,1)S(1)} %reshape.97, s32[]{:T(128)S(6)} %select_n.67, s32[]{:T(128)S(6)} %mul.61, bf16[1840,128]{1,0:T(8,128)(2,1)} %shard_map.119.refs_2_.refs_12_), kind=kLoop, calls=%fused_computation.22 | loop fusion | flops 42 | bytes 106 | tf_op jit(solution)/shard_map/jit(_where)/select_n | solution.py:394
  15.1 0.1 add_add_fusion.2.refs_7_
  15.2 0.1 pad_add_fusion.4.refs_1_.refs_11_
  15.3 0.0 copy-done.1
  15.3 1.0 %copy-done.2 = bf16[1840,128]{1,0:T(8,128)(2,1)S(1)} copy-done((bf16[1840,128]{1,0:T(8,128)(2,1)S(1)}, bf16[1840,128]{1,0:T(8,128)(2,1)}, u32[]{:S(2)}) %copy-start.2) | copy-done | bytes 471064
  16.3 1.3 %shard_map.120.refs_14_ = bf16[4,2,2,32,3072]{4,3,2,1,0:T(8,128)(2,1)S(1)} custom-call(s32[3,14]{1,0:T(4,128)S(1)} %pad_add_fusion.refs_0_.refs_10_, s32[2]{0:T(128)S(1)} %pad_add_fusion.4.refs_1_.refs_11_, bf16[1840,128]{1,0:T(8,128)(2,1)S(1)} %copy-done.2, bf16[36,96,128]{2,1,0:T(8,128)(2,1)S(1)} %bitcast.20, bf16[36,96,128]{2,1,0:T(8,128)(2,1)S(1)} %bitcast.24), custom_call_target="tpu_custom_call" | custom-call | flops 44040192 | bytes 3145728 | tf_op jit(solution)/shard_map/pallas_call | solution.py:253
  17.7 0.0 collective-permute-done.refs_2_
  17.7 3.7 %collective-permute-start.1 = (bf16[944,128]{1,0:T(8,128)(2,1)S(1)}, bf16[944,128]{1,0:T(8,128)(2,1)S(1)}, u32[]{:S(2)}, u32[]{:S(2)}) collective-permute-start(bf16[944,128]{1,0:T(8,128)(2,1)S(1)} %copy-done.8), channel_id=1, source_target_pairs={{0,8},{4,12},{8,0},{12,4},{1,9},{5,13},{9,1},{13,5},{2,10},{6,14},... | collective-permute-start | bytes 725000 | tf_op jit(solution)/shard_map/ppermute | solution.py:416
  21.3 1.5 %collective-permute-start.4 = (bf16[944,128]{1,0:T(8,128)(2,1)S(1)}, bf16[944,128]{1,0:T(8,128)(2,1)S(1)}, u32[]{:S(2)}, u32[]{:S(2)}) collective-permute-start(bf16[944,128]{1,0:T(8,128)(2,1)S(1)} %collective-permute-done.refs_2_), channel_id=1, source_target_pairs={{0,2},{2,0},{1,3},{3,1},{4,6},{6,4},{5,7},{7,5},{8,10},{10,8},{9,1... | collective-permute-start | bytes 725000 | tf_op jit(solution)/shard_map/ppermute | solution.py:327
  22.8 0.0 collective-permute-done.5.refs_8_
  22.8 0.5 collective-permute-start.6
  23.4 7.6 %collective-permute-done.1.refs_2_ = bf16[944,128]{1,0:T(8,128)(2,1)S(1)} collective-permute-done((bf16[944,128]{1,0:T(8,128)(2,1)S(1)}, bf16[944,128]{1,0:T(8,128)(2,1)S(1)}, u32[]{:S(2)}, u32[]{:S(2)}) %collective-permute-start.1) | collective-permute-done | bytes 241696 | tf_op jit(solution)/shard_map/ppermute | solution.py:416
  31.0 1.5 %collective-permute-start.2 = (bf16[944,128]{1,0:T(8,128)(2,1)S(1)}, bf16[944,128]{1,0:T(8,128)(2,1)S(1)}, u32[]{:S(2)}, u32[]{:S(2)}) collective-permute-start(bf16[944,128]{1,0:T(8,128)(2,1)S(1)} %collective-permute-done.1.refs_2_), channel_id=1, source_target_pairs={{0,2},{2,0},{1,3},{3,1},{4,6},{6,4},{5,7},{7,5},{8,10},{10,8},{9,1... | collective-permute-start | bytes 725000 | tf_op jit(solution)/shard_map/ppermute | solution.py:327
  32.6 0.0 collective-permute-done.6.refs_9_
  32.6 0.0 collective-permute-done.4.refs_3_
  32.6 0.0 collective-permute-done.3.refs_13_.refs_6_
  32.6 0.0 slice-start.1
  32.6 3.9 %shard_map.121.refs_7_ = bf16[4,2,2,32,3072]{4,3,2,1,0:T(8,128)(2,1)S(1)} custom-call(s32[3,14]{1,0:T(4,128)S(1)} %get-tuple-element.37.refs_0_, s32[3]{0:T(128)S(1)} %get-tuple-element.35.refs_1_, bf16[944,128]{1,0:T(8,128)(2,1)S(1)} %collective-permute-done.refs_2_, ...), custom_call_target="tpu_custom_call", output_to_operand_aliasing={{}: (14, {})} | custom-call | flops 220200960 | bytes 15728640 | tf_op jit(solution)/shard_map/pallas_call | solution.py:253
  36.5 2.3 %collective-permute-done.2.refs_3_ = bf16[944,128]{1,0:T(8,128)(2,1)S(1)} collective-permute-done((bf16[944,128]{1,0:T(8,128)(2,1)S(1)}, bf16[944,128]{1,0:T(8,128)(2,1)S(1)}, u32[]{:S(2)}, u32[]{:S(2)}) %collective-permute-start.2) | collective-permute-done | bytes 241696 | tf_op jit(solution)/shard_map/ppermute | solution.py:327
  38.9 0.0 collective-permute-done.7.refs_9_
  38.9 0.0 slice-done
  38.9 0.0 copy-start.4
  38.9 0.0 copy-start.5
  38.9 7.5 %shard_map.122 = (bf16[4,2,2,32,3072]{4,3,2,1,0:T(8,128)(2,1)S(1)}, bf16[16,16,1024]{2,1,0:T(8,128)(2,1)S(1)}) custom-call(s32[3,14]{1,0:T(4,128)S(1)} %get-tuple-element.36.refs_0_, s32[3]{0:T(128)S(1)} %get-tuple-element.34.refs_1_, bf16[944,128]{1,0:T(8,128)(2,1)S(1)} %collective-permute-done.1.refs_2_, ...), custom_call_target="tpu_custom_call", output_to_operand_aliasing={{0}: (7, {})} | custom-call | flops 3309305856 | bytes 12582912 | tf_op jit(solution)/shard_map/pallas_call | solution.py:253
  46.4 17.4 %all_to_all.5 = bf16[16,16,1024]{2,1,0:T(8,128)(2,1)S(1)} all-to-all(bf16[16,16,1024]{2,1,0:T(8,128)(2,1)S(1)} %get-tuple-element.26), channel_id=1, replica_groups=mesh['grp'=2,'band'=4,'var'=2,'sub'=2] {'grp','band','var'}, dimensions={0} | all-to-all | bytes 1048576 | tf_op jit(solution)/shard_map/all_to_all | solution.py:428
  63.8 0.1 convert_reduce_fusion
  63.9 0.1 multiply_reduce_fusion
  64.0 0.1 rsqrt.12
  64.1 0.0 copy-done.5
  64.1 0.1 fusion
  64.2 0.6 copy.17
  (24 shorter events, 0.1 us)
Async XLA Ops:
  0.0 10.5 %copy-start.7 = (s32[36,1]{0,1:T(1,128)S(1)}, s32[36,1]{0,1:T(1,128)}, u32[]{:S(2)}) copy-start(s32[36,1]{0,1:T(1,128)} %param.17) | copy-start | bytes 436
  0.0 10.5 %copy-start.6 = (s32[36,1]{0,1:T(1,128)S(1)}, s32[36,1]{0,1:T(1,128)}, u32[]{:S(2)}) copy-start(s32[36,1]{0,1:T(1,128)} %param.13) | copy-start | bytes 436
  3.5 11.8 %copy-start = (bf16[36,4,24,128]{3,2,1,0:T(8,128)(2,1)S(1)}, bf16[36,4,24,128]{3,2,1,0:T(8,128)(2,1)}, u32[]{:S(2)}) copy-start(bf16[36,4,24,128]{3,2,1,0:T(8,128)(2,1)} %param.12) | copy-start | bytes 2654212
  3.5 11.8 %copy-start.1 = (bf16[36,4,24,128]{3,2,1,0:T(8,128)(2,1)S(1)}, bf16[36,4,24,128]{3,2,1,0:T(8,128)(2,1)}, u32[]{:S(2)}) copy-start(bf16[36,4,24,128]{3,2,1,0:T(8,128)(2,1)} %param.16) | copy-start | bytes 2654212
  3.6 35.3 %collective-permute-start.7 = (bf16[3072,1024]{1,0:T(8,128)(2,1)}, bf16[3072,1024]{1,0:T(8,128)(2,1)}, u32[]{:S(2)}, u32[]{:S(2)}) collective-permute-start(bf16[3072,1024]{1,0:T(8,128)(2,1)} %refs_8_.1), channel_id=1, source_target_pairs={{0,1},{1,0},{2,3},{3,2},{4,5},{5,4},{6,7},{7,6},{8,9},{9,8},{10,11... | collective-permute-start | bytes 18874376 | tf_op jit(solution)/shard_map/ppermute | solution.py:327
  4.1 13.6 %collective-permute-start = (bf16[944,128]{1,0:T(8,128)(2,1)}, bf16[944,128]{1,0:T(8,128)(2,1)S(1)}, u32[]{:S(2)}, u32[]{:S(2)}) collective-permute-start(bf16[944,128]{1,0:T(8,128)(2,1)} %get-tuple-element.17), channel_id=1, source_target_pairs={{0,4},{4,8},{8,12},{12,0},{1,5},{5,9},{9,13},{13,1},{2,6},{6,10},{... | collective-permute-start | bytes 725000 | tf_op jit(solution)/shard_map/ppermute | solution.py:380
  6.7 16.1 %collective-permute-start.5 = (bf16[944,128]{1,0:T(8,128)(2,1)}, bf16[944,128]{1,0:T(8,128)(2,1)S(1)}, u32[]{:S(2)}, u32[]{:S(2)}) collective-permute-start(bf16[944,128]{1,0:T(8,128)(2,1)} %get-tuple-element.23), channel_id=1, source_target_pairs={{0,12},{4,0},{8,4},{12,8},{1,13},{5,1},{9,5},{13,9},{2,14},{6,2},{... | collective-permute-start | bytes 725000 | tf_op jit(solution)/shard_map/ppermute | solution.py:380
  8.8 23.8 %collective-permute-start.3 = (bf16[36,96,128]{2,1,0:T(8,128)(2,1)}, bf16[36,96,128]{2,1,0:T(8,128)(2,1)S(1)}, u32[]{:S(2)}, u32[]{:S(2)}) collective-permute-start(bf16[36,96,128]{2,1,0:T(8,128)(2,1)} %get-tuple-element.21), channel_id=1, source_target_pairs={{0,16},{16,0},{1,17},{17,1},{2,18},{18,2},{3,19},{19,3},{4,20},{20... | collective-permute-start | bytes 2654216 | tf_op jit(solution)/shard_map/ppermute | solution.py:327
  11.0 6.6 %copy-start.8 = (bf16[944,128]{1,0:T(8,128)(2,1)S(1)}, bf16[944,128]{1,0:T(8,128)(2,1)}, u32[]{:S(2)}) copy-start(bf16[944,128]{1,0:T(8,128)(2,1)} %get-tuple-element.20) | copy-start | bytes 724996
  15.3 1.0 %copy-start.2 = (bf16[1840,128]{1,0:T(8,128)(2,1)S(1)}, bf16[1840,128]{1,0:T(8,128)(2,1)}, u32[]{:S(2)}) copy-start(bf16[1840,128]{1,0:T(8,128)(2,1)} %shard_map.119.refs_2_.refs_12_) | copy-start | bytes 1413124
  16.3 16.3 %copy-start.3 = (bf16[1840,128]{1,0:T(8,128)(2,1)S(1)}, bf16[1840,128]{1,0:T(8,128)(2,1)}, u32[]{:S(2)}) copy-start(bf16[1840,128]{1,0:T(8,128)(2,1)} %shard_map.119.refs_2_.refs_12_) | copy-start | bytes 1413124
  16.3 22.6 %slice-start = ((s8[6291456]{0:T(1024)(128)(4,1)}), s8[4194304]{0:T(1024)(128)(4,1)S(1)}, s32[]{:S(2)}) async-start(s8[6291456]{0:T(1024)(128)(4,1)} %bitcast.27), calls=%async_computation.1 | async-start | bytes 8388608
  17.7 13.3 %collective-permute-start.1 = (bf16[944,128]{1,0:T(8,128)(2,1)S(1)}, bf16[944,128]{1,0:T(8,128)(2,1)S(1)}, u32[]{:S(2)}, u32[]{:S(2)}) collective-permute-start(bf16[944,128]{1,0:T(8,128)(2,1)S(1)} %copy-done.8), channel_id=1, source_target_pairs={{0,8},{4,12},{8,0},{12,4},{1,9},{5,13},{9,1},{13,5},{2,10},{6,14},... | collective-permute-start | bytes 725000 | tf_op jit(solution)/shard_map/ppermute | solution.py:416
  21.3 11.2 %collective-permute-start.4 = (bf16[944,128]{1,0:T(8,128)(2,1)S(1)}, bf16[944,128]{1,0:T(8,128)(2,1)S(1)}, u32[]{:S(2)}, u32[]{:S(2)}) collective-permute-start(bf16[944,128]{1,0:T(8,128)(2,1)S(1)} %collective-permute-done.refs_2_), channel_id=1, source_target_pairs={{0,2},{2,0},{1,3},{3,1},{4,6},{6,4},{5,7},{7,5},{8,10},{10,8},{9,1... | collective-permute-start | bytes 725000 | tf_op jit(solution)/shard_map/ppermute | solution.py:327
  22.8 9.7 %collective-permute-start.6 = (bf16[944,128]{1,0:T(8,128)(2,1)S(1)}, bf16[944,128]{1,0:T(8,128)(2,1)S(1)}, u32[]{:S(2)}, u32[]{:S(2)}) collective-permute-start(bf16[944,128]{1,0:T(8,128)(2,1)S(1)} %collective-permute-done.5.refs_8_), channel_id=1, source_target_pairs={{0,2},{2,0},{1,3},{3,1},{4,6},{6,4},{5,7},{7,5},{8,10},{10,8},{9,1... | collective-permute-start | bytes 725000 | tf_op jit(solution)/shard_map/ppermute | solution.py:327
  31.0 7.9 %collective-permute-start.2 = (bf16[944,128]{1,0:T(8,128)(2,1)S(1)}, bf16[944,128]{1,0:T(8,128)(2,1)S(1)}, u32[]{:S(2)}, u32[]{:S(2)}) collective-permute-start(bf16[944,128]{1,0:T(8,128)(2,1)S(1)} %collective-permute-done.1.refs_2_), channel_id=1, source_target_pairs={{0,2},{2,0},{1,3},{3,1},{4,6},{6,4},{5,7},{7,5},{8,10},{10,8},{9,1... | collective-permute-start | bytes 725000 | tf_op jit(solution)/shard_map/ppermute | solution.py:327
  32.6 6.3 %slice-start.1 = ((s8[6291456]{0:T(1024)(128)(4,1)}), s8[2097152]{0:T(1024)(128)(4,1)S(1)}, s32[]{:S(2)}) async-start(s8[6291456]{0:T(1024)(128)(4,1)} %bitcast.27), calls=%async_computation.2 | async-start | bytes 4194304
  38.9 25.0 %copy-start.4 = (f32[1024]{0:T(1024)S(1)}, f32[1024]{0:T(1024)}, u32[]{:S(2)}) copy-start(f32[1024]{0:T(1024)} %param.22) | copy-start | bytes 12292
  38.9 25.2 %copy-start.5 = (f32[1024]{0:T(1024)S(1)}, f32[1024]{0:T(1024)}, u32[]{:S(2)}) copy-start(f32[1024]{0:T(1024)} %param.23) | copy-start | bytes 12292

commit v14 on v13

--- a/solution.py
+++ b/solution.py
@@ -24,10 +24,10 @@
 
 
 def pack_kernel(pieces, moved, *refs):
-    ocean_w, atmos_w, ocean_ids, atmos_ids, land = refs[:5]
-    fields, refs = refs[5 : 5 + 2 * moved], refs[5 + 2 * moved :]
+    ocean_w, atmos_w = refs[:2]
+    fields, held = refs[5 : 5 + 2 * moved], refs[5 + 2 * moved :]
     count = len(pieces) + moved
-    stages, sem = refs[:count], refs[-1]
+    stages, (ocean_ids, atmos_ids, land, sem) = held[:count], held[count:]
     me, bands = lax.axis_index("band"), ocean_w.shape[0]
     x, y = lax.axis_index("var"), lax.axis_index("grp")
     cells, tiles = land.shape[-1], land.shape[0]
@@ -62,6 +62,14 @@
         for copy in loads(atmos_w, 0):
             copy.start()
 
+    tables = [
+        pltpu.make_async_copy(source, target, sem.at[count + at])
+        for at, (source, target) in enumerate(zip(refs[2:5], (ocean_ids, atmos_ids, land)))
+    ]
+    for copy in tables:
+        copy.start()
+    for copy in tables:
+        copy.wait()
     fraction = land[...]
     high = fraction.astype(jnp.bfloat16)
     low = (fraction - high.astype(jnp.float32)).astype(jnp.bfloat16)
@@ -88,9 +96,10 @@
     return pl.pallas_call(
         functools.partial(pack_kernel, pieces, len(fields) // 2),
         out_shape=[jax.ShapeDtypeStruct(shape, jnp.bfloat16) for shape in shapes],
-        in_specs=[any_spec] * 2 + [vmem] * 3 + [any_spec] * len(fields),
+        in_specs=[any_spec] * (5 + len(fields)),
         out_specs=[vmem] * len(shapes),
-        scratch_shapes=[pltpu.SemaphoreType.DMA((len(shapes),))],
+        scratch_shapes=[pltpu.VMEM(a.shape, a.dtype) for a in (ocean_ids, atmos_ids, land)]
+        + [pltpu.SemaphoreType.DMA((len(shapes) + 3,))],
         cost_estimate=pl.CostEstimate(flops=0, bytes_accessed=2 << 20, transcendentals=0),
         compiler_params=pltpu.CompilerParams(vmem_limit_bytes=limit << 20),
     )(ocean_w, atmos_w, ocean_ids, atmos_ids, land, *fields)
@@ -411,8 +420,8 @@
         ours, others = [(0, keep)], [(1, theirs)]
         jobs = [job_of(me, [own_w], [cap], [jnp.int32(0)], ours)]
         rows_x = call(jobs, None, groups=2)
-        for at, (piece, (shift, _, _, _)) in enumerate(zip(packed[2:], pieces[2:])):
-            piece, sent[at], rows_x = lax.optimization_barrier((piece, sent[at], rows_x))
+        for piece, (shift, _, _, _) in zip(packed[2:], pieces[2:]):
+            piece, rows_x = lax.optimization_barrier((piece, rows_x))
             sent.append(lax.ppermute(piece, "band", along(shift)))
         crossed = [swap(piece, "var") for piece in sent]
         jobs += [job_at(shift, ours) for shift in order]

time: 65.2 us -> 73.1 us (1.12)
  local copies, waits for them, and re-layouts: 2 us -> 10.4 us
  starting transfers between devices: 14.1 us -> 11.4 us
  other arithmetic: 2.34 us -> 4.35 us
  waiting for transfers between devices: 9.98 us -> 8.55 us
  blocking collectives: 17.4 us -> 18.7 us
    unnamed x22 -> x26, local copies, waits for them, and re-layouts: 1.08 us -> 9.51 us
    ppermute x1, starting transfers between devices: 3.65 us -> 0.85 us  [per_device(): sent.append(lax.ppermute(piece, 'band', along(shift)))]
    ppermute x5, waiting for transfers between devices: 2.35 us -> 0.01 us  [swap(): return lax.ppermute(x, axis, [(0, 1), (1, 0)])]
    pallas_call x3, Pallas kernels: 12.7 us -> 14.2 us  [regrid(): pl.pallas_call(body, out_shape=shapes, in_specs=specs, out_specs=[vmem] *...]
    pallas_call x2, Pallas kernels: 6.1 us -> 4.65 us  [pack(): pl.pallas_call(functools.partial(pack_kernel, pieces, len(fields) // 2),...]
    convert_element_type x4, other arithmetic: 0.7 us -> 2.05 us  [job_of(): tile = parts[0][meta_at + 2 * tiles, :cap].astype(jnp.int32)]
    all_to_all x1, blocking collectives: 17.4 us -> 18.7 us  [per_device(): lax.all_to_all(sent, ('grp', 'band', 'var'), split_axis=0, concat_axis=0,...]
    ppermute x1, waiting for transfers between devices: 7.62 us -> 8.53 us  [per_device(): sent.append(lax.ppermute(piece, 'band', along(shift)))]
  transfers between devices with their start and end apart: 8 -> 8, of which waited for: 2 -> 1; matrix products, arithmetic and copies ran while one was open for 3% -> 6% of each run, Pallas kernels for 12% -> 11%
where the time goes in v14:
time: 73.1 us; the launch traced here: 72.4 us
  Pallas kernels  18.8 us (26%)
  blocking collectives  18.7 us (26%)
  starting transfers between devices  11.4 us (16%)
  local copies, waits for them, and re-layouts  10.4 us (14%)
  waiting for transfers between devices  8.55 us (12%)
  other arithmetic  4.35 us (6%)
    all_to_all x1, blocking collectives, per_device(): lax.all_to_all(sent, ('grp', 'band', 'var'), split_axis=0, concat_axis=0,...  18.7 us
    pallas_call x3, Pallas kernels, regrid(): pl.pallas_call(body, out_shape=shapes, in_specs=specs, out_specs=[vmem] *...  14.2 us
    unnamed x26, local copies, waits for them, and re-layouts  9.51 us
    ppermute x1, waiting for transfers between devices, per_device(): sent.append(lax.ppermute(piece, 'band', along(shift)))  8.53 us
    ppermute x5, starting transfers between devices, swap(): return lax.ppermute(x, axis, [(0, 1), (1, 0)])  5.77 us
    ppermute x2, starting transfers between devices, per_device(): lax.ppermute(piece, 'band', along(shift))  4.75 us
    pallas_call x2, Pallas kernels, pack(): pl.pallas_call(functools.partial(pack_kernel, pieces, len(fields) // 2),...  4.65 us
    convert_element_type x4, other arithmetic, job_of(): tile = parts[0][meta_at + 2 * tiles, :cap].astype(jnp.int32)  2.05 us
  transfers between devices with their start and end apart: 8, of which 1 were waited for; matrix products, arithmetic and copies ran while one was open for 6% of the time, Pallas kernels for 11%

profile of v14, /device:TPU:0, one launch (start us, length us, event | category | flops | bytes accessed | tf_op | source)
XLA Modules:
  0.0 72.4 jit_solution(5496966319220523055)
XLA Ops:
  0.0 2.8 %shard_map.118 = (bf16[944,128]{1,0:T(8,128)(2,1)}, bf16[944,128]{1,0:T(8,128)(2,1)}, bf16[944,128]{1,0:T(8,128)(2,1)}, bf16[36,96,128]{2,1,0:T(8,128)(2,1)}) custom-call(bf16[4,1792,128]{2,1,0:T(8,128)(2,1)} %bitcast.27, bf16[4,1792,128]{2,1,0:T(8,128)(2,1)} %bitcast.29, s32[4,14]{1,0:T(4,128)} %bitcast.33, s32[4,14]{1,0:T(4,128)} %bitcast.35, ...), custom_call_target="tpu_custom_call" | custom-call | bytes 2097152 | tf_op jit(solution)/shard_map/pallas_call | solution.py:96
  2.8 0.5 collective-permute-start.7
  3.3 2.6 %collective-permute-start.3 = (bf16[944,128]{1,0:T(8,128)(2,1)}, bf16[944,128]{1,0:T(8,128)(2,1)}, u32[]{:S(2)}, u32[]{:S(2)}) collective-permute-start(bf16[944,128]{1,0:T(8,128)(2,1)} %get-tuple-element.20), channel_id=1, source_target_pairs={{0,4},{4,8},{8,12},{12,0},{1,5},{5,9},{9,13},{13,1},{2,6},{6,10},{... | collective-permute-start | bytes 725000 | tf_op jit(solution)/shard_map/ppermute | solution.py:389
  5.9 2.1 %collective-permute-start.5 = (bf16[944,128]{1,0:T(8,128)(2,1)}, bf16[944,128]{1,0:T(8,128)(2,1)}, u32[]{:S(2)}, u32[]{:S(2)}) collective-permute-start(bf16[944,128]{1,0:T(8,128)(2,1)} %get-tuple-element.21), channel_id=1, source_target_pairs={{0,12},{4,0},{8,4},{12,8},{1,13},{5,1},{9,5},{13,9},{2,14},{6,2},{... | collective-permute-start | bytes 725000 | tf_op jit(solution)/shard_map/ppermute | solution.py:389
  8.1 1.7 %collective-permute-start.2 = (bf16[36,96,128]{2,1,0:T(8,128)(2,1)}, bf16[36,96,128]{2,1,0:T(8,128)(2,1)}, u32[]{:S(2)}, u32[]{:S(2)}) collective-permute-start(bf16[36,96,128]{2,1,0:T(8,128)(2,1)} %get-tuple-element.19), channel_id=1, source_target_pairs={{0,16},{16,0},{1,17},{17,1},{2,18},{18,2},{3,19},{19,3},{4,20},{20... | collective-permute-start | bytes 2654216 | tf_op jit(solution)/shard_map/ppermute | solution.py:336
  9.7 0.2 convert_reduce_fusion.1
  9.9 0.1 fusion.1
  10.0 0.1 reshape.97
  10.1 0.1 select_reduce_fusion
  10.2 0.1 reshape.89
  10.3 1.9 %shard_map.119.refs_2_.refs_12_ = bf16[1840,128]{1,0:T(8,128)(2,1)} custom-call(bf16[4,1792,128]{2,1,0:T(8,128)(2,1)} %bitcast.28, bf16[4,1792,128]{2,1,0:T(8,128)(2,1)} %bitcast.30, s32[4,14]{1,0:T(4,128)} %bitcast.34, s32[4,14]{1,0:T(4,128)} %bitcast.36, f32[16,128]{1,0:T(8,128)} %bitcast.32), custom_call_target="tpu_custom_call" | custom-call | bytes 2097152 | tf_op jit(solution)/shard_map/pallas_call | solution.py:96
  12.2 0.7 slice_convert_fusion.3
  12.9 0.7 fusion.3
  13.6 0.1 pad_add_fusion.4.refs_1_.refs_11_
  13.7 1.2 %copy-done = bf16[36,4,24,128]{3,2,1,0:T(8,128)(2,1)S(1)} copy-done((bf16[36,4,24,128]{3,2,1,0:T(8,128)(2,1)S(1)}, bf16[36,4,24,128]{3,2,1,0:T(8,128)(2,1)}, u32[]{:S(2)}) %copy-start) | copy-done | bytes 884760
  14.8 1.2 %copy-done.3 = bf16[36,4,24,128]{3,2,1,0:T(8,128)(2,1)S(1)} copy-done((bf16[36,4,24,128]{3,2,1,0:T(8,128)(2,1)S(1)}, bf16[36,4,24,128]{3,2,1,0:T(8,128)(2,1)}, u32[]{:S(2)}) %copy-start.3) | copy-done | bytes 884760
  16.0 1.0 %copy-done.7 = bf16[1840,128]{1,0:T(8,128)(2,1)S(1)} copy-done((bf16[1840,128]{1,0:T(8,128)(2,1)S(1)}, bf16[1840,128]{1,0:T(8,128)(2,1)}, u32[]{:S(2)}) %copy-start.7) | copy-done | bytes 471064
  17.0 1.3 %shard_map.120.refs_14_ = bf16[4,2,2,32,3072]{4,3,2,1,0:T(8,128)(2,1)S(1)} custom-call(s32[3,14]{1,0:T(4,128)S(1)} %pad_add_fusion.refs_0_.refs_10_, s32[2]{0:T(128)S(1)} %pad_add_fusion.4.refs_1_.refs_11_, bf16[1840,128]{1,0:T(8,128)(2,1)S(1)} %copy-done.7, bf16[36,96,128]{2,1,0:T(8,128)(2,1)S(1)} %bitcast.20, bf16[36,96,128]{2,1,0:T(8,128)(2,1)S(1)} %bitcast.24), custom_call_target="tpu_custom_call" | custom-call | flops 44040192 | bytes 3145728 | tf_op jit(solution)/shard_map/pallas_call | solution.py:262
  18.4 0.9 %collective-permute-start = (bf16[944,128]{1,0:T(8,128)(2,1)}, bf16[944,128]{1,0:T(8,128)(2,1)S(1)}, u32[]{:S(2)}, u32[]{:S(2)}) collective-permute-start(bf16[944,128]{1,0:T(8,128)(2,1)} %get-tuple-element.18), channel_id=1, source_target_pairs={{0,8},{4,12},{8,0},{12,4},{1,9},{5,13},{9,1},{13,5},{2,10},{6,14},... | collective-permute-start | bytes 725000 | tf_op jit(solution)/shard_map/ppermute | solution.py:425
  19.2 0.1 add_add_fusion
  19.3 0.1 add_add_fusion.2.refs_7_
  19.4 0.0 collective-permute-done.3.refs_2_
  19.4 0.7 slice_convert_fusion.1
  20.0 1.5 %collective-permute-start.4 = (bf16[944,128]{1,0:T(8,128)(2,1)}, bf16[944,128]{1,0:T(8,128)(2,1)S(1)}, u32[]{:S(2)}, u32[]{:S(2)}) collective-permute-start(bf16[944,128]{1,0:T(8,128)(2,1)} %collective-permute-done.3.refs_2_), channel_id=1, source_target_pairs={{0,2},{2,0},{1,3},{3,1},{4,6},{6,4},{5,7},{7,5},{8,10},{10,8},{9,1... | collective-permute-start | bytes 725000 | tf_op jit(solution)/shard_map/ppermute | solution.py:336
  21.5 0.0 collective-permute-done.5.refs_8_
  21.5 0.5 collective-permute-start.6
  22.1 0.7 slice_convert_fusion
  22.8 8.5 %collective-permute-done.refs_2_ = bf16[944,128]{1,0:T(8,128)(2,1)S(1)} collective-permute-done((bf16[944,128]{1,0:T(8,128)(2,1)}, bf16[944,128]{1,0:T(8,128)(2,1)S(1)}, u32[]{:S(2)}, u32[]{:S(2)}) %collective-permute-start) | collective-permute-done | bytes 241696 | tf_op jit(solution)/shard_map/ppermute | solution.py:425
  31.3 0.7 fusion.6
  32.0 1.6 %collective-permute-start.1 = (bf16[944,128]{1,0:T(8,128)(2,1)S(1)}, bf16[944,128]{1,0:T(8,128)(2,1)S(1)}, u32[]{:S(2)}, u32[]{:S(2)}) collective-permute-start(bf16[944,128]{1,0:T(8,128)(2,1)S(1)} %collective-permute-done.refs_2_), channel_id=1, source_target_pairs={{0,2},{2,0},{1,3},{3,1},{4,6},{6,4},{5,7},{7,5},{8,10},{10,8},{9,1... | collective-permute-start | bytes 725000 | tf_op jit(solution)/shard_map/ppermute | solution.py:336
  33.6 0.0 collective-permute-done.4.refs_3_
  33.6 0.0 collective-permute-done.6.refs_9_
  33.6 0.0 collective-permute-done.2.refs_13_.refs_6_
  33.6 0.0 copy-start.1
  33.6 1.2 %copy-done.1 = bf16[36,4,24,128]{3,2,1,0:T(8,128)(2,1)S(1)} copy-done((bf16[36,4,24,128]{3,2,1,0:T(8,128)(2,1)S(1)}, bf16[36,4,24,128]{3,2,1,0:T(8,128)(2,1)}, u32[]{:S(2)}) %copy-start.1) | copy-done | bytes 884760
  34.8 1.2 %copy-done.4 = bf16[36,4,24,128]{3,2,1,0:T(8,128)(2,1)S(1)} copy-done((bf16[36,4,24,128]{3,2,1,0:T(8,128)(2,1)S(1)}, bf16[36,4,24,128]{3,2,1,0:T(8,128)(2,1)}, u32[]{:S(2)}) %copy-start.4) | copy-done | bytes 884760
  35.9 1.0 %copy-done.8 = bf16[1840,128]{1,0:T(8,128)(2,1)S(1)} copy-done((bf16[1840,128]{1,0:T(8,128)(2,1)S(1)}, bf16[1840,128]{1,0:T(8,128)(2,1)}, u32[]{:S(2)}) %copy-start.8) | copy-done | bytes 471064
  37.0 4.8 %shard_map.121.refs_7_ = bf16[4,2,2,32,3072]{4,3,2,1,0:T(8,128)(2,1)S(1)} custom-call(s32[3,14]{1,0:T(4,128)S(1)} %get-tuple-element.35.refs_0_, s32[3]{0:T(128)S(1)} %get-tuple-element.33.refs_1_, bf16[944,128]{1,0:T(8,128)(2,1)} %collective-permute-done.3.refs_2_, ...), custom_call_target="tpu_custom_call", output_to_operand_aliasing={{}: (14, {})} | custom-call | flops 220200960 | bytes 15728640 | tf_op jit(solution)/shard_map/pallas_call | solution.py:262
  41.8 0.0 collective-permute-done.1.refs_3_
  41.8 0.0 copy-start.6
  41.8 2.8 %copy-done.6 = bf16[3072,1024]{1,0:T(8,128)(2,1)S(1)} copy-done((bf16[3072,1024]{1,0:T(8,128)(2,1)S(1)}, bf16[3072,1024]{1,0:T(8,128)(2,1)}, u32[]{:S(2)}) %copy-start.6) | copy-done | bytes 6291480
  44.6 8.1 %shard_map.122 = (bf16[4,2,2,32,3072]{4,3,2,1,0:T(8,128)(2,1)S(1)}, bf16[16,16,1024]{2,1,0:T(8,128)(2,1)S(1)}) custom-call(s32[3,14]{1,0:T(4,128)S(1)} %get-tuple-element.34.refs_0_, s32[3]{0:T(128)S(1)} %get-tuple-element.32.refs_1_, bf16[944,128]{1,0:T(8,128)(2,1)S(1)} %collective-permute-done.refs_2_, ...), custom_call_target="tpu_custom_call", output_to_operand_aliasing={{0}: (7, {})} | custom-call | flops 3309305856 | bytes 12582912 | tf_op jit(solution)/shard_map/pallas_call | solution.py:262
  52.7 18.7 %all_to_all.5 = bf16[16,16,1024]{2,1,0:T(8,128)(2,1)S(1)} all-to-all(bf16[16,16,1024]{2,1,0:T(8,128)(2,1)S(1)} %get-tuple-element.24), channel_id=1, replica_groups=mesh['grp'=2,'band'=4,'var'=2,'sub'=2] {'grp','band','var'}, dimensions={0} | all-to-all | bytes 1048576 | tf_op jit(solution)/shard_map/all_to_all | solution.py:437
  71.4 0.1 convert_reduce_fusion
  71.5 0.1 multiply_reduce_fusion
  71.6 0.1 rsqrt.12
  71.7 0.1 fusion
  71.8 0.6 copy.17
  (27 shorter events, 0.1 us)
Async XLA Ops:
  0.0 9.7 %copy-start.12 = (s32[36,1]{0,1:T(1,128)S(1)}, s32[36,1]{0,1:T(1,128)}, u32[]{:S(2)}) copy-start(s32[36,1]{0,1:T(1,128)} %param.17) | copy-start | bytes 436
  0.0 9.7 %copy-start.11 = (s32[36,1]{0,1:T(1,128)S(1)}, s32[36,1]{0,1:T(1,128)}, u32[]{:S(2)}) copy-start(s32[36,1]{0,1:T(1,128)} %param.13) | copy-start | bytes 436
  2.8 39.0 %collective-permute-start.7 = (bf16[3072,1024]{1,0:T(8,128)(2,1)}, bf16[3072,1024]{1,0:T(8,128)(2,1)}, u32[]{:S(2)}, u32[]{:S(2)}) collective-permute-start(bf16[3072,1024]{1,0:T(8,128)(2,1)} %refs_8_.1), channel_id=1, source_target_pairs={{0,1},{1,0},{2,3},{3,2},{4,5},{5,4},{6,7},{7,6},{8,9},{9,8},{10,11... | collective-permute-start | bytes 18874376 | tf_op jit(solution)/shard_map/ppermute | solution.py:336
  3.3 16.1 %collective-permute-start.3 = (bf16[944,128]{1,0:T(8,128)(2,1)}, bf16[944,128]{1,0:T(8,128)(2,1)}, u32[]{:S(2)}, u32[]{:S(2)}) collective-permute-start(bf16[944,128]{1,0:T(8,128)(2,1)} %get-tuple-element.20), channel_id=1, source_target_pairs={{0,4},{4,8},{8,12},{12,0},{1,5},{5,9},{9,13},{13,1},{2,6},{6,10},{... | collective-permute-start | bytes 725000 | tf_op jit(solution)/shard_map/ppermute | solution.py:389
  5.9 15.6 %collective-permute-start.5 = (bf16[944,128]{1,0:T(8,128)(2,1)}, bf16[944,128]{1,0:T(8,128)(2,1)}, u32[]{:S(2)}, u32[]{:S(2)}) collective-permute-start(bf16[944,128]{1,0:T(8,128)(2,1)} %get-tuple-element.21), channel_id=1, source_target_pairs={{0,12},{4,0},{8,4},{12,8},{1,13},{5,1},{9,5},{13,9},{2,14},{6,2},{... | collective-permute-start | bytes 725000 | tf_op jit(solution)/shard_map/ppermute | solution.py:389
  8.1 25.5 %collective-permute-start.2 = (bf16[36,96,128]{2,1,0:T(8,128)(2,1)}, bf16[36,96,128]{2,1,0:T(8,128)(2,1)}, u32[]{:S(2)}, u32[]{:S(2)}) collective-permute-start(bf16[36,96,128]{2,1,0:T(8,128)(2,1)} %get-tuple-element.19), channel_id=1, source_target_pairs={{0,16},{16,0},{1,17},{17,1},{2,18},{18,2},{3,19},{19,3},{4,20},{20... | collective-permute-start | bytes 2654216 | tf_op jit(solution)/shard_map/ppermute | solution.py:336
  13.7 1.2 %copy-start = (bf16[36,4,24,128]{3,2,1,0:T(8,128)(2,1)S(1)}, bf16[36,4,24,128]{3,2,1,0:T(8,128)(2,1)}, u32[]{:S(2)}) copy-start(bf16[36,4,24,128]{3,2,1,0:T(8,128)(2,1)} %param.12) | copy-start | bytes 2654212
  14.8 1.2 %copy-start.3 = (bf16[36,4,24,128]{3,2,1,0:T(8,128)(2,1)S(1)}, bf16[36,4,24,128]{3,2,1,0:T(8,128)(2,1)}, u32[]{:S(2)}) copy-start(bf16[36,4,24,128]{3,2,1,0:T(8,128)(2,1)} %param.16) | copy-start | bytes 2654212
  16.0 1.0 %copy-start.7 = (bf16[1840,128]{1,0:T(8,128)(2,1)S(1)}, bf16[1840,128]{1,0:T(8,128)(2,1)}, u32[]{:S(2)}) copy-start(bf16[1840,128]{1,0:T(8,128)(2,1)} %shard_map.119.refs_2_.refs_12_) | copy-start | bytes 1413124
  18.4 12.9 %collective-permute-start = (bf16[944,128]{1,0:T(8,128)(2,1)}, bf16[944,128]{1,0:T(8,128)(2,1)S(1)}, u32[]{:S(2)}, u32[]{:S(2)}) collective-permute-start(bf16[944,128]{1,0:T(8,128)(2,1)} %get-tuple-element.18), channel_id=1, source_target_pairs={{0,8},{4,12},{8,0},{12,4},{1,9},{5,13},{9,1},{13,5},{2,10},{6,14},... | collective-permute-start | bytes 725000 | tf_op jit(solution)/shard_map/ppermute | solution.py:425
  20.0 13.5 %collective-permute-start.4 = (bf16[944,128]{1,0:T(8,128)(2,1)}, bf16[944,128]{1,0:T(8,128)(2,1)S(1)}, u32[]{:S(2)}, u32[]{:S(2)}) collective-permute-start(bf16[944,128]{1,0:T(8,128)(2,1)} %collective-permute-done.3.refs_2_), channel_id=1, source_target_pairs={{0,2},{2,0},{1,3},{3,1},{4,6},{6,4},{5,7},{7,5},{8,10},{10,8},{9,1... | collective-permute-start | bytes 725000 | tf_op jit(solution)/shard_map/ppermute | solution.py:336
  21.5 12.0 %collective-permute-start.6 = (bf16[944,128]{1,0:T(8,128)(2,1)}, bf16[944,128]{1,0:T(8,128)(2,1)S(1)}, u32[]{:S(2)}, u32[]{:S(2)}) collective-permute-start(bf16[944,128]{1,0:T(8,128)(2,1)} %collective-permute-done.5.refs_8_), channel_id=1, source_target_pairs={{0,2},{2,0},{1,3},{3,1},{4,6},{6,4},{5,7},{7,5},{8,10},{10,8},{9,1... | collective-permute-start | bytes 725000 | tf_op jit(solution)/shard_map/ppermute | solution.py:336
  32.0 9.8 %collective-permute-start.1 = (bf16[944,128]{1,0:T(8,128)(2,1)S(1)}, bf16[944,128]{1,0:T(8,128)(2,1)S(1)}, u32[]{:S(2)}, u32[]{:S(2)}) collective-permute-start(bf16[944,128]{1,0:T(8,128)(2,1)S(1)} %collective-permute-done.refs_2_), channel_id=1, source_target_pairs={{0,2},{2,0},{1,3},{3,1},{4,6},{6,4},{5,7},{7,5},{8,10},{10,8},{9,1... | collective-permute-start | bytes 725000 | tf_op jit(solution)/shard_map/ppermute | solution.py:336
  33.6 1.2 %copy-start.1 = (bf16[36,4,24,128]{3,2,1,0:T(8,128)(2,1)S(1)}, bf16[36,4,24,128]{3,2,1,0:T(8,128)(2,1)}, u32[]{:S(2)}) copy-start(bf16[36,4,24,128]{3,2,1,0:T(8,128)(2,1)} %param.12) | copy-start | bytes 2654212
  34.8 1.2 %copy-start.4 = (bf16[36,4,24,128]{3,2,1,0:T(8,128)(2,1)S(1)}, bf16[36,4,24,128]{3,2,1,0:T(8,128)(2,1)}, u32[]{:S(2)}) copy-start(bf16[36,4,24,128]{3,2,1,0:T(8,128)(2,1)} %param.16) | copy-start | bytes 2654212
  35.9 1.0 %copy-start.8 = (bf16[1840,128]{1,0:T(8,128)(2,1)S(1)}, bf16[1840,128]{1,0:T(8,128)(2,1)}, u32[]{:S(2)}) copy-start(bf16[1840,128]{1,0:T(8,128)(2,1)} %shard_map.119.refs_2_.refs_12_) | copy-start | bytes 1413124
  37.0 4.8 %copy-start.2 = (bf16[36,4,24,128]{3,2,1,0:T(8,128)(2,1)S(1)}, bf16[36,4,24,128]{3,2,1,0:T(8,128)(2,1)}, u32[]{:S(2)}) copy-start(bf16[36,4,24,128]{3,2,1,0:T(8,128)(2,1)} %param.12) | copy-start | bytes 2654212
  37.0 4.8 %copy-start.5 = (bf16[36,4,24,128]{3,2,1,0:T(8,128)(2,1)S(1)}, bf16[36,4,24,128]{3,2,1,0:T(8,128)(2,1)}, u32[]{:S(2)}) copy-start(bf16[36,4,24,128]{3,2,1,0:T(8,128)(2,1)} %param.16) | copy-start | bytes 2654212
  41.8 2.8 %copy-start.6 = (bf16[3072,1024]{1,0:T(8,128)(2,1)S(1)}, bf16[3072,1024]{1,0:T(8,128)(2,1)}, u32[]{:S(2)}) copy-start(bf16[3072,1024]{1,0:T(8,128)(2,1)} %refs_8_.1) | copy-start | bytes 18874372
  44.6 26.9 %copy-start.9 = (f32[1024]{0:T(1024)S(1)}, f32[1024]{0:T(1024)}, u32[]{:S(2)}) copy-start(f32[1024]{0:T(1024)} %param.22) | copy-start | bytes 12292
  44.6 27.1 %copy-start.10 = (f32[1024]{0:T(1024)S(1)}, f32[1024]{0:T(1024)}, u32[]{:S(2)}) copy-start(f32[1024]{0:T(1024)} %param.23) | copy-start | bytes 12292

commit v15 on v14

--- a/solution.py
+++ b/solution.py
@@ -390,7 +390,7 @@
             for piece, (shift, _, _, _) in zip(packed[:2], pieces)
         ]
         embed_other, own_land, send = lax.optimization_barrier((embed_weight, land, send))
-        own_w = pack(60, [(0, 0, cap, None)], ocean_w, atmos_w, ocean_ids, atmos_ids, own_land)[0]
+        own_w = pack(54, [(0, 0, cap, None)], ocean_w, atmos_w, ocean_ids, atmos_ids, own_land)[0]
         embed_other = swap(embed_other, "sub")
         keep, theirs = (ocean_f, atmos_f), (swap(send, "grp"),)
         dest = jnp.where(y == 0, ocean_dest, atmos_dest)

time: 73.1 us -> 73.1 us (level)
  no operation moved by 1% of the time
where the time goes in v15:
time: 73.1 us; the launch traced here: 72.4 us
  Pallas kernels  18.8 us (26%)
  blocking collectives  18.7 us (26%)
  starting transfers between devices  11.4 us (16%)
  local copies, waits for them, and re-layouts  10.4 us (14%)
  waiting for transfers between devices  8.55 us (12%)
  other arithmetic  4.35 us (6%)
    all_to_all x1, blocking collectives, per_device(): lax.all_to_all(sent, ('grp', 'band', 'var'), split_axis=0, concat_axis=0,...  18.7 us
    pallas_call x3, Pallas kernels, regrid(): pl.pallas_call(body, out_shape=shapes, in_specs=specs, out_specs=[vmem] *...  14.2 us
    unnamed x26, local copies, waits for them, and re-layouts  9.51 us
    ppermute x1, waiting for transfers between devices, per_device(): sent.append(lax.ppermute(piece, 'band', along(shift)))  8.54 us
    ppermute x5, starting transfers between devices, swap(): return lax.ppermute(x, axis, [(0, 1), (1, 0)])  5.77 us
    ppermute x2, starting transfers between devices, per_device(): lax.ppermute(piece, 'band', along(shift))  4.75 us
    pallas_call x2, Pallas kernels, pack(): pl.pallas_call(functools.partial(pack_kernel, pieces, len(fields) // 2),...  4.65 us
    convert_element_type x4, other arithmetic, job_of(): tile = parts[0][meta_at + 2 * tiles, :cap].astype(jnp.int32)  2.05 us
  transfers between devices with their start and end apart: 8, of which 1 were waited for; matrix products, arithmetic and copies ran while one was open for 6% of the time, Pallas kernels for 11%

profile of v15, /device:TPU:0, one launch (start us, length us, event | category | flops | bytes accessed | tf_op | source)
XLA Modules:
  0.0 72.4 jit_solution(5496966319220523055)
XLA Ops:
  0.0 2.8 %shard_map.118 = (bf16[944,128]{1,0:T(8,128)(2,1)}, bf16[944,128]{1,0:T(8,128)(2,1)}, bf16[944,128]{1,0:T(8,128)(2,1)}, bf16[36,96,128]{2,1,0:T(8,128)(2,1)}) custom-call(bf16[4,1792,128]{2,1,0:T(8,128)(2,1)} %bitcast.27, bf16[4,1792,128]{2,1,0:T(8,128)(2,1)} %bitcast.29, s32[4,14]{1,0:T(4,128)} %bitcast.33, s32[4,14]{1,0:T(4,128)} %bitcast.35, ...), custom_call_target="tpu_custom_call" | custom-call | bytes 2097152 | tf_op jit(solution)/shard_map/pallas_call | solution.py:96
  2.8 0.5 collective-permute-start.7
  3.3 2.6 %collective-permute-start.3 = (bf16[944,128]{1,0:T(8,128)(2,1)}, bf16[944,128]{1,0:T(8,128)(2,1)}, u32[]{:S(2)}, u32[]{:S(2)}) collective-permute-start(bf16[944,128]{1,0:T(8,128)(2,1)} %get-tuple-element.20), channel_id=1, source_target_pairs={{0,4},{4,8},{8,12},{12,0},{1,5},{5,9},{9,13},{13,1},{2,6},{6,10},{... | collective-permute-start | bytes 725000 | tf_op jit(solution)/shard_map/ppermute | solution.py:389
  5.9 2.1 %collective-permute-start.5 = (bf16[944,128]{1,0:T(8,128)(2,1)}, bf16[944,128]{1,0:T(8,128)(2,1)}, u32[]{:S(2)}, u32[]{:S(2)}) collective-permute-start(bf16[944,128]{1,0:T(8,128)(2,1)} %get-tuple-element.21), channel_id=1, source_target_pairs={{0,12},{4,0},{8,4},{12,8},{1,13},{5,1},{9,5},{13,9},{2,14},{6,2},{... | collective-permute-start | bytes 725000 | tf_op jit(solution)/shard_map/ppermute | solution.py:389
  8.1 1.7 %collective-permute-start.2 = (bf16[36,96,128]{2,1,0:T(8,128)(2,1)}, bf16[36,96,128]{2,1,0:T(8,128)(2,1)}, u32[]{:S(2)}, u32[]{:S(2)}) collective-permute-start(bf16[36,96,128]{2,1,0:T(8,128)(2,1)} %get-tuple-element.19), channel_id=1, source_target_pairs={{0,16},{16,0},{1,17},{17,1},{2,18},{18,2},{3,19},{19,3},{4,20},{20... | collective-permute-start | bytes 2654216 | tf_op jit(solution)/shard_map/ppermute | solution.py:336
  9.7 0.2 convert_reduce_fusion.1
  9.9 0.1 fusion.1
  10.0 0.1 reshape.97
  10.1 0.1 select_reduce_fusion
  10.2 0.1 reshape.89
  10.3 1.9 %shard_map.119.refs_2_.refs_12_ = bf16[1840,128]{1,0:T(8,128)(2,1)} custom-call(bf16[4,1792,128]{2,1,0:T(8,128)(2,1)} %bitcast.28, bf16[4,1792,128]{2,1,0:T(8,128)(2,1)} %bitcast.30, s32[4,14]{1,0:T(4,128)} %bitcast.34, s32[4,14]{1,0:T(4,128)} %bitcast.36, f32[16,128]{1,0:T(8,128)} %bitcast.32), custom_call_target="tpu_custom_call" | custom-call | bytes 2097152 | tf_op jit(solution)/shard_map/pallas_call | solution.py:96
  12.2 0.7 slice_convert_fusion.3
  12.9 0.7 fusion.3
  13.6 0.1 pad_add_fusion.4.refs_1_.refs_11_
  13.7 1.2 %copy-done = bf16[36,4,24,128]{3,2,1,0:T(8,128)(2,1)S(1)} copy-done((bf16[36,4,24,128]{3,2,1,0:T(8,128)(2,1)S(1)}, bf16[36,4,24,128]{3,2,1,0:T(8,128)(2,1)}, u32[]{:S(2)}) %copy-start) | copy-done | bytes 884760
  14.8 1.2 %copy-done.3 = bf16[36,4,24,128]{3,2,1,0:T(8,128)(2,1)S(1)} copy-done((bf16[36,4,24,128]{3,2,1,0:T(8,128)(2,1)S(1)}, bf16[36,4,24,128]{3,2,1,0:T(8,128)(2,1)}, u32[]{:S(2)}) %copy-start.3) | copy-done | bytes 884760
  16.0 1.0 %copy-done.7 = bf16[1840,128]{1,0:T(8,128)(2,1)S(1)} copy-done((bf16[1840,128]{1,0:T(8,128)(2,1)S(1)}, bf16[1840,128]{1,0:T(8,128)(2,1)}, u32[]{:S(2)}) %copy-start.7) | copy-done | bytes 471064
  17.0 1.3 %shard_map.120.refs_14_ = bf16[4,2,2,32,3072]{4,3,2,1,0:T(8,128)(2,1)S(1)} custom-call(s32[3,14]{1,0:T(4,128)S(1)} %pad_add_fusion.refs_0_.refs_10_, s32[2]{0:T(128)S(1)} %pad_add_fusion.4.refs_1_.refs_11_, bf16[1840,128]{1,0:T(8,128)(2,1)S(1)} %copy-done.7, bf16[36,96,128]{2,1,0:T(8,128)(2,1)S(1)} %bitcast.20, bf16[36,96,128]{2,1,0:T(8,128)(2,1)S(1)} %bitcast.24), custom_call_target="tpu_custom_call" | custom-call | flops 44040192 | bytes 3145728 | tf_op jit(solution)/shard_map/pallas_call | solution.py:262
  18.4 0.9 %collective-permute-start = (bf16[944,128]{1,0:T(8,128)(2,1)}, bf16[944,128]{1,0:T(8,128)(2,1)S(1)}, u32[]{:S(2)}, u32[]{:S(2)}) collective-permute-start(bf16[944,128]{1,0:T(8,128)(2,1)} %get-tuple-element.18), channel_id=1, source_target_pairs={{0,8},{4,12},{8,0},{12,4},{1,9},{5,13},{9,1},{13,5},{2,10},{6,14},... | collective-permute-start | bytes 725000 | tf_op jit(solution)/shard_map/ppermute | solution.py:425
  19.2 0.1 add_add_fusion
  19.3 0.1 add_add_fusion.2.refs_7_
  19.4 0.0 collective-permute-done.3.refs_2_
  19.4 0.7 slice_convert_fusion.1
  20.0 1.5 %collective-permute-start.4 = (bf16[944,128]{1,0:T(8,128)(2,1)}, bf16[944,128]{1,0:T(8,128)(2,1)S(1)}, u32[]{:S(2)}, u32[]{:S(2)}) collective-permute-start(bf16[944,128]{1,0:T(8,128)(2,1)} %collective-permute-done.3.refs_2_), channel_id=1, source_target_pairs={{0,2},{2,0},{1,3},{3,1},{4,6},{6,4},{5,7},{7,5},{8,10},{10,8},{9,1... | collective-permute-start | bytes 725000 | tf_op jit(solution)/shard_map/ppermute | solution.py:336
  21.5 0.0 collective-permute-done.5.refs_8_
  21.5 0.5 collective-permute-start.6
  22.1 0.7 slice_convert_fusion
  22.8 8.5 %collective-permute-done.refs_2_ = bf16[944,128]{1,0:T(8,128)(2,1)S(1)} collective-permute-done((bf16[944,128]{1,0:T(8,128)(2,1)}, bf16[944,128]{1,0:T(8,128)(2,1)S(1)}, u32[]{:S(2)}, u32[]{:S(2)}) %collective-permute-start) | collective-permute-done | bytes 241696 | tf_op jit(solution)/shard_map/ppermute | solution.py:425
  31.3 0.7 fusion.6
  32.0 1.6 %collective-permute-start.1 = (bf16[944,128]{1,0:T(8,128)(2,1)S(1)}, bf16[944,128]{1,0:T(8,128)(2,1)S(1)}, u32[]{:S(2)}, u32[]{:S(2)}) collective-permute-start(bf16[944,128]{1,0:T(8,128)(2,1)S(1)} %collective-permute-done.refs_2_), channel_id=1, source_target_pairs={{0,2},{2,0},{1,3},{3,1},{4,6},{6,4},{5,7},{7,5},{8,10},{10,8},{9,1... | collective-permute-start | bytes 725000 | tf_op jit(solution)/shard_map/ppermute | solution.py:336
  33.6 0.0 collective-permute-done.4.refs_3_
  33.6 0.0 collective-permute-done.6.refs_9_
  33.6 0.0 copy-start.1
  33.6 1.2 %copy-done.1 = bf16[36,4,24,128]{3,2,1,0:T(8,128)(2,1)S(1)} copy-done((bf16[36,4,24,128]{3,2,1,0:T(8,128)(2,1)S(1)}, bf16[36,4,24,128]{3,2,1,0:T(8,128)(2,1)}, u32[]{:S(2)}) %copy-start.1) | copy-done | bytes 884760
  34.8 1.2 %copy-done.4 = bf16[36,4,24,128]{3,2,1,0:T(8,128)(2,1)S(1)} copy-done((bf16[36,4,24,128]{3,2,1,0:T(8,128)(2,1)S(1)}, bf16[36,4,24,128]{3,2,1,0:T(8,128)(2,1)}, u32[]{:S(2)}) %copy-start.4) | copy-done | bytes 884760
  35.9 1.0 %copy-done.8 = bf16[1840,128]{1,0:T(8,128)(2,1)S(1)} copy-done((bf16[1840,128]{1,0:T(8,128)(2,1)S(1)}, bf16[1840,128]{1,0:T(8,128)(2,1)}, u32[]{:S(2)}) %copy-start.8) | copy-done | bytes 471064
  37.0 4.8 %shard_map.121.refs_7_ = bf16[4,2,2,32,3072]{4,3,2,1,0:T(8,128)(2,1)S(1)} custom-call(s32[3,14]{1,0:T(4,128)S(1)} %get-tuple-element.35.refs_0_, s32[3]{0:T(128)S(1)} %get-tuple-element.33.refs_1_, bf16[944,128]{1,0:T(8,128)(2,1)} %collective-permute-done.3.refs_2_, ...), custom_call_target="tpu_custom_call", output_to_operand_aliasing={{}: (14, {})} | custom-call | flops 220200960 | bytes 15728640 | tf_op jit(solution)/shard_map/pallas_call | solution.py:262
  41.8 0.0 collective-permute-done.1.refs_3_
  41.8 0.0 collective-permute-done.7.refs_9_
  41.8 0.0 copy-start.6
  41.8 2.8 %copy-done.6 = bf16[3072,1024]{1,0:T(8,128)(2,1)S(1)} copy-done((bf16[3072,1024]{1,0:T(8,128)(2,1)S(1)}, bf16[3072,1024]{1,0:T(8,128)(2,1)}, u32[]{:S(2)}) %copy-start.6) | copy-done | bytes 6291480
  44.6 8.1 %shard_map.122 = (bf16[4,2,2,32,3072]{4,3,2,1,0:T(8,128)(2,1)S(1)}, bf16[16,16,1024]{2,1,0:T(8,128)(2,1)S(1)}) custom-call(s32[3,14]{1,0:T(4,128)S(1)} %get-tuple-element.34.refs_0_, s32[3]{0:T(128)S(1)} %get-tuple-element.32.refs_1_, bf16[944,128]{1,0:T(8,128)(2,1)S(1)} %collective-permute-done.refs_2_, ...), custom_call_target="tpu_custom_call", output_to_operand_aliasing={{0}: (7, {})} | custom-call | flops 3309305856 | bytes 12582912 | tf_op jit(solution)/shard_map/pallas_call | solution.py:262
  52.7 18.7 %all_to_all.5 = bf16[16,16,1024]{2,1,0:T(8,128)(2,1)S(1)} all-to-all(bf16[16,16,1024]{2,1,0:T(8,128)(2,1)S(1)} %get-tuple-element.24), channel_id=1, replica_groups=mesh['grp'=2,'band'=4,'var'=2,'sub'=2] {'grp','band','var'}, dimensions={0} | all-to-all | bytes 1048576 | tf_op jit(solution)/shard_map/all_to_all | solution.py:437
  71.4 0.1 convert_reduce_fusion
  71.5 0.1 multiply_reduce_fusion
  71.6 0.1 rsqrt.12
  71.7 0.1 fusion
  71.8 0.6 copy.17
  (27 shorter events, 0.1 us)
Async XLA Ops:
  0.0 9.7 %copy-start.12 = (s32[36,1]{0,1:T(1,128)S(1)}, s32[36,1]{0,1:T(1,128)}, u32[]{:S(2)}) copy-start(s32[36,1]{0,1:T(1,128)} %param.17) | copy-start | bytes 436
  0.0 9.7 %copy-start.11 = (s32[36,1]{0,1:T(1,128)S(1)}, s32[36,1]{0,1:T(1,128)}, u32[]{:S(2)}) copy-start(s32[36,1]{0,1:T(1,128)} %param.13) | copy-start | bytes 436
  2.8 39.0 %collective-permute-start.7 = (bf16[3072,1024]{1,0:T(8,128)(2,1)}, bf16[3072,1024]{1,0:T(8,128)(2,1)}, u32[]{:S(2)}, u32[]{:S(2)}) collective-permute-start(bf16[3072,1024]{1,0:T(8,128)(2,1)} %refs_8_.1), channel_id=1, source_target_pairs={{0,1},{1,0},{2,3},{3,2},{4,5},{5,4},{6,7},{7,6},{8,9},{9,8},{10,11... | collective-permute-start | bytes 18874376 | tf_op jit(solution)/shard_map/ppermute | solution.py:336
  3.3 16.1 %collective-permute-start.3 = (bf16[944,128]{1,0:T(8,128)(2,1)}, bf16[944,128]{1,0:T(8,128)(2,1)}, u32[]{:S(2)}, u32[]{:S(2)}) collective-permute-start(bf16[944,128]{1,0:T(8,128)(2,1)} %get-tuple-element.20), channel_id=1, source_target_pairs={{0,4},{4,8},{8,12},{12,0},{1,5},{5,9},{9,13},{13,1},{2,6},{6,10},{... | collective-permute-start | bytes 725000 | tf_op jit(solution)/shard_map/ppermute | solution.py:389
  5.9 15.6 %collective-permute-start.5 = (bf16[944,128]{1,0:T(8,128)(2,1)}, bf16[944,128]{1,0:T(8,128)(2,1)}, u32[]{:S(2)}, u32[]{:S(2)}) collective-permute-start(bf16[944,128]{1,0:T(8,128)(2,1)} %get-tuple-element.21), channel_id=1, source_target_pairs={{0,12},{4,0},{8,4},{12,8},{1,13},{5,1},{9,5},{13,9},{2,14},{6,2},{... | collective-permute-start | bytes 725000 | tf_op jit(solution)/shard_map/ppermute | solution.py:389
  8.1 25.5 %collective-permute-start.2 = (bf16[36,96,128]{2,1,0:T(8,128)(2,1)}, bf16[36,96,128]{2,1,0:T(8,128)(2,1)}, u32[]{:S(2)}, u32[]{:S(2)}) collective-permute-start(bf16[36,96,128]{2,1,0:T(8,128)(2,1)} %get-tuple-element.19), channel_id=1, source_target_pairs={{0,16},{16,0},{1,17},{17,1},{2,18},{18,2},{3,19},{19,3},{4,20},{20... | collective-permute-start | bytes 2654216 | tf_op jit(solution)/shard_map/ppermute | solution.py:336
  13.7 1.2 %copy-start = (bf16[36,4,24,128]{3,2,1,0:T(8,128)(2,1)S(1)}, bf16[36,4,24,128]{3,2,1,0:T(8,128)(2,1)}, u32[]{:S(2)}) copy-start(bf16[36,4,24,128]{3,2,1,0:T(8,128)(2,1)} %param.12) | copy-start | bytes 2654212
  14.8 1.2 %copy-start.3 = (bf16[36,4,24,128]{3,2,1,0:T(8,128)(2,1)S(1)}, bf16[36,4,24,128]{3,2,1,0:T(8,128)(2,1)}, u32[]{:S(2)}) copy-start(bf16[36,4,24,128]{3,2,1,0:T(8,128)(2,1)} %param.16) | copy-start | bytes 2654212
  16.0 1.0 %copy-start.7 = (bf16[1840,128]{1,0:T(8,128)(2,1)S(1)}, bf16[1840,128]{1,0:T(8,128)(2,1)}, u32[]{:S(2)}) copy-start(bf16[1840,128]{1,0:T(8,128)(2,1)} %shard_map.119.refs_2_.refs_12_) | copy-start | bytes 1413124
  18.4 12.9 %collective-permute-start = (bf16[944,128]{1,0:T(8,128)(2,1)}, bf16[944,128]{1,0:T(8,128)(2,1)S(1)}, u32[]{:S(2)}, u32[]{:S(2)}) collective-permute-start(bf16[944,128]{1,0:T(8,128)(2,1)} %get-tuple-element.18), channel_id=1, source_target_pairs={{0,8},{4,12},{8,0},{12,4},{1,9},{5,13},{9,1},{13,5},{2,10},{6,14},... | collective-permute-start | bytes 725000 | tf_op jit(solution)/shard_map/ppermute | solution.py:425
  20.0 13.5 %collective-permute-start.4 = (bf16[944,128]{1,0:T(8,128)(2,1)}, bf16[944,128]{1,0:T(8,128)(2,1)S(1)}, u32[]{:S(2)}, u32[]{:S(2)}) collective-permute-start(bf16[944,128]{1,0:T(8,128)(2,1)} %collective-permute-done.3.refs_2_), channel_id=1, source_target_pairs={{0,2},{2,0},{1,3},{3,1},{4,6},{6,4},{5,7},{7,5},{8,10},{10,8},{9,1... | collective-permute-start | bytes 725000 | tf_op jit(solution)/shard_map/ppermute | solution.py:336
  21.5 12.0 %collective-permute-start.6 = (bf16[944,128]{1,0:T(8,128)(2,1)}, bf16[944,128]{1,0:T(8,128)(2,1)S(1)}, u32[]{:S(2)}, u32[]{:S(2)}) collective-permute-start(bf16[944,128]{1,0:T(8,128)(2,1)} %collective-permute-done.5.refs_8_), channel_id=1, source_target_pairs={{0,2},{2,0},{1,3},{3,1},{4,6},{6,4},{5,7},{7,5},{8,10},{10,8},{9,1... | collective-permute-start | bytes 725000 | tf_op jit(solution)/shard_map/ppermute | solution.py:336
  32.0 9.8 %collective-permute-start.1 = (bf16[944,128]{1,0:T(8,128)(2,1)S(1)}, bf16[944,128]{1,0:T(8,128)(2,1)S(1)}, u32[]{:S(2)}, u32[]{:S(2)}) collective-permute-start(bf16[944,128]{1,0:T(8,128)(2,1)S(1)} %collective-permute-done.refs_2_), channel_id=1, source_target_pairs={{0,2},{2,0},{1,3},{3,1},{4,6},{6,4},{5,7},{7,5},{8,10},{10,8},{9,1... | collective-permute-start | bytes 725000 | tf_op jit(solution)/shard_map/ppermute | solution.py:336
  33.6 1.2 %copy-start.1 = (bf16[36,4,24,128]{3,2,1,0:T(8,128)(2,1)S(1)}, bf16[36,4,24,128]{3,2,1,0:T(8,128)(2,1)}, u32[]{:S(2)}) copy-start(bf16[36,4,24,128]{3,2,1,0:T(8,128)(2,1)} %param.12) | copy-start | bytes 2654212
  34.8 1.2 %copy-start.4 = (bf16[36,4,24,128]{3,2,1,0:T(8,128)(2,1)S(1)}, bf16[36,4,24,128]{3,2,1,0:T(8,128)(2,1)}, u32[]{:S(2)}) copy-start(bf16[36,4,24,128]{3,2,1,0:T(8,128)(2,1)} %param.16) | copy-start | bytes 2654212
  35.9 1.0 %copy-start.8 = (bf16[1840,128]{1,0:T(8,128)(2,1)S(1)}, bf16[1840,128]{1,0:T(8,128)(2,1)}, u32[]{:S(2)}) copy-start(bf16[1840,128]{1,0:T(8,128)(2,1)} %shard_map.119.refs_2_.refs_12_) | copy-start | bytes 1413124
  37.0 4.8 %copy-start.2 = (bf16[36,4,24,128]{3,2,1,0:T(8,128)(2,1)S(1)}, bf16[36,4,24,128]{3,2,1,0:T(8,128)(2,1)}, u32[]{:S(2)}) copy-start(bf16[36,4,24,128]{3,2,1,0:T(8,128)(2,1)} %param.12) | copy-start | bytes 2654212
  37.0 4.8 %copy-start.5 = (bf16[36,4,24,128]{3,2,1,0:T(8,128)(2,1)S(1)}, bf16[36,4,24,128]{3,2,1,0:T(8,128)(2,1)}, u32[]{:S(2)}) copy-start(bf16[36,4,24,128]{3,2,1,0:T(8,128)(2,1)} %param.16) | copy-start | bytes 2654212
  41.8 2.8 %copy-start.6 = (bf16[3072,1024]{1,0:T(8,128)(2,1)S(1)}, bf16[3072,1024]{1,0:T(8,128)(2,1)}, u32[]{:S(2)}) copy-start(bf16[3072,1024]{1,0:T(8,128)(2,1)} %refs_8_.1) | copy-start | bytes 18874372
  44.6 26.9 %copy-start.9 = (f32[1024]{0:T(1024)S(1)}, f32[1024]{0:T(1024)}, u32[]{:S(2)}) copy-start(f32[1024]{0:T(1024)} %param.22) | copy-start | bytes 12292
  44.6 27.1 %copy-start.10 = (f32[1024]{0:T(1024)S(1)}, f32[1024]{0:T(1024)}, u32[]{:S(2)}) copy-start(f32[1024]{0:T(1024)} %param.23) | copy-start | bytes 12292

commit v16 on v14

--- a/solution.py
+++ b/solution.py
@@ -420,8 +420,8 @@
         ours, others = [(0, keep)], [(1, theirs)]
         jobs = [job_of(me, [own_w], [cap], [jnp.int32(0)], ours)]
         rows_x = call(jobs, None, groups=2)
-        for piece, (shift, _, _, _) in zip(packed[2:], pieces[2:]):
-            piece, rows_x = lax.optimization_barrier((piece, rows_x))
+        for at, (piece, (shift, _, _, _)) in enumerate(zip(packed[2:], pieces[2:])):
+            piece, sent[at], rows_x = lax.optimization_barrier((piece, sent[at], rows_x))
             sent.append(lax.ppermute(piece, "band", along(shift)))
         crossed = [swap(piece, "var") for piece in sent]
         jobs += [job_at(shift, ours) for shift in order]

time: 73.1 us -> 64.5 us (0.88)
  local copies, waits for them, and re-layouts: 10.4 us -> 2 us
  starting transfers between devices: 11.4 us -> 17.5 us
  other arithmetic: 4.35 us -> 2.34 us
  waiting for transfers between devices: 8.55 us -> 6.81 us
  Pallas kernels: 18.8 us -> 17.4 us
  blocking collectives: 18.7 us -> 17.9 us
    unnamed x26 -> x22, local copies, waits for them, and re-layouts: 9.51 us -> 1.08 us
    ppermute x1, starting transfers between devices: 0.85 us -> 6.95 us  [per_device(): sent.append(lax.ppermute(piece, 'band', along(shift)))]
    ppermute x1, waiting for transfers between devices: 8.53 us -> 4.99 us  [per_device(): sent.append(lax.ppermute(piece, 'band', along(shift)))]
    ppermute x5, waiting for transfers between devices: 0.01 us -> 1.81 us  [swap(): return lax.ppermute(x, axis, [(0, 1), (1, 0)])]
    pallas_call x3, Pallas kernels: 14.2 us -> 12.7 us  [regrid(): pl.pallas_call(body, out_shape=shapes, in_specs=specs, out_specs=[vmem] *...]
    convert_element_type x4, other arithmetic: 2.05 us -> 0.7 us  [job_of(): tile = parts[0][meta_at + 2 * tiles, :cap].astype(jnp.int32)]
    all_to_all x1, blocking collectives: 18.7 us -> 17.9 us  [per_device(): lax.all_to_all(sent, ('grp', 'band', 'var'), split_axis=0, concat_axis=0,...]
  transfers between devices with their start and end apart: 8 -> 8, of which waited for: 1 -> 3; matrix products, arithmetic and copies ran while one was open for 6% -> 3% of each run, Pallas kernels for 11% -> 11%
where the time goes in v16:
time: 64.5 us; the launch traced here: 64.1 us
  blocking collectives  17.9 us (28%)
  starting transfers between devices  17.5 us (27%)
  Pallas kernels  17.4 us (27%)
  waiting for transfers between devices  6.81 us (11%)
  other arithmetic  2.34 us (4%)
  local copies, waits for them, and re-layouts  2 us (3%)
    all_to_all x1, blocking collectives, per_device(): lax.all_to_all(sent, ('grp', 'band', 'var'), split_axis=0, concat_axis=0,...  17.9 us
    pallas_call x3, Pallas kernels, regrid(): pl.pallas_call(body, out_shape=shapes, in_specs=specs, out_specs=[vmem] *...  12.7 us
    ppermute x1, starting transfers between devices, per_device(): sent.append(lax.ppermute(piece, 'band', along(shift)))  6.95 us
    ppermute x5, starting transfers between devices, swap(): return lax.ppermute(x, axis, [(0, 1), (1, 0)])  5.77 us
    ppermute x1, waiting for transfers between devices, per_device(): sent.append(lax.ppermute(piece, 'band', along(shift)))  4.99 us
    ppermute x2, starting transfers between devices, per_device(): lax.ppermute(piece, 'band', along(shift))  4.75 us
    pallas_call x2, Pallas kernels, pack(): pl.pallas_call(functools.partial(pack_kernel, pieces, len(fields) // 2),...  4.68 us
    ppermute x5, waiting for transfers between devices, swap(): return lax.ppermute(x, axis, [(0, 1), (1, 0)])  1.81 us
  transfers between devices with their start and end apart: 8, of which 3 were waited for; matrix products, arithmetic and copies ran while one was open for 3% of the time, Pallas kernels for 11%

profile of v16, /device:TPU:0, one launch (start us, length us, event | category | flops | bytes accessed | tf_op | source)
XLA Modules:
  0.0 64.1 jit_solution(2418414087998927661)
XLA Ops:
  0.0 2.8 %shard_map.118 = (bf16[944,128]{1,0:T(8,128)(2,1)}, bf16[944,128]{1,0:T(8,128)(2,1)}, bf16[944,128]{1,0:T(8,128)(2,1)}, bf16[36,96,128]{2,1,0:T(8,128)(2,1)}) custom-call(bf16[4,1792,128]{2,1,0:T(8,128)(2,1)} %bitcast.29, bf16[4,1792,128]{2,1,0:T(8,128)(2,1)} %bitcast.31, s32[4,14]{1,0:T(4,128)} %bitcast.35, s32[4,14]{1,0:T(4,128)} %bitcast.37, ...), custom_call_target="tpu_custom_call" | custom-call | bytes 2097152 | tf_op jit(solution)/shard_map/pallas_call | solution.py:96
  2.8 0.0 copy-start
  2.8 0.0 copy-start.1
  2.8 0.5 collective-permute-start.7
  3.4 2.6 %collective-permute-start = (bf16[944,128]{1,0:T(8,128)(2,1)}, bf16[944,128]{1,0:T(8,128)(2,1)S(1)}, u32[]{:S(2)}, u32[]{:S(2)}) collective-permute-start(bf16[944,128]{1,0:T(8,128)(2,1)} %get-tuple-element.17), channel_id=1, source_target_pairs={{0,4},{4,8},{8,12},{12,0},{1,5},{5,9},{9,13},{13,1},{2,6},{6,10},{... | collective-permute-start | bytes 725000 | tf_op jit(solution)/shard_map/ppermute | solution.py:389
  6.0 2.1 %collective-permute-start.5 = (bf16[944,128]{1,0:T(8,128)(2,1)}, bf16[944,128]{1,0:T(8,128)(2,1)S(1)}, u32[]{:S(2)}, u32[]{:S(2)}) collective-permute-start(bf16[944,128]{1,0:T(8,128)(2,1)} %get-tuple-element.23), channel_id=1, source_target_pairs={{0,12},{4,0},{8,4},{12,8},{1,13},{5,1},{9,5},{13,9},{2,14},{6,2},{... | collective-permute-start | bytes 725000 | tf_op jit(solution)/shard_map/ppermute | solution.py:389
  8.1 1.7 %collective-permute-start.3 = (bf16[36,96,128]{2,1,0:T(8,128)(2,1)}, bf16[36,96,128]{2,1,0:T(8,128)(2,1)S(1)}, u32[]{:S(2)}, u32[]{:S(2)}) collective-permute-start(bf16[36,96,128]{2,1,0:T(8,128)(2,1)} %get-tuple-element.21), channel_id=1, source_target_pairs={{0,16},{16,0},{1,17},{17,1},{2,18},{18,2},{3,19},{19,3},{4,20},{20... | collective-permute-start | bytes 2654216 | tf_op jit(solution)/shard_map/ppermute | solution.py:336
  9.8 0.0 copy-done.7
  9.8 0.0 copy-done.6
  9.8 0.2 convert_reduce_fusion.1
  10.0 0.1 fusion.1
  10.1 0.1 reshape.97
  10.2 0.1 select_reduce_fusion
  10.3 0.1 reshape.89
  10.3 1.9 %shard_map.119.refs_2_.refs_12_ = bf16[1840,128]{1,0:T(8,128)(2,1)} custom-call(bf16[4,1792,128]{2,1,0:T(8,128)(2,1)} %bitcast.30, bf16[4,1792,128]{2,1,0:T(8,128)(2,1)} %bitcast.32, s32[4,14]{1,0:T(4,128)} %bitcast.36, s32[4,14]{1,0:T(4,128)} %bitcast.38, f32[16,128]{1,0:T(8,128)} %bitcast.34), custom_call_target="tpu_custom_call" | custom-call | bytes 2097152 | tf_op jit(solution)/shard_map/pallas_call | solution.py:96
  12.2 0.1 add_add_fusion
  12.3 0.7 %slice_convert_fusion.2 = s32[1,14]{1,0:T(1,128)S(1)} fusion(bf16[1840,128]{1,0:T(8,128)(2,1)} %shard_map.119.refs_2_.refs_12_), kind=kLoop, calls=%fused_computation.30 | loop fusion | flops 14 | bytes 84 | tf_op jit(solution)/shard_map/convert_element_type | solution.py:400
  13.0 0.7 %fusion.3 = s32[1,14]{1,0:T(1,128)S(1)} fusion(pred[4,14]{1,0:T(4,128)(4,1)S(1)} %reshape.97, s32[]{:T(128)S(6)} %select_n.67, s32[]{:T(128)S(6)} %mul.61, bf16[1840,128]{1,0:T(8,128)(2,1)} %shard_map.119.refs_2_.refs_12_), kind=kLoop, calls=%fused_computation.22 | loop fusion | flops 42 | bytes 106 | tf_op jit(solution)/shard_map/jit(_where)/select_n | solution.py:403
  13.7 0.1 add_add_fusion.2.refs_7_
  13.8 0.1 pad_add_fusion.4.refs_1_.refs_11_
  13.9 0.0 copy-done
  13.9 0.0 copy-done.1
  13.9 1.0 %copy-done.2 = bf16[1840,128]{1,0:T(8,128)(2,1)S(1)} copy-done((bf16[1840,128]{1,0:T(8,128)(2,1)S(1)}, bf16[1840,128]{1,0:T(8,128)(2,1)}, u32[]{:S(2)}) %copy-start.2) | copy-done | bytes 471064
  14.9 1.3 %shard_map.120.refs_14_ = bf16[4,2,2,32,3072]{4,3,2,1,0:T(8,128)(2,1)S(1)} custom-call(s32[3,14]{1,0:T(4,128)S(1)} %pad_add_fusion.refs_0_.refs_10_, s32[2]{0:T(128)S(1)} %pad_add_fusion.4.refs_1_.refs_11_, bf16[1840,128]{1,0:T(8,128)(2,1)S(1)} %copy-done.2, bf16[36,96,128]{2,1,0:T(8,128)(2,1)S(1)} %bitcast.20, bf16[36,96,128]{2,1,0:T(8,128)(2,1)S(1)} %bitcast.24), custom_call_target="tpu_custom_call" | custom-call | flops 44040192 | bytes 3145728 | tf_op jit(solution)/shard_map/pallas_call | solution.py:262
  16.2 0.0 collective-permute-done.refs_2_
  16.3 7.0 %collective-permute-start.1 = (bf16[944,128]{1,0:T(8,128)(2,1)S(1)}, bf16[944,128]{1,0:T(8,128)(2,1)S(1)}, u32[]{:S(2)}, u32[]{:S(2)}) collective-permute-start(bf16[944,128]{1,0:T(8,128)(2,1)S(1)} %copy-done.8), channel_id=1, source_target_pairs={{0,8},{4,12},{8,0},{12,4},{1,9},{5,13},{9,1},{13,5},{2,10},{6,14},... | collective-permute-start | bytes 725000 | tf_op jit(solution)/shard_map/ppermute | solution.py:425
  23.2 1.5 %collective-permute-start.4 = (bf16[944,128]{1,0:T(8,128)(2,1)S(1)}, bf16[944,128]{1,0:T(8,128)(2,1)S(1)}, u32[]{:S(2)}, u32[]{:S(2)}) collective-permute-start(bf16[944,128]{1,0:T(8,128)(2,1)S(1)} %collective-permute-done.refs_2_), channel_id=1, source_target_pairs={{0,2},{2,0},{1,3},{3,1},{4,6},{6,4},{5,7},{7,5},{8,10},{10,8},{9,1... | collective-permute-start | bytes 725000 | tf_op jit(solution)/shard_map/ppermute | solution.py:336
  24.7 0.0 collective-permute-done.5.refs_8_
  24.7 0.5 collective-permute-start.6
  25.3 5.0 %collective-permute-done.1.refs_2_ = bf16[944,128]{1,0:T(8,128)(2,1)S(1)} collective-permute-done((bf16[944,128]{1,0:T(8,128)(2,1)S(1)}, bf16[944,128]{1,0:T(8,128)(2,1)S(1)}, u32[]{:S(2)}, u32[]{:S(2)}) %collective-permute-start.1) | collective-permute-done | bytes 241696 | tf_op jit(solution)/shard_map/ppermute | solution.py:425
  30.3 1.6 %collective-permute-start.2 = (bf16[944,128]{1,0:T(8,128)(2,1)S(1)}, bf16[944,128]{1,0:T(8,128)(2,1)S(1)}, u32[]{:S(2)}, u32[]{:S(2)}) collective-permute-start(bf16[944,128]{1,0:T(8,128)(2,1)S(1)} %collective-permute-done.1.refs_2_), channel_id=1, source_target_pairs={{0,2},{2,0},{1,3},{3,1},{4,6},{6,4},{5,7},{7,5},{8,10},{10,8},{9,1... | collective-permute-start | bytes 725000 | tf_op jit(solution)/shard_map/ppermute | solution.py:336
  31.9 0.1 collective-permute-done.6.refs_9_
  32.0 0.0 collective-permute-done.4.refs_3_
  32.0 0.0 collective-permute-done.3.refs_13_.refs_6_
  32.0 0.0 slice-start.1
  32.0 3.9 %shard_map.121.refs_7_ = bf16[4,2,2,32,3072]{4,3,2,1,0:T(8,128)(2,1)S(1)} custom-call(s32[3,14]{1,0:T(4,128)S(1)} %get-tuple-element.37.refs_0_, s32[3]{0:T(128)S(1)} %get-tuple-element.35.refs_1_, bf16[944,128]{1,0:T(8,128)(2,1)S(1)} %collective-permute-done.refs_2_, ...), custom_call_target="tpu_custom_call", output_to_operand_aliasing={{}: (14, {})} | custom-call | flops 220200960 | bytes 15728640 | tf_op jit(solution)/shard_map/pallas_call | solution.py:262
  35.9 1.7 %collective-permute-done.2.refs_3_ = bf16[944,128]{1,0:T(8,128)(2,1)S(1)} collective-permute-done((bf16[944,128]{1,0:T(8,128)(2,1)S(1)}, bf16[944,128]{1,0:T(8,128)(2,1)S(1)}, u32[]{:S(2)}, u32[]{:S(2)}) %collective-permute-start.2) | collective-permute-done | bytes 241696 | tf_op jit(solution)/shard_map/ppermute | solution.py:336
  37.6 0.0 collective-permute-done.7.refs_9_
  37.6 0.0 slice-done.1
  37.6 0.0 copy-start.4
  37.6 0.0 copy-start.5
  37.7 7.5 %shard_map.122 = (bf16[4,2,2,32,3072]{4,3,2,1,0:T(8,128)(2,1)S(1)}, bf16[16,16,1024]{2,1,0:T(8,128)(2,1)S(1)}) custom-call(s32[3,14]{1,0:T(4,128)S(1)} %get-tuple-element.36.refs_0_, s32[3]{0:T(128)S(1)} %get-tuple-element.34.refs_1_, bf16[944,128]{1,0:T(8,128)(2,1)S(1)} %collective-permute-done.1.refs_2_, ...), custom_call_target="tpu_custom_call", output_to_operand_aliasing={{0}: (7, {})} | custom-call | flops 3309305856 | bytes 12582912 | tf_op jit(solution)/shard_map/pallas_call | solution.py:262
  45.1 17.9 %all_to_all.5 = bf16[16,16,1024]{2,1,0:T(8,128)(2,1)S(1)} all-to-all(bf16[16,16,1024]{2,1,0:T(8,128)(2,1)S(1)} %get-tuple-element.26), channel_id=1, replica_groups=mesh['grp'=2,'band'=4,'var'=2,'sub'=2] {'grp','band','var'}, dimensions={0} | all-to-all | bytes 1048576 | tf_op jit(solution)/shard_map/all_to_all | solution.py:437
  63.0 0.1 convert_reduce_fusion
  63.2 0.1 multiply_reduce_fusion
  63.3 0.1 rsqrt.12
  63.4 0.1 fusion
  63.5 0.6 copy.17
  (24 shorter events, 0.1 us)
Async XLA Ops:
  0.0 9.8 %copy-start.7 = (s32[36,1]{0,1:T(1,128)S(1)}, s32[36,1]{0,1:T(1,128)}, u32[]{:S(2)}) copy-start(s32[36,1]{0,1:T(1,128)} %param.17) | copy-start | bytes 436
  0.0 9.8 %copy-start.6 = (s32[36,1]{0,1:T(1,128)S(1)}, s32[36,1]{0,1:T(1,128)}, u32[]{:S(2)}) copy-start(s32[36,1]{0,1:T(1,128)} %param.13) | copy-start | bytes 436
  2.8 11.1 %copy-start = (bf16[36,4,24,128]{3,2,1,0:T(8,128)(2,1)S(1)}, bf16[36,4,24,128]{3,2,1,0:T(8,128)(2,1)}, u32[]{:S(2)}) copy-start(bf16[36,4,24,128]{3,2,1,0:T(8,128)(2,1)} %param.12) | copy-start | bytes 2654212
  2.8 11.1 %copy-start.1 = (bf16[36,4,24,128]{3,2,1,0:T(8,128)(2,1)S(1)}, bf16[36,4,24,128]{3,2,1,0:T(8,128)(2,1)}, u32[]{:S(2)}) copy-start(bf16[36,4,24,128]{3,2,1,0:T(8,128)(2,1)} %param.16) | copy-start | bytes 2654212
  2.8 34.8 %collective-permute-start.7 = (bf16[3072,1024]{1,0:T(8,128)(2,1)}, bf16[3072,1024]{1,0:T(8,128)(2,1)}, u32[]{:S(2)}, u32[]{:S(2)}) collective-permute-start(bf16[3072,1024]{1,0:T(8,128)(2,1)} %refs_8_.1), channel_id=1, source_target_pairs={{0,1},{1,0},{2,3},{3,2},{4,5},{5,4},{6,7},{7,6},{8,9},{9,8},{10,11... | collective-permute-start | bytes 18874376 | tf_op jit(solution)/shard_map/ppermute | solution.py:336
  3.4 12.9 %collective-permute-start = (bf16[944,128]{1,0:T(8,128)(2,1)}, bf16[944,128]{1,0:T(8,128)(2,1)S(1)}, u32[]{:S(2)}, u32[]{:S(2)}) collective-permute-start(bf16[944,128]{1,0:T(8,128)(2,1)} %get-tuple-element.17), channel_id=1, source_target_pairs={{0,4},{4,8},{8,12},{12,0},{1,5},{5,9},{9,13},{13,1},{2,6},{6,10},{... | collective-permute-start | bytes 725000 | tf_op jit(solution)/shard_map/ppermute | solution.py:389
  6.0 18.7 %collective-permute-start.5 = (bf16[944,128]{1,0:T(8,128)(2,1)}, bf16[944,128]{1,0:T(8,128)(2,1)S(1)}, u32[]{:S(2)}, u32[]{:S(2)}) collective-permute-start(bf16[944,128]{1,0:T(8,128)(2,1)} %get-tuple-element.23), channel_id=1, source_target_pairs={{0,12},{4,0},{8,4},{12,8},{1,13},{5,1},{9,5},{13,9},{2,14},{6,2},{... | collective-permute-start | bytes 725000 | tf_op jit(solution)/shard_map/ppermute | solution.py:389
  8.1 23.9 %collective-permute-start.3 = (bf16[36,96,128]{2,1,0:T(8,128)(2,1)}, bf16[36,96,128]{2,1,0:T(8,128)(2,1)S(1)}, u32[]{:S(2)}, u32[]{:S(2)}) collective-permute-start(bf16[36,96,128]{2,1,0:T(8,128)(2,1)} %get-tuple-element.21), channel_id=1, source_target_pairs={{0,16},{16,0},{1,17},{17,1},{2,18},{18,2},{3,19},{19,3},{4,20},{20... | collective-permute-start | bytes 2654216 | tf_op jit(solution)/shard_map/ppermute | solution.py:336
  10.3 5.9 %copy-start.8 = (bf16[944,128]{1,0:T(8,128)(2,1)S(1)}, bf16[944,128]{1,0:T(8,128)(2,1)}, u32[]{:S(2)}) copy-start(bf16[944,128]{1,0:T(8,128)(2,1)} %get-tuple-element.20) | copy-start | bytes 724996
  13.9 1.0 %copy-start.2 = (bf16[1840,128]{1,0:T(8,128)(2,1)S(1)}, bf16[1840,128]{1,0:T(8,128)(2,1)}, u32[]{:S(2)}) copy-start(bf16[1840,128]{1,0:T(8,128)(2,1)} %shard_map.119.refs_2_.refs_12_) | copy-start | bytes 1413124
  14.9 17.1 %copy-start.3 = (bf16[1840,128]{1,0:T(8,128)(2,1)S(1)}, bf16[1840,128]{1,0:T(8,128)(2,1)}, u32[]{:S(2)}) copy-start(bf16[1840,128]{1,0:T(8,128)(2,1)} %shard_map.119.refs_2_.refs_12_) | copy-start | bytes 1413124
  14.9 22.7 %slice-start = ((s8[6291456]{0:T(1024)(128)(4,1)}), s8[4194304]{0:T(1024)(128)(4,1)S(1)}, s32[]{:S(2)}) async-start(s8[6291456]{0:T(1024)(128)(4,1)} %bitcast.27), calls=%async_computation.1 | async-start | bytes 8388608
  16.3 14.0 %collective-permute-start.1 = (bf16[944,128]{1,0:T(8,128)(2,1)S(1)}, bf16[944,128]{1,0:T(8,128)(2,1)S(1)}, u32[]{:S(2)}, u32[]{:S(2)}) collective-permute-start(bf16[944,128]{1,0:T(8,128)(2,1)S(1)} %copy-done.8), channel_id=1, source_target_pairs={{0,8},{4,12},{8,0},{12,4},{1,9},{5,13},{9,1},{13,5},{2,10},{6,14},... | collective-permute-start | bytes 725000 | tf_op jit(solution)/shard_map/ppermute | solution.py:425
  23.2 8.7 %collective-permute-start.4 = (bf16[944,128]{1,0:T(8,128)(2,1)S(1)}, bf16[944,128]{1,0:T(8,128)(2,1)S(1)}, u32[]{:S(2)}, u32[]{:S(2)}) collective-permute-start(bf16[944,128]{1,0:T(8,128)(2,1)S(1)} %collective-permute-done.refs_2_), channel_id=1, source_target_pairs={{0,2},{2,0},{1,3},{3,1},{4,6},{6,4},{5,7},{7,5},{8,10},{10,8},{9,1... | collective-permute-start | bytes 725000 | tf_op jit(solution)/shard_map/ppermute | solution.py:336
  24.7 7.2 %collective-permute-start.6 = (bf16[944,128]{1,0:T(8,128)(2,1)S(1)}, bf16[944,128]{1,0:T(8,128)(2,1)S(1)}, u32[]{:S(2)}, u32[]{:S(2)}) collective-permute-start(bf16[944,128]{1,0:T(8,128)(2,1)S(1)} %collective-permute-done.5.refs_8_), channel_id=1, source_target_pairs={{0,2},{2,0},{1,3},{3,1},{4,6},{6,4},{5,7},{7,5},{8,10},{10,8},{9,1... | collective-permute-start | bytes 725000 | tf_op jit(solution)/shard_map/ppermute | solution.py:336
  30.3 7.3 %collective-permute-start.2 = (bf16[944,128]{1,0:T(8,128)(2,1)S(1)}, bf16[944,128]{1,0:T(8,128)(2,1)S(1)}, u32[]{:S(2)}, u32[]{:S(2)}) collective-permute-start(bf16[944,128]{1,0:T(8,128)(2,1)S(1)} %collective-permute-done.1.refs_2_), channel_id=1, source_target_pairs={{0,2},{2,0},{1,3},{3,1},{4,6},{6,4},{5,7},{7,5},{8,10},{10,8},{9,1... | collective-permute-start | bytes 725000 | tf_op jit(solution)/shard_map/ppermute | solution.py:336
  32.0 5.7 %slice-start.1 = ((s8[6291456]{0:T(1024)(128)(4,1)}), s8[2097152]{0:T(1024)(128)(4,1)S(1)}, s32[]{:S(2)}) async-start(s8[6291456]{0:T(1024)(128)(4,1)} %bitcast.27), calls=%async_computation.2 | async-start | bytes 4194304
  37.6 25.5 %copy-start.4 = (f32[1024]{0:T(1024)S(1)}, f32[1024]{0:T(1024)}, u32[]{:S(2)}) copy-start(f32[1024]{0:T(1024)} %param.22) | copy-start | bytes 12292
  37.6 25.7 %copy-start.5 = (f32[1024]{0:T(1024)S(1)}, f32[1024]{0:T(1024)}, u32[]{:S(2)}) copy-start(f32[1024]{0:T(1024)} %param.23) | copy-start | bytes 12292

commit v17 on v16

--- a/solution.py
+++ b/solution.py
@@ -371,7 +371,7 @@
     land = land_fraction.reshape(tiles, cells)
     blocks = (block_count, steps * local_vars, cells)
     ocean_f, atmos_f = ocean_fields.reshape(blocks), atmos_fields.reshape(blocks)
-    order = ([1, nb - 1] + list(range(2, nb - 1)))[: nb - 1]
+    order = list(range(1, nb))
     along = lambda shift: [(b, (b + shift) % nb) for b in range(nb)]
     call = functools.partial(
         regrid, bands=nb, steps=steps, tiles=tiles, rows=steps * local_vars, cells=cells

time: 64.5 us -> 70.5 us (1.093)
  blocking collectives: 17.9 us -> 23.5 us
  waiting for transfers between devices: 6.81 us -> 11.6 us
  starting transfers between devices: 17.5 us -> 13.2 us
    ppermute x2, waiting for transfers between devices: 0.01 us -> 5.68 us  [per_device(): lax.ppermute(piece, 'band', along(shift))]
    all_to_all x1, blocking collectives: 17.9 us -> 23.5 us  [per_device(): lax.all_to_all(sent, ('grp', 'band', 'var'), split_axis=0, concat_axis=0,...]
    ppermute x1, starting transfers between devices: 6.95 us -> 1.4 us  [per_device(): sent.append(lax.ppermute(piece, 'band', along(shift)))]
    ppermute x1, waiting for transfers between devices: 4.99 us -> 2.42 us  [per_device(): sent.append(lax.ppermute(piece, 'band', along(shift)))]
    ppermute x5, waiting for transfers between devices: 1.81 us -> 3.45 us  [swap(): return lax.ppermute(x, axis, [(0, 1), (1, 0)])]
    ppermute x5, starting transfers between devices: 5.77 us -> 6.59 us  [swap(): return lax.ppermute(x, axis, [(0, 1), (1, 0)])]
  transfers between devices with their start and end apart: 8 -> 8, of which waited for: 3 -> 4; matrix products, arithmetic and copies ran while one was open for 3% -> 3% of each run, Pallas kernels for 11% -> 10%
where the time goes in v17:
time: 70.5 us; the launch traced here: 70.2 us
  blocking collectives  23.5 us (33%)
  Pallas kernels  17.4 us (25%)
  starting transfers between devices  13.2 us (19%)
  waiting for transfers between devices  11.6 us (16%)
  other arithmetic  2.34 us (3%)
  local copies, waits for them, and re-layouts  2 us (3%)
    all_to_all x1, blocking collectives, per_device(): lax.all_to_all(sent, ('grp', 'band', 'var'), split_axis=0, concat_axis=0,...  23.5 us
    pallas_call x3, Pallas kernels, regrid(): pl.pallas_call(body, out_shape=shapes, in_specs=specs, out_specs=[vmem] *...  12.7 us
    ppermute x5, starting transfers between devices, swap(): return lax.ppermute(x, axis, [(0, 1), (1, 0)])  6.59 us
    ppermute x2, waiting for transfers between devices, per_device(): lax.ppermute(piece, 'band', along(shift))  5.68 us
    ppermute x2, starting transfers between devices, per_device(): lax.ppermute(piece, 'band', along(shift))  5.23 us
    pallas_call x2, Pallas kernels, pack(): pl.pallas_call(functools.partial(pack_kernel, pieces, len(fields) // 2),...  4.68 us
    ppermute x5, waiting for transfers between devices, swap(): return lax.ppermute(x, axis, [(0, 1), (1, 0)])  3.45 us
    ppermute x1, waiting for transfers between devices, per_device(): sent.append(lax.ppermute(piece, 'band', along(shift)))  2.42 us
  transfers between devices with their start and end apart: 8, of which 4 were waited for; matrix products, arithmetic and copies ran while one was open for 3% of the time, Pallas kernels for 10%

profile of v17, /device:TPU:0, one launch (start us, length us, event | category | flops | bytes accessed | tf_op | source)
XLA Modules:
  0.0 70.2 jit_solution(9990972431864461409)
XLA Ops:
  0.0 2.8 %shard_map.118 = (bf16[944,128]{1,0:T(8,128)(2,1)}, bf16[944,128]{1,0:T(8,128)(2,1)}, bf16[944,128]{1,0:T(8,128)(2,1)}, bf16[36,96,128]{2,1,0:T(8,128)(2,1)}) custom-call(bf16[4,1792,128]{2,1,0:T(8,128)(2,1)} %bitcast.29, bf16[4,1792,128]{2,1,0:T(8,128)(2,1)} %bitcast.31, s32[4,14]{1,0:T(4,128)} %bitcast.35, s32[4,14]{1,0:T(4,128)} %bitcast.37, ...), custom_call_target="tpu_custom_call" | custom-call | bytes 2097152 | tf_op jit(solution)/shard_map/pallas_call | solution.py:96
  2.8 0.0 copy-start
  2.8 0.0 copy-start.1
  2.8 0.5 collective-permute-start.7
  3.4 2.6 %collective-permute-start = (bf16[944,128]{1,0:T(8,128)(2,1)}, bf16[944,128]{1,0:T(8,128)(2,1)S(1)}, u32[]{:S(2)}, u32[]{:S(2)}) collective-permute-start(bf16[944,128]{1,0:T(8,128)(2,1)} %get-tuple-element.17), channel_id=1, source_target_pairs={{0,4},{4,8},{8,12},{12,0},{1,5},{5,9},{9,13},{13,1},{2,6},{6,10},{... | collective-permute-start | bytes 725000 | tf_op jit(solution)/shard_map/ppermute | solution.py:389
  6.0 2.6 %collective-permute-start.5 = (bf16[944,128]{1,0:T(8,128)(2,1)}, bf16[944,128]{1,0:T(8,128)(2,1)S(1)}, u32[]{:S(2)}, u32[]{:S(2)}) collective-permute-start(bf16[944,128]{1,0:T(8,128)(2,1)} %get-tuple-element.23), channel_id=1, source_target_pairs={{0,8},{4,12},{8,0},{12,4},{1,9},{5,13},{9,1},{13,5},{2,10},{6,14},... | collective-permute-start | bytes 725000 | tf_op jit(solution)/shard_map/ppermute | solution.py:389
  8.6 1.5 %collective-permute-start.3 = (bf16[36,96,128]{2,1,0:T(8,128)(2,1)}, bf16[36,96,128]{2,1,0:T(8,128)(2,1)S(1)}, u32[]{:S(2)}, u32[]{:S(2)}) collective-permute-start(bf16[36,96,128]{2,1,0:T(8,128)(2,1)} %get-tuple-element.21), channel_id=1, source_target_pairs={{0,16},{16,0},{1,17},{17,1},{2,18},{18,2},{3,19},{19,3},{4,20},{20... | collective-permute-start | bytes 2654216 | tf_op jit(solution)/shard_map/ppermute | solution.py:336
  10.1 0.0 copy-done.7
  10.1 0.0 copy-done.6
  10.1 0.2 convert_reduce_fusion.1
  10.3 0.1 fusion.1
  10.4 0.1 reshape.97
  10.5 0.1 select_reduce_fusion
  10.6 0.1 reshape.89
  10.7 1.9 %shard_map.119.refs_2_.refs_12_ = bf16[1840,128]{1,0:T(8,128)(2,1)} custom-call(bf16[4,1792,128]{2,1,0:T(8,128)(2,1)} %bitcast.30, bf16[4,1792,128]{2,1,0:T(8,128)(2,1)} %bitcast.32, s32[4,14]{1,0:T(4,128)} %bitcast.36, s32[4,14]{1,0:T(4,128)} %bitcast.38, f32[16,128]{1,0:T(8,128)} %bitcast.34), custom_call_target="tpu_custom_call" | custom-call | bytes 2097152 | tf_op jit(solution)/shard_map/pallas_call | solution.py:96
  12.6 0.1 add_add_fusion
  12.7 0.7 slice_convert_fusion.2
  13.4 0.7 fusion.3
  14.1 0.1 add_add_fusion.2.refs_7_
  14.1 0.1 pad_add_fusion.4.refs_1_.refs_11_
  14.2 0.0 copy-done.1
  14.2 1.0 %copy-done.2 = bf16[1840,128]{1,0:T(8,128)(2,1)S(1)} copy-done((bf16[1840,128]{1,0:T(8,128)(2,1)S(1)}, bf16[1840,128]{1,0:T(8,128)(2,1)}, u32[]{:S(2)}) %copy-start.2) | copy-done | bytes 471064
  15.3 1.3 %shard_map.120.refs_14_ = bf16[4,2,2,32,3072]{4,3,2,1,0:T(8,128)(2,1)S(1)} custom-call(s32[3,14]{1,0:T(4,128)S(1)} %pad_add_fusion.refs_0_.refs_10_, s32[2]{0:T(128)S(1)} %pad_add_fusion.4.refs_1_.refs_11_, bf16[1840,128]{1,0:T(8,128)(2,1)S(1)} %copy-done.2, bf16[36,96,128]{2,1,0:T(8,128)(2,1)S(1)} %bitcast.20, bf16[36,96,128]{2,1,0:T(8,128)(2,1)S(1)} %bitcast.24), custom_call_target="tpu_custom_call" | custom-call | flops 44040192 | bytes 3145728 | tf_op jit(solution)/shard_map/pallas_call | solution.py:262
  16.6 0.0 collective-permute-done.refs_2_
  16.6 0.0 copy-done.8
  16.6 1.4 %collective-permute-start.1 = (bf16[944,128]{1,0:T(8,128)(2,1)S(1)}, bf16[944,128]{1,0:T(8,128)(2,1)S(1)}, u32[]{:S(2)}, u32[]{:S(2)}) collective-permute-start(bf16[944,128]{1,0:T(8,128)(2,1)S(1)} %copy-done.8), channel_id=1, source_target_pairs={{0,12},{4,0},{8,4},{12,8},{1,13},{5,1},{9,5},{13,9},{2,14},{6,2},{... | collective-permute-start | bytes 725000 | tf_op jit(solution)/shard_map/ppermute | solution.py:425
  18.0 1.5 %collective-permute-start.4 = (bf16[944,128]{1,0:T(8,128)(2,1)S(1)}, bf16[944,128]{1,0:T(8,128)(2,1)S(1)}, u32[]{:S(2)}, u32[]{:S(2)}) collective-permute-start(bf16[944,128]{1,0:T(8,128)(2,1)S(1)} %collective-permute-done.refs_2_), channel_id=1, source_target_pairs={{0,2},{2,0},{1,3},{3,1},{4,6},{6,4},{5,7},{7,5},{8,10},{10,8},{9,1... | collective-permute-start | bytes 725000 | tf_op jit(solution)/shard_map/ppermute | solution.py:336
  19.5 5.7 %collective-permute-done.5.refs_8_ = bf16[944,128]{1,0:T(8,128)(2,1)S(1)} collective-permute-done((bf16[944,128]{1,0:T(8,128)(2,1)}, bf16[944,128]{1,0:T(8,128)(2,1)S(1)}, u32[]{:S(2)}, u32[]{:S(2)}) %collective-permute-start.5) | collective-permute-done | bytes 241696 | tf_op jit(solution)/shard_map/ppermute | solution.py:389
  25.2 1.5 %collective-permute-start.6 = (bf16[944,128]{1,0:T(8,128)(2,1)S(1)}, bf16[944,128]{1,0:T(8,128)(2,1)S(1)}, u32[]{:S(2)}, u32[]{:S(2)}) collective-permute-start(bf16[944,128]{1,0:T(8,128)(2,1)S(1)} %collective-permute-done.5.refs_8_), channel_id=1, source_target_pairs={{0,2},{2,0},{1,3},{3,1},{4,6},{6,4},{5,7},{7,5},{8,10},{10,8},{9,1... | collective-permute-start | bytes 725000 | tf_op jit(solution)/shard_map/ppermute | solution.py:336
  26.7 2.4 %collective-permute-done.1.refs_2_ = bf16[944,128]{1,0:T(8,128)(2,1)S(1)} collective-permute-done((bf16[944,128]{1,0:T(8,128)(2,1)S(1)}, bf16[944,128]{1,0:T(8,128)(2,1)S(1)}, u32[]{:S(2)}, u32[]{:S(2)}) %collective-permute-start.1) | collective-permute-done | bytes 241696 | tf_op jit(solution)/shard_map/ppermute | solution.py:425
  29.1 1.6 %collective-permute-start.2 = (bf16[944,128]{1,0:T(8,128)(2,1)S(1)}, bf16[944,128]{1,0:T(8,128)(2,1)S(1)}, u32[]{:S(2)}, u32[]{:S(2)}) collective-permute-start(bf16[944,128]{1,0:T(8,128)(2,1)S(1)} %collective-permute-done.1.refs_2_), channel_id=1, source_target_pairs={{0,2},{2,0},{1,3},{3,1},{4,6},{6,4},{5,7},{7,5},{8,10},{10,8},{9,1... | collective-permute-start | bytes 725000 | tf_op jit(solution)/shard_map/ppermute | solution.py:336
  30.7 3.2 %collective-permute-done.6.refs_9_ = bf16[944,128]{1,0:T(8,128)(2,1)S(1)} collective-permute-done((bf16[944,128]{1,0:T(8,128)(2,1)S(1)}, bf16[944,128]{1,0:T(8,128)(2,1)S(1)}, u32[]{:S(2)}, u32[]{:S(2)}) %collective-permute-start.6) | collective-permute-done | bytes 241696 | tf_op jit(solution)/shard_map/ppermute | solution.py:336
  33.9 0.0 collective-permute-done.4.refs_3_
  33.9 0.0 collective-permute-done.3.refs_13_.refs_6_
  33.9 0.0 slice-start.1
  33.9 3.9 %shard_map.121.refs_7_ = bf16[4,2,2,32,3072]{4,3,2,1,0:T(8,128)(2,1)S(1)} custom-call(s32[3,14]{1,0:T(4,128)S(1)} %get-tuple-element.37.refs_0_, s32[3]{0:T(128)S(1)} %get-tuple-element.35.refs_1_, bf16[944,128]{1,0:T(8,128)(2,1)S(1)} %collective-permute-done.refs_2_, ...), custom_call_target="tpu_custom_call", output_to_operand_aliasing={{}: (14, {})} | custom-call | flops 220200960 | bytes 15728640 | tf_op jit(solution)/shard_map/pallas_call | solution.py:262
  37.9 0.2 collective-permute-done.2.refs_3_
  38.1 0.0 collective-permute-done.7.refs_9_
  38.1 0.0 copy-start.4
  38.1 0.0 copy-start.5
  38.1 7.5 %shard_map.122 = (bf16[4,2,2,32,3072]{4,3,2,1,0:T(8,128)(2,1)S(1)}, bf16[16,16,1024]{2,1,0:T(8,128)(2,1)S(1)}) custom-call(s32[3,14]{1,0:T(4,128)S(1)} %get-tuple-element.36.refs_0_, s32[3]{0:T(128)S(1)} %get-tuple-element.34.refs_1_, bf16[944,128]{1,0:T(8,128)(2,1)S(1)} %collective-permute-done.1.refs_2_, ...), custom_call_target="tpu_custom_call", output_to_operand_aliasing={{0}: (7, {})} | custom-call | flops 3309305856 | bytes 12582912 | tf_op jit(solution)/shard_map/pallas_call | solution.py:262
  45.6 23.5 %all_to_all.5 = bf16[16,16,1024]{2,1,0:T(8,128)(2,1)S(1)} all-to-all(bf16[16,16,1024]{2,1,0:T(8,128)(2,1)S(1)} %get-tuple-element.26), channel_id=1, replica_groups=mesh['grp'=2,'band'=4,'var'=2,'sub'=2] {'grp','band','var'}, dimensions={0} | all-to-all | bytes 1048576 | tf_op jit(solution)/shard_map/all_to_all | solution.py:437
  69.1 0.1 convert_reduce_fusion
  69.2 0.1 multiply_reduce_fusion
  69.4 0.1 rsqrt.12
  69.4 0.0 copy-done.5
  69.4 0.1 fusion
  69.5 0.6 copy.17
  (24 shorter events, 0.1 us)
Async XLA Ops:
  0.0 10.1 %copy-start.7 = (s32[36,1]{0,1:T(1,128)S(1)}, s32[36,1]{0,1:T(1,128)}, u32[]{:S(2)}) copy-start(s32[36,1]{0,1:T(1,128)} %param.17) | copy-start | bytes 436
  0.0 10.1 %copy-start.6 = (s32[36,1]{0,1:T(1,128)S(1)}, s32[36,1]{0,1:T(1,128)}, u32[]{:S(2)}) copy-start(s32[36,1]{0,1:T(1,128)} %param.13) | copy-start | bytes 436
  2.8 11.4 %copy-start = (bf16[36,4,24,128]{3,2,1,0:T(8,128)(2,1)S(1)}, bf16[36,4,24,128]{3,2,1,0:T(8,128)(2,1)}, u32[]{:S(2)}) copy-start(bf16[36,4,24,128]{3,2,1,0:T(8,128)(2,1)} %param.12) | copy-start | bytes 2654212
  2.8 11.4 %copy-start.1 = (bf16[36,4,24,128]{3,2,1,0:T(8,128)(2,1)S(1)}, bf16[36,4,24,128]{3,2,1,0:T(8,128)(2,1)}, u32[]{:S(2)}) copy-start(bf16[36,4,24,128]{3,2,1,0:T(8,128)(2,1)} %param.16) | copy-start | bytes 2654212
  2.8 35.3 %collective-permute-start.7 = (bf16[3072,1024]{1,0:T(8,128)(2,1)}, bf16[3072,1024]{1,0:T(8,128)(2,1)}, u32[]{:S(2)}, u32[]{:S(2)}) collective-permute-start(bf16[3072,1024]{1,0:T(8,128)(2,1)} %refs_8_.1), channel_id=1, source_target_pairs={{0,1},{1,0},{2,3},{3,2},{4,5},{5,4},{6,7},{7,6},{8,9},{9,8},{10,11... | collective-permute-start | bytes 18874376 | tf_op jit(solution)/shard_map/ppermute | solution.py:336
  3.4 13.2 %collective-permute-start = (bf16[944,128]{1,0:T(8,128)(2,1)}, bf16[944,128]{1,0:T(8,128)(2,1)S(1)}, u32[]{:S(2)}, u32[]{:S(2)}) collective-permute-start(bf16[944,128]{1,0:T(8,128)(2,1)} %get-tuple-element.17), channel_id=1, source_target_pairs={{0,4},{4,8},{8,12},{12,0},{1,5},{5,9},{9,13},{13,1},{2,6},{6,10},{... | collective-permute-start | bytes 725000 | tf_op jit(solution)/shard_map/ppermute | solution.py:389
  6.0 19.2 %collective-permute-start.5 = (bf16[944,128]{1,0:T(8,128)(2,1)}, bf16[944,128]{1,0:T(8,128)(2,1)S(1)}, u32[]{:S(2)}, u32[]{:S(2)}) collective-permute-start(bf16[944,128]{1,0:T(8,128)(2,1)} %get-tuple-element.23), channel_id=1, source_target_pairs={{0,8},{4,12},{8,0},{12,4},{1,9},{5,13},{9,1},{13,5},{2,10},{6,14},... | collective-permute-start | bytes 725000 | tf_op jit(solution)/shard_map/ppermute | solution.py:389
  8.6 25.3 %collective-permute-start.3 = (bf16[36,96,128]{2,1,0:T(8,128)(2,1)}, bf16[36,96,128]{2,1,0:T(8,128)(2,1)S(1)}, u32[]{:S(2)}, u32[]{:S(2)}) collective-permute-start(bf16[36,96,128]{2,1,0:T(8,128)(2,1)} %get-tuple-element.21), channel_id=1, source_target_pairs={{0,16},{16,0},{1,17},{17,1},{2,18},{18,2},{3,19},{19,3},{4,20},{20... | collective-permute-start | bytes 2654216 | tf_op jit(solution)/shard_map/ppermute | solution.py:336
  10.7 5.9 %copy-start.8 = (bf16[944,128]{1,0:T(8,128)(2,1)S(1)}, bf16[944,128]{1,0:T(8,128)(2,1)}, u32[]{:S(2)}) copy-start(bf16[944,128]{1,0:T(8,128)(2,1)} %get-tuple-element.20) | copy-start | bytes 724996
  14.2 1.0 %copy-start.2 = (bf16[1840,128]{1,0:T(8,128)(2,1)S(1)}, bf16[1840,128]{1,0:T(8,128)(2,1)}, u32[]{:S(2)}) copy-start(bf16[1840,128]{1,0:T(8,128)(2,1)} %shard_map.119.refs_2_.refs_12_) | copy-start | bytes 1413124
  15.3 18.7 %copy-start.3 = (bf16[1840,128]{1,0:T(8,128)(2,1)S(1)}, bf16[1840,128]{1,0:T(8,128)(2,1)}, u32[]{:S(2)}) copy-start(bf16[1840,128]{1,0:T(8,128)(2,1)} %shard_map.119.refs_2_.refs_12_) | copy-start | bytes 1413124
  15.3 22.9 %slice-start = ((s8[6291456]{0:T(1024)(128)(4,1)}), s8[4194304]{0:T(1024)(128)(4,1)S(1)}, s32[]{:S(2)}) async-start(s8[6291456]{0:T(1024)(128)(4,1)} %bitcast.27), calls=%async_computation.1 | async-start | bytes 8388608
  16.6 12.5 %collective-permute-start.1 = (bf16[944,128]{1,0:T(8,128)(2,1)S(1)}, bf16[944,128]{1,0:T(8,128)(2,1)S(1)}, u32[]{:S(2)}, u32[]{:S(2)}) collective-permute-start(bf16[944,128]{1,0:T(8,128)(2,1)S(1)} %copy-done.8), channel_id=1, source_target_pairs={{0,12},{4,0},{8,4},{12,8},{1,13},{5,1},{9,5},{13,9},{2,14},{6,2},{... | collective-permute-start | bytes 725000 | tf_op jit(solution)/shard_map/ppermute | solution.py:425
  18.0 15.9 %collective-permute-start.4 = (bf16[944,128]{1,0:T(8,128)(2,1)S(1)}, bf16[944,128]{1,0:T(8,128)(2,1)S(1)}, u32[]{:S(2)}, u32[]{:S(2)}) collective-permute-start(bf16[944,128]{1,0:T(8,128)(2,1)S(1)} %collective-permute-done.refs_2_), channel_id=1, source_target_pairs={{0,2},{2,0},{1,3},{3,1},{4,6},{6,4},{5,7},{7,5},{8,10},{10,8},{9,1... | collective-permute-start | bytes 725000 | tf_op jit(solution)/shard_map/ppermute | solution.py:336
  25.2 8.7 %collective-permute-start.6 = (bf16[944,128]{1,0:T(8,128)(2,1)S(1)}, bf16[944,128]{1,0:T(8,128)(2,1)S(1)}, u32[]{:S(2)}, u32[]{:S(2)}) collective-permute-start(bf16[944,128]{1,0:T(8,128)(2,1)S(1)} %collective-permute-done.5.refs_8_), channel_id=1, source_target_pairs={{0,2},{2,0},{1,3},{3,1},{4,6},{6,4},{5,7},{7,5},{8,10},{10,8},{9,1... | collective-permute-start | bytes 725000 | tf_op jit(solution)/shard_map/ppermute | solution.py:336
  29.1 9.0 %collective-permute-start.2 = (bf16[944,128]{1,0:T(8,128)(2,1)S(1)}, bf16[944,128]{1,0:T(8,128)(2,1)S(1)}, u32[]{:S(2)}, u32[]{:S(2)}) collective-permute-start(bf16[944,128]{1,0:T(8,128)(2,1)S(1)} %collective-permute-done.1.refs_2_), channel_id=1, source_target_pairs={{0,2},{2,0},{1,3},{3,1},{4,6},{6,4},{5,7},{7,5},{8,10},{10,8},{9,1... | collective-permute-start | bytes 725000 | tf_op jit(solution)/shard_map/ppermute | solution.py:336
  33.9 4.2 %slice-start.1 = ((s8[6291456]{0:T(1024)(128)(4,1)}), s8[2097152]{0:T(1024)(128)(4,1)S(1)}, s32[]{:S(2)}) async-start(s8[6291456]{0:T(1024)(128)(4,1)} %bitcast.27), calls=%async_computation.2 | async-start | bytes 4194304
  38.1 31.1 %copy-start.4 = (f32[1024]{0:T(1024)S(1)}, f32[1024]{0:T(1024)}, u32[]{:S(2)}) copy-start(f32[1024]{0:T(1024)} %param.22) | copy-start | bytes 12292
  38.1 31.3 %copy-start.5 = (f32[1024]{0:T(1024)S(1)}, f32[1024]{0:T(1024)}, u32[]{:S(2)}) copy-start(f32[1024]{0:T(1024)} %param.23) | copy-start | bytes 12292

commit v18 on v16

--- a/solution.py
+++ b/solution.py
@@ -106,8 +106,9 @@
 
 
 def run_jobs(steps, jobs, refs, out, acc, scale):
-    local_rows, cells = acc.shape[1] // (scale.shape[0] // 2 - 4), acc.shape[2]
-    tiles = acc.shape[1] // local_rows
+    tiles, cells = scale.shape[0] // 2 - 4, acc.shape[2]
+    stride = acc.shape[1] // (tiles // 2)
+    local_rows = (stride - 8) // 2
     local_vars = local_rows // steps
     half_vars = local_vars // 2
     for table, where, meta, meta_at, parts, groups in jobs:
@@ -141,7 +142,9 @@
                     preferred_element_type=jnp.float32,
                 )
                 dense = dense * scale[pl.ds(table[2, slot], 1), :]
-                span = pl.ds(pl.multiple_of(table[1, slot] * local_rows, local_rows), local_rows)
+                tile = table[1, slot]
+                start = lax.shift_right_logical(tile, 1) * stride + (tile & 1) * local_rows
+                span = pl.ds(pl.multiple_of(start, 8), local_rows)
                 for g in range(len(groups)):
                     acc[g, span, :] += dense[g * local_rows : (g + 1) * local_rows]
         for g, (to, _) in enumerate(groups):
@@ -149,7 +152,7 @@
                 for q in range(2):
                     column = (v % half_vars * 2 + q) * cells
                     rows = [
-                        acc[g, pl.ds(q * local_rows + t * local_vars + v, tiles // 2, 2 * local_rows), :]
+                        acc[g, pl.ds(q * local_rows + t * local_vars + v, tiles // 2, stride), :]
                         for t in range(steps)
                     ]
                     out[where[0], to, v // half_vars, :, pl.ds(column, cells)] = jnp.concatenate(
@@ -237,7 +240,7 @@
     shape = (bands, groups, 2, steps * tiles // 2, rows // steps // 2 * 2 * cells)
     shapes = [jax.ShapeDtypeStruct(shape, jnp.bfloat16)]
     scratch = [
-        pltpu.VMEM((most, tiles * rows, cells), jnp.float32),
+        pltpu.VMEM((most, tiles // 2 * (2 * rows + 8), cells), jnp.float32),
         pltpu.VMEM((2 * tiles + 8, cells), jnp.float32),
     ]
     if last is None:

time: 64.5 us -> 64 us (level)
  Pallas kernels: 17.4 us -> 15.1 us
  waiting for transfers between devices: 6.81 us -> 8.52 us
    pallas_call x3, Pallas kernels: 12.7 us -> 10.4 us  [regrid(): pl.pallas_call(body, out_shape=shapes, in_specs=specs, out_specs=[vmem] *...]
    ppermute x5, waiting for transfers between devices: 1.81 us -> 3.52 us  [swap(): return lax.ppermute(x, axis, [(0, 1), (1, 0)])]
  transfers between devices with their start and end apart: 8 -> 8, of which waited for: 3 -> 3; matrix products, arithmetic and copies ran while one was open for 3% -> 3% of each run, Pallas kernels for 11% -> 8%
where the time goes in v18:
time: 64 us; the launch traced here: 63.7 us
  starting transfers between devices  17.8 us (28%)
  blocking collectives  17.7 us (28%)
  Pallas kernels  15.1 us (24%)
  waiting for transfers between devices  8.52 us (13%)
  other arithmetic  2.34 us (4%)
  local copies, waits for them, and re-layouts  2 us (3%)
    all_to_all x1, blocking collectives, per_device(): lax.all_to_all(sent, ('grp', 'band', 'var'), split_axis=0, concat_axis=0,...  17.7 us
    pallas_call x3, Pallas kernels, regrid(): pl.pallas_call(body, out_shape=shapes, in_specs=specs, out_specs=[vmem] *...  10.4 us
    ppermute x1, starting transfers between devices, per_device(): sent.append(lax.ppermute(piece, 'band', along(shift)))  7.25 us
    ppermute x5, starting transfers between devices, swap(): return lax.ppermute(x, axis, [(0, 1), (1, 0)])  5.77 us
    ppermute x1, waiting for transfers between devices, per_device(): sent.append(lax.ppermute(piece, 'band', along(shift)))  4.99 us
    ppermute x2, starting transfers between devices, per_device(): lax.ppermute(piece, 'band', along(shift))  4.75 us
    pallas_call x2, Pallas kernels, pack(): pl.pallas_call(functools.partial(pack_kernel, pieces, len(fields) // 2),...  4.68 us
    ppermute x5, waiting for transfers between devices, swap(): return lax.ppermute(x, axis, [(0, 1), (1, 0)])  3.52 us
  transfers between devices with their start and end apart: 8, of which 3 were waited for; matrix products, arithmetic and copies ran while one was open for 3% of the time, Pallas kernels for 8%

profile of v18, /device:TPU:0, one launch (start us, length us, event | category | flops | bytes accessed | tf_op | source)
XLA Modules:
  0.0 63.7 jit_solution(5540557947135148464)
XLA Ops:
  0.0 2.8 %shard_map.118 = (bf16[944,128]{1,0:T(8,128)(2,1)}, bf16[944,128]{1,0:T(8,128)(2,1)}, bf16[944,128]{1,0:T(8,128)(2,1)}, bf16[36,96,128]{2,1,0:T(8,128)(2,1)}) custom-call(bf16[4,1792,128]{2,1,0:T(8,128)(2,1)} %bitcast.29, bf16[4,1792,128]{2,1,0:T(8,128)(2,1)} %bitcast.31, s32[4,14]{1,0:T(4,128)} %bitcast.35, s32[4,14]{1,0:T(4,128)} %bitcast.37, ...), custom_call_target="tpu_custom_call" | custom-call | bytes 2097152 | tf_op jit(solution)/shard_map/pallas_call | solution.py:96
  2.8 0.0 copy-start
  2.8 0.0 copy-start.1
  2.8 0.5 collective-permute-start.7
  3.4 2.6 %collective-permute-start = (bf16[944,128]{1,0:T(8,128)(2,1)}, bf16[944,128]{1,0:T(8,128)(2,1)S(1)}, u32[]{:S(2)}, u32[]{:S(2)}) collective-permute-start(bf16[944,128]{1,0:T(8,128)(2,1)} %get-tuple-element.17), channel_id=1, source_target_pairs={{0,4},{4,8},{8,12},{12,0},{1,5},{5,9},{9,13},{13,1},{2,6},{6,10},{... | collective-permute-start | bytes 725000 | tf_op jit(solution)/shard_map/ppermute | solution.py:392
  6.0 2.1 %collective-permute-start.5 = (bf16[944,128]{1,0:T(8,128)(2,1)}, bf16[944,128]{1,0:T(8,128)(2,1)S(1)}, u32[]{:S(2)}, u32[]{:S(2)}) collective-permute-start(bf16[944,128]{1,0:T(8,128)(2,1)} %get-tuple-element.23), channel_id=1, source_target_pairs={{0,12},{4,0},{8,4},{12,8},{1,13},{5,1},{9,5},{13,9},{2,14},{6,2},{... | collective-permute-start | bytes 725000 | tf_op jit(solution)/shard_map/ppermute | solution.py:392
  8.1 1.7 %collective-permute-start.3 = (bf16[36,96,128]{2,1,0:T(8,128)(2,1)}, bf16[36,96,128]{2,1,0:T(8,128)(2,1)S(1)}, u32[]{:S(2)}, u32[]{:S(2)}) collective-permute-start(bf16[36,96,128]{2,1,0:T(8,128)(2,1)} %get-tuple-element.21), channel_id=1, source_target_pairs={{0,16},{16,0},{1,17},{17,1},{2,18},{18,2},{3,19},{19,3},{4,20},{20... | collective-permute-start | bytes 2654216 | tf_op jit(solution)/shard_map/ppermute | solution.py:339
  9.8 0.0 copy-done.7
  9.8 0.0 copy-done.6
  9.8 0.2 convert_reduce_fusion.1
  10.0 0.1 fusion.1
  10.1 0.1 reshape.97
  10.2 0.1 select_reduce_fusion
  10.3 0.1 reshape.89
  10.3 1.9 %shard_map.119.refs_2_.refs_12_ = bf16[1840,128]{1,0:T(8,128)(2,1)} custom-call(bf16[4,1792,128]{2,1,0:T(8,128)(2,1)} %bitcast.30, bf16[4,1792,128]{2,1,0:T(8,128)(2,1)} %bitcast.32, s32[4,14]{1,0:T(4,128)} %bitcast.36, s32[4,14]{1,0:T(4,128)} %bitcast.38, f32[16,128]{1,0:T(8,128)} %bitcast.34), custom_call_target="tpu_custom_call" | custom-call | bytes 2097152 | tf_op jit(solution)/shard_map/pallas_call | solution.py:96
  12.2 0.1 add_add_fusion
  12.3 0.7 %slice_convert_fusion.2 = s32[1,14]{1,0:T(1,128)S(1)} fusion(bf16[1840,128]{1,0:T(8,128)(2,1)} %shard_map.119.refs_2_.refs_12_), kind=kLoop, calls=%fused_computation.30 | loop fusion | flops 14 | bytes 84 | tf_op jit(solution)/shard_map/convert_element_type | solution.py:403
  13.0 0.7 %fusion.3 = s32[1,14]{1,0:T(1,128)S(1)} fusion(pred[4,14]{1,0:T(4,128)(4,1)S(1)} %reshape.97, s32[]{:T(128)S(6)} %select_n.67, s32[]{:T(128)S(6)} %mul.61, bf16[1840,128]{1,0:T(8,128)(2,1)} %shard_map.119.refs_2_.refs_12_), kind=kLoop, calls=%fused_computation.22 | loop fusion | flops 42 | bytes 106 | tf_op jit(solution)/shard_map/jit(_where)/select_n | solution.py:406
  13.7 0.1 add_add_fusion.2.refs_7_
  13.8 0.1 pad_add_fusion.4.refs_1_.refs_11_
  13.9 0.0 copy-done.1
  13.9 1.0 %copy-done.2 = bf16[1840,128]{1,0:T(8,128)(2,1)S(1)} copy-done((bf16[1840,128]{1,0:T(8,128)(2,1)S(1)}, bf16[1840,128]{1,0:T(8,128)(2,1)}, u32[]{:S(2)}) %copy-start.2) | copy-done | bytes 471064
  14.9 1.0 %shard_map.120.refs_14_ = bf16[4,2,2,32,3072]{4,3,2,1,0:T(8,128)(2,1)S(1)} custom-call(s32[3,14]{1,0:T(4,128)S(1)} %pad_add_fusion.refs_0_.refs_10_, s32[2]{0:T(128)S(1)} %pad_add_fusion.4.refs_1_.refs_11_, bf16[1840,128]{1,0:T(8,128)(2,1)S(1)} %copy-done.2, bf16[36,96,128]{2,1,0:T(8,128)(2,1)S(1)} %bitcast.20, bf16[36,96,128]{2,1,0:T(8,128)(2,1)S(1)} %bitcast.24), custom_call_target="tpu_custom_call" | custom-call | flops 44040192 | bytes 3145728 | tf_op jit(solution)/shard_map/pallas_call | solution.py:265
  15.9 0.0 collective-permute-done.refs_2_
  15.9 0.0 copy-done.8
  16.0 7.3 %collective-permute-start.1 = (bf16[944,128]{1,0:T(8,128)(2,1)S(1)}, bf16[944,128]{1,0:T(8,128)(2,1)S(1)}, u32[]{:S(2)}, u32[]{:S(2)}) collective-permute-start(bf16[944,128]{1,0:T(8,128)(2,1)S(1)} %copy-done.8), channel_id=1, source_target_pairs={{0,8},{4,12},{8,0},{12,4},{1,9},{5,13},{9,1},{13,5},{2,10},{6,14},... | collective-permute-start | bytes 725000 | tf_op jit(solution)/shard_map/ppermute | solution.py:428
  23.2 1.5 %collective-permute-start.4 = (bf16[944,128]{1,0:T(8,128)(2,1)S(1)}, bf16[944,128]{1,0:T(8,128)(2,1)S(1)}, u32[]{:S(2)}, u32[]{:S(2)}) collective-permute-start(bf16[944,128]{1,0:T(8,128)(2,1)S(1)} %collective-permute-done.refs_2_), channel_id=1, source_target_pairs={{0,2},{2,0},{1,3},{3,1},{4,6},{6,4},{5,7},{7,5},{8,10},{10,8},{9,1... | collective-permute-start | bytes 725000 | tf_op jit(solution)/shard_map/ppermute | solution.py:339
  24.7 0.0 collective-permute-done.5.refs_8_
  24.7 0.5 collective-permute-start.6
  25.3 5.0 %collective-permute-done.1.refs_2_ = bf16[944,128]{1,0:T(8,128)(2,1)S(1)} collective-permute-done((bf16[944,128]{1,0:T(8,128)(2,1)S(1)}, bf16[944,128]{1,0:T(8,128)(2,1)S(1)}, u32[]{:S(2)}, u32[]{:S(2)}) %collective-permute-start.1) | collective-permute-done | bytes 241696 | tf_op jit(solution)/shard_map/ppermute | solution.py:428
  30.3 1.6 %collective-permute-start.2 = (bf16[944,128]{1,0:T(8,128)(2,1)S(1)}, bf16[944,128]{1,0:T(8,128)(2,1)S(1)}, u32[]{:S(2)}, u32[]{:S(2)}) collective-permute-start(bf16[944,128]{1,0:T(8,128)(2,1)S(1)} %collective-permute-done.1.refs_2_), channel_id=1, source_target_pairs={{0,2},{2,0},{1,3},{3,1},{4,6},{6,4},{5,7},{7,5},{8,10},{10,8},{9,1... | collective-permute-start | bytes 725000 | tf_op jit(solution)/shard_map/ppermute | solution.py:339
  31.9 0.1 collective-permute-done.6.refs_9_
  32.0 0.0 collective-permute-done.4.refs_3_
  32.0 0.0 collective-permute-done.3.refs_13_.refs_6_
  32.0 0.0 slice-start.1
  32.0 2.4 %shard_map.121.refs_7_ = bf16[4,2,2,32,3072]{4,3,2,1,0:T(8,128)(2,1)S(1)} custom-call(s32[3,14]{1,0:T(4,128)S(1)} %get-tuple-element.37.refs_0_, s32[3]{0:T(128)S(1)} %get-tuple-element.35.refs_1_, bf16[944,128]{1,0:T(8,128)(2,1)S(1)} %collective-permute-done.refs_2_, ...), custom_call_target="tpu_custom_call", output_to_operand_aliasing={{}: (14, {})} | custom-call | flops 220200960 | bytes 15728640 | tf_op jit(solution)/shard_map/pallas_call | solution.py:265
  34.4 3.4 %collective-permute-done.2.refs_3_ = bf16[944,128]{1,0:T(8,128)(2,1)S(1)} collective-permute-done((bf16[944,128]{1,0:T(8,128)(2,1)S(1)}, bf16[944,128]{1,0:T(8,128)(2,1)S(1)}, u32[]{:S(2)}, u32[]{:S(2)}) %collective-permute-start.2) | collective-permute-done | bytes 241696 | tf_op jit(solution)/shard_map/ppermute | solution.py:339
  37.8 0.0 collective-permute-done.7.refs_9_
  37.8 0.0 slice-done.1
  37.8 0.0 copy-start.4
  37.8 0.0 copy-start.5
  37.8 7.0 %shard_map.122 = (bf16[4,2,2,32,3072]{4,3,2,1,0:T(8,128)(2,1)S(1)}, bf16[16,16,1024]{2,1,0:T(8,128)(2,1)S(1)}) custom-call(s32[3,14]{1,0:T(4,128)S(1)} %get-tuple-element.36.refs_0_, s32[3]{0:T(128)S(1)} %get-tuple-element.34.refs_1_, bf16[944,128]{1,0:T(8,128)(2,1)S(1)} %collective-permute-done.1.refs_2_, ...), custom_call_target="tpu_custom_call", output_to_operand_aliasing={{0}: (7, {})} | custom-call | flops 3309305856 | bytes 12582912 | tf_op jit(solution)/shard_map/pallas_call | solution.py:265
  44.8 17.7 %all_to_all.5 = bf16[16,16,1024]{2,1,0:T(8,128)(2,1)S(1)} all-to-all(bf16[16,16,1024]{2,1,0:T(8,128)(2,1)S(1)} %get-tuple-element.26), channel_id=1, replica_groups=mesh['grp'=2,'band'=4,'var'=2,'sub'=2] {'grp','band','var'}, dimensions={0} | all-to-all | bytes 1048576 | tf_op jit(solution)/shard_map/all_to_all | solution.py:440
  62.6 0.1 convert_reduce_fusion
  62.7 0.1 multiply_reduce_fusion
  62.8 0.1 rsqrt.12
  62.9 0.1 fusion
  63.0 0.6 copy.17
  (24 shorter events, 0.1 us)
Async XLA Ops:
  0.0 9.8 %copy-start.7 = (s32[36,1]{0,1:T(1,128)S(1)}, s32[36,1]{0,1:T(1,128)}, u32[]{:S(2)}) copy-start(s32[36,1]{0,1:T(1,128)} %param.17) | copy-start | bytes 436
  0.0 9.8 %copy-start.6 = (s32[36,1]{0,1:T(1,128)S(1)}, s32[36,1]{0,1:T(1,128)}, u32[]{:S(2)}) copy-start(s32[36,1]{0,1:T(1,128)} %param.13) | copy-start | bytes 436
  2.8 11.1 %copy-start = (bf16[36,4,24,128]{3,2,1,0:T(8,128)(2,1)S(1)}, bf16[36,4,24,128]{3,2,1,0:T(8,128)(2,1)}, u32[]{:S(2)}) copy-start(bf16[36,4,24,128]{3,2,1,0:T(8,128)(2,1)} %param.12) | copy-start | bytes 2654212
  2.8 11.1 %copy-start.1 = (bf16[36,4,24,128]{3,2,1,0:T(8,128)(2,1)S(1)}, bf16[36,4,24,128]{3,2,1,0:T(8,128)(2,1)}, u32[]{:S(2)}) copy-start(bf16[36,4,24,128]{3,2,1,0:T(8,128)(2,1)} %param.16) | copy-start | bytes 2654212
  2.8 35.0 %collective-permute-start.7 = (bf16[3072,1024]{1,0:T(8,128)(2,1)}, bf16[3072,1024]{1,0:T(8,128)(2,1)}, u32[]{:S(2)}, u32[]{:S(2)}) collective-permute-start(bf16[3072,1024]{1,0:T(8,128)(2,1)} %refs_8_.1), channel_id=1, source_target_pairs={{0,1},{1,0},{2,3},{3,2},{4,5},{5,4},{6,7},{7,6},{8,9},{9,8},{10,11... | collective-permute-start | bytes 18874376 | tf_op jit(solution)/shard_map/ppermute | solution.py:339
  3.4 12.6 %collective-permute-start = (bf16[944,128]{1,0:T(8,128)(2,1)}, bf16[944,128]{1,0:T(8,128)(2,1)S(1)}, u32[]{:S(2)}, u32[]{:S(2)}) collective-permute-start(bf16[944,128]{1,0:T(8,128)(2,1)} %get-tuple-element.17), channel_id=1, source_target_pairs={{0,4},{4,8},{8,12},{12,0},{1,5},{5,9},{9,13},{13,1},{2,6},{6,10},{... | collective-permute-start | bytes 725000 | tf_op jit(solution)/shard_map/ppermute | solution.py:392
  6.0 18.7 %collective-permute-start.5 = (bf16[944,128]{1,0:T(8,128)(2,1)}, bf16[944,128]{1,0:T(8,128)(2,1)S(1)}, u32[]{:S(2)}, u32[]{:S(2)}) collective-permute-start(bf16[944,128]{1,0:T(8,128)(2,1)} %get-tuple-element.23), channel_id=1, source_target_pairs={{0,12},{4,0},{8,4},{12,8},{1,13},{5,1},{9,5},{13,9},{2,14},{6,2},{... | collective-permute-start | bytes 725000 | tf_op jit(solution)/shard_map/ppermute | solution.py:392
  8.1 23.9 %collective-permute-start.3 = (bf16[36,96,128]{2,1,0:T(8,128)(2,1)}, bf16[36,96,128]{2,1,0:T(8,128)(2,1)S(1)}, u32[]{:S(2)}, u32[]{:S(2)}) collective-permute-start(bf16[36,96,128]{2,1,0:T(8,128)(2,1)} %get-tuple-element.21), channel_id=1, source_target_pairs={{0,16},{16,0},{1,17},{17,1},{2,18},{18,2},{3,19},{19,3},{4,20},{20... | collective-permute-start | bytes 2654216 | tf_op jit(solution)/shard_map/ppermute | solution.py:339
  10.3 5.6 %copy-start.8 = (bf16[944,128]{1,0:T(8,128)(2,1)S(1)}, bf16[944,128]{1,0:T(8,128)(2,1)}, u32[]{:S(2)}) copy-start(bf16[944,128]{1,0:T(8,128)(2,1)} %get-tuple-element.20) | copy-start | bytes 724996
  13.9 1.0 %copy-start.2 = (bf16[1840,128]{1,0:T(8,128)(2,1)S(1)}, bf16[1840,128]{1,0:T(8,128)(2,1)}, u32[]{:S(2)}) copy-start(bf16[1840,128]{1,0:T(8,128)(2,1)} %shard_map.119.refs_2_.refs_12_) | copy-start | bytes 1413124
  14.9 17.1 %copy-start.3 = (bf16[1840,128]{1,0:T(8,128)(2,1)S(1)}, bf16[1840,128]{1,0:T(8,128)(2,1)}, u32[]{:S(2)}) copy-start(bf16[1840,128]{1,0:T(8,128)(2,1)} %shard_map.119.refs_2_.refs_12_) | copy-start | bytes 1413124
  14.9 22.9 %slice-start = ((s8[6291456]{0:T(1024)(128)(4,1)}), s8[4194304]{0:T(1024)(128)(4,1)S(1)}, s32[]{:S(2)}) async-start(s8[6291456]{0:T(1024)(128)(4,1)} %bitcast.27), calls=%async_computation.1 | async-start | bytes 8388608
  16.0 14.3 %collective-permute-start.1 = (bf16[944,128]{1,0:T(8,128)(2,1)S(1)}, bf16[944,128]{1,0:T(8,128)(2,1)S(1)}, u32[]{:S(2)}, u32[]{:S(2)}) collective-permute-start(bf16[944,128]{1,0:T(8,128)(2,1)S(1)} %copy-done.8), channel_id=1, source_target_pairs={{0,8},{4,12},{8,0},{12,4},{1,9},{5,13},{9,1},{13,5},{2,10},{6,14},... | collective-permute-start | bytes 725000 | tf_op jit(solution)/shard_map/ppermute | solution.py:428
  23.2 8.7 %collective-permute-start.4 = (bf16[944,128]{1,0:T(8,128)(2,1)S(1)}, bf16[944,128]{1,0:T(8,128)(2,1)S(1)}, u32[]{:S(2)}, u32[]{:S(2)}) collective-permute-start(bf16[944,128]{1,0:T(8,128)(2,1)S(1)} %collective-permute-done.refs_2_), channel_id=1, source_target_pairs={{0,2},{2,0},{1,3},{3,1},{4,6},{6,4},{5,7},{7,5},{8,10},{10,8},{9,1... | collective-permute-start | bytes 725000 | tf_op jit(solution)/shard_map/ppermute | solution.py:339
  24.7 7.2 %collective-permute-start.6 = (bf16[944,128]{1,0:T(8,128)(2,1)S(1)}, bf16[944,128]{1,0:T(8,128)(2,1)S(1)}, u32[]{:S(2)}, u32[]{:S(2)}) collective-permute-start(bf16[944,128]{1,0:T(8,128)(2,1)S(1)} %collective-permute-done.5.refs_8_), channel_id=1, source_target_pairs={{0,2},{2,0},{1,3},{3,1},{4,6},{6,4},{5,7},{7,5},{8,10},{10,8},{9,1... | collective-permute-start | bytes 725000 | tf_op jit(solution)/shard_map/ppermute | solution.py:339
  30.3 7.5 %collective-permute-start.2 = (bf16[944,128]{1,0:T(8,128)(2,1)S(1)}, bf16[944,128]{1,0:T(8,128)(2,1)S(1)}, u32[]{:S(2)}, u32[]{:S(2)}) collective-permute-start(bf16[944,128]{1,0:T(8,128)(2,1)S(1)} %collective-permute-done.1.refs_2_), channel_id=1, source_target_pairs={{0,2},{2,0},{1,3},{3,1},{4,6},{6,4},{5,7},{7,5},{8,10},{10,8},{9,1... | collective-permute-start | bytes 725000 | tf_op jit(solution)/shard_map/ppermute | solution.py:339
  32.0 5.8 %slice-start.1 = ((s8[6291456]{0:T(1024)(128)(4,1)}), s8[2097152]{0:T(1024)(128)(4,1)S(1)}, s32[]{:S(2)}) async-start(s8[6291456]{0:T(1024)(128)(4,1)} %bitcast.27), calls=%async_computation.2 | async-start | bytes 4194304
  37.8 24.9 %copy-start.4 = (f32[1024]{0:T(1024)S(1)}, f32[1024]{0:T(1024)}, u32[]{:S(2)}) copy-start(f32[1024]{0:T(1024)} %param.22) | copy-start | bytes 12292
  37.8 25.1 %copy-start.5 = (f32[1024]{0:T(1024)S(1)}, f32[1024]{0:T(1024)}, u32[]{:S(2)}) copy-start(f32[1024]{0:T(1024)} %param.23) | copy-start | bytes 12292

commit v19 on v18

--- a/solution.py
+++ b/solution.py
@@ -258,7 +258,7 @@
         scratch += [
             pltpu.VMEM((height, width), jnp.bfloat16),
             pltpu.VMEM((total, width), jnp.float32),
-            pltpu.SemaphoreType.DMA((6,)),
+            pltpu.SemaphoreType.DMA((3,)),
         ]
         limit, moved = 24 << 20, 4 * height * width
         flops += 4 * total * height * width

time: 64 us -> 63.8 us (level)
  transfers between devices with their start and end apart: 8 -> 8, of which waited for: 3 -> 3; matrix products, arithmetic and copies ran while one was open for 3% -> 4% of each run, Pallas kernels for 8% -> 8%
where the time goes in v19:
time: 63.8 us; the launch traced here: 63.5 us
  starting transfers between devices  17.8 us (28%)
  blocking collectives  17.7 us (28%)
  Pallas kernels  14.9 us (23%)
  waiting for transfers between devices  8.53 us (13%)
  other arithmetic  2.34 us (4%)
  local copies, waits for them, and re-layouts  2 us (3%)
    all_to_all x1, blocking collectives, per_device(): lax.all_to_all(sent, ('grp', 'band', 'var'), split_axis=0, concat_axis=0,...  17.7 us
    pallas_call x3, Pallas kernels, regrid(): pl.pallas_call(body, out_shape=shapes, in_specs=specs, out_specs=[vmem] *...  10.2 us
    ppermute x1, starting transfers between devices, per_device(): sent.append(lax.ppermute(piece, 'band', along(shift)))  7.26 us
    ppermute x5, starting transfers between devices, swap(): return lax.ppermute(x, axis, [(0, 1), (1, 0)])  5.77 us
    ppermute x1, waiting for transfers between devices, per_device(): sent.append(lax.ppermute(piece, 'band', along(shift)))  4.99 us
    ppermute x2, starting transfers between devices, per_device(): lax.ppermute(piece, 'band', along(shift))  4.75 us
    pallas_call x2, Pallas kernels, pack(): pl.pallas_call(functools.partial(pack_kernel, pieces, len(fields) // 2),...  4.68 us
    ppermute x5, waiting for transfers between devices, swap(): return lax.ppermute(x, axis, [(0, 1), (1, 0)])  3.53 us
  transfers between devices with their start and end apart: 8, of which 3 were waited for; matrix products, arithmetic and copies ran while one was open for 4% of the time, Pallas kernels for 8%

profile of v19, /device:TPU:0, one launch (start us, length us, event | category | flops | bytes accessed | tf_op | source)
XLA Modules:
  0.0 63.5 jit_solution(7148600433685096600)
XLA Ops:
  0.0 2.8 %shard_map.118 = (bf16[944,128]{1,0:T(8,128)(2,1)}, bf16[944,128]{1,0:T(8,128)(2,1)}, bf16[944,128]{1,0:T(8,128)(2,1)}, bf16[36,96,128]{2,1,0:T(8,128)(2,1)}) custom-call(bf16[4,1792,128]{2,1,0:T(8,128)(2,1)} %bitcast.29, bf16[4,1792,128]{2,1,0:T(8,128)(2,1)} %bitcast.31, s32[4,14]{1,0:T(4,128)} %bitcast.35, s32[4,14]{1,0:T(4,128)} %bitcast.37, ...), custom_call_target="tpu_custom_call" | custom-call | bytes 2097152 | tf_op jit(solution)/shard_map/pallas_call | solution.py:96
  2.8 0.0 copy-start
  2.8 0.0 copy-start.1
  2.8 0.5 collective-permute-start.7
  3.4 2.6 %collective-permute-start = (bf16[944,128]{1,0:T(8,128)(2,1)}, bf16[944,128]{1,0:T(8,128)(2,1)S(1)}, u32[]{:S(2)}, u32[]{:S(2)}) collective-permute-start(bf16[944,128]{1,0:T(8,128)(2,1)} %get-tuple-element.17), channel_id=1, source_target_pairs={{0,4},{4,8},{8,12},{12,0},{1,5},{5,9},{9,13},{13,1},{2,6},{6,10},{... | collective-permute-start | bytes 725000 | tf_op jit(solution)/shard_map/ppermute | solution.py:392
  6.0 2.1 %collective-permute-start.5 = (bf16[944,128]{1,0:T(8,128)(2,1)}, bf16[944,128]{1,0:T(8,128)(2,1)S(1)}, u32[]{:S(2)}, u32[]{:S(2)}) collective-permute-start(bf16[944,128]{1,0:T(8,128)(2,1)} %get-tuple-element.23), channel_id=1, source_target_pairs={{0,12},{4,0},{8,4},{12,8},{1,13},{5,1},{9,5},{13,9},{2,14},{6,2},{... | collective-permute-start | bytes 725000 | tf_op jit(solution)/shard_map/ppermute | solution.py:392
  8.1 1.7 %collective-permute-start.3 = (bf16[36,96,128]{2,1,0:T(8,128)(2,1)}, bf16[36,96,128]{2,1,0:T(8,128)(2,1)S(1)}, u32[]{:S(2)}, u32[]{:S(2)}) collective-permute-start(bf16[36,96,128]{2,1,0:T(8,128)(2,1)} %get-tuple-element.21), channel_id=1, source_target_pairs={{0,16},{16,0},{1,17},{17,1},{2,18},{18,2},{3,19},{19,3},{4,20},{20... | collective-permute-start | bytes 2654216 | tf_op jit(solution)/shard_map/ppermute | solution.py:339
  9.8 0.0 copy-done.7
  9.8 0.0 copy-done.6
  9.8 0.2 convert_reduce_fusion.1
  10.0 0.1 fusion.1
  10.1 0.1 reshape.97
  10.2 0.1 select_reduce_fusion
  10.3 0.1 reshape.89
  10.3 1.9 %shard_map.119.refs_2_.refs_12_ = bf16[1840,128]{1,0:T(8,128)(2,1)} custom-call(bf16[4,1792,128]{2,1,0:T(8,128)(2,1)} %bitcast.30, bf16[4,1792,128]{2,1,0:T(8,128)(2,1)} %bitcast.32, s32[4,14]{1,0:T(4,128)} %bitcast.36, s32[4,14]{1,0:T(4,128)} %bitcast.38, f32[16,128]{1,0:T(8,128)} %bitcast.34), custom_call_target="tpu_custom_call" | custom-call | bytes 2097152 | tf_op jit(solution)/shard_map/pallas_call | solution.py:96
  12.2 0.1 add_add_fusion
  12.3 0.7 %slice_convert_fusion.2 = s32[1,14]{1,0:T(1,128)S(1)} fusion(bf16[1840,128]{1,0:T(8,128)(2,1)} %shard_map.119.refs_2_.refs_12_), kind=kLoop, calls=%fused_computation.30 | loop fusion | flops 14 | bytes 84 | tf_op jit(solution)/shard_map/convert_element_type | solution.py:403
  13.0 0.7 %fusion.3 = s32[1,14]{1,0:T(1,128)S(1)} fusion(pred[4,14]{1,0:T(4,128)(4,1)S(1)} %reshape.97, s32[]{:T(128)S(6)} %select_n.67, s32[]{:T(128)S(6)} %mul.61, bf16[1840,128]{1,0:T(8,128)(2,1)} %shard_map.119.refs_2_.refs_12_), kind=kLoop, calls=%fused_computation.22 | loop fusion | flops 42 | bytes 106 | tf_op jit(solution)/shard_map/jit(_where)/select_n | solution.py:406
  13.7 0.1 add_add_fusion.2.refs_7_
  13.8 0.1 pad_add_fusion.4.refs_1_.refs_11_
  13.9 0.0 copy-done
  13.9 0.0 copy-done.1
  13.9 1.0 %copy-done.2 = bf16[1840,128]{1,0:T(8,128)(2,1)S(1)} copy-done((bf16[1840,128]{1,0:T(8,128)(2,1)S(1)}, bf16[1840,128]{1,0:T(8,128)(2,1)}, u32[]{:S(2)}) %copy-start.2) | copy-done | bytes 471064
  14.9 1.0 %shard_map.120.refs_14_ = bf16[4,2,2,32,3072]{4,3,2,1,0:T(8,128)(2,1)S(1)} custom-call(s32[3,14]{1,0:T(4,128)S(1)} %pad_add_fusion.refs_0_.refs_10_, s32[2]{0:T(128)S(1)} %pad_add_fusion.4.refs_1_.refs_11_, bf16[1840,128]{1,0:T(8,128)(2,1)S(1)} %copy-done.2, bf16[36,96,128]{2,1,0:T(8,128)(2,1)S(1)} %bitcast.20, bf16[36,96,128]{2,1,0:T(8,128)(2,1)S(1)} %bitcast.24), custom_call_target="tpu_custom_call" | custom-call | flops 44040192 | bytes 3145728 | tf_op jit(solution)/shard_map/pallas_call | solution.py:265
  15.9 0.0 collective-permute-done.refs_2_
  16.0 7.3 %collective-permute-start.1 = (bf16[944,128]{1,0:T(8,128)(2,1)S(1)}, bf16[944,128]{1,0:T(8,128)(2,1)S(1)}, u32[]{:S(2)}, u32[]{:S(2)}) collective-permute-start(bf16[944,128]{1,0:T(8,128)(2,1)S(1)} %copy-done.8), channel_id=1, source_target_pairs={{0,8},{4,12},{8,0},{12,4},{1,9},{5,13},{9,1},{13,5},{2,10},{6,14},... | collective-permute-start | bytes 725000 | tf_op jit(solution)/shard_map/ppermute | solution.py:428
  23.2 1.5 %collective-permute-start.4 = (bf16[944,128]{1,0:T(8,128)(2,1)S(1)}, bf16[944,128]{1,0:T(8,128)(2,1)S(1)}, u32[]{:S(2)}, u32[]{:S(2)}) collective-permute-start(bf16[944,128]{1,0:T(8,128)(2,1)S(1)} %collective-permute-done.refs_2_), channel_id=1, source_target_pairs={{0,2},{2,0},{1,3},{3,1},{4,6},{6,4},{5,7},{7,5},{8,10},{10,8},{9,1... | collective-permute-start | bytes 725000 | tf_op jit(solution)/shard_map/ppermute | solution.py:339
  24.7 0.0 collective-permute-done.5.refs_8_
  24.7 0.5 collective-permute-start.6
  25.3 5.0 %collective-permute-done.1.refs_2_ = bf16[944,128]{1,0:T(8,128)(2,1)S(1)} collective-permute-done((bf16[944,128]{1,0:T(8,128)(2,1)S(1)}, bf16[944,128]{1,0:T(8,128)(2,1)S(1)}, u32[]{:S(2)}, u32[]{:S(2)}) %collective-permute-start.1) | collective-permute-done | bytes 241696 | tf_op jit(solution)/shard_map/ppermute | solution.py:428
  30.3 1.6 %collective-permute-start.2 = (bf16[944,128]{1,0:T(8,128)(2,1)S(1)}, bf16[944,128]{1,0:T(8,128)(2,1)S(1)}, u32[]{:S(2)}, u32[]{:S(2)}) collective-permute-start(bf16[944,128]{1,0:T(8,128)(2,1)S(1)} %collective-permute-done.1.refs_2_), channel_id=1, source_target_pairs={{0,2},{2,0},{1,3},{3,1},{4,6},{6,4},{5,7},{7,5},{8,10},{10,8},{9,1... | collective-permute-start | bytes 725000 | tf_op jit(solution)/shard_map/ppermute | solution.py:339
  31.9 0.1 collective-permute-done.6.refs_9_
  32.0 0.0 collective-permute-done.4.refs_3_
  32.0 0.0 collective-permute-done.3.refs_13_.refs_6_
  32.0 0.0 slice-start.1
  32.0 2.4 %shard_map.121.refs_7_ = bf16[4,2,2,32,3072]{4,3,2,1,0:T(8,128)(2,1)S(1)} custom-call(s32[3,14]{1,0:T(4,128)S(1)} %get-tuple-element.37.refs_0_, s32[3]{0:T(128)S(1)} %get-tuple-element.35.refs_1_, bf16[944,128]{1,0:T(8,128)(2,1)S(1)} %collective-permute-done.refs_2_, ...), custom_call_target="tpu_custom_call", output_to_operand_aliasing={{}: (14, {})} | custom-call | flops 220200960 | bytes 15728640 | tf_op jit(solution)/shard_map/pallas_call | solution.py:265
  34.4 3.4 %collective-permute-done.2.refs_3_ = bf16[944,128]{1,0:T(8,128)(2,1)S(1)} collective-permute-done((bf16[944,128]{1,0:T(8,128)(2,1)S(1)}, bf16[944,128]{1,0:T(8,128)(2,1)S(1)}, u32[]{:S(2)}, u32[]{:S(2)}) %collective-permute-start.2) | collective-permute-done | bytes 241696 | tf_op jit(solution)/shard_map/ppermute | solution.py:339
  37.8 0.0 collective-permute-done.7.refs_9_
  37.8 0.0 slice-done.1
  37.8 0.0 copy-start.4
  37.8 0.0 copy-start.5
  37.8 6.8 %shard_map.122 = (bf16[4,2,2,32,3072]{4,3,2,1,0:T(8,128)(2,1)S(1)}, bf16[16,16,1024]{2,1,0:T(8,128)(2,1)S(1)}) custom-call(s32[3,14]{1,0:T(4,128)S(1)} %get-tuple-element.36.refs_0_, s32[3]{0:T(128)S(1)} %get-tuple-element.34.refs_1_, bf16[944,128]{1,0:T(8,128)(2,1)S(1)} %collective-permute-done.1.refs_2_, ...), custom_call_target="tpu_custom_call", output_to_operand_aliasing={{0}: (7, {})} | custom-call | flops 3309305856 | bytes 12582912 | tf_op jit(solution)/shard_map/pallas_call | solution.py:265
  44.7 17.7 %all_to_all.5 = bf16[16,16,1024]{2,1,0:T(8,128)(2,1)S(1)} all-to-all(bf16[16,16,1024]{2,1,0:T(8,128)(2,1)S(1)} %get-tuple-element.26), channel_id=1, replica_groups=mesh['grp'=2,'band'=4,'var'=2,'sub'=2] {'grp','band','var'}, dimensions={0} | all-to-all | bytes 1048576 | tf_op jit(solution)/shard_map/all_to_all | solution.py:440
  62.4 0.1 convert_reduce_fusion
  62.5 0.1 multiply_reduce_fusion
  62.7 0.1 rsqrt.12
  62.8 0.1 fusion
  62.9 0.6 copy.17
  (24 shorter events, 0.1 us)
Async XLA Ops:
  0.0 9.8 %copy-start.7 = (s32[36,1]{0,1:T(1,128)S(1)}, s32[36,1]{0,1:T(1,128)}, u32[]{:S(2)}) copy-start(s32[36,1]{0,1:T(1,128)} %param.17) | copy-start | bytes 436
  0.0 9.8 %copy-start.6 = (s32[36,1]{0,1:T(1,128)S(1)}, s32[36,1]{0,1:T(1,128)}, u32[]{:S(2)}) copy-start(s32[36,1]{0,1:T(1,128)} %param.13) | copy-start | bytes 436
  2.8 11.1 %copy-start = (bf16[36,4,24,128]{3,2,1,0:T(8,128)(2,1)S(1)}, bf16[36,4,24,128]{3,2,1,0:T(8,128)(2,1)}, u32[]{:S(2)}) copy-start(bf16[36,4,24,128]{3,2,1,0:T(8,128)(2,1)} %param.12) | copy-start | bytes 2654212
  2.8 11.1 %copy-start.1 = (bf16[36,4,24,128]{3,2,1,0:T(8,128)(2,1)S(1)}, bf16[36,4,24,128]{3,2,1,0:T(8,128)(2,1)}, u32[]{:S(2)}) copy-start(bf16[36,4,24,128]{3,2,1,0:T(8,128)(2,1)} %param.16) | copy-start | bytes 2654212
  2.8 35.0 %collective-permute-start.7 = (bf16[3072,1024]{1,0:T(8,128)(2,1)}, bf16[3072,1024]{1,0:T(8,128)(2,1)}, u32[]{:S(2)}, u32[]{:S(2)}) collective-permute-start(bf16[3072,1024]{1,0:T(8,128)(2,1)} %refs_8_.1), channel_id=1, source_target_pairs={{0,1},{1,0},{2,3},{3,2},{4,5},{5,4},{6,7},{7,6},{8,9},{9,8},{10,11... | collective-permute-start | bytes 18874376 | tf_op jit(solution)/shard_map/ppermute | solution.py:339
  3.4 12.6 %collective-permute-start = (bf16[944,128]{1,0:T(8,128)(2,1)}, bf16[944,128]{1,0:T(8,128)(2,1)S(1)}, u32[]{:S(2)}, u32[]{:S(2)}) collective-permute-start(bf16[944,128]{1,0:T(8,128)(2,1)} %get-tuple-element.17), channel_id=1, source_target_pairs={{0,4},{4,8},{8,12},{12,0},{1,5},{5,9},{9,13},{13,1},{2,6},{6,10},{... | collective-permute-start | bytes 725000 | tf_op jit(solution)/shard_map/ppermute | solution.py:392
  6.0 18.7 %collective-permute-start.5 = (bf16[944,128]{1,0:T(8,128)(2,1)}, bf16[944,128]{1,0:T(8,128)(2,1)S(1)}, u32[]{:S(2)}, u32[]{:S(2)}) collective-permute-start(bf16[944,128]{1,0:T(8,128)(2,1)} %get-tuple-element.23), channel_id=1, source_target_pairs={{0,12},{4,0},{8,4},{12,8},{1,13},{5,1},{9,5},{13,9},{2,14},{6,2},{... | collective-permute-start | bytes 725000 | tf_op jit(solution)/shard_map/ppermute | solution.py:392
  8.1 23.9 %collective-permute-start.3 = (bf16[36,96,128]{2,1,0:T(8,128)(2,1)}, bf16[36,96,128]{2,1,0:T(8,128)(2,1)S(1)}, u32[]{:S(2)}, u32[]{:S(2)}) collective-permute-start(bf16[36,96,128]{2,1,0:T(8,128)(2,1)} %get-tuple-element.21), channel_id=1, source_target_pairs={{0,16},{16,0},{1,17},{17,1},{2,18},{18,2},{3,19},{19,3},{4,20},{20... | collective-permute-start | bytes 2654216 | tf_op jit(solution)/shard_map/ppermute | solution.py:339
  10.3 5.6 %copy-start.8 = (bf16[944,128]{1,0:T(8,128)(2,1)S(1)}, bf16[944,128]{1,0:T(8,128)(2,1)}, u32[]{:S(2)}) copy-start(bf16[944,128]{1,0:T(8,128)(2,1)} %get-tuple-element.20) | copy-start | bytes 724996
  13.9 1.0 %copy-start.2 = (bf16[1840,128]{1,0:T(8,128)(2,1)S(1)}, bf16[1840,128]{1,0:T(8,128)(2,1)}, u32[]{:S(2)}) copy-start(bf16[1840,128]{1,0:T(8,128)(2,1)} %shard_map.119.refs_2_.refs_12_) | copy-start | bytes 1413124
  14.9 17.1 %copy-start.3 = (bf16[1840,128]{1,0:T(8,128)(2,1)S(1)}, bf16[1840,128]{1,0:T(8,128)(2,1)}, u32[]{:S(2)}) copy-start(bf16[1840,128]{1,0:T(8,128)(2,1)} %shard_map.119.refs_2_.refs_12_) | copy-start | bytes 1413124
  14.9 22.9 %slice-start = ((s8[6291456]{0:T(1024)(128)(4,1)}), s8[4194304]{0:T(1024)(128)(4,1)S(1)}, s32[]{:S(2)}) async-start(s8[6291456]{0:T(1024)(128)(4,1)} %bitcast.27), calls=%async_computation.1 | async-start | bytes 8388608
  16.0 14.3 %collective-permute-start.1 = (bf16[944,128]{1,0:T(8,128)(2,1)S(1)}, bf16[944,128]{1,0:T(8,128)(2,1)S(1)}, u32[]{:S(2)}, u32[]{:S(2)}) collective-permute-start(bf16[944,128]{1,0:T(8,128)(2,1)S(1)} %copy-done.8), channel_id=1, source_target_pairs={{0,8},{4,12},{8,0},{12,4},{1,9},{5,13},{9,1},{13,5},{2,10},{6,14},... | collective-permute-start | bytes 725000 | tf_op jit(solution)/shard_map/ppermute | solution.py:428
  23.2 8.7 %collective-permute-start.4 = (bf16[944,128]{1,0:T(8,128)(2,1)S(1)}, bf16[944,128]{1,0:T(8,128)(2,1)S(1)}, u32[]{:S(2)}, u32[]{:S(2)}) collective-permute-start(bf16[944,128]{1,0:T(8,128)(2,1)S(1)} %collective-permute-done.refs_2_), channel_id=1, source_target_pairs={{0,2},{2,0},{1,3},{3,1},{4,6},{6,4},{5,7},{7,5},{8,10},{10,8},{9,1... | collective-permute-start | bytes 725000 | tf_op jit(solution)/shard_map/ppermute | solution.py:339
  24.7 7.2 %collective-permute-start.6 = (bf16[944,128]{1,0:T(8,128)(2,1)S(1)}, bf16[944,128]{1,0:T(8,128)(2,1)S(1)}, u32[]{:S(2)}, u32[]{:S(2)}) collective-permute-start(bf16[944,128]{1,0:T(8,128)(2,1)S(1)} %collective-permute-done.5.refs_8_), channel_id=1, source_target_pairs={{0,2},{2,0},{1,3},{3,1},{4,6},{6,4},{5,7},{7,5},{8,10},{10,8},{9,1... | collective-permute-start | bytes 725000 | tf_op jit(solution)/shard_map/ppermute | solution.py:339
  30.3 7.5 %collective-permute-start.2 = (bf16[944,128]{1,0:T(8,128)(2,1)S(1)}, bf16[944,128]{1,0:T(8,128)(2,1)S(1)}, u32[]{:S(2)}, u32[]{:S(2)}) collective-permute-start(bf16[944,128]{1,0:T(8,128)(2,1)S(1)} %collective-permute-done.1.refs_2_), channel_id=1, source_target_pairs={{0,2},{2,0},{1,3},{3,1},{4,6},{6,4},{5,7},{7,5},{8,10},{10,8},{9,1... | collective-permute-start | bytes 725000 | tf_op jit(solution)/shard_map/ppermute | solution.py:339
  32.0 5.8 %slice-start.1 = ((s8[6291456]{0:T(1024)(128)(4,1)}), s8[2097152]{0:T(1024)(128)(4,1)S(1)}, s32[]{:S(2)}) async-start(s8[6291456]{0:T(1024)(128)(4,1)} %bitcast.27), calls=%async_computation.2 | async-start | bytes 4194304
  37.8 24.7 %copy-start.4 = (f32[1024]{0:T(1024)S(1)}, f32[1024]{0:T(1024)}, u32[]{:S(2)}) copy-start(f32[1024]{0:T(1024)} %param.22) | copy-start | bytes 12292
  37.8 24.9 %copy-start.5 = (f32[1024]{0:T(1024)S(1)}, f32[1024]{0:T(1024)}, u32[]{:S(2)}) copy-start(f32[1024]{0:T(1024)} %param.23) | copy-start | bytes 12292
